TPU v7x, 32 devices: a whole 2x2x4 slice. The times are simulated.
32 devices in a mesh: member: 8 (over z, x), region: 4 (over y, core).
Axes of the slice: x: 2, y: 2, z: 4, core: 2. Of those that a mesh axis runs over, the one named last changes fastest.
Arguments:
- ensemble: bfloat16 [1024, 4, 8, 512], P('member', 'region'), may hold values from -6 to 6
- obs_store: bfloat16 [4, 8, 5, 128, 1024], P('region', 'member'), may hold values from -4 to 4
- block_ids: int32 [4, 8, 3], P('region', 'member'), may hold values from 0 to 4, as said below
- block_src: int32 [4, 8, 3], P('region', 'member'), may hold values from 0 to 2, as said below
- block_count: int32 [4, 8], P('region', 'member'), may hold values from 1 to 3, as said below
Outputs:
- analysis: bfloat16 [1024, 4, 8, 512], P('member', 'region')
Inputs may be any that keep to these rules, and one draw needn't show every extreme that they name: `block_ids`: within one patch's list the first 3 entries are distinct store indices. `block_src`: region 0 never names the region below and region 4 - 1 never names the region above. `block_count`: every region has a patch with 3 blocks.
All inputs are finite; a program needn't handle non-finite values.
Results may differ from a plain program's by a relative error of at most 0.0021.
Values may be sent and summed in bfloat16 or wider, within the bound.
No kernel may reach another device: no remote copies, remote signals or barrier semaphores. Data moves between devices by JAX's collectives and lax.ppermute only.
A program may use at most 64 MiB of HBM per device.

v0:
```python
import jax
import jax.numpy as jnp
from jax import lax
from jax.sharding import PartitionSpec as P

K = 1024
OBS_DEV = 5
MAXB = 3


def padded(cells, sides, width):
    for axis, dim in sides:
        count = lax.axis_size(axis)
        ends = count - 1
        head = lax.slice_in_dim(cells, 0, width, axis=dim)
        tail = lax.slice_in_dim(cells, cells.shape[dim] - width, cells.shape[dim], axis=dim)
        cells = jnp.concatenate(
            [
                lax.ppermute(tail, axis, [(i, (i + 1) % count) for i in range(ends)]),
                cells,
                lax.ppermute(head, axis, [((i + 1) % count, i) for i in range(ends)]),
            ],
            axis=dim,
        )
    return cells


def transform(gram_matrix, slab_items):
    members = slab_items.reshape(slab_items.shape[0], slab_items.shape[3])
    first_term = jnp.dot(gram_matrix, members, preferred_element_type=jnp.float32).astype(
        jnp.bfloat16
    )
    second_term = jnp.dot(gram_matrix, first_term, preferred_element_type=jnp.float32)
    fresh = members.astype(jnp.float32) - first_term.astype(jnp.float32) + second_term
    return fresh.astype(jnp.bfloat16).reshape(slab_items.shape)


def shards(ensemble, obs_store, block_ids, block_src, block_count):
    own_ids = block_ids[0, 0]
    own_src = block_src[0, 0]
    rims = padded(obs_store, (("region", 0),), 1)
    pooled = rims.reshape(3 * OBS_DEV, rims.shape[3], rims.shape[4])
    chosen = jnp.take(pooled, own_src * OBS_DEV + own_ids, axis=0)
    live_slots = jnp.arange(MAXB, dtype=jnp.int32) < block_count[0, 0]
    chosen = jnp.where(live_slots[:, None, None], chosen, jnp.zeros((), chosen.dtype))
    stacked = chosen.reshape(-1, chosen.shape[2])
    gram_full = lax.dot_general(
        stacked, stacked, (((0,), (0,)), ((), ())), preferred_element_type=jnp.float32
    )
    gram_matrix = (gram_full / (2.0 * K)).astype(jnp.bfloat16)
    moved = transform(
        gram_matrix, lax.all_to_all(ensemble, "member", split_axis=2, concat_axis=0, tiled=True)
    )
    return lax.all_to_all(moved, "member", split_axis=0, concat_axis=2, tiled=True)


def solution(mesh):
    return jax.shard_map(
        shards,
        mesh=mesh,
        in_specs=(
            P("member", "region", None, None),
            P("region", "member", None, None, None),
            P("region", "member", None),
            P("region", "member", None),
            P("region", "member"),
        ),
        out_specs=P("member", "region", None, None),
        check_vma=False,
    )
```

profile of v0, /device:TPU:0, one launch (start us, length us, event | category | flops | bytes accessed | tf_op | source)
XLA Modules:
  0.0 80.1 jit_solution(11419266490828619703)
XLA Ops:
  0.0 1.4 %collective-permute-start.1 = (bf16[1,1,5,128,1024]{4,3,2,1,0:T(8,128)(2,1)}, bf16[1,1,5,128,1024]{4,3,2,1,0:T(8,128)(2,1)}, u32[]{:S(2)}, u32[]{:S(2)}) collective-permute-start(bf16[1,1,5,128,1024]{4,3,2,1,0:T(8,128)(2,1)} %param.6), channel_id=1, source_target_pairs={{1,0},{2,1},{3,2},{5,4},{6,5},{7,6},{9,8},{10,9},{11,10},{13,12},{... | collective-permute-start | bytes 3932168 | tf_op jit(solution)/shard_map/ppermute | solution.py:21
  1.4 4.1 %collective-permute-start = (bf16[1,1,5,128,1024]{4,3,2,1,0:T(8,128)(2,1)}, bf16[1,1,5,128,1024]{4,3,2,1,0:T(8,128)(2,1)}, u32[]{:S(2)}, u32[]{:S(2)}) collective-permute-start(bf16[1,1,5,128,1024]{4,3,2,1,0:T(8,128)(2,1)} %param.6), channel_id=1, source_target_pairs={{0,1},{1,2},{2,3},{4,5},{5,6},{6,7},{8,9},{9,10},{10,11},{12,13},{... | collective-permute-start | bytes 3932168 | tf_op jit(solution)/shard_map/ppermute | solution.py:19
  5.6 2.5 %copy.22 = bf16[128,1,8,512]{3,0,1,2:T(8,128)(2,1)} copy(bf16[128,1,8,512]{3,2,1,0:T(8,128)(2,1)} %param.5) | data formatting | bytes 2097152 | tf_op args[0]
  8.1 7.3 %all-to-all-start = ((bf16[128,1,8,512]{3,0,1,2:T(8,128)(2,1)}), bf16[128,1,8,512]{3,0,1,2:T(8,128)(2,1)S(1)}, u32[]{:S(2)}, u32[]{:S(2)}) async-start(bf16[128,1,8,512]{3,0,1,2:T(8,128)(2,1)} %copy.22), calls=%async_computation | async-start | bytes 2097152 | tf_op jit(solution)/shard_map/all_to_all | solution.py:52
  16.0 0.0 copy-done.1
  16.0 0.0 copy-done.2
  16.1 0.0 collective-permute-done.1
  16.1 0.0 collective-permute-done
  16.1 3.4 %pad_maximum_fusion = bf16[3,1,5,128,1024]{4,3,2,1,0:T(8,128)(2,1)} fusion(bf16[1,1,5,128,1024]{4,3,2,1,0:T(8,128)(2,1)} %collective-permute-done.1, bf16[1,1,5,128,1024]{4,3,2,1,0:T(8,128)(2,1)S(1)} %copy-done, bf16[1,1,5,128,1024]{4,3,2,1,0:T(8,128)(2,1)} %collective-permute-done), kind=kLoop, calls=%fused_computation.3 | loop fusion | flops 3932160 | bytes 7864320 | tf_op jit(solution)/shard_map/concatenate | solution.py:17
  19.5 2.7 %gather_fusion = bf16[3,128,1024]{2,1,0:T(8,128)(2,1)S(1)} fusion(bf16[15,128,1024]{2,1,0:T(8,128)(2,1)} %bitcast.30, s32[1024]{0:T(1024)S(1)} %pad_clamp_fusion), kind=kCustom, calls=%fused_computation | custom fusion | bytes 1572876 | tf_op jit(solution)/shard_map/jit(_take)/gather | solution.py:43
  22.2 2.7 %fusion = bf16[1024,1024]{1,0:T(8,128)(2,1)} fusion(bf16[3,128,1024]{2,1,0:T(8,128)(2,1)S(1)} %gather_fusion, pred[3]{0:T(512)(128)(4,1)S(1)} %get-tuple-element.5, pred[3]{0:T(512)(128)(4,1)S(1)} %get-tuple-element.6), kind=kOutput, calls=%fused_computation.2 | convolution fusion | flops 808189952 | bytes 2883590 | tf_op jit(solution)/shard_map/dot_general | solution.py:47
  25.0 16.4 %all-to-all-done = bf16[128,1,8,512]{3,0,1,2:T(8,128)(2,1)S(1)} async-done(((bf16[128,1,8,512]{3,0,1,2:T(8,128)(2,1)}), bf16[128,1,8,512]{3,0,1,2:T(8,128)(2,1)S(1)}, u32[]{:S(2)}, u32[]{:S(2)}) %all-to-all-start) | async-done | bytes 1048608 | tf_op jit(solution)/shard_map/all_to_all | solution.py:52
  41.3 0.6 copy.31
  41.9 0.3 copy.24
  42.2 1.2 %convolution_convert_fusion = bf16[1024,512]{1,0:T(8,128)(2,1)S(1)} fusion(bf16[1024,1024]{1,0:T(8,128)(2,1)S(1)} %copy-done.3, bf16[1024,512]{1,0:T(8,128)(2,1)S(1)} %bitcast.33), kind=kOutput, calls=%fused_computation.5 | convolution fusion | flops 1074266112 | bytes 4194304 | tf_op jit(solution)/shard_map/dot_general | solution.py:30
  43.5 0.3 copy-done.4
  43.8 1.3 %fusion.1 = bf16[1024,1,1,512]{3,0,2,1:T(8,128)(2,1)S(1)} fusion(bf16[1024,1024]{1,0:T(8,128)(2,1)S(1)} %copy-done.4, bf16[1024,512]{1,0:T(8,128)(2,1)S(1)} %convolution_convert_fusion, bf16[1024,512]{1,0:T(8,128)(2,1)S(1)} %bitcast.34), kind=kOutput, calls=%fused_computation.6 | convolution fusion | flops 1076363264 | bytes 5242880 | tf_op jit(solution)/shard_map/dot_general | solution.py:33
  45.1 0.5 broadcast.63
  45.6 1.5 %reduce = bf16[1024,512]{1,0:T(8,128)(2,1)S(1)} reduce(bf16[1024,1,1,512]{3,0,2,1:T(8,128)(2,1)S(1)} %fusion.1, bf16[]{:T(256)} %broadcast.63), dimensions={1,2}, to_apply=%copy.26.reduce_sub_computation | reduce | bytes 2097154 | tf_op jit(solution)/shard_map/reshape | solution.py:35
  47.1 0.8 reshape.70
  47.9 29.3 %all_to_all.33 = bf16[8,2,32768]{2,1,0:T(2,128)(2,1)S(1)} all-to-all(bf16[8,2,32768]{2,1,0:T(2,128)(2,1)S(1)} %reshape.70), channel_id=1, replica_groups=mesh['member'=8,'region'=4] {'member'}, dimensions={0} | all-to-all | bytes 2097152 | tf_op jit(solution)/shard_map/all_to_all | solution.py:54
  77.2 1.0 %reshape.71 = bf16[1024,1,1,512]{3,2,1,0:T(2,128)(2,1)S(1)} reshape(bf16[8,2,32768]{2,1,0:T(2,128)(2,1)S(1)} %all_to_all.33) | data formatting | bytes 2097152
  78.3 0.3 copy.29
  78.5 1.5 %copy.27 = bf16[128,1,8,512]{3,2,1,0:T(8,128)(2,1)} copy(bf16[128,1,8,512]{3,0,2,1:T(8,128)(2,1)S(1)} %bitcast.31) | data formatting | bytes 2097152 | tf_op jit(solution)/shard_map/all_to_all | solution.py:54
  (10 shorter events, 0.0 us)
Async XLA Ops:
  0.0 16.1 %copy-start = (bf16[1,1,5,128,1024]{4,3,2,1,0:T(8,128)(2,1)S(1)}, bf16[1,1,5,128,1024]{4,3,2,1,0:T(8,128)(2,1)}, u32[]{:S(2)}) copy-start(bf16[1,1,5,128,1024]{4,3,2,1,0:T(8,128)(2,1)} %param.6) | copy-start | bytes 3932164
  0.0 16.0 %copy-start.1 = (s32[1,1,3]{2,1,0:T(1,128)S(1)}, s32[1,1,3]{2,1,0:T(1,128)}, u32[]{:S(2)}) copy-start(s32[1,1,3]{2,1,0:T(1,128)} %param.7) | copy-start | bytes 40
  0.0 16.0 %copy-start.2 = (s32[1,1,3]{2,1,0:T(1,128)S(1)}, s32[1,1,3]{2,1,0:T(1,128)}, u32[]{:S(2)}) copy-start(s32[1,1,3]{2,1,0:T(1,128)} %param.8) | copy-start | bytes 40
  0.0 16.1 %collective-permute-start.1 = (bf16[1,1,5,128,1024]{4,3,2,1,0:T(8,128)(2,1)}, bf16[1,1,5,128,1024]{4,3,2,1,0:T(8,128)(2,1)}, u32[]{:S(2)}, u32[]{:S(2)}) collective-permute-start(bf16[1,1,5,128,1024]{4,3,2,1,0:T(8,128)(2,1)} %param.6), channel_id=1, source_target_pairs={{1,0},{2,1},{3,2},{5,4},{6,5},{7,6},{9,8},{10,9},{11,10},{13,12},{... | collective-permute-start | bytes 3932168 | tf_op jit(solution)/shard_map/ppermute | solution.py:21
  1.4 14.6 %collective-permute-start = (bf16[1,1,5,128,1024]{4,3,2,1,0:T(8,128)(2,1)}, bf16[1,1,5,128,1024]{4,3,2,1,0:T(8,128)(2,1)}, u32[]{:S(2)}, u32[]{:S(2)}) collective-permute-start(bf16[1,1,5,128,1024]{4,3,2,1,0:T(8,128)(2,1)} %param.6), channel_id=1, source_target_pairs={{0,1},{1,2},{2,3},{4,5},{5,6},{6,7},{8,9},{9,10},{10,11},{12,13},{... | collective-permute-start | bytes 3932168 | tf_op jit(solution)/shard_map/ppermute | solution.py:19
  8.1 33.2 %all-to-all-start = ((bf16[128,1,8,512]{3,0,1,2:T(8,128)(2,1)}), bf16[128,1,8,512]{3,0,1,2:T(8,128)(2,1)S(1)}, u32[]{:S(2)}, u32[]{:S(2)}) async-start(bf16[128,1,8,512]{3,0,1,2:T(8,128)(2,1)} %copy.22), calls=%async_computation | async-start | bytes 2097152 | tf_op jit(solution)/shard_map/all_to_all | solution.py:52
  25.0 17.3 %copy-start.3 = (bf16[1024,1024]{1,0:T(8,128)(2,1)S(1)}, bf16[1024,1024]{1,0:T(8,128)(2,1)}, u32[]{:S(2)}) copy-start(bf16[1024,1024]{1,0:T(8,128)(2,1)} %fusion) | copy-start | bytes 6291460
  42.2 1.6 %copy-start.4 = (bf16[1024,1024]{1,0:T(8,128)(2,1)S(1)}, bf16[1024,1024]{1,0:T(8,128)(2,1)}, u32[]{:S(2)}) copy-start(bf16[1024,1024]{1,0:T(8,128)(2,1)} %fusion) | copy-start | bytes 6291460
where the time goes:
time: 80.5 us; the launch traced here: 80.1 us
  blocking collectives  29.3 us (36%)
  waiting for transfers between devices  16.4 us (20%)
  starting transfers between devices  12.8 us (16%)
  local copies, waits for them, and re-layouts  10.6 us (13%)
  matrix products  5.24 us (7%)
  other arithmetic  4.9 us (6%)
    all_to_all x1, blocking collectives, shards(): lax.all_to_all(moved, 'member', split_axis=0, concat_axis=2, tiled=True)  29.3 us
    all_to_all x1, waiting for transfers between devices, shards(): lax.all_to_all(ensemble, 'member', split_axis=2, concat_axis=0, tiled=True)  16.4 us
    all_to_all x1, starting transfers between devices, shards(): lax.all_to_all(ensemble, 'member', split_axis=2, concat_axis=0, tiled=True)  7.27 us
    unnamed x14, local copies, waits for them, and re-layouts  4.97 us
    ppermute x1, starting transfers between devices, padded(): lax.ppermute(tail, axis, [(i, (i + 1) % count) for i in range(ends)])  4.14 us
    concatenate x1, other arithmetic, padded(): jnp.concatenate([lax.ppermute(tail, axis, [(i, (i + 1) % count) for i in...  3.42 us
    dot_general x1, matrix products, shards(): lax.dot_general(stacked, stacked, (((0,), (0,)), ((), ())), preferred_ele...  2.73 us
    gather x1, local copies, waits for them, and re-layouts, shards(): chosen = jnp.take(pooled, own_src * OBS_DEV + own_ids, axis=0)  2.71 us
  transfers between devices with their start and end apart: 3, of which 1 were waited for; matrix products, arithmetic and copies ran while one was open for 14% of the time, Pallas kernels for 0%

commit v1 on v0

v1 whole, which is shorter than its diff:
```python
import functools

import jax
import jax.numpy as jnp
from jax import lax
from jax.experimental import pallas as pl
from jax.experimental.pallas import tpu as pltpu
from jax.sharding import PartitionSpec as P

CHUNKS = 2
LIMIT = 40 * 1024 * 1024


def rows_per_group(rows, patches):
    return min(rows, max(16, 256 // patches))


def shuffle_matrix(height, outer, inner):
    row = lax.broadcasted_iota(jnp.int32, (height, height), 0)
    column = lax.broadcasted_iota(jnp.int32, (height, height), 1)
    source = lax.rem(row, inner) * outer + lax.div(row, inner)
    return jnp.where(column == source, 1.0, 0.0).astype(jnp.bfloat16)


def split_kernel(patches, members_ref, *out_refs):
    rows = out_refs[0].shape[1]
    width = out_refs[0].shape[2]
    group = rows_per_group(rows, patches)
    height = group * patches
    shuffle = shuffle_matrix(height, patches, group)
    for step in range(rows // group):
        block = members_ref[step * height : (step + 1) * height, :]
        moved = jnp.dot(shuffle, block, preferred_element_type=jnp.float32)
        moved = moved.astype(jnp.bfloat16).reshape(patches, group, block.shape[1])
        for chunk, out_ref in enumerate(out_refs):
            out_ref[:, step * group : (step + 1) * group, :] = moved[
                :, :, chunk * width : (chunk + 1) * width
            ]


def merge_kernel(patches, *refs):
    chunk_refs, out_ref = refs[:-1], refs[-1]
    rows = chunk_refs[0].shape[1]
    width = chunk_refs[0].shape[2]
    group = rows_per_group(rows, patches)
    height = group * patches
    shuffle = shuffle_matrix(height, group, patches)
    for step in range(rows // group):
        for chunk, chunk_ref in enumerate(chunk_refs):
            block = chunk_ref[:, step * group : (step + 1) * group, :].reshape(height, width)
            moved = jnp.dot(shuffle, block, preferred_element_type=jnp.float32)
            out_ref[
                step * height : (step + 1) * height, chunk * width : (chunk + 1) * width
            ] = moved.astype(jnp.bfloat16)


def gram_kernel(scale, ids_ref, src_ref, count_ref, below, own, above, gram_ref, stacked, sem):
    slots = ids_ref.shape[0]
    rows = own.shape[1]
    for slot in range(slots):
        live = slot < count_ref[0]
        target = stacked.at[pl.ds(slot * rows, rows), :]
        for code, store in enumerate((below, own, above)):

            @pl.when(live & (src_ref[slot] == code))
            def _():
                pltpu.make_async_copy(store.at[ids_ref[slot]], target, sem.at[slot]).start()

        @pl.when(jnp.logical_not(live))
        def _():
            target[...] = jnp.zeros(target.shape, target.dtype)

    for slot in range(slots):

        @pl.when(slot < count_ref[0])
        def _():
            target = stacked.at[pl.ds(slot * rows, rows), :]
            pltpu.make_async_copy(own.at[0], target, sem.at[slot]).wait()

    size = gram_ref.shape[0]
    part = min(size, 256)
    for step in range(size // part):
        block = lax.dot_general(
            stacked[:, step * part : (step + 1) * part],
            stacked[...],
            (((0,), (0,)), ((), ())),
            preferred_element_type=jnp.float32,
        )
        gram_ref[step * part : (step + 1) * part, :] = (block * scale).astype(jnp.bfloat16)


def transform_kernel(gram_ref, members_ref, out_ref, first):
    size = gram_ref.shape[0]
    part = min(size, 256)
    for step in range(size // part):
        here = slice(step * part, (step + 1) * part)
        first[here, :] = jnp.dot(
            gram_ref[here, :], members_ref[...], preferred_element_type=jnp.float32
        ).astype(jnp.bfloat16)
    for step in range(size // part):
        here = slice(step * part, (step + 1) * part)
        second = jnp.dot(gram_ref[here, :], first[...], preferred_element_type=jnp.float32)
        fresh = members_ref[here, :].astype(jnp.float32) - first[here, :].astype(jnp.float32)
        out_ref[here, :] = (fresh + second).astype(jnp.bfloat16)


def vmem():
    return pl.BlockSpec(memory_space=pltpu.VMEM)


def params():
    return pltpu.CompilerParams(vmem_limit_bytes=LIMIT)


def cost(flops, nbytes):
    return pl.CostEstimate(flops=flops, bytes_accessed=nbytes, transcendentals=0)


def neighbours(store):
    count = lax.axis_size("region")
    up = [(i, i + 1) for i in range(count - 1)]
    down = [(i + 1, i) for i in range(count - 1)]
    return lax.ppermute(store, "region", up), lax.ppermute(store, "region", down)


def shards(ensemble, obs_store, block_ids, block_src, block_count):
    rows, _, patches, values = ensemble.shape
    store = obs_store.reshape(obs_store.shape[2:])
    size = store.shape[2]
    slots = block_ids.shape[2]
    width = values // CHUNKS
    below, above = neighbours(store)

    pieces = pl.pallas_call(
        functools.partial(split_kernel, patches),
        out_shape=[jax.ShapeDtypeStruct((patches, rows, width), jnp.bfloat16)] * CHUNKS,
        in_specs=[vmem()],
        out_specs=[vmem()] * CHUNKS,
        compiler_params=params(),
        cost_estimate=cost(2 * 256 * rows * patches * values, 4 * rows * patches * values),
        name="split",
    )(ensemble.reshape(rows * patches, values))
    arrived = [
        lax.all_to_all(piece, "member", split_axis=0, concat_axis=0, tiled=True)
        for piece in pieces
    ]

    smem = pl.BlockSpec(memory_space=pltpu.SMEM)
    anywhere = pl.BlockSpec(memory_space=pl.ANY)
    gram = pl.pallas_call(
        functools.partial(gram_kernel, 1.0 / (2.0 * size)),
        out_shape=jax.ShapeDtypeStruct((size, size), jnp.bfloat16),
        in_specs=[smem] * 3 + [anywhere] * 3,
        out_specs=vmem(),
        scratch_shapes=[
            pltpu.VMEM((slots * store.shape[1], size), jnp.bfloat16),
            pltpu.SemaphoreType.DMA((slots,)),
        ],
        compiler_params=params(),
        cost_estimate=cost(2 * slots * store.shape[1] * size * size, 4 * size * size),
        name="gram",
    )(
        block_ids.reshape(slots),
        block_src.reshape(slots),
        block_count.reshape(1),
        below,
        store,
        above,
    )

    returned = []
    for piece in arrived:
        moved = pl.pallas_call(
            transform_kernel,
            out_shape=jax.ShapeDtypeStruct((size, width), jnp.bfloat16),
            in_specs=[vmem()] * 2,
            out_specs=vmem(),
            scratch_shapes=[pltpu.VMEM((size, width), jnp.bfloat16)],
            compiler_params=params(),
            cost_estimate=cost(4 * size * size * width, 2 * size * size + 4 * size * width),
            name="transform",
        )(gram, piece.reshape(size, width))
        returned.append(
            lax.all_to_all(
                moved.reshape(patches, rows, width),
                "member",
                split_axis=0,
                concat_axis=0,
                tiled=True,
            )
        )

    fresh = pl.pallas_call(
        functools.partial(merge_kernel, patches),
        out_shape=jax.ShapeDtypeStruct((rows * patches, values), jnp.bfloat16),
        in_specs=[vmem()] * CHUNKS,
        out_specs=vmem(),
        compiler_params=params(),
        cost_estimate=cost(2 * 256 * rows * patches * values, 4 * rows * patches * values),
        name="merge",
    )(*returned)
    return fresh.reshape(ensemble.shape)


def solution(mesh):
    return jax.shard_map(
        shards,
        mesh=mesh,
        in_specs=(
            P("member", "region", None, None),
            P("region", "member", None, None, None),
            P("region", "member", None),
            P("region", "member", None),
            P("region", "member"),
        ),
        out_specs=P("member", "region", None, None),
        check_vma=False,
    )
```

time: 80.5 us -> 81.3 us (level)
  waiting for transfers between devices: 16.4 us -> 30.1 us
  blocking collectives: 29.3 us -> 18.1 us
  Pallas kernels: 0 us -> 10.1 us
  local copies, waits for them, and re-layouts: 10.6 us -> 3.73 us
  matrix products: 5.24 us -> 0 us
  starting transfers between devices: 12.8 us -> 18 us
  other arithmetic: 4.9 us -> 0 us
    all_to_all x1 -> x3, waiting for transfers between devices: 16.4 us -> 30.1 us  [the longest x2 17.9 us: shards(): lax.all_to_all(piece, 'member', split_axis=0, concat_axis=0, tiled=True)]
    all_to_all x1, blocking collectives: 29.3 us -> 18.1 us  [shards(): lax.all_to_all(moved.reshape(patches, rows, width), 'member', split_axis=...]
    pallas_call x0 -> x5, Pallas kernels: none -> 10.1 us  [the longest x2 4.4 us: shards(): pl.pallas_call(transform_kernel, out_shape=jax.ShapeDtypeStruct((size, wi...]
    all_to_all x1 -> x3, starting transfers between devices: 7.27 us -> 15.1 us  [the longest x2 11.5 us: shards(): lax.all_to_all(piece, 'member', split_axis=0, concat_axis=0, tiled=True)]
    dot_general x3 -> x0, matrix products: 5.24 us -> none  [the longest x1 2.73 us: shards(): lax.dot_general(stacked, stacked, (((0,), (0,)), ((), ())), preferred_ele...]
    concatenate x1 -> x0, other arithmetic: 3.42 us -> none  [padded(): jnp.concatenate([lax.ppermute(tail, axis, [(i, (i + 1) % count) for i in...]
    ppermute x2, starting transfers between devices: 5.55 us -> 2.83 us  [the longest x1 1.54 us: neighbours(): lax.ppermute(store, 'region', up)]
    gather x1 -> x0, local copies, waits for them, and re-layouts: 2.71 us -> none  [shards(): chosen = jnp.take(pooled, own_src * OBS_DEV + own_ids, axis=0)]
  transfers between devices with their start and end apart: 3 -> 5, of which waited for: 1 -> 3; matrix products, arithmetic and copies ran while one was open for 14% -> 0% of each run, Pallas kernels for 0% -> 9%
where the time goes in v1:
time: 81.3 us; the launch traced here: 80.7 us
  waiting for transfers between devices  30.1 us (37%)
  blocking collectives  18.1 us (22%)
  starting transfers between devices  18 us (22%)
  Pallas kernels  10.1 us (12%)
  local copies, waits for them, and re-layouts  3.73 us (5%)
    all_to_all x1, blocking collectives, shards(): lax.all_to_all(moved.reshape(patches, rows, width), 'member', split_axis=...  18.1 us
    all_to_all x2, waiting for transfers between devices, shards(): lax.all_to_all(piece, 'member', split_axis=0, concat_axis=0, tiled=True)  17.9 us
    all_to_all x1, waiting for transfers between devices, shards(): lax.all_to_all(moved.reshape(patches, rows, width), 'member', split_axis=...  12.2 us
    all_to_all x2, starting transfers between devices, shards(): lax.all_to_all(piece, 'member', split_axis=0, concat_axis=0, tiled=True)  11.5 us
    pallas_call x2, Pallas kernels, shards(): pl.pallas_call(transform_kernel, out_shape=jax.ShapeDtypeStruct((size, wi...  4.4 us
    unnamed x16, local copies, waits for them, and re-layouts  3.73 us
    all_to_all x1, starting transfers between devices, shards(): lax.all_to_all(moved.reshape(patches, rows, width), 'member', split_axis=...  3.6 us
    pallas_call x1, Pallas kernels, shards(): pl.pallas_call(functools.partial(gram_kernel, 1.0 / (2.0 * size)), out_sh...  2.82 us
  transfers between devices with their start and end apart: 5, of which 3 were waited for; matrix products, arithmetic and copies ran while one was open for 0% of the time, Pallas kernels for 9%

profile of v1, /device:TPU:0, one launch (start us, length us, event | category | flops | bytes accessed | tf_op | source)
XLA Modules:
  0.0 80.7 jit_solution(7361328347045163523)
XLA Ops:
  0.0 1.3 %copy-done.3 = bf16[128,1,8,512]{3,2,1,0:T(8,128)(2,1)S(1)} copy-done((bf16[128,1,8,512]{3,2,1,0:T(8,128)(2,1)S(1)}, bf16[128,1,8,512]{3,2,1,0:T(8,128)(2,1)}, u32[]{:S(2)}) %copy-start.3) | copy-done | bytes 1048600
  1.3 1.4 %split.1 = (bf16[8,128,256]{2,1,0:T(8,128)(2,1)}, bf16[8,128,256]{2,1,0:T(8,128)(2,1)}) custom-call(bf16[1024,512]{1,0:T(8,128)(2,1)S(1)} %bitcast.16), custom_call_target="tpu_custom_call" | custom-call | flops 268435456 | bytes 2097152 | tf_op jit(solution)/shard_map/split/pallas_call | solution.py:134
  2.8 7.4 %all-to-all-start = ((bf16[8,128,256]{2,1,0:T(8,128)(2,1)}), bf16[8,128,256]{2,1,0:T(8,128)(2,1)S(1)}, u32[]{:S(2)}, u32[]{:S(2)}) async-start(bf16[8,128,256]{2,1,0:T(8,128)(2,1)} %get-tuple-element.7), calls=%async_computation | async-start | bytes 1048576 | tf_op jit(solution)/shard_map/all_to_all | solution.py:144
  10.1 0.0 copy-done
  10.1 1.5 %collective-permute-start = (bf16[5,128,1024]{2,1,0:T(8,128)(2,1)S(1)}, bf16[5,128,1024]{2,1,0:T(8,128)(2,1)S(1)}, u32[]{:S(2)}, u32[]{:S(2)}) collective-permute-start(bf16[5,128,1024]{2,1,0:T(8,128)(2,1)S(1)} %bitcast.13), channel_id=1, source_target_pairs={{0,1},{1,2},{2,3},{4,5},{5,6},{6,7},{8,9},{9,10},{10,11},{12,13},{... | collective-permute-start | bytes 3932168 | tf_op jit(solution)/shard_map/ppermute | solution.py:123
  11.7 1.3 %collective-permute-start.1 = (bf16[5,128,1024]{2,1,0:T(8,128)(2,1)S(1)}, bf16[5,128,1024]{2,1,0:T(8,128)(2,1)}, u32[]{:S(2)}, u32[]{:S(2)}) collective-permute-start(bf16[5,128,1024]{2,1,0:T(8,128)(2,1)S(1)} %bitcast.14), channel_id=1, source_target_pairs={{1,0},{2,1},{3,2},{5,4},{6,5},{7,6},{9,8},{10,9},{11,10},{13,12},{... | collective-permute-start | bytes 3932168 | tf_op jit(solution)/shard_map/ppermute | solution.py:123
  13.0 11.6 %all-to-all-done = bf16[8,128,256]{2,1,0:T(8,128)(2,1)S(1)} async-done(((bf16[8,128,256]{2,1,0:T(8,128)(2,1)}), bf16[8,128,256]{2,1,0:T(8,128)(2,1)S(1)}, u32[]{:S(2)}, u32[]{:S(2)}) %all-to-all-start) | async-done | bytes 524320 | tf_op jit(solution)/shard_map/all_to_all | solution.py:144
  24.6 4.2 %all-to-all-start.2 = ((bf16[8,128,256]{2,1,0:T(8,128)(2,1)}), bf16[8,128,256]{2,1,0:T(8,128)(2,1)}, u32[]{:S(2)}, u32[]{:S(2)}) async-start(bf16[8,128,256]{2,1,0:T(8,128)(2,1)} %get-tuple-element.8), calls=%async_computation.2 | async-start | bytes 1048576 | tf_op jit(solution)/shard_map/all_to_all | solution.py:144
  29.4 0.0 collective-permute-done.below
  29.4 0.0 copy-start.1
  29.5 1.1 %copy-done.1 = bf16[5,128,1024]{2,1,0:T(8,128)(2,1)} copy-done((bf16[5,128,1024]{2,1,0:T(8,128)(2,1)}, bf16[5,128,1024]{2,1,0:T(8,128)(2,1)S(1)}, u32[]{:S(2)}) %copy-start.1) | copy-done | bytes 1310744
  30.5 0.0 collective-permute-done.1.above
  30.5 0.0 copy-done.4
  30.5 0.0 copy-done.7
  30.6 0.0 copy-start.2
  30.6 1.3 %copy-done.2 = bf16[5,128,1024]{2,1,0:T(8,128)(2,1)S(1)} copy-done((bf16[5,128,1024]{2,1,0:T(8,128)(2,1)S(1)}, bf16[5,128,1024]{2,1,0:T(8,128)(2,1)}, u32[]{:S(2)}) %copy-start.2) | copy-done | bytes 1310744
  31.9 2.8 %gram.1.gram_ref = bf16[1024,1024]{1,0:T(8,128)(2,1)S(1)} custom-call(s32[3]{0:T(128)S(1)} %bitcast.19, s32[3]{0:T(128)S(1)} %bitcast.20, s32[1]{0:T(128)} %bitcast.12.count_ref, bf16[5,128,1024]{2,1,0:T(8,128)(2,1)S(1)} %copy-done.2, bf16[5,128,1024]{2,1,0:T(8,128)(2,1)S(1)} %bitcast.15, bf16[5,128,1024]{2,1,0:T(8,128)(2,1)} %collective-permute-done.1.above), custom_call_target="tpu_custom_call" | custom-call | flops 805306368 | bytes 4194304 | tf_op jit(solution)/shard_map/gram/pallas_call | solution.py:150
  34.7 2.1 %transform.2 = bf16[1024,256]{1,0:T(8,128)(2,1)} custom-call(bf16[1024,1024]{1,0:T(8,128)(2,1)S(1)} %gram.1.gram_ref, bf16[1024,256]{1,0:T(8,128)(2,1)S(1)} %bitcast.17), custom_call_target="tpu_custom_call" | custom-call | flops 1073741824 | bytes 3145728 | tf_op jit(solution)/shard_map/transform/pallas_call | solution.py:173
  36.8 6.3 %all-to-all-done.2 = bf16[8,128,256]{2,1,0:T(8,128)(2,1)} async-done(((bf16[8,128,256]{2,1,0:T(8,128)(2,1)}), bf16[8,128,256]{2,1,0:T(8,128)(2,1)}, u32[]{:S(2)}, u32[]{:S(2)}) %all-to-all-start.2) | async-done | bytes 524320 | tf_op jit(solution)/shard_map/all_to_all | solution.py:144
  43.1 3.6 %all-to-all-start.1 = ((bf16[8,128,256]{2,1,0:T(8,128)(2,1)}), bf16[8,128,256]{2,1,0:T(8,128)(2,1)S(1)}, u32[]{:S(2)}, u32[]{:S(2)}) async-start(bf16[8,128,256]{2,1,0:T(8,128)(2,1)} %bitcast.6), calls=%async_computation.1 | async-start | bytes 1048576 | tf_op jit(solution)/shard_map/all_to_all | solution.py:184
  46.7 2.3 %transform.3 = bf16[1024,256]{1,0:T(8,128)(2,1)S(1)} custom-call(bf16[1024,1024]{1,0:T(8,128)(2,1)S(1)} %gram.1.gram_ref, bf16[1024,256]{1,0:T(8,128)(2,1)} %bitcast.7.members_ref), custom_call_target="tpu_custom_call" | custom-call | flops 1073741824 | bytes 3145728 | tf_op jit(solution)/shard_map/transform/pallas_call | solution.py:173
  49.0 12.2 %all-to-all-done.1.refs_0_ = bf16[8,128,256]{2,1,0:T(8,128)(2,1)S(1)} async-done(((bf16[8,128,256]{2,1,0:T(8,128)(2,1)}), bf16[8,128,256]{2,1,0:T(8,128)(2,1)S(1)}, u32[]{:S(2)}, u32[]{:S(2)}) %all-to-all-start.1) | async-done | bytes 524320 | tf_op jit(solution)/shard_map/all_to_all | solution.py:184
  61.2 18.1 %all_to_all.20.refs_1_ = bf16[8,128,256]{2,1,0:T(8,128)(2,1)S(1)} all-to-all(bf16[8,128,256]{2,1,0:T(8,128)(2,1)S(1)} %bitcast.18), channel_id=1, replica_groups=mesh['member'=8,'region'=4] {'member'}, dimensions={0} | all-to-all | bytes 1048576 | tf_op jit(solution)/shard_map/all_to_all | solution.py:184
  79.3 1.4 %merge.1 = bf16[1024,512]{1,0:T(8,128)(2,1)} custom-call(bf16[8,128,256]{2,1,0:T(8,128)(2,1)S(1)} %all-to-all-done.1.refs_0_, bf16[8,128,256]{2,1,0:T(8,128)(2,1)S(1)} %all_to_all.20.refs_1_), custom_call_target="tpu_custom_call" | custom-call | flops 268435456 | bytes 2097152 | tf_op jit(solution)/shard_map/merge/pallas_call | solution.py:193
  (8 shorter events, 0.0 us)
Async XLA Ops:
  0.0 10.1 %copy-start = (bf16[1,1,5,128,1024]{4,3,2,1,0:T(8,128)(2,1)S(1)}, bf16[1,1,5,128,1024]{4,3,2,1,0:T(8,128)(2,1)}, u32[]{:S(2)}) copy-start(bf16[1,1,5,128,1024]{4,3,2,1,0:T(8,128)(2,1)} %param.6) | copy-start | bytes 3932164
  0.0 1.3 %copy-start.3 = (bf16[128,1,8,512]{3,2,1,0:T(8,128)(2,1)S(1)}, bf16[128,1,8,512]{3,2,1,0:T(8,128)(2,1)}, u32[]{:S(2)}) copy-start(bf16[128,1,8,512]{3,2,1,0:T(8,128)(2,1)} %param.5) | copy-start | bytes 3145732
  2.8 27.8 %copy-start.6 = (s32[1,1,3]{2,1,0:T(1,128)S(1)}, s32[1,1,3]{2,1,0:T(1,128)}, u32[]{:S(2)}) copy-start(s32[1,1,3]{2,1,0:T(1,128)} %param.7) | copy-start | bytes 40
  2.8 27.8 %copy-start.7 = (s32[1,1,3]{2,1,0:T(1,128)S(1)}, s32[1,1,3]{2,1,0:T(1,128)}, u32[]{:S(2)}) copy-start(s32[1,1,3]{2,1,0:T(1,128)} %param.8) | copy-start | bytes 40
  2.8 21.9 %all-to-all-start = ((bf16[8,128,256]{2,1,0:T(8,128)(2,1)}), bf16[8,128,256]{2,1,0:T(8,128)(2,1)S(1)}, u32[]{:S(2)}, u32[]{:S(2)}) async-start(bf16[8,128,256]{2,1,0:T(8,128)(2,1)} %get-tuple-element.7), calls=%async_computation | async-start | bytes 1048576 | tf_op jit(solution)/shard_map/all_to_all | solution.py:144
  10.1 19.3 %collective-permute-start = (bf16[5,128,1024]{2,1,0:T(8,128)(2,1)S(1)}, bf16[5,128,1024]{2,1,0:T(8,128)(2,1)S(1)}, u32[]{:S(2)}, u32[]{:S(2)}) collective-permute-start(bf16[5,128,1024]{2,1,0:T(8,128)(2,1)S(1)} %bitcast.13), channel_id=1, source_target_pairs={{0,1},{1,2},{2,3},{4,5},{5,6},{6,7},{8,9},{9,10},{10,11},{12,13},{... | collective-permute-start | bytes 3932168 | tf_op jit(solution)/shard_map/ppermute | solution.py:123
  11.7 18.8 %collective-permute-start.1 = (bf16[5,128,1024]{2,1,0:T(8,128)(2,1)S(1)}, bf16[5,128,1024]{2,1,0:T(8,128)(2,1)}, u32[]{:S(2)}, u32[]{:S(2)}) collective-permute-start(bf16[5,128,1024]{2,1,0:T(8,128)(2,1)S(1)} %bitcast.14), channel_id=1, source_target_pairs={{1,0},{2,1},{3,2},{5,4},{6,5},{7,6},{9,8},{10,9},{11,10},{13,12},{... | collective-permute-start | bytes 3932168 | tf_op jit(solution)/shard_map/ppermute | solution.py:123
  24.6 5.9 %copy-start.4 = (bf16[8,128,256]{2,1,0:T(8,128)(2,1)}, bf16[8,128,256]{2,1,0:T(8,128)(2,1)S(1)}, u32[]{:S(2)}) copy-start(bf16[8,128,256]{2,1,0:T(8,128)(2,1)S(1)} %all-to-all-done) | copy-start | bytes 1572868
  24.6 18.4 %all-to-all-start.2 = ((bf16[8,128,256]{2,1,0:T(8,128)(2,1)}), bf16[8,128,256]{2,1,0:T(8,128)(2,1)}, u32[]{:S(2)}, u32[]{:S(2)}) async-start(bf16[8,128,256]{2,1,0:T(8,128)(2,1)} %get-tuple-element.8), calls=%async_computation.2 | async-start | bytes 1048576 | tf_op jit(solution)/shard_map/all_to_all | solution.py:144
  29.4 1.1 %copy-start.1 = (bf16[5,128,1024]{2,1,0:T(8,128)(2,1)}, bf16[5,128,1024]{2,1,0:T(8,128)(2,1)S(1)}, u32[]{:S(2)}) copy-start(bf16[5,128,1024]{2,1,0:T(8,128)(2,1)S(1)} %collective-permute-done.below) | copy-start | bytes 3932164
  30.6 1.3 %copy-start.2 = (bf16[5,128,1024]{2,1,0:T(8,128)(2,1)S(1)}, bf16[5,128,1024]{2,1,0:T(8,128)(2,1)}, u32[]{:S(2)}) copy-start(bf16[5,128,1024]{2,1,0:T(8,128)(2,1)} %copy-done.1) | copy-start | bytes 3932164
  31.9 2.8 %copy-start.5 = (bf16[8,128,256]{2,1,0:T(8,128)(2,1)S(1)}, bf16[8,128,256]{2,1,0:T(8,128)(2,1)}, u32[]{:S(2)}) copy-start(bf16[8,128,256]{2,1,0:T(8,128)(2,1)} %copy-done.4) | copy-start | bytes 1572868
  43.1 18.1 %all-to-all-start.1 = ((bf16[8,128,256]{2,1,0:T(8,128)(2,1)}), bf16[8,128,256]{2,1,0:T(8,128)(2,1)S(1)}, u32[]{:S(2)}, u32[]{:S(2)}) async-start(bf16[8,128,256]{2,1,0:T(8,128)(2,1)} %bitcast.6), calls=%async_computation.1 | async-start | bytes 1048576 | tf_op jit(solution)/shard_map/all_to_all | solution.py:184

commit v2 on v1

v2 whole, which is shorter than its diff:
```python
import functools

import jax
import jax.numpy as jnp
from jax import lax
from jax.experimental import pallas as pl
from jax.experimental.pallas import tpu as pltpu
from jax.sharding import PartitionSpec as P

LIMIT = 40 * 1024 * 1024


def rows_per_group(rows, patches):
    return min(rows, max(16, 256 // patches))


def partners(count):
    return list(range(count - 1, 0, -1))


def ppermute(value, axis, step):
    count = lax.axis_size(axis)
    return lax.ppermute(value, axis, [(i, i ^ step) for i in range(count)])


def split_kernel(me_ref, members_ref, *out_refs):
    patches = len(out_refs)
    rows = out_refs[0].shape[0]
    group = rows_per_group(rows, patches)
    height = group * patches
    row = lax.broadcasted_iota(jnp.int32, (height, height), 0)
    column = lax.broadcasted_iota(jnp.int32, (height, height), 1)
    source = lax.rem(row, group) * patches + (lax.div(row, group) ^ me_ref[0])
    shuffle = jnp.where(column == source, 1.0, 0.0).astype(jnp.bfloat16)
    for step in range(rows // group):
        block = members_ref[step * height : (step + 1) * height, :]
        moved = jnp.dot(shuffle, block, preferred_element_type=jnp.float32)
        moved = moved.astype(jnp.bfloat16)
        for k, out_ref in enumerate(out_refs):
            out_ref[step * group : (step + 1) * group, :] = moved[k * group : (k + 1) * group, :]


def merge_kernel(me_ref, *refs):
    piece_refs, out_ref = refs[:-1], refs[-1]
    patches = len(piece_refs)
    rows = piece_refs[0].shape[0]
    group = rows_per_group(rows, patches)
    height = group * patches
    row = lax.broadcasted_iota(jnp.int32, (height, height), 0)
    column = lax.broadcasted_iota(jnp.int32, (height, height), 1)
    source = (lax.rem(row, patches) ^ me_ref[0]) * group + lax.div(row, patches)
    shuffle = jnp.where(column == source, 1.0, 0.0).astype(jnp.bfloat16)
    for step in range(rows // group):
        here = slice(step * group, (step + 1) * group)
        block = jnp.concatenate([piece_ref[here, :] for piece_ref in piece_refs], axis=0)
        moved = jnp.dot(shuffle, block, preferred_element_type=jnp.float32)
        out_ref[step * height : (step + 1) * height, :] = moved.astype(jnp.bfloat16)


def gram_kernel(scale, ids_ref, src_ref, count_ref, below, own, above, gram_ref, stacked, sem):
    slots = ids_ref.shape[0]
    rows = own.shape[1]
    for slot in range(slots):
        live = slot < count_ref[0]
        target = stacked.at[pl.ds(slot * rows, rows), :]
        for code, store in enumerate((below, own, above)):

            @pl.when(live & (src_ref[slot] == code))
            def _():
                pltpu.make_async_copy(store.at[ids_ref[slot]], target, sem.at[slot]).start()

        @pl.when(jnp.logical_not(live))
        def _():
            target[...] = jnp.zeros(target.shape, target.dtype)

    for slot in range(slots):

        @pl.when(slot < count_ref[0])
        def _():
            target = stacked.at[pl.ds(slot * rows, rows), :]
            pltpu.make_async_copy(own.at[0], target, sem.at[slot]).wait()

    size = gram_ref.shape[0]
    part = min(size, 256)
    for step in range(size // part):
        block = lax.dot_general(
            stacked[:, step * part : (step + 1) * part],
            stacked[...],
            (((0,), (0,)), ((), ())),
            preferred_element_type=jnp.float32,
        )
        gram_ref[step * part : (step + 1) * part, :] = (block * scale).astype(jnp.bfloat16)


def transform_kernel(count, me_ref, gram_ref, *refs):
    piece_refs, out_refs = refs[:count], refs[count : 2 * count]
    members, first, fresh = refs[2 * count :]
    rows = piece_refs[0].shape[0]

    def place(k):
        return pl.ds(pl.multiple_of((me_ref[0] ^ k) * rows, rows), rows)

    for k in range(count):
        members[place(k), :] = piece_refs[k][...]
    size = gram_ref.shape[0]
    part = min(size, 256)
    for step in range(size // part):
        here = slice(step * part, (step + 1) * part)
        first[here, :] = jnp.dot(
            gram_ref[here, :], members[...], preferred_element_type=jnp.float32
        ).astype(jnp.bfloat16)
    for step in range(size // part):
        here = slice(step * part, (step + 1) * part)
        second = jnp.dot(gram_ref[here, :], first[...], preferred_element_type=jnp.float32)
        rest = members[here, :].astype(jnp.float32) - first[here, :].astype(jnp.float32)
        fresh[here, :] = (rest + second).astype(jnp.bfloat16)
    for k in range(count):
        out_refs[k][...] = fresh[place(k), :]


def vmem():
    return pl.BlockSpec(memory_space=pltpu.VMEM)


def params():
    return pltpu.CompilerParams(vmem_limit_bytes=LIMIT)


def cost(flops, nbytes):
    return pl.CostEstimate(flops=flops, bytes_accessed=nbytes, transcendentals=0)


def neighbours(store):
    count = lax.axis_size("region")
    up = [(i, i + 1) for i in range(count - 1)]
    down = [(i + 1, i) for i in range(count - 1)]
    return lax.ppermute(store, "region", up), lax.ppermute(store, "region", down)


def shards(ensemble, obs_store, block_ids, block_src, block_count):
    rows, _, patches, values = ensemble.shape
    store = obs_store.reshape(obs_store.shape[2:])
    size = store.shape[2]
    slots = block_ids.shape[2]
    me = lax.axis_index("member").astype(jnp.int32).reshape(1)
    below, above = neighbours(store)
    smem = pl.BlockSpec(memory_space=pltpu.SMEM)
    anywhere = pl.BlockSpec(memory_space=pl.ANY)
    piece_shape = jax.ShapeDtypeStruct((rows, values), jnp.bfloat16)

    pieces = pl.pallas_call(
        split_kernel,
        out_shape=[piece_shape] * patches,
        in_specs=[smem, vmem()],
        out_specs=[vmem()] * patches,
        compiler_params=params(),
        cost_estimate=cost(2 * 256 * rows * patches * values, 4 * rows * patches * values),
        name="split",
    )(me, ensemble.reshape(rows * patches, values))
    arrived = [pieces[0]] + [None] * (patches - 1)
    for k in partners(patches):
        arrived[k] = ppermute(pieces[k], "member", k)

    gram = pl.pallas_call(
        functools.partial(gram_kernel, 1.0 / (2.0 * size)),
        out_shape=jax.ShapeDtypeStruct((size, size), jnp.bfloat16),
        in_specs=[smem] * 3 + [anywhere] * 3,
        out_specs=vmem(),
        scratch_shapes=[
            pltpu.VMEM((slots * store.shape[1], size), jnp.bfloat16),
            pltpu.SemaphoreType.DMA((slots,)),
        ],
        compiler_params=params(),
        cost_estimate=cost(2 * slots * store.shape[1] * size * size, 4 * size * size),
        name="gram",
    )(
        block_ids.reshape(slots),
        block_src.reshape(slots),
        block_count.reshape(1),
        below,
        store,
        above,
    )

    moved = pl.pallas_call(
        functools.partial(transform_kernel, patches),
        out_shape=[piece_shape] * patches,
        in_specs=[smem] + [vmem()] * (1 + patches),
        out_specs=[vmem()] * patches,
        scratch_shapes=[pltpu.VMEM((size, values), jnp.bfloat16)] * 3,
        compiler_params=params(),
        cost_estimate=cost(4 * size * size * values, 2 * size * size + 4 * size * values),
        name="transform",
    )(me, gram, *arrived)
    returned = [moved[0]] + [None] * (patches - 1)
    for k in partners(patches):
        returned[k] = ppermute(moved[k], "member", k)

    fresh = pl.pallas_call(
        merge_kernel,
        out_shape=jax.ShapeDtypeStruct((rows * patches, values), jnp.bfloat16),
        in_specs=[smem] + [vmem()] * patches,
        out_specs=vmem(),
        compiler_params=params(),
        cost_estimate=cost(2 * 256 * rows * patches * values, 4 * rows * patches * values),
        name="merge",
    )(me, *returned)
    return fresh.reshape(ensemble.shape)


def solution(mesh):
    return jax.shard_map(
        shards,
        mesh=mesh,
        in_specs=(
            P("member", "region", None, None),
            P("region", "member", None, None, None),
            P("region", "member", None),
            P("region", "member", None),
            P("region", "member"),
        ),
        out_specs=P("member", "region", None, None),
        check_vma=False,
    )
```

time: 81.3 us -> 70 us (0.86)
  the two profiles are of different devices: /device:TPU:0 before, /device:TPU:8 now
where the time goes in v2:
time: 70 us; the launch traced here: 69.7 us
  waiting for transfers between devices  34 us (49%)
  starting transfers between devices  24.8 us (35%)
  Pallas kernels  6.37 us (9%)
  local copies, waits for them, and re-layouts  3.84 us (5%)
  between operations  0.74 us (1%)
    ppermute x14, waiting for transfers between devices, ppermute(): return lax.ppermute(value, axis, [(i, i ^ step) for i in range(count)])  34 us
    ppermute x14, starting transfers between devices, ppermute(): return lax.ppermute(value, axis, [(i, i ^ step) for i in range(count)])  21.7 us
    unnamed x8, local copies, waits for them, and re-layouts  3.84 us
    pallas_call x1, Pallas kernels, shards(): pl.pallas_call(functools.partial(transform_kernel, patches), out_shape=[p...  2.53 us
    pallas_call x1, Pallas kernels, shards(): pl.pallas_call(functools.partial(gram_kernel, 1.0 / (2.0 * size)), out_sh...  2 us
    ppermute x1, starting transfers between devices, neighbours(): lax.ppermute(store, 'region', up)  1.81 us
    pallas_call x1, Pallas kernels, shards(): pl.pallas_call(merge_kernel, out_shape=jax.ShapeDtypeStruct((rows * patch...  1.41 us
  transfers between devices with their start and end apart: 16, of which 10 were waited for; matrix products, arithmetic and copies ran while one was open for 0% of the time, Pallas kernels for 3%

profile of v2, /device:TPU:8, one launch (start us, length us, event | category | flops | bytes accessed | tf_op | source)
XLA Modules:
  0.0 69.7 jit_solution(8032313076442789316)
XLA Ops:
  0.0 1.8 %collective-permute-start = (bf16[5,128,1024]{2,1,0:T(8,128)(2,1)}, bf16[5,128,1024]{2,1,0:T(8,128)(2,1)S(1)}, u32[]{:S(2)}, u32[]{:S(2)}) collective-permute-start(bf16[5,128,1024]{2,1,0:T(8,128)(2,1)} %bitcast.10), channel_id=1, source_target_pairs={{0,1},{1,2},{2,3},{4,5},{5,6},{6,7},{8,9},{9,10},{10,11},{12,13},{... | collective-permute-start | bytes 3932168 | tf_op jit(solution)/shard_map/ppermute | solution.py:137
  1.8 1.3 %collective-permute-start.1 = (bf16[5,128,1024]{2,1,0:T(8,128)(2,1)}, bf16[5,128,1024]{2,1,0:T(8,128)(2,1)S(1)}, u32[]{:S(2)}, u32[]{:S(2)}) collective-permute-start(bf16[5,128,1024]{2,1,0:T(8,128)(2,1)} %bitcast.11), channel_id=1, source_target_pairs={{1,0},{2,1},{3,2},{5,4},{6,5},{7,6},{9,8},{10,9},{11,10},{13,12},{... | collective-permute-start | bytes 3932168 | tf_op jit(solution)/shard_map/ppermute | solution.py:137
  4.8 1.6 %collective-permute-start.2 = (bf16[128,512]{1,0:T(8,128)(2,1)S(1)}, bf16[128,512]{1,0:T(8,128)(2,1)S(1)}, u32[]{:S(2)}, u32[]{:S(2)}) collective-permute-start(bf16[128,512]{1,0:T(8,128)(2,1)S(1)} %get-tuple-element.22), channel_id=1, source_target_pairs={{0,4},{4,0},{8,12},{12,8},{16,20},{20,16},{24,28},{28,24},{1,5},{5... | collective-permute-start | bytes 393224 | tf_op jit(solution)/shard_map/ppermute | solution.py:23
  6.8 1.5 %collective-permute-start.4 = (bf16[128,512]{1,0:T(8,128)(2,1)S(1)}, bf16[128,512]{1,0:T(8,128)(2,1)S(1)}, u32[]{:S(2)}, u32[]{:S(2)}) collective-permute-start(bf16[128,512]{1,0:T(8,128)(2,1)S(1)} %get-tuple-element.24), channel_id=1, source_target_pairs={{0,12},{4,8},{8,4},{12,0},{16,28},{20,24},{24,20},{28,16},{1,13},{... | collective-permute-start | bytes 393224 | tf_op jit(solution)/shard_map/ppermute | solution.py:23
  8.3 1.5 %collective-permute-done.2.refs_1_ = bf16[128,512]{1,0:T(8,128)(2,1)S(1)} collective-permute-done((bf16[128,512]{1,0:T(8,128)(2,1)S(1)}, bf16[128,512]{1,0:T(8,128)(2,1)S(1)}, u32[]{:S(2)}, u32[]{:S(2)}) %collective-permute-start.2) | collective-permute-done | bytes 131104 | tf_op jit(solution)/shard_map/ppermute | solution.py:23
  9.8 2.6 %collective-permute-start.5 = (bf16[128,512]{1,0:T(8,128)(2,1)S(1)}, bf16[128,512]{1,0:T(8,128)(2,1)S(1)}, u32[]{:S(2)}, u32[]{:S(2)}) collective-permute-start(bf16[128,512]{1,0:T(8,128)(2,1)S(1)} %get-tuple-element.25), channel_id=1, source_target_pairs={{0,16},{4,20},{8,24},{12,28},{16,0},{20,4},{24,8},{28,12},{1,17},{... | collective-permute-start | bytes 393224 | tf_op jit(solution)/shard_map/ppermute | solution.py:23
  12.4 1.7 %collective-permute-start.6 = (bf16[128,512]{1,0:T(8,128)(2,1)S(1)}, bf16[128,512]{1,0:T(8,128)(2,1)S(1)}, u32[]{:S(2)}, u32[]{:S(2)}) collective-permute-start(bf16[128,512]{1,0:T(8,128)(2,1)S(1)} %get-tuple-element.26), channel_id=1, source_target_pairs={{0,20},{4,16},{8,28},{12,24},{16,4},{20,0},{24,12},{28,8},{1,21},{... | collective-permute-start | bytes 393224 | tf_op jit(solution)/shard_map/ppermute | solution.py:23
  15.3 1.9 %collective-permute-start.8 = (bf16[128,512]{1,0:T(8,128)(2,1)S(1)}, bf16[128,512]{1,0:T(8,128)(2,1)S(1)}, u32[]{:S(2)}, u32[]{:S(2)}) collective-permute-start(bf16[128,512]{1,0:T(8,128)(2,1)S(1)} %get-tuple-element.28), channel_id=1, source_target_pairs={{0,28},{4,24},{8,20},{12,16},{16,12},{20,8},{24,4},{28,0},{1,29},{... | collective-permute-start | bytes 393224 | tf_op jit(solution)/shard_map/ppermute | solution.py:23
  17.8 1.3 %copy-done = bf16[1,1,5,128,1024]{4,3,2,1,0:T(8,128)(2,1)S(1)} copy-done((bf16[1,1,5,128,1024]{4,3,2,1,0:T(8,128)(2,1)S(1)}, bf16[1,1,5,128,1024]{4,3,2,1,0:T(8,128)(2,1)}, u32[]{:S(2)}) %copy-start) | copy-done | bytes 1310744
  20.4 2.0 %gram.1.gram_ref = bf16[1024,1024]{1,0:T(8,128)(2,1)S(1)} custom-call(s32[3]{0:T(128)S(1)} %bitcast.14, s32[3]{0:T(128)S(1)} %bitcast.15, s32[1]{0:T(128)} %bitcast.9.count_ref, bf16[5,128,1024]{2,1,0:T(8,128)(2,1)S(1)} %collective-permute-done.below, bf16[5,128,1024]{2,1,0:T(8,128)(2,1)S(1)} %bitcast.12, bf16[5,128,1024]{2,1,0:T(8,128)(2,1)S(1)} %collective-permute-done.1.above), custom_call_target="tpu_custom_call" | custom-call | flops 805306368 | bytes 4194304 | tf_op jit(solution)/shard_map/gram/pallas_call | solution.py:164
  22.4 3.4 %collective-permute-done.5.refs_4_ = bf16[128,512]{1,0:T(8,128)(2,1)S(1)} collective-permute-done((bf16[128,512]{1,0:T(8,128)(2,1)S(1)}, bf16[128,512]{1,0:T(8,128)(2,1)S(1)}, u32[]{:S(2)}, u32[]{:S(2)}) %collective-permute-start.5) | collective-permute-done | bytes 131104 | tf_op jit(solution)/shard_map/ppermute | solution.py:23
  25.8 4.2 %collective-permute-done.6.refs_5_ = bf16[128,512]{1,0:T(8,128)(2,1)S(1)} collective-permute-done((bf16[128,512]{1,0:T(8,128)(2,1)S(1)}, bf16[128,512]{1,0:T(8,128)(2,1)S(1)}, u32[]{:S(2)}, u32[]{:S(2)}) %collective-permute-start.6) | collective-permute-done | bytes 131104 | tf_op jit(solution)/shard_map/ppermute | solution.py:23
  30.0 2.9 %collective-permute-done.7.refs_6_ = bf16[128,512]{1,0:T(8,128)(2,1)S(1)} collective-permute-done((bf16[128,512]{1,0:T(8,128)(2,1)S(1)}, bf16[128,512]{1,0:T(8,128)(2,1)S(1)}, u32[]{:S(2)}, u32[]{:S(2)}) %collective-permute-start.7) | collective-permute-done | bytes 131104 | tf_op jit(solution)/shard_map/ppermute | solution.py:23
  33.0 3.5 %collective-permute-done.8.refs_7_ = bf16[128,512]{1,0:T(8,128)(2,1)S(1)} collective-permute-done((bf16[128,512]{1,0:T(8,128)(2,1)S(1)}, bf16[128,512]{1,0:T(8,128)(2,1)S(1)}, u32[]{:S(2)}, u32[]{:S(2)}) %collective-permute-start.8) | collective-permute-done | bytes 131104 | tf_op jit(solution)/shard_map/ppermute | solution.py:23
  36.4 2.5 %transform.1 = (bf16[128,512]{1,0:T(8,128)(2,1)S(1)}, bf16[128,512]{1,0:T(8,128)(2,1)S(1)}, bf16[128,512]{1,0:T(8,128)(2,1)S(1)}, bf16[128,512]{1,0:T(8,128)(2,1...) custom-call(s32[1]{0:T(128)} %bitcast.me_ref, ...), custom_call_target="tpu_custom_call" | custom-call | flops 2147483648 | bytes 4194304 | tf_op jit(solution)/shard_map/transform/pallas_call | solution.py:185
  39.9 2.6 %collective-permute-start.11 = (bf16[128,512]{1,0:T(8,128)(2,1)S(1)}, bf16[128,512]{1,0:T(8,128)(2,1)S(1)}, u32[]{:S(2)}, u32[]{:S(2)}) collective-permute-start(bf16[128,512]{1,0:T(8,128)(2,1)S(1)} %get-tuple-element.32), channel_id=1, source_target_pairs={{0,12},{4,8},{8,4},{12,0},{16,28},{20,24},{24,20},{28,16},{1,13},{... | collective-permute-start | bytes 393224 | tf_op jit(solution)/shard_map/ppermute | solution.py:23
  42.5 2.2 %collective-permute-start.12 = (bf16[128,512]{1,0:T(8,128)(2,1)S(1)}, bf16[128,512]{1,0:T(8,128)(2,1)S(1)}, u32[]{:S(2)}, u32[]{:S(2)}) collective-permute-start(bf16[128,512]{1,0:T(8,128)(2,1)S(1)} %get-tuple-element.33), channel_id=1, source_target_pairs={{0,16},{4,20},{8,24},{12,28},{16,0},{20,4},{24,8},{28,12},{1,17},{... | collective-permute-start | bytes 393224 | tf_op jit(solution)/shard_map/ppermute | solution.py:23
  45.7 2.3 %collective-permute-start.14 = (bf16[128,512]{1,0:T(8,128)(2,1)S(1)}, bf16[128,512]{1,0:T(8,128)(2,1)S(1)}, u32[]{:S(2)}, u32[]{:S(2)}) collective-permute-start(bf16[128,512]{1,0:T(8,128)(2,1)S(1)} %get-tuple-element.35), channel_id=1, source_target_pairs={{0,24},{4,28},{8,16},{12,20},{16,8},{20,12},{24,0},{28,4},{1,25},{... | collective-permute-start | bytes 393224 | tf_op jit(solution)/shard_map/ppermute | solution.py:23
  48.1 1.7 %collective-permute-start.15 = (bf16[128,512]{1,0:T(8,128)(2,1)S(1)}, bf16[128,512]{1,0:T(8,128)(2,1)S(1)}, u32[]{:S(2)}, u32[]{:S(2)}) collective-permute-start(bf16[128,512]{1,0:T(8,128)(2,1)S(1)} %get-tuple-element.36), channel_id=1, source_target_pairs={{0,28},{4,24},{8,20},{12,16},{16,12},{20,8},{24,4},{28,0},{1,29},{... | collective-permute-start | bytes 393224 | tf_op jit(solution)/shard_map/ppermute | solution.py:23
  50.3 9.6 %collective-permute-done.12.refs_4_ = bf16[128,512]{1,0:T(8,128)(2,1)S(1)} collective-permute-done((bf16[128,512]{1,0:T(8,128)(2,1)S(1)}, bf16[128,512]{1,0:T(8,128)(2,1)S(1)}, u32[]{:S(2)}, u32[]{:S(2)}) %collective-permute-start.12) | collective-permute-done | bytes 131104 | tf_op jit(solution)/shard_map/ppermute | solution.py:23
  59.9 2.8 %collective-permute-done.13.refs_5_ = bf16[128,512]{1,0:T(8,128)(2,1)S(1)} collective-permute-done((bf16[128,512]{1,0:T(8,128)(2,1)S(1)}, bf16[128,512]{1,0:T(8,128)(2,1)S(1)}, u32[]{:S(2)}, u32[]{:S(2)}) %collective-permute-start.13) | collective-permute-done | bytes 131104 | tf_op jit(solution)/shard_map/ppermute | solution.py:23
  62.7 3.3 %collective-permute-done.14.refs_6_ = bf16[128,512]{1,0:T(8,128)(2,1)S(1)} collective-permute-done((bf16[128,512]{1,0:T(8,128)(2,1)S(1)}, bf16[128,512]{1,0:T(8,128)(2,1)S(1)}, u32[]{:S(2)}, u32[]{:S(2)}) %collective-permute-start.14) | collective-permute-done | bytes 131104 | tf_op jit(solution)/shard_map/ppermute | solution.py:23
  66.0 2.4 %collective-permute-done.15.refs_7_ = bf16[128,512]{1,0:T(8,128)(2,1)S(1)} collective-permute-done((bf16[128,512]{1,0:T(8,128)(2,1)S(1)}, bf16[128,512]{1,0:T(8,128)(2,1)S(1)}, u32[]{:S(2)}, u32[]{:S(2)}) %collective-permute-start.15) | collective-permute-done | bytes 131104 | tf_op jit(solution)/shard_map/ppermute | solution.py:23
  68.3 1.4 %merge.1 = bf16[1024,512]{1,0:T(8,128)(2,1)} custom-call(s32[1]{0:T(128)} %bitcast.me_ref, bf16[128,512]{1,0:T(8,128)(2,1)S(1)} %get-tuple-element.29.refs_0_, bf16[128,512]{1,0:T(8,128)(2,1)S(1)} %collective-permute-done.9.refs_1_, bf16[128,512]{1,0:T(8,128)(2,1)S(1)} %collective-permute-done.10.refs_2_, ...), custom_call_target="tpu_custom_call" | custom-call | flops 268435456 | bytes 2097152 | tf_op jit(solution)/shard_map/merge/pallas_call | solution.py:199
  (20 shorter events, 7.0 us)
Async XLA Ops:
  0.0 14.2 %collective-permute-start = (bf16[5,128,1024]{2,1,0:T(8,128)(2,1)}, bf16[5,128,1024]{2,1,0:T(8,128)(2,1)S(1)}, u32[]{:S(2)}, u32[]{:S(2)}) collective-permute-start(bf16[5,128,1024]{2,1,0:T(8,128)(2,1)} %bitcast.10), channel_id=1, source_target_pairs={{0,1},{1,2},{2,3},{4,5},{5,6},{6,7},{8,9},{9,10},{10,11},{12,13},{... | collective-permute-start | bytes 3932168 | tf_op jit(solution)/shard_map/ppermute | solution.py:137
  1.8 13.4 %collective-permute-start.1 = (bf16[5,128,1024]{2,1,0:T(8,128)(2,1)}, bf16[5,128,1024]{2,1,0:T(8,128)(2,1)S(1)}, u32[]{:S(2)}, u32[]{:S(2)}) collective-permute-start(bf16[5,128,1024]{2,1,0:T(8,128)(2,1)} %bitcast.11), channel_id=1, source_target_pairs={{1,0},{2,1},{3,2},{5,4},{6,5},{7,6},{9,8},{10,9},{11,10},{13,12},{... | collective-permute-start | bytes 3932168 | tf_op jit(solution)/shard_map/ppermute | solution.py:137
  3.1 1.2 %copy-start.1 = (bf16[128,1,8,512]{3,2,1,0:T(8,128)(2,1)S(1)}, bf16[128,1,8,512]{3,2,1,0:T(8,128)(2,1)}, u32[]{:S(2)}) copy-start(bf16[128,1,8,512]{3,2,1,0:T(8,128)(2,1)} %param.5) | copy-start | bytes 3145732
  4.8 5.0 %collective-permute-start.2 = (bf16[128,512]{1,0:T(8,128)(2,1)S(1)}, bf16[128,512]{1,0:T(8,128)(2,1)S(1)}, u32[]{:S(2)}, u32[]{:S(2)}) collective-permute-start(bf16[128,512]{1,0:T(8,128)(2,1)S(1)} %get-tuple-element.22), channel_id=1, source_target_pairs={{0,4},{4,0},{8,12},{12,8},{16,20},{20,16},{24,28},{28,24},{1,5},{5... | collective-permute-start | bytes 393224 | tf_op jit(solution)/shard_map/ppermute | solution.py:23
  6.3 6.1 %collective-permute-start.3 = (bf16[128,512]{1,0:T(8,128)(2,1)S(1)}, bf16[128,512]{1,0:T(8,128)(2,1)S(1)}, u32[]{:S(2)}, u32[]{:S(2)}) collective-permute-start(bf16[128,512]{1,0:T(8,128)(2,1)S(1)} %get-tuple-element.23), channel_id=1, source_target_pairs={{0,8},{4,12},{8,0},{12,4},{16,24},{20,28},{24,16},{28,20},{1,9},{5... | collective-permute-start | bytes 393224 | tf_op jit(solution)/shard_map/ppermute | solution.py:23
  6.8 15.6 %collective-permute-start.4 = (bf16[128,512]{1,0:T(8,128)(2,1)S(1)}, bf16[128,512]{1,0:T(8,128)(2,1)S(1)}, u32[]{:S(2)}, u32[]{:S(2)}) collective-permute-start(bf16[128,512]{1,0:T(8,128)(2,1)S(1)} %get-tuple-element.24), channel_id=1, source_target_pairs={{0,12},{4,8},{8,4},{12,0},{16,28},{20,24},{24,20},{28,16},{1,13},{... | collective-permute-start | bytes 393224 | tf_op jit(solution)/shard_map/ppermute | solution.py:23
  9.8 16.0 %collective-permute-start.5 = (bf16[128,512]{1,0:T(8,128)(2,1)S(1)}, bf16[128,512]{1,0:T(8,128)(2,1)S(1)}, u32[]{:S(2)}, u32[]{:S(2)}) collective-permute-start(bf16[128,512]{1,0:T(8,128)(2,1)S(1)} %get-tuple-element.25), channel_id=1, source_target_pairs={{0,16},{4,20},{8,24},{12,28},{16,0},{20,4},{24,8},{28,12},{1,17},{... | collective-permute-start | bytes 393224 | tf_op jit(solution)/shard_map/ppermute | solution.py:23
  12.4 17.6 %collective-permute-start.6 = (bf16[128,512]{1,0:T(8,128)(2,1)S(1)}, bf16[128,512]{1,0:T(8,128)(2,1)S(1)}, u32[]{:S(2)}, u32[]{:S(2)}) collective-permute-start(bf16[128,512]{1,0:T(8,128)(2,1)S(1)} %get-tuple-element.26), channel_id=1, source_target_pairs={{0,20},{4,16},{8,28},{12,24},{16,4},{20,0},{24,12},{28,8},{1,21},{... | collective-permute-start | bytes 393224 | tf_op jit(solution)/shard_map/ppermute | solution.py:23
  14.2 18.8 %collective-permute-start.7 = (bf16[128,512]{1,0:T(8,128)(2,1)S(1)}, bf16[128,512]{1,0:T(8,128)(2,1)S(1)}, u32[]{:S(2)}, u32[]{:S(2)}) collective-permute-start(bf16[128,512]{1,0:T(8,128)(2,1)S(1)} %get-tuple-element.27), channel_id=1, source_target_pairs={{0,24},{4,28},{8,16},{12,20},{16,8},{20,12},{24,0},{28,4},{1,25},{... | collective-permute-start | bytes 393224 | tf_op jit(solution)/shard_map/ppermute | solution.py:23
  15.3 21.1 %collective-permute-start.8 = (bf16[128,512]{1,0:T(8,128)(2,1)S(1)}, bf16[128,512]{1,0:T(8,128)(2,1)S(1)}, u32[]{:S(2)}, u32[]{:S(2)}) collective-permute-start(bf16[128,512]{1,0:T(8,128)(2,1)S(1)} %get-tuple-element.28), channel_id=1, source_target_pairs={{0,28},{4,24},{8,20},{12,16},{16,12},{20,8},{24,4},{28,0},{1,29},{... | collective-permute-start | bytes 393224 | tf_op jit(solution)/shard_map/ppermute | solution.py:23
  17.8 1.3 %copy-start = (bf16[1,1,5,128,1024]{4,3,2,1,0:T(8,128)(2,1)S(1)}, bf16[1,1,5,128,1024]{4,3,2,1,0:T(8,128)(2,1)}, u32[]{:S(2)}) copy-start(bf16[1,1,5,128,1024]{4,3,2,1,0:T(8,128)(2,1)} %param.6) | copy-start | bytes 3932164
  19.1 0.7 copy-start.2
  19.8 0.7 copy-start.3
  39.0 6.8 %collective-permute-start.9 = (bf16[128,512]{1,0:T(8,128)(2,1)S(1)}, bf16[128,512]{1,0:T(8,128)(2,1)S(1)}, u32[]{:S(2)}, u32[]{:S(2)}) collective-permute-start(bf16[128,512]{1,0:T(8,128)(2,1)S(1)} %get-tuple-element.30), channel_id=1, source_target_pairs={{0,4},{4,0},{8,12},{12,8},{16,20},{20,16},{24,28},{28,24},{1,5},{5... | collective-permute-start | bytes 393224 | tf_op jit(solution)/shard_map/ppermute | solution.py:23
  39.9 8.2 %collective-permute-start.10 = (bf16[128,512]{1,0:T(8,128)(2,1)S(1)}, bf16[128,512]{1,0:T(8,128)(2,1)S(1)}, u32[]{:S(2)}, u32[]{:S(2)}) collective-permute-start(bf16[128,512]{1,0:T(8,128)(2,1)S(1)} %get-tuple-element.31), channel_id=1, source_target_pairs={{0,8},{4,12},{8,0},{12,4},{16,24},{20,28},{24,16},{28,20},{1,9},{5... | collective-permute-start | bytes 393224 | tf_op jit(solution)/shard_map/ppermute | solution.py:23
  39.9 10.4 %collective-permute-start.11 = (bf16[128,512]{1,0:T(8,128)(2,1)S(1)}, bf16[128,512]{1,0:T(8,128)(2,1)S(1)}, u32[]{:S(2)}, u32[]{:S(2)}) collective-permute-start(bf16[128,512]{1,0:T(8,128)(2,1)S(1)} %get-tuple-element.32), channel_id=1, source_target_pairs={{0,12},{4,8},{8,4},{12,0},{16,28},{20,24},{24,20},{28,16},{1,13},{... | collective-permute-start | bytes 393224 | tf_op jit(solution)/shard_map/ppermute | solution.py:23
  42.5 17.4 %collective-permute-start.12 = (bf16[128,512]{1,0:T(8,128)(2,1)S(1)}, bf16[128,512]{1,0:T(8,128)(2,1)S(1)}, u32[]{:S(2)}, u32[]{:S(2)}) collective-permute-start(bf16[128,512]{1,0:T(8,128)(2,1)S(1)} %get-tuple-element.33), channel_id=1, source_target_pairs={{0,16},{4,20},{8,24},{12,28},{16,0},{20,4},{24,8},{28,12},{1,17},{... | collective-permute-start | bytes 393224 | tf_op jit(solution)/shard_map/ppermute | solution.py:23
  44.7 18.0 %collective-permute-start.13 = (bf16[128,512]{1,0:T(8,128)(2,1)S(1)}, bf16[128,512]{1,0:T(8,128)(2,1)S(1)}, u32[]{:S(2)}, u32[]{:S(2)}) collective-permute-start(bf16[128,512]{1,0:T(8,128)(2,1)S(1)} %get-tuple-element.34), channel_id=1, source_target_pairs={{0,20},{4,16},{8,28},{12,24},{16,4},{20,0},{24,12},{28,8},{1,21},{... | collective-permute-start | bytes 393224 | tf_op jit(solution)/shard_map/ppermute | solution.py:23
  45.7 20.2 %collective-permute-start.14 = (bf16[128,512]{1,0:T(8,128)(2,1)S(1)}, bf16[128,512]{1,0:T(8,128)(2,1)S(1)}, u32[]{:S(2)}, u32[]{:S(2)}) collective-permute-start(bf16[128,512]{1,0:T(8,128)(2,1)S(1)} %get-tuple-element.35), channel_id=1, source_target_pairs={{0,24},{4,28},{8,16},{12,20},{16,8},{20,12},{24,0},{28,4},{1,25},{... | collective-permute-start | bytes 393224 | tf_op jit(solution)/shard_map/ppermute | solution.py:23
  48.1 20.3 %collective-permute-start.15 = (bf16[128,512]{1,0:T(8,128)(2,1)S(1)}, bf16[128,512]{1,0:T(8,128)(2,1)S(1)}, u32[]{:S(2)}, u32[]{:S(2)}) collective-permute-start(bf16[128,512]{1,0:T(8,128)(2,1)S(1)} %get-tuple-element.36), channel_id=1, source_target_pairs={{0,28},{4,24},{8,20},{12,16},{16,12},{20,8},{24,4},{28,0},{1,29},{... | collective-permute-start | bytes 393224 | tf_op jit(solution)/shard_map/ppermute | solution.py:23

commit v3 on v2

--- a/solution.py
+++ b/solution.py
@@ -15,7 +15,12 @@
 
 
 def partners(count):
-    return list(range(count - 1, 0, -1))
+    far = list(range(count - 1, count // 2 - 1, -1))
+    near = list(range(count // 2 - 1, 0, -1))
+    order = []
+    for i in range(len(far)):
+        order += far[i : i + 1] + near[i : i + 1]
+    return order
 
 
 def ppermute(value, axis, step):
@@ -57,17 +62,35 @@
         out_ref[step * height : (step + 1) * height, :] = moved.astype(jnp.bfloat16)
 
 
-def gram_kernel(scale, ids_ref, src_ref, count_ref, below, own, above, gram_ref, stacked, sem):
-    slots = ids_ref.shape[0]
+def gram_kernel(
+    scale, region_ref, ids_hbm, src_hbm, count_hbm, own, even, odd, gram_ref,
+    ids_ref, src_ref, count_ref, stacked, table_sem, sem,
+):
+    tables = [
+        pltpu.make_async_copy(hbm, smem, table_sem.at[i])
+        for i, (hbm, smem) in enumerate(
+            ((ids_hbm, ids_ref), (src_hbm, src_ref), (count_hbm, count_ref))
+        )
+    ]
+    for copy in tables:
+        copy.start()
+    for copy in tables:
+        copy.wait()
+    slots = ids_ref.shape[2]
     rows = own.shape[1]
+    parity = lax.rem(region_ref[0], 2)
+    count = count_ref[0, 0]
     for slot in range(slots):
-        live = slot < count_ref[0]
+        live = slot < count
         target = stacked.at[pl.ds(slot * rows, rows), :]
-        for code, store in enumerate((below, own, above)):
-
-            @pl.when(live & (src_ref[slot] == code))
+        source = src_ref[0, 0, slot]
+        where = jnp.where(source == 1, 0, jnp.where((source == 2) == (parity == 0), 1, 2))
+        for code, store in enumerate((own, even, odd)):
+
+            @pl.when(live & (where == code))
             def _():
-                pltpu.make_async_copy(store.at[ids_ref[slot]], target, sem.at[slot]).start()
+                block = store.at[ids_ref[0, 0, slot]]
+                pltpu.make_async_copy(block, target, sem.at[slot]).start()
 
         @pl.when(jnp.logical_not(live))
         def _():
@@ -75,7 +98,7 @@
 
     for slot in range(slots):
 
-        @pl.when(slot < count_ref[0])
+        @pl.when(slot < count)
         def _():
             target = stacked.at[pl.ds(slot * rows, rows), :]
             pltpu.make_async_copy(own.at[0], target, sem.at[slot]).wait()
@@ -132,9 +155,9 @@
 
 def neighbours(store):
     count = lax.axis_size("region")
-    up = [(i, i + 1) for i in range(count - 1)]
-    down = [(i + 1, i) for i in range(count - 1)]
-    return lax.ppermute(store, "region", up), lax.ppermute(store, "region", down)
+    even = [(i, i ^ 1) for i in range(count) if i ^ 1 < count]
+    odd = [(i, ((i + 1) ^ 1) - 1) for i in range(count) if 0 <= ((i + 1) ^ 1) - 1 < count]
+    return lax.ppermute(store, "region", even), lax.ppermute(store, "region", odd)
 
 
 def shards(ensemble, obs_store, block_ids, block_src, block_count):
@@ -143,9 +166,9 @@
     size = store.shape[2]
     slots = block_ids.shape[2]
     me = lax.axis_index("member").astype(jnp.int32).reshape(1)
-    below, above = neighbours(store)
+    region = lax.axis_index("region").astype(jnp.int32).reshape(1)
     smem = pl.BlockSpec(memory_space=pltpu.SMEM)
-    anywhere = pl.BlockSpec(memory_space=pl.ANY)
+    hbm = pl.BlockSpec(memory_space=pltpu.HBM)
     piece_shape = jax.ShapeDtypeStruct((rows, values), jnp.bfloat16)
 
     pieces = pl.pallas_call(
@@ -157,6 +180,8 @@
         cost_estimate=cost(2 * 256 * rows * patches * values, 4 * rows * patches * values),
         name="split",
     )(me, ensemble.reshape(rows * patches, values))
+    store, pieces = lax.optimization_barrier((store, pieces))
+    even, odd = neighbours(store)
     arrived = [pieces[0]] + [None] * (patches - 1)
     for k in partners(patches):
         arrived[k] = ppermute(pieces[k], "member", k)
@@ -164,23 +189,20 @@
     gram = pl.pallas_call(
         functools.partial(gram_kernel, 1.0 / (2.0 * size)),
         out_shape=jax.ShapeDtypeStruct((size, size), jnp.bfloat16),
-        in_specs=[smem] * 3 + [anywhere] * 3,
+        in_specs=[smem] + [hbm] * 6,
         out_specs=vmem(),
         scratch_shapes=[
+            pltpu.SMEM(block_ids.shape, jnp.int32),
+            pltpu.SMEM(block_src.shape, jnp.int32),
+            pltpu.SMEM(block_count.shape, jnp.int32),
             pltpu.VMEM((slots * store.shape[1], size), jnp.bfloat16),
+            pltpu.SemaphoreType.DMA((3,)),
             pltpu.SemaphoreType.DMA((slots,)),
         ],
         compiler_params=params(),
         cost_estimate=cost(2 * slots * store.shape[1] * size * size, 4 * size * size),
         name="gram",
-    )(
-        block_ids.reshape(slots),
-        block_src.reshape(slots),
-        block_count.reshape(1),
-        below,
-        store,
-        above,
-    )
+    )(region, block_ids, block_src, block_count, store, even, odd)
 
     moved = pl.pallas_call(
         functools.partial(transform_kernel, patches),

time: 70 us -> 71.2 us (1.017)
  Pallas kernels: 6.37 us -> 8.16 us
  waiting for transfers between devices: 34 us -> 32.8 us
    ppermute x14, waiting for transfers between devices: 34 us -> 32.8 us  [ppermute(): return lax.ppermute(value, axis, [(i, i ^ step) for i in range(count)])]
    pallas_call x1, Pallas kernels: 2.53 us -> 3.62 us  [shards(): pl.pallas_call(functools.partial(transform_kernel, patches), out_shape=[p...]
  transfers between devices with their start and end apart: 16 -> 16, of which waited for: 10 -> 9; matrix products, arithmetic and copies ran while one was open for 0% -> 0% of each run, Pallas kernels for 3% -> 3%
where the time goes in v3:
time: 71.2 us; the launch traced here: 71 us
  waiting for transfers between devices  32.8 us (46%)
  starting transfers between devices  25.5 us (36%)
  Pallas kernels  8.16 us (11%)
  local copies, waits for them, and re-layouts  3.84 us (5%)
    ppermute x14, waiting for transfers between devices, ppermute(): return lax.ppermute(value, axis, [(i, i ^ step) for i in range(count)])  32.8 us
    ppermute x14, starting transfers between devices, ppermute(): return lax.ppermute(value, axis, [(i, i ^ step) for i in range(count)])  21.9 us
    unnamed x8, local copies, waits for them, and re-layouts  3.84 us
    pallas_call x1, Pallas kernels, shards(): pl.pallas_call(functools.partial(transform_kernel, patches), out_shape=[p...  3.62 us
    ppermute x1, starting transfers between devices, neighbours(): lax.ppermute(store, 'region', even)  2.87 us
    pallas_call x1, Pallas kernels, shards(): pl.pallas_call(functools.partial(gram_kernel, 1.0 / (2.0 * size)), out_sh...  2.04 us
  transfers between devices with their start and end apart: 16, of which 9 were waited for; matrix products, arithmetic and copies ran while one was open for 0% of the time, Pallas kernels for 3%

profile of v3, /device:TPU:8, one launch (start us, length us, event | category | flops | bytes accessed | tf_op | source)
XLA Modules:
  0.0 71.0 jit_solution(14481816628699212311)
XLA Ops:
  0.0 1.2 %copy-done.1 = bf16[128,1,8,512]{3,2,1,0:T(8,128)(2,1)S(1)} copy-done((bf16[128,1,8,512]{3,2,1,0:T(8,128)(2,1)S(1)}, bf16[128,1,8,512]{3,2,1,0:T(8,128)(2,1)}, u32[]{:S(2)}) %copy-start.1) | copy-done | bytes 1048600
  3.1 2.9 %collective-permute-start = (bf16[5,128,1024]{2,1,0:T(8,128)(2,1)}, bf16[5,128,1024]{2,1,0:T(8,128)(2,1)S(1)}, u32[]{:S(2)}, u32[]{:S(2)}) collective-permute-start(bf16[5,128,1024]{2,1,0:T(8,128)(2,1)} %bitcast.8), channel_id=1, source_target_pairs={{0,1},{1,0},{2,3},{3,2},{4,5},{5,4},{6,7},{7,6},{8,9},{9,8},{10,11... | collective-permute-start | bytes 3932168 | tf_op jit(solution)/shard_map/ppermute | solution.py:160
  5.9 1.5 %collective-permute-start.2 = (bf16[128,512]{1,0:T(8,128)(2,1)S(1)}, bf16[128,512]{1,0:T(8,128)(2,1)S(1)}, u32[]{:S(2)}, u32[]{:S(2)}) collective-permute-start(bf16[128,512]{1,0:T(8,128)(2,1)S(1)} %get-tuple-element.40), channel_id=1, source_target_pairs={{0,4},{4,0},{8,12},{12,8},{16,20},{20,16},{24,28},{28,24},{1,5},{5... | collective-permute-start | bytes 393224 | tf_op jit(solution)/shard_map/ppermute | solution.py:28
  7.9 1.5 %collective-permute-start.4 = (bf16[128,512]{1,0:T(8,128)(2,1)}, bf16[128,512]{1,0:T(8,128)(2,1)S(1)}, u32[]{:S(2)}, u32[]{:S(2)}) collective-permute-start(bf16[128,512]{1,0:T(8,128)(2,1)} %get-tuple-element.42), channel_id=1, source_target_pairs={{0,12},{4,8},{8,4},{12,0},{16,28},{20,24},{24,20},{28,16},{1,13},{... | collective-permute-start | bytes 393224 | tf_op jit(solution)/shard_map/ppermute | solution.py:28
  9.4 2.0 %collective-permute-done.2.refs_1_ = bf16[128,512]{1,0:T(8,128)(2,1)S(1)} collective-permute-done((bf16[128,512]{1,0:T(8,128)(2,1)S(1)}, bf16[128,512]{1,0:T(8,128)(2,1)S(1)}, u32[]{:S(2)}, u32[]{:S(2)}) %collective-permute-start.2) | collective-permute-done | bytes 131104 | tf_op jit(solution)/shard_map/ppermute | solution.py:28
  11.4 2.6 %collective-permute-start.5 = (bf16[128,512]{1,0:T(8,128)(2,1)}, bf16[128,512]{1,0:T(8,128)(2,1)}, u32[]{:S(2)}, u32[]{:S(2)}) collective-permute-start(bf16[128,512]{1,0:T(8,128)(2,1)} %get-tuple-element.43), channel_id=1, source_target_pairs={{0,16},{4,20},{8,24},{12,28},{16,0},{20,4},{24,8},{28,12},{1,17},{... | collective-permute-start | bytes 393224 | tf_op jit(solution)/shard_map/ppermute | solution.py:28
  14.0 2.4 %collective-permute-start.6 = (bf16[128,512]{1,0:T(8,128)(2,1)S(1)}, bf16[128,512]{1,0:T(8,128)(2,1)}, u32[]{:S(2)}, u32[]{:S(2)}) collective-permute-start(bf16[128,512]{1,0:T(8,128)(2,1)S(1)} %get-tuple-element.44), channel_id=1, source_target_pairs={{0,20},{4,16},{8,28},{12,24},{16,4},{20,0},{24,12},{28,8},{1,21},{... | collective-permute-start | bytes 393224 | tf_op jit(solution)/shard_map/ppermute | solution.py:28
  16.9 2.5 %collective-permute-start.8 = (bf16[128,512]{1,0:T(8,128)(2,1)S(1)}, bf16[128,512]{1,0:T(8,128)(2,1)}, u32[]{:S(2)}, u32[]{:S(2)}) collective-permute-start(bf16[128,512]{1,0:T(8,128)(2,1)S(1)} %get-tuple-element.46), channel_id=1, source_target_pairs={{0,28},{4,24},{8,20},{12,16},{16,12},{20,8},{24,4},{28,0},{1,29},{... | collective-permute-start | bytes 393224 | tf_op jit(solution)/shard_map/ppermute | solution.py:28
  20.0 1.3 %copy-done = bf16[1,1,5,128,1024]{4,3,2,1,0:T(8,128)(2,1)S(1)} copy-done((bf16[1,1,5,128,1024]{4,3,2,1,0:T(8,128)(2,1)S(1)}, bf16[1,1,5,128,1024]{4,3,2,1,0:T(8,128)(2,1)}, u32[]{:S(2)}) %copy-start) | copy-done | bytes 1310744
  22.6 2.0 %gram.1.gram_ref = bf16[1024,1024]{1,0:T(8,128)(2,1)S(1)} custom-call(s32[1]{0:T(128)} %bitcast.1.region_ref, s32[1,1,3]{2,1,0:T(1,128)S(1)} %copy-done.2, s32[1,1,3]{2,1,0:T(1,128)S(1)} %copy-done.3, s32[1,1]{1,0:T(1,128)S(6)} %copy.7.count_hbm, bf16[5,128,1024]{2,1,0:T(8,128)(2,1)S(1)} %bitcast.9, bf16[5,128,1024]{2,1,0:T(8,128)(2,1)S(1)} %collective-permute-done.even, ...), custom_call_target="tpu_custom_call" | custom-call | flops 805306368 | bytes 4194304 | tf_op jit(solution)/shard_map/gram/pallas_call | solution.py:189
  25.7 5.6 %collective-permute-done.6.refs_5_ = bf16[128,512]{1,0:T(8,128)(2,1)} collective-permute-done((bf16[128,512]{1,0:T(8,128)(2,1)S(1)}, bf16[128,512]{1,0:T(8,128)(2,1)}, u32[]{:S(2)}, u32[]{:S(2)}) %collective-permute-start.6) | collective-permute-done | bytes 131104 | tf_op jit(solution)/shard_map/ppermute | solution.py:28
  31.3 2.8 %collective-permute-done.7.refs_6_ = bf16[128,512]{1,0:T(8,128)(2,1)} collective-permute-done((bf16[128,512]{1,0:T(8,128)(2,1)S(1)}, bf16[128,512]{1,0:T(8,128)(2,1)}, u32[]{:S(2)}, u32[]{:S(2)}) %collective-permute-start.7) | collective-permute-done | bytes 131104 | tf_op jit(solution)/shard_map/ppermute | solution.py:28
  34.1 2.8 %collective-permute-done.8.refs_7_ = bf16[128,512]{1,0:T(8,128)(2,1)} collective-permute-done((bf16[128,512]{1,0:T(8,128)(2,1)S(1)}, bf16[128,512]{1,0:T(8,128)(2,1)}, u32[]{:S(2)}, u32[]{:S(2)}) %collective-permute-start.8) | collective-permute-done | bytes 131104 | tf_op jit(solution)/shard_map/ppermute | solution.py:28
  36.9 3.6 %transform.1 = (bf16[128,512]{1,0:T(8,128)(2,1)S(1)}, bf16[128,512]{1,0:T(8,128)(2,1)S(1)}, bf16[128,512]{1,0:T(8,128)(2,1)S(1)}, bf16[128,512]{1,0:T(8,128)(2,1...) custom-call(s32[1]{0:T(128)} %bitcast.me_ref, ...), custom_call_target="tpu_custom_call" | custom-call | flops 2147483648 | bytes 4194304 | tf_op jit(solution)/shard_map/transform/pallas_call | solution.py:207
  41.4 2.7 %collective-permute-start.11 = (bf16[128,512]{1,0:T(8,128)(2,1)S(1)}, bf16[128,512]{1,0:T(8,128)(2,1)S(1)}, u32[]{:S(2)}, u32[]{:S(2)}) collective-permute-start(bf16[128,512]{1,0:T(8,128)(2,1)S(1)} %get-tuple-element.50), channel_id=1, source_target_pairs={{0,12},{4,8},{8,4},{12,0},{16,28},{20,24},{24,20},{28,16},{1,13},{... | collective-permute-start | bytes 393224 | tf_op jit(solution)/shard_map/ppermute | solution.py:28
  44.1 2.0 %collective-permute-start.12 = (bf16[128,512]{1,0:T(8,128)(2,1)S(1)}, bf16[128,512]{1,0:T(8,128)(2,1)S(1)}, u32[]{:S(2)}, u32[]{:S(2)}) collective-permute-start(bf16[128,512]{1,0:T(8,128)(2,1)S(1)} %get-tuple-element.51), channel_id=1, source_target_pairs={{0,16},{4,20},{8,24},{12,28},{16,0},{20,4},{24,8},{28,12},{1,17},{... | collective-permute-start | bytes 393224 | tf_op jit(solution)/shard_map/ppermute | solution.py:28
  46.1 1.2 %collective-permute-start.13 = (bf16[128,512]{1,0:T(8,128)(2,1)S(1)}, bf16[128,512]{1,0:T(8,128)(2,1)S(1)}, u32[]{:S(2)}, u32[]{:S(2)}) collective-permute-start(bf16[128,512]{1,0:T(8,128)(2,1)S(1)} %get-tuple-element.52), channel_id=1, source_target_pairs={{0,20},{4,16},{8,28},{12,24},{16,4},{20,0},{24,12},{28,8},{1,21},{... | collective-permute-start | bytes 393224 | tf_op jit(solution)/shard_map/ppermute | solution.py:28
  47.3 2.4 %collective-permute-start.14 = (bf16[128,512]{1,0:T(8,128)(2,1)S(1)}, bf16[128,512]{1,0:T(8,128)(2,1)S(1)}, u32[]{:S(2)}, u32[]{:S(2)}) collective-permute-start(bf16[128,512]{1,0:T(8,128)(2,1)S(1)} %get-tuple-element.53), channel_id=1, source_target_pairs={{0,24},{4,28},{8,16},{12,20},{16,8},{20,12},{24,0},{28,4},{1,25},{... | collective-permute-start | bytes 393224 | tf_op jit(solution)/shard_map/ppermute | solution.py:28
  49.6 1.4 %collective-permute-start.15 = (bf16[128,512]{1,0:T(8,128)(2,1)S(1)}, bf16[128,512]{1,0:T(8,128)(2,1)S(1)}, u32[]{:S(2)}, u32[]{:S(2)}) collective-permute-start(bf16[128,512]{1,0:T(8,128)(2,1)S(1)} %get-tuple-element.54), channel_id=1, source_target_pairs={{0,28},{4,24},{8,20},{12,16},{16,12},{20,8},{24,4},{28,0},{1,29},{... | collective-permute-start | bytes 393224 | tf_op jit(solution)/shard_map/ppermute | solution.py:28
  51.0 10.1 %collective-permute-done.12.refs_4_ = bf16[128,512]{1,0:T(8,128)(2,1)S(1)} collective-permute-done((bf16[128,512]{1,0:T(8,128)(2,1)S(1)}, bf16[128,512]{1,0:T(8,128)(2,1)S(1)}, u32[]{:S(2)}, u32[]{:S(2)}) %collective-permute-start.12) | collective-permute-done | bytes 131104 | tf_op jit(solution)/shard_map/ppermute | solution.py:28
  61.1 2.8 %collective-permute-done.13.refs_5_ = bf16[128,512]{1,0:T(8,128)(2,1)S(1)} collective-permute-done((bf16[128,512]{1,0:T(8,128)(2,1)S(1)}, bf16[128,512]{1,0:T(8,128)(2,1)S(1)}, u32[]{:S(2)}, u32[]{:S(2)}) %collective-permute-start.13) | collective-permute-done | bytes 131104 | tf_op jit(solution)/shard_map/ppermute | solution.py:28
  63.9 3.3 %collective-permute-done.14.refs_6_ = bf16[128,512]{1,0:T(8,128)(2,1)S(1)} collective-permute-done((bf16[128,512]{1,0:T(8,128)(2,1)S(1)}, bf16[128,512]{1,0:T(8,128)(2,1)S(1)}, u32[]{:S(2)}, u32[]{:S(2)}) %collective-permute-start.14) | collective-permute-done | bytes 131104 | tf_op jit(solution)/shard_map/ppermute | solution.py:28
  67.2 2.3 %collective-permute-done.15.refs_7_ = bf16[128,512]{1,0:T(8,128)(2,1)S(1)} collective-permute-done((bf16[128,512]{1,0:T(8,128)(2,1)S(1)}, bf16[128,512]{1,0:T(8,128)(2,1)S(1)}, u32[]{:S(2)}, u32[]{:S(2)}) %collective-permute-start.15) | collective-permute-done | bytes 131104 | tf_op jit(solution)/shard_map/ppermute | solution.py:28
  69.6 1.4 %merge.1 = bf16[1024,512]{1,0:T(8,128)(2,1)} custom-call(s32[1]{0:T(128)} %bitcast.me_ref, bf16[128,512]{1,0:T(8,128)(2,1)S(1)} %get-tuple-element.47.refs_0_, bf16[128,512]{1,0:T(8,128)(2,1)S(1)} %collective-permute-done.9.refs_1_, bf16[128,512]{1,0:T(8,128)(2,1)S(1)} %collective-permute-done.10.refs_2_, ...), custom_call_target="tpu_custom_call" | custom-call | flops 268435456 | bytes 2097152 | tf_op jit(solution)/shard_map/merge/pallas_call | solution.py:221
  (20 shorter events, 6.0 us)
Async XLA Ops:
  0.0 1.2 %copy-start.1 = (bf16[128,1,8,512]{3,2,1,0:T(8,128)(2,1)S(1)}, bf16[128,1,8,512]{3,2,1,0:T(8,128)(2,1)}, u32[]{:S(2)}) copy-start(bf16[128,1,8,512]{3,2,1,0:T(8,128)(2,1)} %param.5) | copy-start | bytes 3145732
  2.3 14.1 %collective-permute-start.1 = (bf16[5,128,1024]{2,1,0:T(8,128)(2,1)}, bf16[5,128,1024]{2,1,0:T(8,128)(2,1)S(1)}, u32[]{:S(2)}, u32[]{:S(2)}) collective-permute-start(bf16[5,128,1024]{2,1,0:T(8,128)(2,1)} %bitcast.7), channel_id=1, source_target_pairs={{1,2},{2,1},{5,6},{6,5},{9,10},{10,9},{13,14},{14,13},{17,18},{18,... | collective-permute-start | bytes 3932168 | tf_op jit(solution)/shard_map/ppermute | solution.py:160
  3.1 13.8 %collective-permute-start = (bf16[5,128,1024]{2,1,0:T(8,128)(2,1)}, bf16[5,128,1024]{2,1,0:T(8,128)(2,1)S(1)}, u32[]{:S(2)}, u32[]{:S(2)}) collective-permute-start(bf16[5,128,1024]{2,1,0:T(8,128)(2,1)} %bitcast.8), channel_id=1, source_target_pairs={{0,1},{1,0},{2,3},{3,2},{4,5},{5,4},{6,7},{7,6},{8,9},{9,8},{10,11... | collective-permute-start | bytes 3932168 | tf_op jit(solution)/shard_map/ppermute | solution.py:160
  5.9 5.5 %collective-permute-start.2 = (bf16[128,512]{1,0:T(8,128)(2,1)S(1)}, bf16[128,512]{1,0:T(8,128)(2,1)S(1)}, u32[]{:S(2)}, u32[]{:S(2)}) collective-permute-start(bf16[128,512]{1,0:T(8,128)(2,1)S(1)} %get-tuple-element.40), channel_id=1, source_target_pairs={{0,4},{4,0},{8,12},{12,8},{16,20},{20,16},{24,28},{28,24},{1,5},{5... | collective-permute-start | bytes 393224 | tf_op jit(solution)/shard_map/ppermute | solution.py:28
  7.4 6.6 %collective-permute-start.3 = (bf16[128,512]{1,0:T(8,128)(2,1)S(1)}, bf16[128,512]{1,0:T(8,128)(2,1)S(1)}, u32[]{:S(2)}, u32[]{:S(2)}) collective-permute-start(bf16[128,512]{1,0:T(8,128)(2,1)S(1)} %get-tuple-element.41), channel_id=1, source_target_pairs={{0,8},{4,12},{8,0},{12,4},{16,24},{20,28},{24,16},{28,20},{1,9},{5... | collective-permute-start | bytes 393224 | tf_op jit(solution)/shard_map/ppermute | solution.py:28
  7.9 16.8 %collective-permute-start.4 = (bf16[128,512]{1,0:T(8,128)(2,1)}, bf16[128,512]{1,0:T(8,128)(2,1)S(1)}, u32[]{:S(2)}, u32[]{:S(2)}) collective-permute-start(bf16[128,512]{1,0:T(8,128)(2,1)} %get-tuple-element.42), channel_id=1, source_target_pairs={{0,12},{4,8},{8,4},{12,0},{16,28},{20,24},{24,20},{28,16},{1,13},{... | collective-permute-start | bytes 393224 | tf_op jit(solution)/shard_map/ppermute | solution.py:28
  11.4 14.3 %collective-permute-start.5 = (bf16[128,512]{1,0:T(8,128)(2,1)}, bf16[128,512]{1,0:T(8,128)(2,1)}, u32[]{:S(2)}, u32[]{:S(2)}) collective-permute-start(bf16[128,512]{1,0:T(8,128)(2,1)} %get-tuple-element.43), channel_id=1, source_target_pairs={{0,16},{4,20},{8,24},{12,28},{16,0},{20,4},{24,8},{28,12},{1,17},{... | collective-permute-start | bytes 393224 | tf_op jit(solution)/shard_map/ppermute | solution.py:28
  14.0 17.3 %collective-permute-start.6 = (bf16[128,512]{1,0:T(8,128)(2,1)S(1)}, bf16[128,512]{1,0:T(8,128)(2,1)}, u32[]{:S(2)}, u32[]{:S(2)}) collective-permute-start(bf16[128,512]{1,0:T(8,128)(2,1)S(1)} %get-tuple-element.44), channel_id=1, source_target_pairs={{0,20},{4,16},{8,28},{12,24},{16,4},{20,0},{24,12},{28,8},{1,21},{... | collective-permute-start | bytes 393224 | tf_op jit(solution)/shard_map/ppermute | solution.py:28
  16.4 17.8 %collective-permute-start.7 = (bf16[128,512]{1,0:T(8,128)(2,1)S(1)}, bf16[128,512]{1,0:T(8,128)(2,1)}, u32[]{:S(2)}, u32[]{:S(2)}) collective-permute-start(bf16[128,512]{1,0:T(8,128)(2,1)S(1)} %get-tuple-element.45), channel_id=1, source_target_pairs={{0,24},{4,28},{8,16},{12,20},{16,8},{20,12},{24,0},{28,4},{1,25},{... | collective-permute-start | bytes 393224 | tf_op jit(solution)/shard_map/ppermute | solution.py:28
  16.9 20.0 %collective-permute-start.8 = (bf16[128,512]{1,0:T(8,128)(2,1)S(1)}, bf16[128,512]{1,0:T(8,128)(2,1)}, u32[]{:S(2)}, u32[]{:S(2)}) collective-permute-start(bf16[128,512]{1,0:T(8,128)(2,1)S(1)} %get-tuple-element.46), channel_id=1, source_target_pairs={{0,28},{4,24},{8,20},{12,16},{16,12},{20,8},{24,4},{28,0},{1,29},{... | collective-permute-start | bytes 393224 | tf_op jit(solution)/shard_map/ppermute | solution.py:28
  20.0 1.3 %copy-start = (bf16[1,1,5,128,1024]{4,3,2,1,0:T(8,128)(2,1)S(1)}, bf16[1,1,5,128,1024]{4,3,2,1,0:T(8,128)(2,1)}, u32[]{:S(2)}) copy-start(bf16[1,1,5,128,1024]{4,3,2,1,0:T(8,128)(2,1)} %param.6) | copy-start | bytes 3932164
  21.3 0.7 copy-start.2
  22.0 0.7 copy-start.3
  40.5 6.7 %collective-permute-start.9 = (bf16[128,512]{1,0:T(8,128)(2,1)S(1)}, bf16[128,512]{1,0:T(8,128)(2,1)S(1)}, u32[]{:S(2)}, u32[]{:S(2)}) collective-permute-start(bf16[128,512]{1,0:T(8,128)(2,1)S(1)} %get-tuple-element.48), channel_id=1, source_target_pairs={{0,4},{4,0},{8,12},{12,8},{16,20},{20,16},{24,28},{28,24},{1,5},{5... | collective-permute-start | bytes 393224 | tf_op jit(solution)/shard_map/ppermute | solution.py:28
  41.4 8.2 %collective-permute-start.10 = (bf16[128,512]{1,0:T(8,128)(2,1)S(1)}, bf16[128,512]{1,0:T(8,128)(2,1)S(1)}, u32[]{:S(2)}, u32[]{:S(2)}) collective-permute-start(bf16[128,512]{1,0:T(8,128)(2,1)S(1)} %get-tuple-element.49), channel_id=1, source_target_pairs={{0,8},{4,12},{8,0},{12,4},{16,24},{20,28},{24,16},{28,20},{1,9},{5... | collective-permute-start | bytes 393224 | tf_op jit(solution)/shard_map/ppermute | solution.py:28
  41.4 9.6 %collective-permute-start.11 = (bf16[128,512]{1,0:T(8,128)(2,1)S(1)}, bf16[128,512]{1,0:T(8,128)(2,1)S(1)}, u32[]{:S(2)}, u32[]{:S(2)}) collective-permute-start(bf16[128,512]{1,0:T(8,128)(2,1)S(1)} %get-tuple-element.50), channel_id=1, source_target_pairs={{0,12},{4,8},{8,4},{12,0},{16,28},{20,24},{24,20},{28,16},{1,13},{... | collective-permute-start | bytes 393224 | tf_op jit(solution)/shard_map/ppermute | solution.py:28
  44.1 17.0 %collective-permute-start.12 = (bf16[128,512]{1,0:T(8,128)(2,1)S(1)}, bf16[128,512]{1,0:T(8,128)(2,1)S(1)}, u32[]{:S(2)}, u32[]{:S(2)}) collective-permute-start(bf16[128,512]{1,0:T(8,128)(2,1)S(1)} %get-tuple-element.51), channel_id=1, source_target_pairs={{0,16},{4,20},{8,24},{12,28},{16,0},{20,4},{24,8},{28,12},{1,17},{... | collective-permute-start | bytes 393224 | tf_op jit(solution)/shard_map/ppermute | solution.py:28
  46.1 17.9 %collective-permute-start.13 = (bf16[128,512]{1,0:T(8,128)(2,1)S(1)}, bf16[128,512]{1,0:T(8,128)(2,1)S(1)}, u32[]{:S(2)}, u32[]{:S(2)}) collective-permute-start(bf16[128,512]{1,0:T(8,128)(2,1)S(1)} %get-tuple-element.52), channel_id=1, source_target_pairs={{0,20},{4,16},{8,28},{12,24},{16,4},{20,0},{24,12},{28,8},{1,21},{... | collective-permute-start | bytes 393224 | tf_op jit(solution)/shard_map/ppermute | solution.py:28
  47.3 20.0 %collective-permute-start.14 = (bf16[128,512]{1,0:T(8,128)(2,1)S(1)}, bf16[128,512]{1,0:T(8,128)(2,1)S(1)}, u32[]{:S(2)}, u32[]{:S(2)}) collective-permute-start(bf16[128,512]{1,0:T(8,128)(2,1)S(1)} %get-tuple-element.53), channel_id=1, source_target_pairs={{0,24},{4,28},{8,16},{12,20},{16,8},{20,12},{24,0},{28,4},{1,25},{... | collective-permute-start | bytes 393224 | tf_op jit(solution)/shard_map/ppermute | solution.py:28
  49.6 20.0 %collective-permute-start.15 = (bf16[128,512]{1,0:T(8,128)(2,1)S(1)}, bf16[128,512]{1,0:T(8,128)(2,1)S(1)}, u32[]{:S(2)}, u32[]{:S(2)}) collective-permute-start(bf16[128,512]{1,0:T(8,128)(2,1)S(1)} %get-tuple-element.54), channel_id=1, source_target_pairs={{0,28},{4,24},{8,20},{12,16},{16,12},{20,8},{24,4},{28,0},{1,29},{... | collective-permute-start | bytes 393224 | tf_op jit(solution)/shard_map/ppermute | solution.py:28

commit v4 on v3

--- a/solution.py
+++ b/solution.py
@@ -7,7 +7,8 @@
 from jax.experimental.pallas import tpu as pltpu
 from jax.sharding import PartitionSpec as P
 
-LIMIT = 40 * 1024 * 1024
+EARLY = 2
+LIMIT = 16 * 1024 * 1024
 
 
 def rows_per_group(rows, patches):
@@ -20,10 +21,12 @@
     order = []
     for i in range(len(far)):
         order += far[i : i + 1] + near[i : i + 1]
-    return order
+    return order + [0]
 
 
 def ppermute(value, axis, step):
+    if step == 0:
+        return value
     count = lax.axis_size(axis)
     return lax.ppermute(value, axis, [(i, i ^ step) for i in range(count)])
 
@@ -45,9 +48,9 @@
             out_ref[step * group : (step + 1) * group, :] = moved[k * group : (k + 1) * group, :]
 
 
-def merge_kernel(me_ref, *refs):
-    piece_refs, out_ref = refs[:-1], refs[-1]
-    patches = len(piece_refs)
+def merge_kernel(order, me_ref, *refs):
+    patches = len(order)
+    piece_refs, out_ref = dict(zip(order, refs)), refs[-1]
     rows = piece_refs[0].shape[0]
     group = rows_per_group(rows, patches)
     height = group * patches
@@ -57,7 +60,7 @@
     shuffle = jnp.where(column == source, 1.0, 0.0).astype(jnp.bfloat16)
     for step in range(rows // group):
         here = slice(step * group, (step + 1) * group)
-        block = jnp.concatenate([piece_ref[here, :] for piece_ref in piece_refs], axis=0)
+        block = jnp.concatenate([piece_refs[k][here, :] for k in range(patches)], axis=0)
         moved = jnp.dot(shuffle, block, preferred_element_type=jnp.float32)
         out_ref[step * height : (step + 1) * height, :] = moved.astype(jnp.bfloat16)
 
@@ -115,10 +118,12 @@
         gram_ref[step * part : (step + 1) * part, :] = (block * scale).astype(jnp.bfloat16)
 
 
-def transform_kernel(count, me_ref, gram_ref, *refs):
-    piece_refs, out_refs = refs[:count], refs[count : 2 * count]
-    members, first, fresh = refs[2 * count :]
-    rows = piece_refs[0].shape[0]
+def transform_kernel(order, me_ref, *refs):
+    count = len(order)
+    piece_refs = dict(zip(order, refs[:EARLY] + refs[EARLY + 1 : count + 1]))
+    gram_ref, out_refs = refs[EARLY], refs[count + 1 : 2 * count + 1]
+    members, first, fresh = refs[2 * count + 1 :]
+    rows = out_refs[0].shape[0]
 
     def place(k):
         return pl.ds(pl.multiple_of((me_ref[0] ^ k) * rows, rows), rows)
@@ -182,9 +187,8 @@
     )(me, ensemble.reshape(rows * patches, values))
     store, pieces = lax.optimization_barrier((store, pieces))
     even, odd = neighbours(store)
-    arrived = [pieces[0]] + [None] * (patches - 1)
-    for k in partners(patches):
-        arrived[k] = ppermute(pieces[k], "member", k)
+    order = partners(patches)
+    arrived = [ppermute(pieces[k], "member", k) for k in order]
 
     gram = pl.pallas_call(
         functools.partial(gram_kernel, 1.0 / (2.0 * size)),
@@ -205,7 +209,7 @@
     )(region, block_ids, block_src, block_count, store, even, odd)
 
     moved = pl.pallas_call(
-        functools.partial(transform_kernel, patches),
+        functools.partial(transform_kernel, order),
         out_shape=[piece_shape] * patches,
         in_specs=[smem] + [vmem()] * (1 + patches),
         out_specs=[vmem()] * patches,
@@ -213,13 +217,11 @@
         compiler_params=params(),
         cost_estimate=cost(4 * size * size * values, 2 * size * size + 4 * size * values),
         name="transform",
-    )(me, gram, *arrived)
-    returned = [moved[0]] + [None] * (patches - 1)
-    for k in partners(patches):
-        returned[k] = ppermute(moved[k], "member", k)
+    )(me, *arrived[:EARLY], gram, *arrived[EARLY:])
+    returned = [ppermute(moved[k], "member", k) for k in order]
 
     fresh = pl.pallas_call(
-        merge_kernel,
+        functools.partial(merge_kernel, order),
         out_shape=jax.ShapeDtypeStruct((rows * patches, values), jnp.bfloat16),
         in_specs=[smem] + [vmem()] * patches,
         out_specs=vmem(),

time: 71.2 us -> 64.1 us (0.900)
  the two profiles are of different devices: /device:TPU:8 before, /device:TPU:0 now
where the time goes in v4:
time: 64.1 us; the launch traced here: 63.9 us
  starting transfers between devices  26.6 us (41%)
  waiting for transfers between devices  24.6 us (38%)
  Pallas kernels  8.14 us (13%)
  local copies, waits for them, and re-layouts  3.84 us (6%)
  between operations  0.72 us (1%)
    ppermute x14, waiting for transfers between devices, ppermute(): return lax.ppermute(value, axis, [(i, i ^ step) for i in range(count)])  24.6 us
    ppermute x14, starting transfers between devices, ppermute(): return lax.ppermute(value, axis, [(i, i ^ step) for i in range(count)])  21.5 us
    ppermute x1, starting transfers between devices, neighbours(): lax.ppermute(store, 'region', even)  4.31 us
    unnamed x8, local copies, waits for them, and re-layouts  3.84 us
    pallas_call x1, Pallas kernels, shards(): pl.pallas_call(functools.partial(transform_kernel, order), out_shape=[pie...  3.62 us
    pallas_call x1, Pallas kernels, shards(): pl.pallas_call(functools.partial(gram_kernel, 1.0 / (2.0 * size)), out_sh...  2.02 us
    pallas_call x1, Pallas kernels, shards(): pl.pallas_call(functools.partial(merge_kernel, order), out_shape=jax.Shap...  1.41 us
  transfers between devices with their start and end apart: 16, of which 10 were waited for; matrix products, arithmetic and copies ran while one was open for 0% of the time, Pallas kernels for 3%

profile of v4, /device:TPU:0, one launch (start us, length us, event | category | flops | bytes accessed | tf_op | source)
XLA Modules:
  0.0 63.9 jit_solution(11447820826647924911)
XLA Ops:
  0.0 1.2 %copy-done.1 = bf16[128,1,8,512]{3,2,1,0:T(8,128)(2,1)S(1)} copy-done((bf16[128,1,8,512]{3,2,1,0:T(8,128)(2,1)S(1)}, bf16[128,1,8,512]{3,2,1,0:T(8,128)(2,1)}, u32[]{:S(2)}) %copy-start.1) | copy-done | bytes 1048600
  1.2 1.1 %split.1 = (bf16[128,512]{1,0:T(8,128)(2,1)S(1)}, bf16[128,512]{1,0:T(8,128)(2,1)S(1)}, bf16[128,512]{1,0:T(8,128)(2,1)}, bf16[128,512]{1,0:T(8,128)(2,1)S(1)}, ...) custom-call(s32[1]{0:T(128)} %bitcast.me_ref, ...), custom_call_target="tpu_custom_call" | custom-call | flops 268435456 | bytes 2097152 | tf_op jit(solution)/shard_map/split/pallas_call | solution.py:179
  3.0 4.3 %collective-permute-start.2 = (bf16[5,128,1024]{2,1,0:T(8,128)(2,1)}, bf16[5,128,1024]{2,1,0:T(8,128)(2,1)S(1)}, u32[]{:S(2)}, u32[]{:S(2)}) collective-permute-start(bf16[5,128,1024]{2,1,0:T(8,128)(2,1)} %bitcast.8), channel_id=1, source_target_pairs={{0,1},{1,0},{2,3},{3,2},{4,5},{5,4},{6,7},{7,6},{8,9},{9,8},{10,11... | collective-permute-start | bytes 3932168 | tf_op jit(solution)/shard_map/ppermute | solution.py:165
  7.4 4.5 %collective-permute-start = (bf16[128,512]{1,0:T(8,128)(2,1)S(1)}, bf16[128,512]{1,0:T(8,128)(2,1)S(1)}, u32[]{:S(2)}, u32[]{:S(2)}) collective-permute-start(bf16[128,512]{1,0:T(8,128)(2,1)S(1)} %get-tuple-element.38), channel_id=1, source_target_pairs={{0,28},{4,24},{8,20},{12,16},{16,12},{20,8},{24,4},{28,0},{1,29},{... | collective-permute-start | bytes 393224 | tf_op jit(solution)/shard_map/ppermute | solution.py:31
  11.9 0.9 %collective-permute-start.4 = (bf16[128,512]{1,0:T(8,128)(2,1)}, bf16[128,512]{1,0:T(8,128)(2,1)S(1)}, u32[]{:S(2)}, u32[]{:S(2)}) collective-permute-start(bf16[128,512]{1,0:T(8,128)(2,1)} %get-tuple-element.41), channel_id=1, source_target_pairs={{0,24},{4,28},{8,16},{12,20},{16,8},{20,12},{24,0},{28,4},{1,25},{... | collective-permute-start | bytes 393224 | tf_op jit(solution)/shard_map/ppermute | solution.py:31
  12.8 3.7 %collective-permute-done.refs_0_ = bf16[128,512]{1,0:T(8,128)(2,1)S(1)} collective-permute-done((bf16[128,512]{1,0:T(8,128)(2,1)S(1)}, bf16[128,512]{1,0:T(8,128)(2,1)S(1)}, u32[]{:S(2)}, u32[]{:S(2)}) %collective-permute-start) | collective-permute-done | bytes 131104 | tf_op jit(solution)/shard_map/ppermute | solution.py:31
  16.4 3.5 %collective-permute-start.5 = (bf16[128,512]{1,0:T(8,128)(2,1)}, bf16[128,512]{1,0:T(8,128)(2,1)}, u32[]{:S(2)}, u32[]{:S(2)}) collective-permute-start(bf16[128,512]{1,0:T(8,128)(2,1)} %get-tuple-element.42), channel_id=1, source_target_pairs={{0,8},{4,12},{8,0},{12,4},{16,24},{20,28},{24,16},{28,20},{1,9},{5... | collective-permute-start | bytes 393224 | tf_op jit(solution)/shard_map/ppermute | solution.py:31
  21.6 0.9 %collective-permute-start.7 = (bf16[128,512]{1,0:T(8,128)(2,1)S(1)}, bf16[128,512]{1,0:T(8,128)(2,1)}, u32[]{:S(2)}, u32[]{:S(2)}) collective-permute-start(bf16[128,512]{1,0:T(8,128)(2,1)S(1)} %get-tuple-element.44), channel_id=1, source_target_pairs={{0,4},{4,0},{8,12},{12,8},{16,20},{20,16},{24,28},{28,24},{1,5},{5... | collective-permute-start | bytes 393224 | tf_op jit(solution)/shard_map/ppermute | solution.py:31
  22.5 2.7 %collective-permute-start.8 = (bf16[128,512]{1,0:T(8,128)(2,1)S(1)}, bf16[128,512]{1,0:T(8,128)(2,1)}, u32[]{:S(2)}, u32[]{:S(2)}) collective-permute-start(bf16[128,512]{1,0:T(8,128)(2,1)S(1)} %get-tuple-element.45), channel_id=1, source_target_pairs={{0,16},{4,20},{8,24},{12,28},{16,0},{20,4},{24,8},{28,12},{1,17},{... | collective-permute-start | bytes 393224 | tf_op jit(solution)/shard_map/ppermute | solution.py:31
  25.8 1.3 %copy-done = bf16[1,1,5,128,1024]{4,3,2,1,0:T(8,128)(2,1)S(1)} copy-done((bf16[1,1,5,128,1024]{4,3,2,1,0:T(8,128)(2,1)S(1)}, bf16[1,1,5,128,1024]{4,3,2,1,0:T(8,128)(2,1)}, u32[]{:S(2)}) %copy-start) | copy-done | bytes 1310744
  28.4 2.0 %gram.1.refs_2_ = bf16[1024,1024]{1,0:T(8,128)(2,1)S(1)} custom-call(s32[1]{0:T(128)} %bitcast.3.region_ref, s32[1,1,3]{2,1,0:T(1,128)S(1)} %copy-done.2, s32[1,1,3]{2,1,0:T(1,128)S(1)} %copy-done.3, s32[1,1]{1,0:T(1,128)S(6)} %copy.7.count_hbm, bf16[5,128,1024]{2,1,0:T(8,128)(2,1)S(1)} %bitcast.9, bf16[5,128,1024]{2,1,0:T(8,128)(2,1)S(1)} %collective-permute-done.2.even, ...), custom_call_target="tpu_custom_call" | custom-call | flops 805306368 | bytes 4194304 | tf_op jit(solution)/shard_map/gram/pallas_call | solution.py:193
  30.5 2.4 %collective-permute-done.6.refs_5_ = bf16[128,512]{1,0:T(8,128)(2,1)} collective-permute-done((bf16[128,512]{1,0:T(8,128)(2,1)S(1)}, bf16[128,512]{1,0:T(8,128)(2,1)}, u32[]{:S(2)}, u32[]{:S(2)}) %collective-permute-start.6) | collective-permute-done | bytes 131104 | tf_op jit(solution)/shard_map/ppermute | solution.py:31
  32.9 1.8 %collective-permute-done.8.refs_7_ = bf16[128,512]{1,0:T(8,128)(2,1)} collective-permute-done((bf16[128,512]{1,0:T(8,128)(2,1)S(1)}, bf16[128,512]{1,0:T(8,128)(2,1)}, u32[]{:S(2)}, u32[]{:S(2)}) %collective-permute-start.8) | collective-permute-done | bytes 131104 | tf_op jit(solution)/shard_map/ppermute | solution.py:31
  34.7 3.6 %transform.1 = (bf16[128,512]{1,0:T(8,128)(2,1)S(1)}, bf16[128,512]{1,0:T(8,128)(2,1)S(1)}, bf16[128,512]{1,0:T(8,128)(2,1)S(1)}, bf16[128,512]{1,0:T(8,128)(2,1...) custom-call(s32[1]{0:T(128)} %bitcast.me_ref, ...), custom_call_target="tpu_custom_call" | custom-call | flops 2147483648 | bytes 4194304 | tf_op jit(solution)/shard_map/transform/pallas_call | solution.py:211
  38.3 2.1 %collective-permute-start.9 = (bf16[128,512]{1,0:T(8,128)(2,1)S(1)}, bf16[128,512]{1,0:T(8,128)(2,1)S(1)}, u32[]{:S(2)}, u32[]{:S(2)}) collective-permute-start(bf16[128,512]{1,0:T(8,128)(2,1)S(1)} %get-tuple-element.47), channel_id=1, source_target_pairs={{0,28},{4,24},{8,20},{12,16},{16,12},{20,8},{24,4},{28,0},{1,29},{... | collective-permute-start | bytes 393224 | tf_op jit(solution)/shard_map/ppermute | solution.py:31
  40.5 1.7 %collective-permute-start.11 = (bf16[128,512]{1,0:T(8,128)(2,1)S(1)}, bf16[128,512]{1,0:T(8,128)(2,1)S(1)}, u32[]{:S(2)}, u32[]{:S(2)}) collective-permute-start(bf16[128,512]{1,0:T(8,128)(2,1)S(1)} %get-tuple-element.49), channel_id=1, source_target_pairs={{0,24},{4,28},{8,16},{12,20},{16,8},{20,12},{24,0},{28,4},{1,25},{... | collective-permute-start | bytes 393224 | tf_op jit(solution)/shard_map/ppermute | solution.py:31
  42.2 2.0 %collective-permute-start.12 = (bf16[128,512]{1,0:T(8,128)(2,1)S(1)}, bf16[128,512]{1,0:T(8,128)(2,1)S(1)}, u32[]{:S(2)}, u32[]{:S(2)}) collective-permute-start(bf16[128,512]{1,0:T(8,128)(2,1)S(1)} %get-tuple-element.50), channel_id=1, source_target_pairs={{0,8},{4,12},{8,0},{12,4},{16,24},{20,28},{24,16},{28,20},{1,9},{5... | collective-permute-start | bytes 393224 | tf_op jit(solution)/shard_map/ppermute | solution.py:31
  44.2 1.8 %collective-permute-start.13 = (bf16[128,512]{1,0:T(8,128)(2,1)S(1)}, bf16[128,512]{1,0:T(8,128)(2,1)S(1)}, u32[]{:S(2)}, u32[]{:S(2)}) collective-permute-start(bf16[128,512]{1,0:T(8,128)(2,1)S(1)} %get-tuple-element.51), channel_id=1, source_target_pairs={{0,20},{4,16},{8,28},{12,24},{16,4},{20,0},{24,12},{28,8},{1,21},{... | collective-permute-start | bytes 393224 | tf_op jit(solution)/shard_map/ppermute | solution.py:31
  46.0 1.6 %collective-permute-done.9.refs_0_ = bf16[128,512]{1,0:T(8,128)(2,1)S(1)} collective-permute-done((bf16[128,512]{1,0:T(8,128)(2,1)S(1)}, bf16[128,512]{1,0:T(8,128)(2,1)S(1)}, u32[]{:S(2)}, u32[]{:S(2)}) %collective-permute-start.9) | collective-permute-done | bytes 131104 | tf_op jit(solution)/shard_map/ppermute | solution.py:31
  48.2 3.6 %collective-permute-done.10.refs_1_ = bf16[128,512]{1,0:T(8,128)(2,1)S(1)} collective-permute-done((bf16[128,512]{1,0:T(8,128)(2,1)S(1)}, bf16[128,512]{1,0:T(8,128)(2,1)S(1)}, u32[]{:S(2)}, u32[]{:S(2)}) %collective-permute-start.10) | collective-permute-done | bytes 131104 | tf_op jit(solution)/shard_map/ppermute | solution.py:31
  52.4 2.9 %collective-permute-done.12.refs_3_ = bf16[128,512]{1,0:T(8,128)(2,1)S(1)} collective-permute-done((bf16[128,512]{1,0:T(8,128)(2,1)S(1)}, bf16[128,512]{1,0:T(8,128)(2,1)S(1)}, u32[]{:S(2)}, u32[]{:S(2)}) %collective-permute-start.12) | collective-permute-done | bytes 131104 | tf_op jit(solution)/shard_map/ppermute | solution.py:31
  55.2 5.7 %collective-permute-done.13.refs_4_ = bf16[128,512]{1,0:T(8,128)(2,1)S(1)} collective-permute-done((bf16[128,512]{1,0:T(8,128)(2,1)S(1)}, bf16[128,512]{1,0:T(8,128)(2,1)S(1)}, u32[]{:S(2)}, u32[]{:S(2)}) %collective-permute-start.13) | collective-permute-done | bytes 131104 | tf_op jit(solution)/shard_map/ppermute | solution.py:31
  60.9 1.5 %collective-permute-done.15.refs_6_ = bf16[128,512]{1,0:T(8,128)(2,1)S(1)} collective-permute-done((bf16[128,512]{1,0:T(8,128)(2,1)S(1)}, bf16[128,512]{1,0:T(8,128)(2,1)S(1)}, u32[]{:S(2)}, u32[]{:S(2)}) %collective-permute-start.15) | collective-permute-done | bytes 131104 | tf_op jit(solution)/shard_map/ppermute | solution.py:31
  62.5 1.4 %merge.1 = bf16[1024,512]{1,0:T(8,128)(2,1)} custom-call(s32[1]{0:T(128)} %bitcast.me_ref, bf16[128,512]{1,0:T(8,128)(2,1)S(1)} %collective-permute-done.9.refs_0_, bf16[128,512]{1,0:T(8,128)(2,1)S(1)} %collective-permute-done.10.refs_1_, bf16[128,512]{1,0:T(8,128)(2,1)S(1)} %collective-permute-done.11.refs_2_, ...), custom_call_target="tpu_custom_call" | custom-call | flops 268435456 | bytes 2097152 | tf_op jit(solution)/shard_map/merge/pallas_call | solution.py:223
  (20 shorter events, 4.8 us)
Async XLA Ops:
  0.0 1.2 %copy-start.1 = (bf16[128,1,8,512]{3,2,1,0:T(8,128)(2,1)S(1)}, bf16[128,1,8,512]{3,2,1,0:T(8,128)(2,1)}, u32[]{:S(2)}) copy-start(bf16[128,1,8,512]{3,2,1,0:T(8,128)(2,1)} %param.5) | copy-start | bytes 3145732
  2.3 19.3 %collective-permute-start.3 = (bf16[5,128,1024]{2,1,0:T(8,128)(2,1)}, bf16[5,128,1024]{2,1,0:T(8,128)(2,1)S(1)}, u32[]{:S(2)}, u32[]{:S(2)}) collective-permute-start(bf16[5,128,1024]{2,1,0:T(8,128)(2,1)} %bitcast.7), channel_id=1, source_target_pairs={{1,2},{2,1},{5,6},{6,5},{9,10},{10,9},{13,14},{14,13},{17,18},{18,... | collective-permute-start | bytes 3932168 | tf_op jit(solution)/shard_map/ppermute | solution.py:165
  3.0 19.4 %collective-permute-start.2 = (bf16[5,128,1024]{2,1,0:T(8,128)(2,1)}, bf16[5,128,1024]{2,1,0:T(8,128)(2,1)S(1)}, u32[]{:S(2)}, u32[]{:S(2)}) collective-permute-start(bf16[5,128,1024]{2,1,0:T(8,128)(2,1)} %bitcast.8), channel_id=1, source_target_pairs={{0,1},{1,0},{2,3},{3,2},{4,5},{5,4},{6,7},{7,6},{8,9},{9,8},{10,11... | collective-permute-start | bytes 3932168 | tf_op jit(solution)/shard_map/ppermute | solution.py:165
  7.4 9.1 %collective-permute-start = (bf16[128,512]{1,0:T(8,128)(2,1)S(1)}, bf16[128,512]{1,0:T(8,128)(2,1)S(1)}, u32[]{:S(2)}, u32[]{:S(2)}) collective-permute-start(bf16[128,512]{1,0:T(8,128)(2,1)S(1)} %get-tuple-element.38), channel_id=1, source_target_pairs={{0,28},{4,24},{8,20},{12,16},{16,12},{20,8},{24,4},{28,0},{1,29},{... | collective-permute-start | bytes 393224 | tf_op jit(solution)/shard_map/ppermute | solution.py:31
  11.9 8.9 %collective-permute-start.1 = (bf16[128,512]{1,0:T(8,128)(2,1)S(1)}, bf16[128,512]{1,0:T(8,128)(2,1)S(1)}, u32[]{:S(2)}, u32[]{:S(2)}) collective-permute-start(bf16[128,512]{1,0:T(8,128)(2,1)S(1)} %get-tuple-element.39), channel_id=1, source_target_pairs={{0,12},{4,8},{8,4},{12,0},{16,28},{20,24},{24,20},{28,16},{1,13},{... | collective-permute-start | bytes 393224 | tf_op jit(solution)/shard_map/ppermute | solution.py:31
  11.9 18.6 %collective-permute-start.4 = (bf16[128,512]{1,0:T(8,128)(2,1)}, bf16[128,512]{1,0:T(8,128)(2,1)S(1)}, u32[]{:S(2)}, u32[]{:S(2)}) collective-permute-start(bf16[128,512]{1,0:T(8,128)(2,1)} %get-tuple-element.41), channel_id=1, source_target_pairs={{0,24},{4,28},{8,16},{12,20},{16,8},{20,12},{24,0},{28,4},{1,25},{... | collective-permute-start | bytes 393224 | tf_op jit(solution)/shard_map/ppermute | solution.py:31
  16.4 14.0 %collective-permute-start.5 = (bf16[128,512]{1,0:T(8,128)(2,1)}, bf16[128,512]{1,0:T(8,128)(2,1)}, u32[]{:S(2)}, u32[]{:S(2)}) collective-permute-start(bf16[128,512]{1,0:T(8,128)(2,1)} %get-tuple-element.42), channel_id=1, source_target_pairs={{0,8},{4,12},{8,0},{12,4},{16,24},{20,28},{24,16},{28,20},{1,9},{5... | collective-permute-start | bytes 393224 | tf_op jit(solution)/shard_map/ppermute | solution.py:31
  20.8 12.1 %collective-permute-start.6 = (bf16[128,512]{1,0:T(8,128)(2,1)S(1)}, bf16[128,512]{1,0:T(8,128)(2,1)}, u32[]{:S(2)}, u32[]{:S(2)}) collective-permute-start(bf16[128,512]{1,0:T(8,128)(2,1)S(1)} %get-tuple-element.43), channel_id=1, source_target_pairs={{0,20},{4,16},{8,28},{12,24},{16,4},{20,0},{24,12},{28,8},{1,21},{... | collective-permute-start | bytes 393224 | tf_op jit(solution)/shard_map/ppermute | solution.py:31
  21.6 11.3 %collective-permute-start.7 = (bf16[128,512]{1,0:T(8,128)(2,1)S(1)}, bf16[128,512]{1,0:T(8,128)(2,1)}, u32[]{:S(2)}, u32[]{:S(2)}) collective-permute-start(bf16[128,512]{1,0:T(8,128)(2,1)S(1)} %get-tuple-element.44), channel_id=1, source_target_pairs={{0,4},{4,0},{8,12},{12,8},{16,20},{20,16},{24,28},{28,24},{1,5},{5... | collective-permute-start | bytes 393224 | tf_op jit(solution)/shard_map/ppermute | solution.py:31
  22.5 12.2 %collective-permute-start.8 = (bf16[128,512]{1,0:T(8,128)(2,1)S(1)}, bf16[128,512]{1,0:T(8,128)(2,1)}, u32[]{:S(2)}, u32[]{:S(2)}) collective-permute-start(bf16[128,512]{1,0:T(8,128)(2,1)S(1)} %get-tuple-element.45), channel_id=1, source_target_pairs={{0,16},{4,20},{8,24},{12,28},{16,0},{20,4},{24,8},{28,12},{1,17},{... | collective-permute-start | bytes 393224 | tf_op jit(solution)/shard_map/ppermute | solution.py:31
  25.8 1.3 %copy-start = (bf16[1,1,5,128,1024]{4,3,2,1,0:T(8,128)(2,1)S(1)}, bf16[1,1,5,128,1024]{4,3,2,1,0:T(8,128)(2,1)}, u32[]{:S(2)}) copy-start(bf16[1,1,5,128,1024]{4,3,2,1,0:T(8,128)(2,1)} %param.6) | copy-start | bytes 3932164
  27.1 0.7 %copy-start.2 = (s32[1,1,3]{2,1,0:T(1,128)S(1)}, s32[1,1,3]{2,1,0:T(1,128)}, u32[]{:S(2)}) copy-start(s32[1,1,3]{2,1,0:T(1,128)} %ids_hbm.1) | copy-start | bytes 40
  27.8 0.7 %copy-start.3 = (s32[1,1,3]{2,1,0:T(1,128)S(1)}, s32[1,1,3]{2,1,0:T(1,128)}, u32[]{:S(2)}) copy-start(s32[1,1,3]{2,1,0:T(1,128)} %src_hbm.1) | copy-start | bytes 40
  38.3 9.3 %collective-permute-start.9 = (bf16[128,512]{1,0:T(8,128)(2,1)S(1)}, bf16[128,512]{1,0:T(8,128)(2,1)S(1)}, u32[]{:S(2)}, u32[]{:S(2)}) collective-permute-start(bf16[128,512]{1,0:T(8,128)(2,1)S(1)} %get-tuple-element.47), channel_id=1, source_target_pairs={{0,28},{4,24},{8,20},{12,16},{16,12},{20,8},{24,4},{28,0},{1,29},{... | collective-permute-start | bytes 393224 | tf_op jit(solution)/shard_map/ppermute | solution.py:31
  40.5 11.3 %collective-permute-start.10 = (bf16[128,512]{1,0:T(8,128)(2,1)S(1)}, bf16[128,512]{1,0:T(8,128)(2,1)S(1)}, u32[]{:S(2)}, u32[]{:S(2)}) collective-permute-start(bf16[128,512]{1,0:T(8,128)(2,1)S(1)} %get-tuple-element.48), channel_id=1, source_target_pairs={{0,12},{4,8},{8,4},{12,0},{16,28},{20,24},{24,20},{28,16},{1,13},{... | collective-permute-start | bytes 393224 | tf_op jit(solution)/shard_map/ppermute | solution.py:31
  40.5 11.9 %collective-permute-start.11 = (bf16[128,512]{1,0:T(8,128)(2,1)S(1)}, bf16[128,512]{1,0:T(8,128)(2,1)S(1)}, u32[]{:S(2)}, u32[]{:S(2)}) collective-permute-start(bf16[128,512]{1,0:T(8,128)(2,1)S(1)} %get-tuple-element.49), channel_id=1, source_target_pairs={{0,24},{4,28},{8,16},{12,20},{16,8},{20,12},{24,0},{28,4},{1,25},{... | collective-permute-start | bytes 393224 | tf_op jit(solution)/shard_map/ppermute | solution.py:31
  42.2 13.0 %collective-permute-start.12 = (bf16[128,512]{1,0:T(8,128)(2,1)S(1)}, bf16[128,512]{1,0:T(8,128)(2,1)S(1)}, u32[]{:S(2)}, u32[]{:S(2)}) collective-permute-start(bf16[128,512]{1,0:T(8,128)(2,1)S(1)} %get-tuple-element.50), channel_id=1, source_target_pairs={{0,8},{4,12},{8,0},{12,4},{16,24},{20,28},{24,16},{28,20},{1,9},{5... | collective-permute-start | bytes 393224 | tf_op jit(solution)/shard_map/ppermute | solution.py:31
  44.2 16.7 %collective-permute-start.13 = (bf16[128,512]{1,0:T(8,128)(2,1)S(1)}, bf16[128,512]{1,0:T(8,128)(2,1)S(1)}, u32[]{:S(2)}, u32[]{:S(2)}) collective-permute-start(bf16[128,512]{1,0:T(8,128)(2,1)S(1)} %get-tuple-element.51), channel_id=1, source_target_pairs={{0,20},{4,16},{8,28},{12,24},{16,4},{20,0},{24,12},{28,8},{1,21},{... | collective-permute-start | bytes 393224 | tf_op jit(solution)/shard_map/ppermute | solution.py:31
  47.6 13.3 %collective-permute-start.14 = (bf16[128,512]{1,0:T(8,128)(2,1)S(1)}, bf16[128,512]{1,0:T(8,128)(2,1)S(1)}, u32[]{:S(2)}, u32[]{:S(2)}) collective-permute-start(bf16[128,512]{1,0:T(8,128)(2,1)S(1)} %get-tuple-element.52), channel_id=1, source_target_pairs={{0,4},{4,0},{8,12},{12,8},{16,20},{20,16},{24,28},{28,24},{1,5},{5... | collective-permute-start | bytes 393224 | tf_op jit(solution)/shard_map/ppermute | solution.py:31
  51.8 10.7 %collective-permute-start.15 = (bf16[128,512]{1,0:T(8,128)(2,1)S(1)}, bf16[128,512]{1,0:T(8,128)(2,1)S(1)}, u32[]{:S(2)}, u32[]{:S(2)}) collective-permute-start(bf16[128,512]{1,0:T(8,128)(2,1)S(1)} %get-tuple-element.53), channel_id=1, source_target_pairs={{0,16},{4,20},{8,24},{12,28},{16,0},{20,4},{24,8},{28,12},{1,17},{... | collective-permute-start | bytes 393224 | tf_op jit(solution)/shard_map/ppermute | solution.py:31

commit v5 on v4

v5 whole, which is shorter than its diff:
```python
import functools

import jax
import jax.numpy as jnp
from jax import lax
from jax.experimental import pallas as pl
from jax.experimental.pallas import tpu as pltpu
from jax.sharding import PartitionSpec as P

SHARES = (1, 1)
CHUNKS = len(SHARES)
EARLY = 7
LIMIT = 16 * 1024 * 1024


def rows_per_group(rows, patches):
    return min(rows, max(16, 256 // patches))


def far_steps(count):
    return list(range(count - 1, count // 2 - 1, -1))


def near_steps(count):
    return list(range(count // 2 - 1, 0, -1)) + [0]


def span(values, chunk):
    unit = values // sum(SHARES)
    start = sum(SHARES[:chunk]) * unit
    return slice(start, start + SHARES[chunk] * unit)


def ppermute(value, axis, step):
    if step == 0:
        return value
    count = lax.axis_size(axis)
    return lax.ppermute(value, axis, [(i, i ^ step) for i in range(count)])


def after(value, *earlier):
    return lax.optimization_barrier((value, *earlier))[0] if earlier else value


def inward_waits(count):
    far, near = far_steps(count), near_steps(count)[:-1]
    waits = {far[i]: [far[i - 2]] for i in range(2, len(far))}
    for i, k in enumerate(near[:-1]):
        waits[k] = [far[i]]
    return waits


def outward_waits(count):
    far, near = far_steps(count), near_steps(count)[:-1]
    line = [(k, chunk) for chunk in range(CHUNKS) for k in far]
    waits = {line[i]: [line[i - 2]] for i in range(2, len(line))}
    for chunk in range(CHUNKS):
        for i, k in enumerate(near):
            waits[(k, chunk)] = [(far[i], chunk)]
            if chunk + 1 < CHUNKS:
                waits[(far[i], chunk + 1)].append((k, chunk))
    return waits


def split_kernel(keys, patches, me_ref, members_ref, *out_refs):
    rows = out_refs[0].shape[0]
    group = rows_per_group(rows, patches)
    height = group * patches
    base = min(keys)
    tall = (1 + max(keys) - base) * group
    row = lax.broadcasted_iota(jnp.int32, (tall, height), 0)
    column = lax.broadcasted_iota(jnp.int32, (tall, height), 1)
    source = lax.rem(row, group) * patches + ((base + lax.div(row, group)) ^ me_ref[0])
    shuffle = jnp.where(column == source, 1.0, 0.0).astype(jnp.bfloat16)
    for step in range(rows // group):
        block = members_ref[step * height : (step + 1) * height, :]
        moved = jnp.dot(shuffle, block, preferred_element_type=jnp.float32)
        moved = moved.astype(jnp.bfloat16)
        here = slice(step * group, (step + 1) * group)
        for k, out_ref in zip(keys, out_refs):
            out_ref[here, :] = moved[(k - base) * group : (k - base + 1) * group, :]


def merge_kernel(keys, me_ref, *refs):
    pieces, out_ref = dict(zip(keys, refs)), refs[-1]
    patches = 1 + max(k for k, _ in keys)
    rows = out_ref.shape[0] // patches
    values = out_ref.shape[1]
    group = rows_per_group(rows, patches)
    height = group * patches
    row = lax.broadcasted_iota(jnp.int32, (height, height), 0)
    column = lax.broadcasted_iota(jnp.int32, (height, height), 1)
    source = (lax.rem(row, patches) ^ me_ref[0]) * group + lax.div(row, patches)
    shuffle = jnp.where(column == source, 1.0, 0.0).astype(jnp.bfloat16)
    for step in range(rows // group):
        here = slice(step * group, (step + 1) * group)
        for chunk in range(CHUNKS):
            parts = [pieces[(k, chunk)][here, :] for k in range(patches)]
            block = jnp.concatenate(parts, axis=0)
            moved = jnp.dot(shuffle, block, preferred_element_type=jnp.float32)
            out_ref[step * height : (step + 1) * height, span(values, chunk)] = moved.astype(
                jnp.bfloat16
            )


def gram_kernel(
    scale, region_ref, ids_hbm, src_hbm, count_hbm, own, even, odd, gram_ref,
    ids_ref, src_ref, count_ref, stacked, table_sem, sem,
):
    tables = [
        pltpu.make_async_copy(hbm, smem, table_sem.at[i])
        for i, (hbm, smem) in enumerate(
            ((ids_hbm, ids_ref), (src_hbm, src_ref), (count_hbm, count_ref))
        )
    ]
    for copy in tables:
        copy.start()
    for copy in tables:
        copy.wait()
    slots = ids_ref.shape[2]
    rows = own.shape[1]
    parity = lax.rem(region_ref[0], 2)
    count = count_ref[0, 0]
    for slot in range(slots):
        live = slot < count
        target = stacked.at[pl.ds(slot * rows, rows), :]
        source = src_ref[0, 0, slot]
        where = jnp.where(source == 1, 0, jnp.where((source == 2) == (parity == 0), 1, 2))
        for code, store in enumerate((own, even, odd)):

            @pl.when(live & (where == code))
            def _():
                block = store.at[ids_ref[0, 0, slot]]
                pltpu.make_async_copy(block, target, sem.at[slot]).start()

        @pl.when(jnp.logical_not(live))
        def _():
            target[...] = jnp.zeros(target.shape, target.dtype)

    for slot in range(slots):

        @pl.when(slot < count)
        def _():
            target = stacked.at[pl.ds(slot * rows, rows), :]
            pltpu.make_async_copy(own.at[0], target, sem.at[slot]).wait()

    total = lax.dot_general(
        stacked[...], stacked[...], (((0,), (0,)), ((), ())), preferred_element_type=jnp.float32
    )
    gram_ref[...] = (total * scale).astype(jnp.bfloat16)


def transform_kernel(values, chunk, keys, out_keys, me_ref, *refs):
    count = len(keys)
    pieces = dict(zip(keys, refs[:EARLY] + refs[EARLY + 1 : count + 1]))
    gram_ref, out_refs = refs[EARLY], refs[count + 1 : -3]
    members, first, fresh = refs[-3:]
    rows = gram_ref.shape[0] // count

    def place(k):
        return pl.ds(pl.multiple_of((me_ref[0] ^ k) * rows, rows), rows)

    for k, piece in pieces.items():
        members[place(k), :] = piece[:, span(values, chunk)]
    gram = gram_ref[...]
    first[...] = jnp.dot(gram, members[...], preferred_element_type=jnp.float32).astype(
        jnp.bfloat16
    )
    second = jnp.dot(gram, first[...], preferred_element_type=jnp.float32)
    rest = members[...].astype(jnp.float32) - first[...].astype(jnp.float32)
    fresh[...] = (rest + second).astype(jnp.bfloat16)
    for k, out_ref in zip(out_keys, out_refs):
        out_ref[...] = fresh[place(k), :]


def vmem():
    return pl.BlockSpec(memory_space=pltpu.VMEM)


def params():
    return pltpu.CompilerParams(vmem_limit_bytes=LIMIT)


def cost(flops, nbytes):
    return pl.CostEstimate(flops=flops, bytes_accessed=nbytes, transcendentals=0)


def neighbours(store):
    count = lax.axis_size("region")
    even = [(i, i ^ 1) for i in range(count) if i ^ 1 < count]
    odd = [(i, ((i + 1) ^ 1) - 1) for i in range(count) if 0 <= ((i + 1) ^ 1) - 1 < count]
    return lax.ppermute(store, "region", even), lax.ppermute(store, "region", odd)


def shards(ensemble, obs_store, block_ids, block_src, block_count):
    rows, _, patches, values = ensemble.shape
    store = obs_store.reshape(obs_store.shape[2:])
    size = store.shape[2]
    slots = block_ids.shape[2]
    me = lax.axis_index("member").astype(jnp.int32).reshape(1)
    region = lax.axis_index("region").astype(jnp.int32).reshape(1)
    smem = pl.BlockSpec(memory_space=pltpu.SMEM)
    hbm = pl.BlockSpec(memory_space=pltpu.HBM)
    widths = [values * share // sum(SHARES) for share in SHARES]

    def piece_shape(width):
        return jax.ShapeDtypeStruct((rows, width), jnp.bfloat16)

    def split(keys, members):
        share = rows * patches * values
        return pl.pallas_call(
            functools.partial(split_kernel, keys, patches),
            out_shape=[piece_shape(values)] * len(keys),
            in_specs=[smem, vmem()],
            out_specs=[vmem()] * len(keys),
            compiler_params=params(),
            cost_estimate=cost(256 * share, 3 * share),
            name="split",
        )(me, members)

    far, near = far_steps(patches), near_steps(patches)
    steps = far + near
    members = ensemble.reshape(rows * patches, values)
    far_pieces = split(far, members)
    near_pieces = split(near, after(members, far_pieces[0]))
    arrived = {}
    waits = inward_waits(patches)
    for k, piece in zip(steps, far_pieces + near_pieces):
        earlier = [arrived[other] for other in waits.get(k, [])]
        arrived[k] = ppermute(after(piece, *earlier), "member", k)
    even, odd = neighbours(after(store, far_pieces[0]))

    gram = pl.pallas_call(
        functools.partial(gram_kernel, 1.0 / (2.0 * size)),
        out_shape=jax.ShapeDtypeStruct((size, size), jnp.bfloat16),
        in_specs=[smem] + [hbm] * 6,
        out_specs=vmem(),
        scratch_shapes=[
            pltpu.SMEM(block_ids.shape, jnp.int32),
            pltpu.SMEM(block_src.shape, jnp.int32),
            pltpu.SMEM(block_count.shape, jnp.int32),
            pltpu.VMEM((slots * store.shape[1], size), jnp.bfloat16),
            pltpu.SemaphoreType.DMA((3,)),
            pltpu.SemaphoreType.DMA((slots,)),
        ],
        compiler_params=params(),
        cost_estimate=cost(2 * slots * store.shape[1] * size * size, 4 * size * size),
        name="gram",
    )(region, block_ids, block_src, block_count, store, even, odd)

    returned = {}
    waits = outward_waits(patches)
    inputs = [arrived[k] for k in steps]
    for chunk in range(CHUNKS):
        width = widths[chunk]
        moved = pl.pallas_call(
            functools.partial(transform_kernel, values, chunk, steps, steps),
            out_shape=[piece_shape(width)] * len(steps),
            in_specs=[smem] + [vmem()] * (1 + len(steps)),
            out_specs=[vmem()] * len(steps),
            scratch_shapes=[pltpu.VMEM((size, width), jnp.bfloat16)] * 3,
            compiler_params=params(),
            cost_estimate=cost(4 * size * size * width, 2 * size * size + 4 * size * width),
            name="transform",
        )(me, *inputs[:EARLY], gram, *inputs[EARLY:])
        for k, piece in zip(steps, moved):
            earlier = [returned[other] for other in waits.get((k, chunk), [])]
            returned[(k, chunk)] = ppermute(after(piece, *earlier), "member", k)

    keys = [(k, chunk) for chunk in range(CHUNKS) for k in steps]
    fresh = pl.pallas_call(
        functools.partial(merge_kernel, keys),
        out_shape=jax.ShapeDtypeStruct((rows * patches, values), jnp.bfloat16),
        in_specs=[smem] + [vmem()] * len(keys),
        out_specs=vmem(),
        compiler_params=params(),
        cost_estimate=cost(2 * 256 * rows * patches * values, 4 * rows * patches * values),
        name="merge",
    )(me, *[returned[key] for key in keys])
    return fresh.reshape(ensemble.shape)


def solution(mesh):
    return jax.shard_map(
        shards,
        mesh=mesh,
        in_specs=(
            P("member", "region", None, None),
            P("region", "member", None, None, None),
            P("region", "member", None),
            P("region", "member", None),
            P("region", "member"),
        ),
        out_specs=P("member", "region", None, None),
        check_vma=False,
    )
```

time: 64.1 us -> 78.2 us (1.22)
  starting transfers between devices: 26.6 us -> 45.7 us
  waiting for transfers between devices: 24.6 us -> 15.9 us
  Pallas kernels: 8.14 us -> 11.9 us
    ppermute x14 -> x21, starting transfers between devices: 21.5 us -> 40.7 us  [ppermute(): return lax.ppermute(value, axis, [(i, i ^ step) for i in range(count)])]
    ppermute x14 -> x21, waiting for transfers between devices: 24.6 us -> 15.9 us  [ppermute(): return lax.ppermute(value, axis, [(i, i ^ step) for i in range(count)])]
    pallas_call x3 -> x5, Pallas kernels: 6.11 us -> 9.89 us  [the longest x2 6.41 us: shards(): pl.pallas_call(functools.partial(transform_kernel, values, chunk, steps,...]
    unnamed x8 -> x12, local copies, waits for them, and re-layouts: 3.84 us -> 3.65 us
  transfers between devices with their start and end apart: 16 -> 23, of which waited for: 10 -> 9; matrix products, arithmetic and copies ran while one was open for 0% -> 0% of each run, Pallas kernels for 3% -> 8%
where the time goes in v5:
time: 78.2 us; the launch traced here: 78 us
  starting transfers between devices  45.7 us (58%)
  waiting for transfers between devices  15.9 us (20%)
  Pallas kernels  11.9 us (15%)
  local copies, waits for them, and re-layouts  3.65 us (5%)
  between operations  0.8 us (1%)
    ppermute x21, starting transfers between devices, ppermute(): return lax.ppermute(value, axis, [(i, i ^ step) for i in range(count)])  40.7 us
    ppermute x21, waiting for transfers between devices, ppermute(): return lax.ppermute(value, axis, [(i, i ^ step) for i in range(count)])  15.9 us
    pallas_call x2, Pallas kernels, shards(): pl.pallas_call(functools.partial(transform_kernel, values, chunk, steps,...  6.41 us
    ppermute x1, starting transfers between devices, neighbours(): lax.ppermute(store, 'region', even)  4.31 us
    unnamed x12, local copies, waits for them, and re-layouts  3.65 us
    pallas_call x2, Pallas kernels, split(): pl.pallas_call(functools.partial(split_kernel, keys, patches), out_shape=...  2.06 us
    pallas_call x1, Pallas kernels, shards(): pl.pallas_call(functools.partial(gram_kernel, 1.0 / (2.0 * size)), out_sh...  2.03 us
  transfers between devices with their start and end apart: 23, of which 9 were waited for; matrix products, arithmetic and copies ran while one was open for 0% of the time, Pallas kernels for 8%

profile of v5, /device:TPU:0, one launch (start us, length us, event | category | flops | bytes accessed | tf_op | source)
XLA Modules:
  0.0 78.0 jit_solution(14008214036033058968)
XLA Ops:
  0.0 1.2 %copy-done = bf16[128,1,8,512]{3,2,1,0:T(8,128)(2,1)S(1)} copy-done((bf16[128,1,8,512]{3,2,1,0:T(8,128)(2,1)S(1)}, bf16[128,1,8,512]{3,2,1,0:T(8,128)(2,1)}, u32[]{:S(2)}) %copy-start) | copy-done | bytes 1048600
  3.0 4.3 %collective-permute-start.7 = (bf16[5,128,1024]{2,1,0:T(8,128)(2,1)}, bf16[5,128,1024]{2,1,0:T(8,128)(2,1)S(1)}, u32[]{:S(2)}, u32[]{:S(2)}) collective-permute-start(bf16[5,128,1024]{2,1,0:T(8,128)(2,1)} %bitcast.10), channel_id=1, source_target_pairs={{0,1},{1,0},{2,3},{3,2},{4,5},{5,4},{6,7},{7,6},{8,9},{9,8},{10,11... | collective-permute-start | bytes 3932168 | tf_op jit(solution)/shard_map/ppermute | solution.py:192
  7.3 3.6 %collective-permute-start.1 = (bf16[128,512]{1,0:T(8,128)(2,1)S(1)}, bf16[128,512]{1,0:T(8,128)(2,1)S(1)}, u32[]{:S(2)}, u32[]{:S(2)}) collective-permute-start(bf16[128,512]{1,0:T(8,128)(2,1)S(1)} %get-tuple-element.48), channel_id=1, source_target_pairs={{0,24},{4,28},{8,16},{12,20},{16,8},{20,12},{24,0},{28,4},{1,25},{... | collective-permute-start | bytes 393224 | tf_op jit(solution)/shard_map/ppermute | solution.py:38
  14.8 8.4 %collective-permute-start.3 = (bf16[128,512]{1,0:T(8,128)(2,1)}, bf16[128,512]{1,0:T(8,128)(2,1)S(1)}, u32[]{:S(2)}, u32[]{:S(2)}) collective-permute-start(bf16[128,512]{1,0:T(8,128)(2,1)} %get-tuple-element.52), channel_id=1, source_target_pairs={{0,16},{4,20},{8,24},{12,28},{16,0},{20,4},{24,8},{28,12},{1,17},{... | collective-permute-start | bytes 393224 | tf_op jit(solution)/shard_map/ppermute | solution.py:38
  23.3 3.7 %collective-permute-start.2 = (bf16[128,512]{1,0:T(8,128)(2,1)}, bf16[128,512]{1,0:T(8,128)(2,1)S(1)}, u32[]{:S(2)}, u32[]{:S(2)}) collective-permute-start(bf16[128,512]{1,0:T(8,128)(2,1)} %get-tuple-element.50), channel_id=1, source_target_pairs={{0,20},{4,16},{8,28},{12,24},{16,4},{20,0},{24,12},{28,8},{1,21},{... | collective-permute-start | bytes 393224 | tf_op jit(solution)/shard_map/ppermute | solution.py:38
  28.1 2.9 %collective-permute-start.4 = (bf16[128,512]{1,0:T(8,128)(2,1)}, bf16[128,512]{1,0:T(8,128)(2,1)}, u32[]{:S(2)}, u32[]{:S(2)}) collective-permute-start(bf16[128,512]{1,0:T(8,128)(2,1)} %get-tuple-element.55), channel_id=1, source_target_pairs={{0,12},{4,8},{8,4},{12,0},{16,28},{20,24},{24,20},{28,16},{1,13},{... | collective-permute-start | bytes 393224 | tf_op jit(solution)/shard_map/ppermute | solution.py:38
  31.7 1.3 %copy-done.3 = bf16[5,128,1024]{2,1,0:T(8,128)(2,1)S(1)} copy-done((bf16[5,128,1024]{2,1,0:T(8,128)(2,1)S(1)}, bf16[5,128,1024]{2,1,0:T(8,128)(2,1)}, u32[]{:S(2)}) %copy-start.3) | copy-done | bytes 1310744
  33.0 2.0 %gram.1.refs_7_ = bf16[1024,1024]{1,0:T(8,128)(2,1)S(1)} custom-call(s32[1]{0:T(128)} %bitcast.2.region_ref, s32[1,1,3]{2,1,0:T(1,128)S(1)} %copy-done.4, s32[1,1,3]{2,1,0:T(1,128)S(1)} %copy-done.5, s32[1,1]{1,0:T(1,128)S(6)} %copy.7.count_hbm, bf16[5,128,1024]{2,1,0:T(8,128)(2,1)S(1)} %bitcast.11, bf16[5,128,1024]{2,1,0:T(8,128)(2,1)S(1)} %copy-done.3, ...), custom_call_target="tpu_custom_call" | custom-call | flops 805306368 | bytes 4194304 | tf_op jit(solution)/shard_map/gram/pallas_call | solution.py:233
  35.1 3.6 %collective-permute-done.4.refs_4_ = bf16[128,512]{1,0:T(8,128)(2,1)} collective-permute-done((bf16[128,512]{1,0:T(8,128)(2,1)}, bf16[128,512]{1,0:T(8,128)(2,1)}, u32[]{:S(2)}, u32[]{:S(2)}) %collective-permute-start.4) | collective-permute-done | bytes 131104 | tf_op jit(solution)/shard_map/ppermute | solution.py:38
  38.7 3.2 %transform.2 = (bf16[128,256]{1,0:T(8,128)(2,1)S(1)}, bf16[128,256]{1,0:T(8,128)(2,1)S(1)}, bf16[128,256]{1,0:T(8,128)(2,1)S(1)}, bf16[128,256]{1,0:T(8,128)(2,1...) custom-call(s32[1]{0:T(128)} %bitcast.me_ref, ...), custom_call_target="tpu_custom_call" | custom-call | flops 1073741824 | bytes 3145728 | tf_op jit(solution)/shard_map/transform/pallas_call | solution.py:256
  42.9 1.5 %collective-permute-start.10 = (bf16[128,256]{1,0:T(8,128)(2,1)S(1)}, bf16[128,256]{1,0:T(8,128)(2,1)S(1)}, u32[]{:S(2)}, u32[]{:S(2)}) collective-permute-start(bf16[128,256]{1,0:T(8,128)(2,1)S(1)} %get-tuple-element.62), channel_id=1, source_target_pairs={{0,24},{4,28},{8,16},{12,20},{16,8},{20,12},{24,0},{28,4},{1,25},{... | collective-permute-start | bytes 196616 | tf_op jit(solution)/shard_map/ppermute | solution.py:38
  44.4 5.1 %collective-permute-done.9.refs_0_ = bf16[128,256]{1,0:T(8,128)(2,1)S(1)} collective-permute-done((bf16[128,256]{1,0:T(8,128)(2,1)S(1)}, bf16[128,256]{1,0:T(8,128)(2,1)S(1)}, u32[]{:S(2)}, u32[]{:S(2)}) %collective-permute-start.9) | collective-permute-done | bytes 65568 | tf_op jit(solution)/shard_map/ppermute | solution.py:38
  49.5 2.0 %collective-permute-start.13 = (bf16[128,256]{1,0:T(8,128)(2,1)S(1)}, bf16[128,256]{1,0:T(8,128)(2,1)S(1)}, u32[]{:S(2)}, u32[]{:S(2)}) collective-permute-start(bf16[128,256]{1,0:T(8,128)(2,1)S(1)} %get-tuple-element.68), channel_id=1, source_target_pairs={{0,12},{4,8},{8,4},{12,0},{16,28},{20,24},{24,20},{28,16},{1,13},{... | collective-permute-start | bytes 196616 | tf_op jit(solution)/shard_map/ppermute | solution.py:38
  51.5 3.2 %transform.3 = (bf16[128,256]{1,0:T(8,128)(2,1)S(1)}, bf16[128,256]{1,0:T(8,128)(2,1)S(1)}, bf16[128,256]{1,0:T(8,128)(2,1)S(1)}, bf16[128,256]{1,0:T(8,128)(2,1...) custom-call(s32[1]{0:T(128)} %bitcast.me_ref, ...), custom_call_target="tpu_custom_call" | custom-call | flops 1073741824 | bytes 3145728 | tf_op jit(solution)/shard_map/transform/pallas_call | solution.py:256
  54.8 3.8 %collective-permute-start.14 = (bf16[128,256]{1,0:T(8,128)(2,1)S(1)}, bf16[128,256]{1,0:T(8,128)(2,1)S(1)}, u32[]{:S(2)}, u32[]{:S(2)}) collective-permute-start(bf16[128,256]{1,0:T(8,128)(2,1)S(1)} %get-tuple-element.70), channel_id=1, source_target_pairs={{0,8},{4,12},{8,0},{12,4},{16,24},{20,28},{24,16},{28,20},{1,9},{5... | collective-permute-start | bytes 196616 | tf_op jit(solution)/shard_map/ppermute | solution.py:38
  58.6 2.0 %collective-permute-start.16 = (bf16[128,256]{1,0:T(8,128)(2,1)S(1)}, bf16[128,256]{1,0:T(8,128)(2,1)S(1)}, u32[]{:S(2)}, u32[]{:S(2)}) collective-permute-start(bf16[128,256]{1,0:T(8,128)(2,1)S(1)} %get-tuple-element.75), channel_id=1, source_target_pairs={{0,28},{4,24},{8,20},{12,16},{16,12},{20,8},{24,4},{28,0},{1,29},{... | collective-permute-start | bytes 196616 | tf_op jit(solution)/shard_map/ppermute | solution.py:38
  61.7 2.2 %collective-permute-start.17 = (bf16[128,256]{1,0:T(8,128)(2,1)S(1)}, bf16[128,256]{1,0:T(8,128)(2,1)S(1)}, u32[]{:S(2)}, u32[]{:S(2)}) collective-permute-start(bf16[128,256]{1,0:T(8,128)(2,1)S(1)} %get-tuple-element.77), channel_id=1, source_target_pairs={{0,24},{4,28},{8,16},{12,20},{16,8},{20,12},{24,0},{28,4},{1,25},{... | collective-permute-start | bytes 196616 | tf_op jit(solution)/shard_map/ppermute | solution.py:38
  63.9 2.2 %collective-permute-done.16.refs_8_ = bf16[128,256]{1,0:T(8,128)(2,1)S(1)} collective-permute-done((bf16[128,256]{1,0:T(8,128)(2,1)S(1)}, bf16[128,256]{1,0:T(8,128)(2,1)S(1)}, u32[]{:S(2)}, u32[]{:S(2)}) %collective-permute-start.16) | collective-permute-done | bytes 65568 | tf_op jit(solution)/shard_map/ppermute | solution.py:38
  66.1 1.9 %collective-permute-start.20 = (bf16[128,256]{1,0:T(8,128)(2,1)S(1)}, bf16[128,256]{1,0:T(8,128)(2,1)S(1)}, u32[]{:S(2)}, u32[]{:S(2)}) collective-permute-start(bf16[128,256]{1,0:T(8,128)(2,1)S(1)} %get-tuple-element.83), channel_id=1, source_target_pairs={{0,12},{4,8},{8,4},{12,0},{16,28},{20,24},{24,20},{28,16},{1,13},{... | collective-permute-start | bytes 196616 | tf_op jit(solution)/shard_map/ppermute | solution.py:38
  68.1 2.3 %collective-permute-start.19 = (bf16[128,256]{1,0:T(8,128)(2,1)S(1)}, bf16[128,256]{1,0:T(8,128)(2,1)S(1)}, u32[]{:S(2)}, u32[]{:S(2)}) collective-permute-start(bf16[128,256]{1,0:T(8,128)(2,1)S(1)} %get-tuple-element.81), channel_id=1, source_target_pairs={{0,16},{4,20},{8,24},{12,28},{16,0},{20,4},{24,8},{28,12},{1,17},{... | collective-permute-start | bytes 196616 | tf_op jit(solution)/shard_map/ppermute | solution.py:38
  70.3 1.7 %collective-permute-start.21 = (bf16[128,256]{1,0:T(8,128)(2,1)S(1)}, bf16[128,256]{1,0:T(8,128)(2,1)S(1)}, u32[]{:S(2)}, u32[]{:S(2)}) collective-permute-start(bf16[128,256]{1,0:T(8,128)(2,1)S(1)} %get-tuple-element.85), channel_id=1, source_target_pairs={{0,8},{4,12},{8,0},{12,4},{16,24},{20,28},{24,16},{28,20},{1,9},{5... | collective-permute-start | bytes 196616 | tf_op jit(solution)/shard_map/ppermute | solution.py:38
  72.3 1.8 %collective-permute-start.22 = (bf16[128,256]{1,0:T(8,128)(2,1)S(1)}, bf16[128,256]{1,0:T(8,128)(2,1)S(1)}, u32[]{:S(2)}, u32[]{:S(2)}) collective-permute-start(bf16[128,256]{1,0:T(8,128)(2,1)S(1)} %get-tuple-element.87), channel_id=1, source_target_pairs={{0,4},{4,0},{8,12},{12,8},{16,20},{20,16},{24,28},{28,24},{1,5},{5... | collective-permute-start | bytes 196616 | tf_op jit(solution)/shard_map/ppermute | solution.py:38
  74.6 2.0 %collective-permute-done.22.refs_14_ = bf16[128,256]{1,0:T(8,128)(2,1)S(1)} collective-permute-done((bf16[128,256]{1,0:T(8,128)(2,1)S(1)}, bf16[128,256]{1,0:T(8,128)(2,1)S(1)}, u32[]{:S(2)}, u32[]{:S(2)}) %collective-permute-start.22) | collective-permute-done | bytes 65568 | tf_op jit(solution)/shard_map/ppermute | solution.py:38
  76.6 1.4 %merge.1 = bf16[1024,512]{1,0:T(8,128)(2,1)} custom-call(s32[1]{0:T(128)} %bitcast.me_ref, bf16[128,256]{1,0:T(8,128)(2,1)S(1)} %collective-permute-done.9.refs_0_, bf16[128,256]{1,0:T(8,128)(2,1)S(1)} %collective-permute-done.10.refs_1_, bf16[128,256]{1,0:T(8,128)(2,1)S(1)} %collective-permute-done.11.refs_2_, ...), custom_call_target="tpu_custom_call" | custom-call | flops 268435456 | bytes 2097152 | tf_op jit(solution)/shard_map/merge/pallas_call | solution.py:271
  (40 shorter events, 9.6 us)
Async XLA Ops:
  0.0 31.7 %copy-start.4 = (s32[1,1,3]{2,1,0:T(1,128)S(1)}, s32[1,1,3]{2,1,0:T(1,128)}, u32[]{:S(2)}) copy-start(s32[1,1,3]{2,1,0:T(1,128)} %ids_hbm.1) | copy-start | bytes 40
  2.2 24.7 %collective-permute-start.8 = (bf16[5,128,1024]{2,1,0:T(8,128)(2,1)}, bf16[5,128,1024]{2,1,0:T(8,128)(2,1)S(1)}, u32[]{:S(2)}, u32[]{:S(2)}) collective-permute-start(bf16[5,128,1024]{2,1,0:T(8,128)(2,1)} %bitcast.9), channel_id=1, source_target_pairs={{1,2},{2,1},{5,6},{6,5},{9,10},{10,9},{13,14},{14,13},{17,18},{18,... | collective-permute-start | bytes 3932168 | tf_op jit(solution)/shard_map/ppermute | solution.py:192
  3.0 24.0 %collective-permute-start.7 = (bf16[5,128,1024]{2,1,0:T(8,128)(2,1)}, bf16[5,128,1024]{2,1,0:T(8,128)(2,1)S(1)}, u32[]{:S(2)}, u32[]{:S(2)}) collective-permute-start(bf16[5,128,1024]{2,1,0:T(8,128)(2,1)} %bitcast.10), channel_id=1, source_target_pairs={{0,1},{1,0},{2,3},{3,2},{4,5},{5,4},{6,7},{7,6},{8,9},{9,8},{10,11... | collective-permute-start | bytes 3932168 | tf_op jit(solution)/shard_map/ppermute | solution.py:192
  7.3 7.5 %collective-permute-start.1 = (bf16[128,512]{1,0:T(8,128)(2,1)S(1)}, bf16[128,512]{1,0:T(8,128)(2,1)S(1)}, u32[]{:S(2)}, u32[]{:S(2)}) collective-permute-start(bf16[128,512]{1,0:T(8,128)(2,1)S(1)} %get-tuple-element.48), channel_id=1, source_target_pairs={{0,24},{4,28},{8,16},{12,20},{16,8},{20,12},{24,0},{28,4},{1,25},{... | collective-permute-start | bytes 393224 | tf_op jit(solution)/shard_map/ppermute | solution.py:38
  10.9 12.4 %collective-permute-start = (bf16[128,512]{1,0:T(8,128)(2,1)S(1)}, bf16[128,512]{1,0:T(8,128)(2,1)S(1)}, u32[]{:S(2)}, u32[]{:S(2)}) collective-permute-start(bf16[128,512]{1,0:T(8,128)(2,1)S(1)} %get-tuple-element.47), channel_id=1, source_target_pairs={{0,28},{4,24},{8,20},{12,16},{16,12},{20,8},{24,4},{28,0},{1,29},{... | collective-permute-start | bytes 393224 | tf_op jit(solution)/shard_map/ppermute | solution.py:38
  13.1 21.9 %collective-permute-start.6 = (bf16[128,512]{1,0:T(8,128)(2,1)}, bf16[128,512]{1,0:T(8,128)(2,1)S(1)}, u32[]{:S(2)}, u32[]{:S(2)}) collective-permute-start(bf16[128,512]{1,0:T(8,128)(2,1)} %get-tuple-element.58), channel_id=1, source_target_pairs={{0,4},{4,0},{8,12},{12,8},{16,20},{20,16},{24,28},{28,24},{1,5},{5... | collective-permute-start | bytes 393224 | tf_op jit(solution)/shard_map/ppermute | solution.py:38
  14.8 20.2 %collective-permute-start.3 = (bf16[128,512]{1,0:T(8,128)(2,1)}, bf16[128,512]{1,0:T(8,128)(2,1)S(1)}, u32[]{:S(2)}, u32[]{:S(2)}) collective-permute-start(bf16[128,512]{1,0:T(8,128)(2,1)} %get-tuple-element.52), channel_id=1, source_target_pairs={{0,16},{4,20},{8,24},{12,28},{16,0},{20,4},{24,8},{28,12},{1,17},{... | collective-permute-start | bytes 393224 | tf_op jit(solution)/shard_map/ppermute | solution.py:38
  23.3 11.8 %collective-permute-start.2 = (bf16[128,512]{1,0:T(8,128)(2,1)}, bf16[128,512]{1,0:T(8,128)(2,1)S(1)}, u32[]{:S(2)}, u32[]{:S(2)}) collective-permute-start(bf16[128,512]{1,0:T(8,128)(2,1)} %get-tuple-element.50), channel_id=1, source_target_pairs={{0,20},{4,16},{8,28},{12,24},{16,4},{20,0},{24,12},{28,8},{1,21},{... | collective-permute-start | bytes 393224 | tf_op jit(solution)/shard_map/ppermute | solution.py:38
  27.0 8.1 %collective-permute-start.5 = (bf16[128,512]{1,0:T(8,128)(2,1)}, bf16[128,512]{1,0:T(8,128)(2,1)S(1)}, u32[]{:S(2)}, u32[]{:S(2)}) collective-permute-start(bf16[128,512]{1,0:T(8,128)(2,1)} %get-tuple-element.57), channel_id=1, source_target_pairs={{0,8},{4,12},{8,0},{12,4},{16,24},{20,28},{24,16},{28,20},{1,9},{5... | collective-permute-start | bytes 393224 | tf_op jit(solution)/shard_map/ppermute | solution.py:38
  28.1 10.6 %collective-permute-start.4 = (bf16[128,512]{1,0:T(8,128)(2,1)}, bf16[128,512]{1,0:T(8,128)(2,1)}, u32[]{:S(2)}, u32[]{:S(2)}) collective-permute-start(bf16[128,512]{1,0:T(8,128)(2,1)} %get-tuple-element.55), channel_id=1, source_target_pairs={{0,12},{4,8},{8,4},{12,0},{16,28},{20,24},{24,20},{28,16},{1,13},{... | collective-permute-start | bytes 393224 | tf_op jit(solution)/shard_map/ppermute | solution.py:38
  41.9 7.5 %collective-permute-start.9 = (bf16[128,256]{1,0:T(8,128)(2,1)S(1)}, bf16[128,256]{1,0:T(8,128)(2,1)S(1)}, u32[]{:S(2)}, u32[]{:S(2)}) collective-permute-start(bf16[128,256]{1,0:T(8,128)(2,1)S(1)} %get-tuple-element.61), channel_id=1, source_target_pairs={{0,28},{4,24},{8,20},{12,16},{16,12},{20,8},{24,4},{28,0},{1,29},{... | collective-permute-start | bytes 196616 | tf_op jit(solution)/shard_map/ppermute | solution.py:38
  42.9 11.8 %collective-permute-start.10 = (bf16[128,256]{1,0:T(8,128)(2,1)S(1)}, bf16[128,256]{1,0:T(8,128)(2,1)S(1)}, u32[]{:S(2)}, u32[]{:S(2)}) collective-permute-start(bf16[128,256]{1,0:T(8,128)(2,1)S(1)} %get-tuple-element.62), channel_id=1, source_target_pairs={{0,24},{4,28},{8,16},{12,20},{16,8},{20,12},{24,0},{28,4},{1,25},{... | collective-permute-start | bytes 196616 | tf_op jit(solution)/shard_map/ppermute | solution.py:38
  49.5 9.1 %collective-permute-start.11 = (bf16[128,256]{1,0:T(8,128)(2,1)S(1)}, bf16[128,256]{1,0:T(8,128)(2,1)S(1)}, u32[]{:S(2)}, u32[]{:S(2)}) collective-permute-start(bf16[128,256]{1,0:T(8,128)(2,1)S(1)} %get-tuple-element.64), channel_id=1, source_target_pairs={{0,20},{4,16},{8,28},{12,24},{16,4},{20,0},{24,12},{28,8},{1,21},{... | collective-permute-start | bytes 196616 | tf_op jit(solution)/shard_map/ppermute | solution.py:38
  49.5 9.1 %collective-permute-start.13 = (bf16[128,256]{1,0:T(8,128)(2,1)S(1)}, bf16[128,256]{1,0:T(8,128)(2,1)S(1)}, u32[]{:S(2)}, u32[]{:S(2)}) collective-permute-start(bf16[128,256]{1,0:T(8,128)(2,1)S(1)} %get-tuple-element.68), channel_id=1, source_target_pairs={{0,12},{4,8},{8,4},{12,0},{16,28},{20,24},{24,20},{28,16},{1,13},{... | collective-permute-start | bytes 196616 | tf_op jit(solution)/shard_map/ppermute | solution.py:38
  54.7 6.5 %collective-permute-start.12 = (bf16[128,256]{1,0:T(8,128)(2,1)S(1)}, bf16[128,256]{1,0:T(8,128)(2,1)S(1)}, u32[]{:S(2)}, u32[]{:S(2)}) collective-permute-start(bf16[128,256]{1,0:T(8,128)(2,1)S(1)} %get-tuple-element.66), channel_id=1, source_target_pairs={{0,16},{4,20},{8,24},{12,28},{16,0},{20,4},{24,8},{28,12},{1,17},{... | collective-permute-start | bytes 196616 | tf_op jit(solution)/shard_map/ppermute | solution.py:38
  54.8 6.9 %collective-permute-start.14 = (bf16[128,256]{1,0:T(8,128)(2,1)S(1)}, bf16[128,256]{1,0:T(8,128)(2,1)S(1)}, u32[]{:S(2)}, u32[]{:S(2)}) collective-permute-start(bf16[128,256]{1,0:T(8,128)(2,1)S(1)} %get-tuple-element.70), channel_id=1, source_target_pairs={{0,8},{4,12},{8,0},{12,4},{16,24},{20,28},{24,16},{28,20},{1,9},{5... | collective-permute-start | bytes 196616 | tf_op jit(solution)/shard_map/ppermute | solution.py:38
  58.6 5.3 %collective-permute-start.15 = (bf16[128,256]{1,0:T(8,128)(2,1)S(1)}, bf16[128,256]{1,0:T(8,128)(2,1)S(1)}, u32[]{:S(2)}, u32[]{:S(2)}) collective-permute-start(bf16[128,256]{1,0:T(8,128)(2,1)S(1)} %get-tuple-element.72), channel_id=1, source_target_pairs={{0,4},{4,0},{8,12},{12,8},{16,20},{20,16},{24,28},{28,24},{1,5},{5... | collective-permute-start | bytes 196616 | tf_op jit(solution)/shard_map/ppermute | solution.py:38
  58.6 7.5 %collective-permute-start.16 = (bf16[128,256]{1,0:T(8,128)(2,1)S(1)}, bf16[128,256]{1,0:T(8,128)(2,1)S(1)}, u32[]{:S(2)}, u32[]{:S(2)}) collective-permute-start(bf16[128,256]{1,0:T(8,128)(2,1)S(1)} %get-tuple-element.75), channel_id=1, source_target_pairs={{0,28},{4,24},{8,20},{12,16},{16,12},{20,8},{24,4},{28,0},{1,29},{... | collective-permute-start | bytes 196616 | tf_op jit(solution)/shard_map/ppermute | solution.py:38
  61.7 6.4 %collective-permute-start.17 = (bf16[128,256]{1,0:T(8,128)(2,1)S(1)}, bf16[128,256]{1,0:T(8,128)(2,1)S(1)}, u32[]{:S(2)}, u32[]{:S(2)}) collective-permute-start(bf16[128,256]{1,0:T(8,128)(2,1)S(1)} %get-tuple-element.77), channel_id=1, source_target_pairs={{0,24},{4,28},{8,16},{12,20},{16,8},{20,12},{24,0},{28,4},{1,25},{... | collective-permute-start | bytes 196616 | tf_op jit(solution)/shard_map/ppermute | solution.py:38
  66.1 6.2 %collective-permute-start.18 = (bf16[128,256]{1,0:T(8,128)(2,1)S(1)}, bf16[128,256]{1,0:T(8,128)(2,1)S(1)}, u32[]{:S(2)}, u32[]{:S(2)}) collective-permute-start(bf16[128,256]{1,0:T(8,128)(2,1)S(1)} %get-tuple-element.79), channel_id=1, source_target_pairs={{0,20},{4,16},{8,28},{12,24},{16,4},{20,0},{24,12},{28,8},{1,21},{... | collective-permute-start | bytes 196616 | tf_op jit(solution)/shard_map/ppermute | solution.py:38
  66.1 8.0 %collective-permute-start.20 = (bf16[128,256]{1,0:T(8,128)(2,1)S(1)}, bf16[128,256]{1,0:T(8,128)(2,1)S(1)}, u32[]{:S(2)}, u32[]{:S(2)}) collective-permute-start(bf16[128,256]{1,0:T(8,128)(2,1)S(1)} %get-tuple-element.83), channel_id=1, source_target_pairs={{0,12},{4,8},{8,4},{12,0},{16,28},{20,24},{24,20},{28,16},{1,13},{... | collective-permute-start | bytes 196616 | tf_op jit(solution)/shard_map/ppermute | solution.py:38
  68.1 6.1 %collective-permute-start.19 = (bf16[128,256]{1,0:T(8,128)(2,1)S(1)}, bf16[128,256]{1,0:T(8,128)(2,1)S(1)}, u32[]{:S(2)}, u32[]{:S(2)}) collective-permute-start(bf16[128,256]{1,0:T(8,128)(2,1)S(1)} %get-tuple-element.81), channel_id=1, source_target_pairs={{0,16},{4,20},{8,24},{12,28},{16,0},{20,4},{24,8},{28,12},{1,17},{... | collective-permute-start | bytes 196616 | tf_op jit(solution)/shard_map/ppermute | solution.py:38
  70.3 4.3 %collective-permute-start.21 = (bf16[128,256]{1,0:T(8,128)(2,1)S(1)}, bf16[128,256]{1,0:T(8,128)(2,1)S(1)}, u32[]{:S(2)}, u32[]{:S(2)}) collective-permute-start(bf16[128,256]{1,0:T(8,128)(2,1)S(1)} %get-tuple-element.85), channel_id=1, source_target_pairs={{0,8},{4,12},{8,0},{12,4},{16,24},{20,28},{24,16},{28,20},{1,9},{5... | collective-permute-start | bytes 196616 | tf_op jit(solution)/shard_map/ppermute | solution.py:38
  72.3 4.3 %collective-permute-start.22 = (bf16[128,256]{1,0:T(8,128)(2,1)S(1)}, bf16[128,256]{1,0:T(8,128)(2,1)S(1)}, u32[]{:S(2)}, u32[]{:S(2)}) collective-permute-start(bf16[128,256]{1,0:T(8,128)(2,1)S(1)} %get-tuple-element.87), channel_id=1, source_target_pairs={{0,4},{4,0},{8,12},{12,8},{16,20},{20,16},{24,28},{28,24},{1,5},{5... | collective-permute-start | bytes 196616 | tf_op jit(solution)/shard_map/ppermute | solution.py:38
  (5 other events, 65.8 us)

commit v6 on v4

--- a/solution.py
+++ b/solution.py
@@ -158,11 +158,10 @@
     return pl.CostEstimate(flops=flops, bytes_accessed=nbytes, transcendentals=0)
 
 
-def neighbours(store):
+def swap(store, first):
     count = lax.axis_size("region")
-    even = [(i, i ^ 1) for i in range(count) if i ^ 1 < count]
-    odd = [(i, ((i + 1) ^ 1) - 1) for i in range(count) if 0 <= ((i + 1) ^ 1) - 1 < count]
-    return lax.ppermute(store, "region", even), lax.ppermute(store, "region", odd)
+    pairs = [(i, i + 1) for i in range(first, count - 1, 2)]
+    return lax.ppermute(store, "region", pairs + [(j, i) for i, j in pairs])
 
 
 def shards(ensemble, obs_store, block_ids, block_src, block_count):
@@ -176,6 +175,7 @@
     hbm = pl.BlockSpec(memory_space=pltpu.HBM)
     piece_shape = jax.ShapeDtypeStruct((rows, values), jnp.bfloat16)
 
+    odd, even = swap(store, 1), swap(store, 0)
     pieces = pl.pallas_call(
         split_kernel,
         out_shape=[piece_shape] * patches,
@@ -185,8 +185,6 @@
         cost_estimate=cost(2 * 256 * rows * patches * values, 4 * rows * patches * values),
         name="split",
     )(me, ensemble.reshape(rows * patches, values))
-    store, pieces = lax.optimization_barrier((store, pieces))
-    even, odd = neighbours(store)
     order = partners(patches)
     arrived = [ppermute(pieces[k], "member", k) for k in order]
 

time: 64.1 us -> 63.7 us (level)
  transfers between devices with their start and end apart: 16 -> 16, of which waited for: 10 -> 9; matrix products, arithmetic and copies ran while one was open for 0% -> 0% of each run, Pallas kernels for 3% -> 5%
where the time goes in v6:
time: 63.7 us; the launch traced here: 63.5 us
  starting transfers between devices  26.3 us (41%)
  waiting for transfers between devices  24.4 us (38%)
  Pallas kernels  8.13 us (13%)
  local copies, waits for them, and re-layouts  3.85 us (6%)
  between operations  0.72 us (1%)
    ppermute x14, waiting for transfers between devices, ppermute(): return lax.ppermute(value, axis, [(i, i ^ step) for i in range(count)])  24.4 us
    ppermute x14, starting transfers between devices, ppermute(): return lax.ppermute(value, axis, [(i, i ^ step) for i in range(count)])  21.3 us
    ppermute x2, starting transfers between devices, swap(): return lax.ppermute(store, 'region', pairs + [(j, i) for i, j in pairs])  5.05 us
    unnamed x8, local copies, waits for them, and re-layouts  3.85 us
    pallas_call x1, Pallas kernels, shards(): pl.pallas_call(functools.partial(transform_kernel, order), out_shape=[pie...  3.56 us
    pallas_call x1, Pallas kernels, shards(): pl.pallas_call(functools.partial(gram_kernel, 1.0 / (2.0 * size)), out_sh...  2.03 us
    pallas_call x1, Pallas kernels, shards(): pl.pallas_call(functools.partial(merge_kernel, order), out_shape=jax.Shap...  1.41 us
  transfers between devices with their start and end apart: 16, of which 9 were waited for; matrix products, arithmetic and copies ran while one was open for 0% of the time, Pallas kernels for 5%

profile of v6, /device:TPU:0, one launch (start us, length us, event | category | flops | bytes accessed | tf_op | source)
XLA Modules:
  0.0 63.5 jit_solution(7866007087787894250)
XLA Ops:
  0.7 4.3 %collective-permute-start.2 = (bf16[5,128,1024]{2,1,0:T(8,128)(2,1)}, bf16[5,128,1024]{2,1,0:T(8,128)(2,1)S(1)}, u32[]{:S(2)}, u32[]{:S(2)}) collective-permute-start(bf16[5,128,1024]{2,1,0:T(8,128)(2,1)} %bitcast.8), channel_id=1, source_target_pairs={{0,1},{2,3},{1,0},{3,2},{4,5},{6,7},{5,4},{7,6},{8,9},{10,11},{9,8... | collective-permute-start | bytes 3932168 | tf_op jit(solution)/shard_map/ppermute | solution.py:164
  5.1 1.2 %copy-done.1 = bf16[128,1,8,512]{3,2,1,0:T(8,128)(2,1)S(1)} copy-done((bf16[128,1,8,512]{3,2,1,0:T(8,128)(2,1)S(1)}, bf16[128,1,8,512]{3,2,1,0:T(8,128)(2,1)}, u32[]{:S(2)}) %copy-start.1) | copy-done | bytes 1048600
  6.3 1.1 %split.1 = (bf16[128,512]{1,0:T(8,128)(2,1)S(1)}, bf16[128,512]{1,0:T(8,128)(2,1)S(1)}, bf16[128,512]{1,0:T(8,128)(2,1)}, bf16[128,512]{1,0:T(8,128)(2,1)S(1)}, ...) custom-call(s32[1]{0:T(128)} %bitcast.me_ref, ...), custom_call_target="tpu_custom_call" | custom-call | flops 268435456 | bytes 2097152 | tf_op jit(solution)/shard_map/split/pallas_call | solution.py:179
  7.4 4.5 %collective-permute-start = (bf16[128,512]{1,0:T(8,128)(2,1)S(1)}, bf16[128,512]{1,0:T(8,128)(2,1)S(1)}, u32[]{:S(2)}, u32[]{:S(2)}) collective-permute-start(bf16[128,512]{1,0:T(8,128)(2,1)S(1)} %get-tuple-element.21), channel_id=1, source_target_pairs={{0,28},{4,24},{8,20},{12,16},{16,12},{20,8},{24,4},{28,0},{1,29},{... | collective-permute-start | bytes 393224 | tf_op jit(solution)/shard_map/ppermute | solution.py:31
  12.8 3.7 %collective-permute-done.refs_0_ = bf16[128,512]{1,0:T(8,128)(2,1)S(1)} collective-permute-done((bf16[128,512]{1,0:T(8,128)(2,1)S(1)}, bf16[128,512]{1,0:T(8,128)(2,1)S(1)}, u32[]{:S(2)}, u32[]{:S(2)}) %collective-permute-start) | collective-permute-done | bytes 131104 | tf_op jit(solution)/shard_map/ppermute | solution.py:31
  16.5 3.5 %collective-permute-start.5 = (bf16[128,512]{1,0:T(8,128)(2,1)}, bf16[128,512]{1,0:T(8,128)(2,1)S(1)}, u32[]{:S(2)}, u32[]{:S(2)}) collective-permute-start(bf16[128,512]{1,0:T(8,128)(2,1)} %get-tuple-element.24), channel_id=1, source_target_pairs={{0,8},{4,12},{8,0},{12,4},{16,24},{20,28},{24,16},{28,20},{1,9},{5... | collective-permute-start | bytes 393224 | tf_op jit(solution)/shard_map/ppermute | solution.py:31
  20.0 0.9 %collective-permute-done.1.refs_1_ = bf16[128,512]{1,0:T(8,128)(2,1)S(1)} collective-permute-done((bf16[128,512]{1,0:T(8,128)(2,1)S(1)}, bf16[128,512]{1,0:T(8,128)(2,1)S(1)}, u32[]{:S(2)}, u32[]{:S(2)}) %collective-permute-start.1) | collective-permute-done | bytes 131104 | tf_op jit(solution)/shard_map/ppermute | solution.py:31
  21.6 0.9 %collective-permute-start.7 = (bf16[128,512]{1,0:T(8,128)(2,1)S(1)}, bf16[128,512]{1,0:T(8,128)(2,1)}, u32[]{:S(2)}, u32[]{:S(2)}) collective-permute-start(bf16[128,512]{1,0:T(8,128)(2,1)S(1)} %get-tuple-element.26), channel_id=1, source_target_pairs={{0,4},{4,0},{8,12},{12,8},{16,20},{20,16},{24,28},{28,24},{1,5},{5... | collective-permute-start | bytes 393224 | tf_op jit(solution)/shard_map/ppermute | solution.py:31
  22.5 2.8 %collective-permute-start.8 = (bf16[128,512]{1,0:T(8,128)(2,1)S(1)}, bf16[128,512]{1,0:T(8,128)(2,1)}, u32[]{:S(2)}, u32[]{:S(2)}) collective-permute-start(bf16[128,512]{1,0:T(8,128)(2,1)S(1)} %get-tuple-element.27), channel_id=1, source_target_pairs={{0,16},{4,20},{8,24},{12,28},{16,0},{20,4},{24,8},{28,12},{1,17},{... | collective-permute-start | bytes 393224 | tf_op jit(solution)/shard_map/ppermute | solution.py:31
  26.0 1.3 %copy-done = bf16[1,1,5,128,1024]{4,3,2,1,0:T(8,128)(2,1)S(1)} copy-done((bf16[1,1,5,128,1024]{4,3,2,1,0:T(8,128)(2,1)S(1)}, bf16[1,1,5,128,1024]{4,3,2,1,0:T(8,128)(2,1)}, u32[]{:S(2)}) %copy-start) | copy-done | bytes 1310744
  28.6 2.0 %gram.1.refs_2_ = bf16[1024,1024]{1,0:T(8,128)(2,1)S(1)} custom-call(s32[1]{0:T(128)} %bitcast.2.region_ref, s32[1,1,3]{2,1,0:T(1,128)S(1)} %copy-done.2, s32[1,1,3]{2,1,0:T(1,128)S(1)} %copy-done.3, s32[1,1]{1,0:T(1,128)S(6)} %copy.7.count_hbm, bf16[5,128,1024]{2,1,0:T(8,128)(2,1)S(1)} %bitcast.9, bf16[5,128,1024]{2,1,0:T(8,128)(2,1)S(1)} %collective-permute-done.2.even, ...), custom_call_target="tpu_custom_call" | custom-call | flops 805306368 | bytes 4194304 | tf_op jit(solution)/shard_map/gram/pallas_call | solution.py:191
  30.6 2.5 %collective-permute-done.6.refs_5_ = bf16[128,512]{1,0:T(8,128)(2,1)} collective-permute-done((bf16[128,512]{1,0:T(8,128)(2,1)}, bf16[128,512]{1,0:T(8,128)(2,1)}, u32[]{:S(2)}, u32[]{:S(2)}) %collective-permute-start.6) | collective-permute-done | bytes 131104 | tf_op jit(solution)/shard_map/ppermute | solution.py:31
  33.1 1.7 %collective-permute-done.8.refs_7_ = bf16[128,512]{1,0:T(8,128)(2,1)} collective-permute-done((bf16[128,512]{1,0:T(8,128)(2,1)S(1)}, bf16[128,512]{1,0:T(8,128)(2,1)}, u32[]{:S(2)}, u32[]{:S(2)}) %collective-permute-start.8) | collective-permute-done | bytes 131104 | tf_op jit(solution)/shard_map/ppermute | solution.py:31
  34.8 3.6 %transform.1 = (bf16[128,512]{1,0:T(8,128)(2,1)S(1)}, bf16[128,512]{1,0:T(8,128)(2,1)S(1)}, bf16[128,512]{1,0:T(8,128)(2,1)S(1)}, bf16[128,512]{1,0:T(8,128)(2,1...) custom-call(s32[1]{0:T(128)} %bitcast.me_ref, ...), custom_call_target="tpu_custom_call" | custom-call | flops 2147483648 | bytes 4194304 | tf_op jit(solution)/shard_map/transform/pallas_call | solution.py:209
  38.3 2.3 %collective-permute-start.9 = (bf16[128,512]{1,0:T(8,128)(2,1)S(1)}, bf16[128,512]{1,0:T(8,128)(2,1)S(1)}, u32[]{:S(2)}, u32[]{:S(2)}) collective-permute-start(bf16[128,512]{1,0:T(8,128)(2,1)S(1)} %get-tuple-element.29), channel_id=1, source_target_pairs={{0,28},{4,24},{8,20},{12,16},{16,12},{20,8},{24,4},{28,0},{1,29},{... | collective-permute-start | bytes 393224 | tf_op jit(solution)/shard_map/ppermute | solution.py:31
  40.6 1.3 %collective-permute-start.11 = (bf16[128,512]{1,0:T(8,128)(2,1)S(1)}, bf16[128,512]{1,0:T(8,128)(2,1)S(1)}, u32[]{:S(2)}, u32[]{:S(2)}) collective-permute-start(bf16[128,512]{1,0:T(8,128)(2,1)S(1)} %get-tuple-element.31), channel_id=1, source_target_pairs={{0,24},{4,28},{8,16},{12,20},{16,8},{20,12},{24,0},{28,4},{1,25},{... | collective-permute-start | bytes 393224 | tf_op jit(solution)/shard_map/ppermute | solution.py:31
  42.0 2.3 %collective-permute-start.12 = (bf16[128,512]{1,0:T(8,128)(2,1)S(1)}, bf16[128,512]{1,0:T(8,128)(2,1)S(1)}, u32[]{:S(2)}, u32[]{:S(2)}) collective-permute-start(bf16[128,512]{1,0:T(8,128)(2,1)S(1)} %get-tuple-element.32), channel_id=1, source_target_pairs={{0,8},{4,12},{8,0},{12,4},{16,24},{20,28},{24,16},{28,20},{1,9},{5... | collective-permute-start | bytes 393224 | tf_op jit(solution)/shard_map/ppermute | solution.py:31
  44.3 1.7 %collective-permute-start.13 = (bf16[128,512]{1,0:T(8,128)(2,1)S(1)}, bf16[128,512]{1,0:T(8,128)(2,1)S(1)}, u32[]{:S(2)}, u32[]{:S(2)}) collective-permute-start(bf16[128,512]{1,0:T(8,128)(2,1)S(1)} %get-tuple-element.33), channel_id=1, source_target_pairs={{0,20},{4,16},{8,28},{12,24},{16,4},{20,0},{24,12},{28,8},{1,21},{... | collective-permute-start | bytes 393224 | tf_op jit(solution)/shard_map/ppermute | solution.py:31
  45.9 1.7 %collective-permute-done.9.refs_0_ = bf16[128,512]{1,0:T(8,128)(2,1)S(1)} collective-permute-done((bf16[128,512]{1,0:T(8,128)(2,1)S(1)}, bf16[128,512]{1,0:T(8,128)(2,1)S(1)}, u32[]{:S(2)}, u32[]{:S(2)}) %collective-permute-start.9) | collective-permute-done | bytes 131104 | tf_op jit(solution)/shard_map/ppermute | solution.py:31
  47.9 4.8 %collective-permute-done.10.refs_1_ = bf16[128,512]{1,0:T(8,128)(2,1)S(1)} collective-permute-done((bf16[128,512]{1,0:T(8,128)(2,1)S(1)}, bf16[128,512]{1,0:T(8,128)(2,1)S(1)}, u32[]{:S(2)}, u32[]{:S(2)}) %collective-permute-start.10) | collective-permute-done | bytes 131104 | tf_op jit(solution)/shard_map/ppermute | solution.py:31
  52.9 1.6 %collective-permute-done.12.refs_3_ = bf16[128,512]{1,0:T(8,128)(2,1)S(1)} collective-permute-done((bf16[128,512]{1,0:T(8,128)(2,1)S(1)}, bf16[128,512]{1,0:T(8,128)(2,1)S(1)}, u32[]{:S(2)}, u32[]{:S(2)}) %collective-permute-start.12) | collective-permute-done | bytes 131104 | tf_op jit(solution)/shard_map/ppermute | solution.py:31
  54.5 6.4 %collective-permute-done.13.refs_4_ = bf16[128,512]{1,0:T(8,128)(2,1)S(1)} collective-permute-done((bf16[128,512]{1,0:T(8,128)(2,1)S(1)}, bf16[128,512]{1,0:T(8,128)(2,1)S(1)}, u32[]{:S(2)}, u32[]{:S(2)}) %collective-permute-start.13) | collective-permute-done | bytes 131104 | tf_op jit(solution)/shard_map/ppermute | solution.py:31
  60.9 1.2 %collective-permute-done.15.refs_6_ = bf16[128,512]{1,0:T(8,128)(2,1)S(1)} collective-permute-done((bf16[128,512]{1,0:T(8,128)(2,1)S(1)}, bf16[128,512]{1,0:T(8,128)(2,1)S(1)}, u32[]{:S(2)}, u32[]{:S(2)}) %collective-permute-start.15) | collective-permute-done | bytes 131104 | tf_op jit(solution)/shard_map/ppermute | solution.py:31
  62.1 1.4 %merge.1 = bf16[1024,512]{1,0:T(8,128)(2,1)} custom-call(s32[1]{0:T(128)} %bitcast.me_ref, bf16[128,512]{1,0:T(8,128)(2,1)S(1)} %collective-permute-done.9.refs_0_, bf16[128,512]{1,0:T(8,128)(2,1)S(1)} %collective-permute-done.10.refs_1_, bf16[128,512]{1,0:T(8,128)(2,1)S(1)} %collective-permute-done.11.refs_2_, ...), custom_call_target="tpu_custom_call" | custom-call | flops 268435456 | bytes 2097152 | tf_op jit(solution)/shard_map/merge/pallas_call | solution.py:221
  (20 shorter events, 4.1 us)
Async XLA Ops:
  0.0 21.6 %collective-permute-start.3 = (bf16[5,128,1024]{2,1,0:T(8,128)(2,1)}, bf16[5,128,1024]{2,1,0:T(8,128)(2,1)S(1)}, u32[]{:S(2)}, u32[]{:S(2)}) collective-permute-start(bf16[5,128,1024]{2,1,0:T(8,128)(2,1)} %bitcast.7), channel_id=1, source_target_pairs={{1,2},{2,1},{5,6},{6,5},{9,10},{10,9},{13,14},{14,13},{17,18},{18,... | collective-permute-start | bytes 3932168 | tf_op jit(solution)/shard_map/ppermute | solution.py:164
  0.7 21.8 %collective-permute-start.2 = (bf16[5,128,1024]{2,1,0:T(8,128)(2,1)}, bf16[5,128,1024]{2,1,0:T(8,128)(2,1)S(1)}, u32[]{:S(2)}, u32[]{:S(2)}) collective-permute-start(bf16[5,128,1024]{2,1,0:T(8,128)(2,1)} %bitcast.8), channel_id=1, source_target_pairs={{0,1},{2,3},{1,0},{3,2},{4,5},{6,7},{5,4},{7,6},{8,9},{10,11},{9,8... | collective-permute-start | bytes 3932168 | tf_op jit(solution)/shard_map/ppermute | solution.py:164
  5.1 1.2 %copy-start.1 = (bf16[128,1,8,512]{3,2,1,0:T(8,128)(2,1)S(1)}, bf16[128,1,8,512]{3,2,1,0:T(8,128)(2,1)}, u32[]{:S(2)}) copy-start(bf16[128,1,8,512]{3,2,1,0:T(8,128)(2,1)} %param.5) | copy-start | bytes 3145732
  7.4 9.1 %collective-permute-start = (bf16[128,512]{1,0:T(8,128)(2,1)S(1)}, bf16[128,512]{1,0:T(8,128)(2,1)S(1)}, u32[]{:S(2)}, u32[]{:S(2)}) collective-permute-start(bf16[128,512]{1,0:T(8,128)(2,1)S(1)} %get-tuple-element.21), channel_id=1, source_target_pairs={{0,28},{4,24},{8,20},{12,16},{16,12},{20,8},{24,4},{28,0},{1,29},{... | collective-permute-start | bytes 393224 | tf_op jit(solution)/shard_map/ppermute | solution.py:31
  11.9 9.0 %collective-permute-start.1 = (bf16[128,512]{1,0:T(8,128)(2,1)S(1)}, bf16[128,512]{1,0:T(8,128)(2,1)S(1)}, u32[]{:S(2)}, u32[]{:S(2)}) collective-permute-start(bf16[128,512]{1,0:T(8,128)(2,1)S(1)} %get-tuple-element.22), channel_id=1, source_target_pairs={{0,12},{4,8},{8,4},{12,0},{16,28},{20,24},{24,20},{28,16},{1,13},{... | collective-permute-start | bytes 393224 | tf_op jit(solution)/shard_map/ppermute | solution.py:31
  11.9 18.7 %collective-permute-start.4 = (bf16[128,512]{1,0:T(8,128)(2,1)}, bf16[128,512]{1,0:T(8,128)(2,1)S(1)}, u32[]{:S(2)}, u32[]{:S(2)}) collective-permute-start(bf16[128,512]{1,0:T(8,128)(2,1)} %get-tuple-element.23), channel_id=1, source_target_pairs={{0,24},{4,28},{8,16},{12,20},{16,8},{20,12},{24,0},{28,4},{1,25},{... | collective-permute-start | bytes 393224 | tf_op jit(solution)/shard_map/ppermute | solution.py:31
  16.5 14.1 %collective-permute-start.5 = (bf16[128,512]{1,0:T(8,128)(2,1)}, bf16[128,512]{1,0:T(8,128)(2,1)S(1)}, u32[]{:S(2)}, u32[]{:S(2)}) collective-permute-start(bf16[128,512]{1,0:T(8,128)(2,1)} %get-tuple-element.24), channel_id=1, source_target_pairs={{0,8},{4,12},{8,0},{12,4},{16,24},{20,28},{24,16},{28,20},{1,9},{5... | collective-permute-start | bytes 393224 | tf_op jit(solution)/shard_map/ppermute | solution.py:31
  20.9 12.2 %collective-permute-start.6 = (bf16[128,512]{1,0:T(8,128)(2,1)}, bf16[128,512]{1,0:T(8,128)(2,1)}, u32[]{:S(2)}, u32[]{:S(2)}) collective-permute-start(bf16[128,512]{1,0:T(8,128)(2,1)} %get-tuple-element.25), channel_id=1, source_target_pairs={{0,20},{4,16},{8,28},{12,24},{16,4},{20,0},{24,12},{28,8},{1,21},{... | collective-permute-start | bytes 393224 | tf_op jit(solution)/shard_map/ppermute | solution.py:31
  21.6 11.5 %collective-permute-start.7 = (bf16[128,512]{1,0:T(8,128)(2,1)S(1)}, bf16[128,512]{1,0:T(8,128)(2,1)}, u32[]{:S(2)}, u32[]{:S(2)}) collective-permute-start(bf16[128,512]{1,0:T(8,128)(2,1)S(1)} %get-tuple-element.26), channel_id=1, source_target_pairs={{0,4},{4,0},{8,12},{12,8},{16,20},{20,16},{24,28},{28,24},{1,5},{5... | collective-permute-start | bytes 393224 | tf_op jit(solution)/shard_map/ppermute | solution.py:31
  22.5 12.2 %collective-permute-start.8 = (bf16[128,512]{1,0:T(8,128)(2,1)S(1)}, bf16[128,512]{1,0:T(8,128)(2,1)}, u32[]{:S(2)}, u32[]{:S(2)}) collective-permute-start(bf16[128,512]{1,0:T(8,128)(2,1)S(1)} %get-tuple-element.27), channel_id=1, source_target_pairs={{0,16},{4,20},{8,24},{12,28},{16,0},{20,4},{24,8},{28,12},{1,17},{... | collective-permute-start | bytes 393224 | tf_op jit(solution)/shard_map/ppermute | solution.py:31
  25.9 1.3 %copy-start = (bf16[1,1,5,128,1024]{4,3,2,1,0:T(8,128)(2,1)S(1)}, bf16[1,1,5,128,1024]{4,3,2,1,0:T(8,128)(2,1)}, u32[]{:S(2)}) copy-start(bf16[1,1,5,128,1024]{4,3,2,1,0:T(8,128)(2,1)} %param.6) | copy-start | bytes 3932164
  27.3 0.7 %copy-start.2 = (s32[1,1,3]{2,1,0:T(1,128)S(1)}, s32[1,1,3]{2,1,0:T(1,128)}, u32[]{:S(2)}) copy-start(s32[1,1,3]{2,1,0:T(1,128)} %ids_hbm.1) | copy-start | bytes 40
  27.9 0.7 %copy-start.3 = (s32[1,1,3]{2,1,0:T(1,128)S(1)}, s32[1,1,3]{2,1,0:T(1,128)}, u32[]{:S(2)}) copy-start(s32[1,1,3]{2,1,0:T(1,128)} %src_hbm.1) | copy-start | bytes 40
  38.3 9.3 %collective-permute-start.9 = (bf16[128,512]{1,0:T(8,128)(2,1)S(1)}, bf16[128,512]{1,0:T(8,128)(2,1)S(1)}, u32[]{:S(2)}, u32[]{:S(2)}) collective-permute-start(bf16[128,512]{1,0:T(8,128)(2,1)S(1)} %get-tuple-element.29), channel_id=1, source_target_pairs={{0,28},{4,24},{8,20},{12,16},{16,12},{20,8},{24,4},{28,0},{1,29},{... | collective-permute-start | bytes 393224 | tf_op jit(solution)/shard_map/ppermute | solution.py:31
  40.6 12.1 %collective-permute-start.10 = (bf16[128,512]{1,0:T(8,128)(2,1)S(1)}, bf16[128,512]{1,0:T(8,128)(2,1)S(1)}, u32[]{:S(2)}, u32[]{:S(2)}) collective-permute-start(bf16[128,512]{1,0:T(8,128)(2,1)S(1)} %get-tuple-element.30), channel_id=1, source_target_pairs={{0,12},{4,8},{8,4},{12,0},{16,28},{20,24},{24,20},{28,16},{1,13},{... | collective-permute-start | bytes 393224 | tf_op jit(solution)/shard_map/ppermute | solution.py:31
  40.6 12.2 %collective-permute-start.11 = (bf16[128,512]{1,0:T(8,128)(2,1)S(1)}, bf16[128,512]{1,0:T(8,128)(2,1)S(1)}, u32[]{:S(2)}, u32[]{:S(2)}) collective-permute-start(bf16[128,512]{1,0:T(8,128)(2,1)S(1)} %get-tuple-element.31), channel_id=1, source_target_pairs={{0,24},{4,28},{8,16},{12,20},{16,8},{20,12},{24,0},{28,4},{1,25},{... | collective-permute-start | bytes 393224 | tf_op jit(solution)/shard_map/ppermute | solution.py:31
  42.0 12.5 %collective-permute-start.12 = (bf16[128,512]{1,0:T(8,128)(2,1)S(1)}, bf16[128,512]{1,0:T(8,128)(2,1)S(1)}, u32[]{:S(2)}, u32[]{:S(2)}) collective-permute-start(bf16[128,512]{1,0:T(8,128)(2,1)S(1)} %get-tuple-element.32), channel_id=1, source_target_pairs={{0,8},{4,12},{8,0},{12,4},{16,24},{20,28},{24,16},{28,20},{1,9},{5... | collective-permute-start | bytes 393224 | tf_op jit(solution)/shard_map/ppermute | solution.py:31
  44.3 16.6 %collective-permute-start.13 = (bf16[128,512]{1,0:T(8,128)(2,1)S(1)}, bf16[128,512]{1,0:T(8,128)(2,1)S(1)}, u32[]{:S(2)}, u32[]{:S(2)}) collective-permute-start(bf16[128,512]{1,0:T(8,128)(2,1)S(1)} %get-tuple-element.33), channel_id=1, source_target_pairs={{0,20},{4,16},{8,28},{12,24},{16,4},{20,0},{24,12},{28,8},{1,21},{... | collective-permute-start | bytes 393224 | tf_op jit(solution)/shard_map/ppermute | solution.py:31
  47.6 13.3 %collective-permute-start.14 = (bf16[128,512]{1,0:T(8,128)(2,1)S(1)}, bf16[128,512]{1,0:T(8,128)(2,1)S(1)}, u32[]{:S(2)}, u32[]{:S(2)}) collective-permute-start(bf16[128,512]{1,0:T(8,128)(2,1)S(1)} %get-tuple-element.34), channel_id=1, source_target_pairs={{0,4},{4,0},{8,12},{12,8},{16,20},{20,16},{24,28},{28,24},{1,5},{5... | collective-permute-start | bytes 393224 | tf_op jit(solution)/shard_map/ppermute | solution.py:31
  52.7 9.4 %collective-permute-start.15 = (bf16[128,512]{1,0:T(8,128)(2,1)S(1)}, bf16[128,512]{1,0:T(8,128)(2,1)S(1)}, u32[]{:S(2)}, u32[]{:S(2)}) collective-permute-start(bf16[128,512]{1,0:T(8,128)(2,1)S(1)} %get-tuple-element.35), channel_id=1, source_target_pairs={{0,16},{4,20},{8,24},{12,28},{16,0},{20,4},{24,8},{28,12},{1,17},{... | collective-permute-start | bytes 393224 | tf_op jit(solution)/shard_map/ppermute | solution.py:31

commit v7 on v6

--- a/solution.py
+++ b/solution.py
@@ -7,12 +7,18 @@
 from jax.experimental.pallas import tpu as pltpu
 from jax.sharding import PartitionSpec as P
 
-EARLY = 2
 LIMIT = 16 * 1024 * 1024
 
 
 def rows_per_group(rows, patches):
     return min(rows, max(16, 256 // patches))
+
+
+PARTS = 8
+
+
+def is_late(k, count):
+    return k // (count // PARTS) == PARTS // 2
 
 
 def partners(count):
@@ -21,7 +27,14 @@
     order = []
     for i in range(len(far)):
         order += far[i : i + 1] + near[i : i + 1]
-    return order + [0]
+    return order
+
+
+def inward(count):
+    order = [k for k in partners(count) if not is_late(k, count)]
+    last_far = order.index(min(k for k in order if k >= count // 2))
+    order.insert(min(3, last_far), order.pop(last_far))
+    return order + [k for k in partners(count) if is_late(k, count)]
 
 
 def ppermute(value, axis, step):
@@ -31,8 +44,8 @@
     return lax.ppermute(value, axis, [(i, i ^ step) for i in range(count)])
 
 
-def split_kernel(me_ref, members_ref, *out_refs):
-    patches = len(out_refs)
+def split_kernel(steps, me_ref, members_ref, *out_refs):
+    patches = len(steps)
     rows = out_refs[0].shape[0]
     group = rows_per_group(rows, patches)
     height = group * patches
@@ -44,7 +57,7 @@
         block = members_ref[step * height : (step + 1) * height, :]
         moved = jnp.dot(shuffle, block, preferred_element_type=jnp.float32)
         moved = moved.astype(jnp.bfloat16)
-        for k, out_ref in enumerate(out_refs):
+        for k, out_ref in zip(steps, out_refs):
             out_ref[step * group : (step + 1) * group, :] = moved[k * group : (k + 1) * group, :]
 
 
@@ -118,32 +131,59 @@
         gram_ref[step * part : (step + 1) * part, :] = (block * scale).astype(jnp.bfloat16)
 
 
-def transform_kernel(order, me_ref, *refs):
-    count = len(order)
-    piece_refs = dict(zip(order, refs[:EARLY] + refs[EARLY + 1 : count + 1]))
-    gram_ref, out_refs = refs[EARLY], refs[count + 1 : 2 * count + 1]
-    members, first, fresh = refs[2 * count + 1 :]
-    rows = out_refs[0].shape[0]
-
-    def place(k):
-        return pl.ds(pl.multiple_of((me_ref[0] ^ k) * rows, rows), rows)
-
-    for k in range(count):
-        members[place(k), :] = piece_refs[k][...]
+def block(me_ref, j, width, rows):
+    return pl.ds(pl.multiple_of((lax.div(me_ref[0], width) ^ j) * rows, rows), rows)
+
+
+def within(me_ref, k, quarter, rows):
+    return pl.ds(pl.multiple_of(lax.rem(me_ref[0] ^ k, quarter) * rows, rows), rows)
+
+
+def early_kernel(steps, me_ref, gram_ref, *refs):
+    piece_refs, (acc_ref, members_ref) = refs[:-2], refs[-2:]
+    rows = piece_refs[0].shape[0]
     size = gram_ref.shape[0]
-    part = min(size, 256)
-    for step in range(size // part):
-        here = slice(step * part, (step + 1) * part)
-        first[here, :] = jnp.dot(
-            gram_ref[here, :], members[...], preferred_element_type=jnp.float32
-        ).astype(jnp.bfloat16)
-    for step in range(size // part):
-        here = slice(step * part, (step + 1) * part)
-        second = jnp.dot(gram_ref[here, :], first[...], preferred_element_type=jnp.float32)
-        rest = members[here, :].astype(jnp.float32) - first[here, :].astype(jnp.float32)
-        fresh[here, :] = (rest + second).astype(jnp.bfloat16)
-    for k in range(count):
-        out_refs[k][...] = fresh[place(k), :]
+    there = block(me_ref, PARTS // 2, size // rows // PARTS, size // PARTS)
+    members_ref[there, :] = jnp.zeros((size // PARTS, members_ref.shape[1]), members_ref.dtype)
+    for k, piece in zip(steps, piece_refs):
+        members_ref[pl.ds(pl.multiple_of((me_ref[0] ^ k) * rows, rows), rows), :] = piece[...]
+    tall = size // 4
+    for step in range(4):
+        here = slice(step * tall, (step + 1) * tall)
+        acc_ref[here, :] = jnp.dot(
+            gram_ref[here, :], members_ref[...], preferred_element_type=jnp.float32
+        )
+
+
+def late_kernel(late_steps, out_steps, me_ref, gram_ref, acc_ref, members_ref, *refs):
+    count = len(late_steps)
+    late_refs, outs = refs[:count], dict(zip(out_steps, refs[count:-3]))
+    first, late, fresh = refs[-3:]
+    rows = late_refs[0].shape[0]
+    size = gram_ref.shape[0]
+    width = late.shape[0] // rows
+    for k, piece in zip(late_steps, late_refs):
+        late[within(me_ref, k, width, rows), :] = piece[...]
+    there = block(me_ref, PARTS // 2, width, late.shape[0])
+    tall = size // 4
+    for step in range(4):
+        here = slice(step * tall, (step + 1) * tall)
+        part = jnp.dot(gram_ref[here, there], late[...], preferred_element_type=jnp.float32)
+        first[here, :] = (acc_ref[here, :] + part).astype(jnp.bfloat16)
+    quarter = tall // rows
+    for j in (3, 2, 1, 0):
+        there = block(me_ref, j, quarter, tall)
+        second = jnp.dot(gram_ref[there, :], first[...], preferred_element_type=jnp.float32)
+        rest = members_ref[there, :].astype(jnp.float32) - first[there, :].astype(jnp.float32)
+        fresh[...] = rest + second
+        for k in late_steps:
+            if k // quarter == j:
+                here = within(me_ref, k, quarter, rows)
+                fresh[here, :] += late[within(me_ref, k, width, rows), :].astype(jnp.float32)
+        for k, out_ref in outs.items():
+            if k // quarter == j:
+                here = within(me_ref, k, quarter, rows)
+                out_ref[...] = fresh[here, :].astype(jnp.bfloat16)
 
 
 def vmem():
@@ -176,8 +216,9 @@
     piece_shape = jax.ShapeDtypeStruct((rows, values), jnp.bfloat16)
 
     odd, even = swap(store, 1), swap(store, 0)
+    steps = [0] + inward(patches)
     pieces = pl.pallas_call(
-        split_kernel,
+        functools.partial(split_kernel, steps),
         out_shape=[piece_shape] * patches,
         in_specs=[smem, vmem()],
         out_specs=[vmem()] * patches,
@@ -185,8 +226,7 @@
         cost_estimate=cost(2 * 256 * rows * patches * values, 4 * rows * patches * values),
         name="split",
     )(me, ensemble.reshape(rows * patches, values))
-    order = partners(patches)
-    arrived = [ppermute(pieces[k], "member", k) for k in order]
+    arrived = {k: ppermute(piece, "member", k) for k, piece in zip(steps, pieces)}
 
     gram = pl.pallas_call(
         functools.partial(gram_kernel, 1.0 / (2.0 * size)),
@@ -206,17 +246,35 @@
         name="gram",
     )(region, block_ids, block_src, block_count, store, even, odd)
 
+    early = [k for k in steps if not is_late(k, patches)]
+    late = [k for k in steps if is_late(k, patches)]
+    matrix = jax.ShapeDtypeStruct((size, values), jnp.bfloat16)
+    acc, members = pl.pallas_call(
+        functools.partial(early_kernel, early),
+        out_shape=[jax.ShapeDtypeStruct((size, values), jnp.float32), matrix],
+        in_specs=[smem] + [vmem()] * (1 + len(early)),
+        out_specs=[vmem()] * 2,
+        compiler_params=params(),
+        cost_estimate=cost(2 * size * size * values, 2 * size * size + 8 * size * values),
+        name="early",
+    )(me, gram, *[arrived[k] for k in early])
+    back = partners(patches) + [0]
     moved = pl.pallas_call(
-        functools.partial(transform_kernel, order),
+        functools.partial(late_kernel, late, back),
         out_shape=[piece_shape] * patches,
-        in_specs=[smem] + [vmem()] * (1 + patches),
+        in_specs=[smem] + [vmem()] * (3 + len(late)),
         out_specs=[vmem()] * patches,
-        scratch_shapes=[pltpu.VMEM((size, values), jnp.bfloat16)] * 3,
-        compiler_params=params(),
-        cost_estimate=cost(4 * size * size * values, 2 * size * size + 4 * size * values),
-        name="transform",
-    )(me, *arrived[:EARLY], gram, *arrived[EARLY:])
-    returned = [ppermute(moved[k], "member", k) for k in order]
+        scratch_shapes=[
+            pltpu.VMEM((size, values), jnp.bfloat16),
+            pltpu.VMEM((size // PARTS, values), jnp.bfloat16),
+            pltpu.VMEM((size // 4, values), jnp.float32),
+        ],
+        compiler_params=params(),
+        cost_estimate=cost(3 * size * size * values, 2 * size * size + 10 * size * values),
+        name="late",
+    )(me, gram, acc, members, *[arrived[k] for k in late])
+    order = back
+    returned = [ppermute(piece, "member", k) for k, piece in zip(back, moved)]
 
     fresh = pl.pallas_call(
         functools.partial(merge_kernel, order),

time: 63.7 us -> 62.4 us (0.980)
  waiting for transfers between devices: 24.4 us -> 22.1 us
    ppermute x14, waiting for transfers between devices: 24.4 us -> 22.1 us  [ppermute(): return lax.ppermute(value, axis, [(i, i ^ step) for i in range(count)])]
    pallas_call x2 -> x3, Pallas kernels: 4.69 us -> 5.21 us  [the longest x1 2.34 us: shards(): pl.pallas_call(functools.partial(early_kernel, early), out_shape=[jax.Sha...]
  transfers between devices with their start and end apart: 16 -> 16, of which waited for: 9 -> 9; matrix products, arithmetic and copies ran while one was open for 0% -> 0% of each run, Pallas kernels for 5% -> 9%
where the time goes in v7:
time: 62.4 us; the launch traced here: 62.2 us
  starting transfers between devices  26.8 us (43%)
  waiting for transfers between devices  22.1 us (35%)
  Pallas kernels  8.66 us (14%)
  local copies, waits for them, and re-layouts  3.85 us (6%)
  between operations  0.72 us (1%)
    ppermute x14, waiting for transfers between devices, ppermute(): return lax.ppermute(value, axis, [(i, i ^ step) for i in range(count)])  22.1 us
    ppermute x14, starting transfers between devices, ppermute(): return lax.ppermute(value, axis, [(i, i ^ step) for i in range(count)])  21.7 us
    ppermute x2, starting transfers between devices, swap(): return lax.ppermute(store, 'region', pairs + [(j, i) for i, j in pairs])  5.05 us
    unnamed x8, local copies, waits for them, and re-layouts  3.85 us
    pallas_call x1, Pallas kernels, shards(): pl.pallas_call(functools.partial(early_kernel, early), out_shape=[jax.Sha...  2.34 us
    pallas_call x1, Pallas kernels, shards(): pl.pallas_call(functools.partial(gram_kernel, 1.0 / (2.0 * size)), out_sh...  2.03 us
    pallas_call x1, Pallas kernels, shards(): pl.pallas_call(functools.partial(late_kernel, late, back), out_shape=[pie...  1.75 us
    pallas_call x1, Pallas kernels, shards(): pl.pallas_call(functools.partial(merge_kernel, order), out_shape=jax.Shap...  1.41 us
  transfers between devices with their start and end apart: 16, of which 9 were waited for; matrix products, arithmetic and copies ran while one was open for 0% of the time, Pallas kernels for 9%

profile of v7, /device:TPU:0, one launch (start us, length us, event | category | flops | bytes accessed | tf_op | source)
XLA Modules:
  0.0 62.2 jit_solution(13304307366235594725)
XLA Ops:
  0.7 4.3 %collective-permute-start = (bf16[5,128,1024]{2,1,0:T(8,128)(2,1)}, bf16[5,128,1024]{2,1,0:T(8,128)(2,1)S(1)}, u32[]{:S(2)}, u32[]{:S(2)}) collective-permute-start(bf16[5,128,1024]{2,1,0:T(8,128)(2,1)} %bitcast.8), channel_id=1, source_target_pairs={{0,1},{2,3},{1,0},{3,2},{4,5},{6,7},{5,4},{7,6},{8,9},{10,11},{9,8... | collective-permute-start | bytes 3932168 | tf_op jit(solution)/shard_map/ppermute | solution.py:204
  5.1 1.2 %copy-done.1 = bf16[128,1,8,512]{3,2,1,0:T(8,128)(2,1)S(1)} copy-done((bf16[128,1,8,512]{3,2,1,0:T(8,128)(2,1)S(1)}, bf16[128,1,8,512]{3,2,1,0:T(8,128)(2,1)}, u32[]{:S(2)}) %copy-start.1) | copy-done | bytes 1048600
  6.3 1.1 %split.1 = (bf16[128,512]{1,0:T(8,128)(2,1)S(1)}, bf16[128,512]{1,0:T(8,128)(2,1)S(1)}, bf16[128,512]{1,0:T(8,128)(2,1)S(1)}, bf16[128,512]{1,0:T(8,128)(2,1)}, ...) custom-call(s32[1]{0:T(128)} %bitcast.me_ref, ...), custom_call_target="tpu_custom_call" | custom-call | flops 268435456 | bytes 2097152 | tf_op jit(solution)/shard_map/split/pallas_call | solution.py:220
  7.4 4.5 %collective-permute-start.2 = (bf16[128,512]{1,0:T(8,128)(2,1)S(1)}, bf16[128,512]{1,0:T(8,128)(2,1)S(1)}, u32[]{:S(2)}, u32[]{:S(2)}) collective-permute-start(bf16[128,512]{1,0:T(8,128)(2,1)S(1)} %get-tuple-element.24), channel_id=1, source_target_pairs={{0,28},{4,24},{8,20},{12,16},{16,12},{20,8},{24,4},{28,0},{1,29},{... | collective-permute-start | bytes 393224 | tf_op jit(solution)/shard_map/ppermute | solution.py:44
  12.8 3.7 %collective-permute-done.2.refs_1_ = bf16[128,512]{1,0:T(8,128)(2,1)S(1)} collective-permute-done((bf16[128,512]{1,0:T(8,128)(2,1)S(1)}, bf16[128,512]{1,0:T(8,128)(2,1)S(1)}, u32[]{:S(2)}, u32[]{:S(2)}) %collective-permute-start.2) | collective-permute-done | bytes 131104 | tf_op jit(solution)/shard_map/ppermute | solution.py:44
  16.5 4.3 %collective-permute-start.5 = (bf16[128,512]{1,0:T(8,128)(2,1)}, bf16[128,512]{1,0:T(8,128)(2,1)}, u32[]{:S(2)}, u32[]{:S(2)}) collective-permute-start(bf16[128,512]{1,0:T(8,128)(2,1)} %get-tuple-element.27), channel_id=1, source_target_pairs={{0,20},{4,16},{8,28},{12,24},{16,4},{20,0},{24,12},{28,8},{1,21},{... | collective-permute-start | bytes 393224 | tf_op jit(solution)/shard_map/ppermute | solution.py:44
  21.6 1.0 %collective-permute-start.7 = (bf16[128,512]{1,0:T(8,128)(2,1)S(1)}, bf16[128,512]{1,0:T(8,128)(2,1)}, u32[]{:S(2)}, u32[]{:S(2)}) collective-permute-start(bf16[128,512]{1,0:T(8,128)(2,1)S(1)} %get-tuple-element.29), channel_id=1, source_target_pairs={{0,4},{4,0},{8,12},{12,8},{16,20},{20,16},{24,28},{28,24},{1,5},{5... | collective-permute-start | bytes 393224 | tf_op jit(solution)/shard_map/ppermute | solution.py:44
  23.3 1.8 %collective-permute-start.8 = (bf16[128,512]{1,0:T(8,128)(2,1)S(1)}, bf16[128,512]{1,0:T(8,128)(2,1)S(1)}, u32[]{:S(2)}, u32[]{:S(2)}) collective-permute-start(bf16[128,512]{1,0:T(8,128)(2,1)S(1)} %get-tuple-element.32), channel_id=1, source_target_pairs={{0,16},{4,20},{8,24},{12,28},{16,0},{20,4},{24,8},{28,12},{1,17},{... | collective-permute-start | bytes 393224 | tf_op jit(solution)/shard_map/ppermute | solution.py:44
  25.1 1.3 %copy-done = bf16[1,1,5,128,1024]{4,3,2,1,0:T(8,128)(2,1)S(1)} copy-done((bf16[1,1,5,128,1024]{4,3,2,1,0:T(8,128)(2,1)S(1)}, bf16[1,1,5,128,1024]{4,3,2,1,0:T(8,128)(2,1)}, u32[]{:S(2)}) %copy-start) | copy-done | bytes 1310744
  27.7 2.0 %gram.1.gram_ref = bf16[1024,1024]{1,0:T(8,128)(2,1)S(1)} custom-call(s32[1]{0:T(128)} %bitcast.1.region_ref, s32[1,1,3]{2,1,0:T(1,128)S(1)} %copy-done.2, s32[1,1,3]{2,1,0:T(1,128)S(1)} %copy-done.3, s32[1,1]{1,0:T(1,128)S(6)} %copy.7.count_hbm, bf16[5,128,1024]{2,1,0:T(8,128)(2,1)S(1)} %bitcast.9, bf16[5,128,1024]{2,1,0:T(8,128)(2,1)S(1)} %collective-permute-done.even, ...), custom_call_target="tpu_custom_call" | custom-call | flops 805306368 | bytes 4194304 | tf_op jit(solution)/shard_map/gram/pallas_call | solution.py:231
  29.8 2.8 %collective-permute-done.5.refs_4_ = bf16[128,512]{1,0:T(8,128)(2,1)} collective-permute-done((bf16[128,512]{1,0:T(8,128)(2,1)}, bf16[128,512]{1,0:T(8,128)(2,1)}, u32[]{:S(2)}, u32[]{:S(2)}) %collective-permute-start.5) | collective-permute-done | bytes 131104 | tf_op jit(solution)/shard_map/ppermute | solution.py:44
  32.6 2.3 %early.1 = (f32[1024,512]{1,0:T(8,128)S(1)}, bf16[1024,512]{1,0:T(8,128)(2,1)S(1)}) custom-call(s32[1]{0:T(128)} %bitcast.me_ref, bf16[1024,1024]{1,0:T(8,128)(2,1)S(1)} %gram.1.gram_ref, bf16[128,512]{1,0:T(8,128)(2,1)S(1)} %get-tuple-element.23.refs_0_, bf16[128,512]{1,0:T(8,128)(2,1)S(1)} %collective-permute-done.2.refs_1_, ...), custom_call_target="tpu_custom_call" | custom-call | flops 1073741824 | bytes 6291456 | tf_op jit(solution)/shard_map/early/pallas_call | solution.py:252
  35.0 1.8 %late.1 = (bf16[128,512]{1,0:T(8,128)(2,1)S(1)}, bf16[128,512]{1,0:T(8,128)(2,1)S(1)}, bf16[128,512]{1,0:T(8,128)(2,1)S(1)}, bf16[128,512]{1,0:T(8,128)(2,1)S(1)...) custom-call(s32[1]{0:T(128)} %bitcast.me_ref, ...), custom_call_target="tpu_custom_call" | custom-call | flops 1610612736 | bytes 7340032 | tf_op jit(solution)/shard_map/late/pallas_call | solution.py:262
  36.7 3.3 %collective-permute-start.9 = (bf16[128,512]{1,0:T(8,128)(2,1)S(1)}, bf16[128,512]{1,0:T(8,128)(2,1)S(1)}, u32[]{:S(2)}, u32[]{:S(2)}) collective-permute-start(bf16[128,512]{1,0:T(8,128)(2,1)S(1)} %get-tuple-element.33), channel_id=1, source_target_pairs={{0,28},{4,24},{8,20},{12,16},{16,12},{20,8},{24,4},{28,0},{1,29},{... | collective-permute-start | bytes 393224 | tf_op jit(solution)/shard_map/ppermute | solution.py:44
  40.0 1.5 %collective-permute-start.11 = (bf16[128,512]{1,0:T(8,128)(2,1)S(1)}, bf16[128,512]{1,0:T(8,128)(2,1)S(1)}, u32[]{:S(2)}, u32[]{:S(2)}) collective-permute-start(bf16[128,512]{1,0:T(8,128)(2,1)S(1)} %get-tuple-element.35), channel_id=1, source_target_pairs={{0,24},{4,28},{8,16},{12,20},{16,8},{20,12},{24,0},{28,4},{1,25},{... | collective-permute-start | bytes 393224 | tf_op jit(solution)/shard_map/ppermute | solution.py:44
  41.5 1.1 %collective-permute-start.12 = (bf16[128,512]{1,0:T(8,128)(2,1)S(1)}, bf16[128,512]{1,0:T(8,128)(2,1)S(1)}, u32[]{:S(2)}, u32[]{:S(2)}) collective-permute-start(bf16[128,512]{1,0:T(8,128)(2,1)S(1)} %get-tuple-element.36), channel_id=1, source_target_pairs={{0,8},{4,12},{8,0},{12,4},{16,24},{20,28},{24,16},{28,20},{1,9},{5... | collective-permute-start | bytes 393224 | tf_op jit(solution)/shard_map/ppermute | solution.py:44
  42.7 1.8 %collective-permute-start.13 = (bf16[128,512]{1,0:T(8,128)(2,1)S(1)}, bf16[128,512]{1,0:T(8,128)(2,1)S(1)}, u32[]{:S(2)}, u32[]{:S(2)}) collective-permute-start(bf16[128,512]{1,0:T(8,128)(2,1)S(1)} %get-tuple-element.37), channel_id=1, source_target_pairs={{0,20},{4,16},{8,28},{12,24},{16,4},{20,0},{24,12},{28,8},{1,21},{... | collective-permute-start | bytes 393224 | tf_op jit(solution)/shard_map/ppermute | solution.py:44
  44.4 1.7 %collective-permute-done.9.refs_0_ = bf16[128,512]{1,0:T(8,128)(2,1)S(1)} collective-permute-done((bf16[128,512]{1,0:T(8,128)(2,1)S(1)}, bf16[128,512]{1,0:T(8,128)(2,1)S(1)}, u32[]{:S(2)}, u32[]{:S(2)}) %collective-permute-start.9) | collective-permute-done | bytes 131104 | tf_op jit(solution)/shard_map/ppermute | solution.py:44
  46.1 1.4 %collective-permute-start.14 = (bf16[128,512]{1,0:T(8,128)(2,1)S(1)}, bf16[128,512]{1,0:T(8,128)(2,1)S(1)}, u32[]{:S(2)}, u32[]{:S(2)}) collective-permute-start(bf16[128,512]{1,0:T(8,128)(2,1)S(1)} %get-tuple-element.38), channel_id=1, source_target_pairs={{0,4},{4,0},{8,12},{12,8},{16,20},{20,16},{24,28},{28,24},{1,5},{5... | collective-permute-start | bytes 393224 | tf_op jit(solution)/shard_map/ppermute | solution.py:44
  47.4 3.8 %collective-permute-done.10.refs_1_ = bf16[128,512]{1,0:T(8,128)(2,1)S(1)} collective-permute-done((bf16[128,512]{1,0:T(8,128)(2,1)S(1)}, bf16[128,512]{1,0:T(8,128)(2,1)S(1)}, u32[]{:S(2)}, u32[]{:S(2)}) %collective-permute-start.10) | collective-permute-done | bytes 131104 | tf_op jit(solution)/shard_map/ppermute | solution.py:44
  51.7 0.9 %collective-permute-done.12.refs_3_ = bf16[128,512]{1,0:T(8,128)(2,1)S(1)} collective-permute-done((bf16[128,512]{1,0:T(8,128)(2,1)S(1)}, bf16[128,512]{1,0:T(8,128)(2,1)S(1)}, u32[]{:S(2)}, u32[]{:S(2)}) %collective-permute-start.12) | collective-permute-done | bytes 131104 | tf_op jit(solution)/shard_map/ppermute | solution.py:44
  52.6 6.6 %collective-permute-done.13.refs_4_ = bf16[128,512]{1,0:T(8,128)(2,1)S(1)} collective-permute-done((bf16[128,512]{1,0:T(8,128)(2,1)S(1)}, bf16[128,512]{1,0:T(8,128)(2,1)S(1)}, u32[]{:S(2)}, u32[]{:S(2)}) %collective-permute-start.13) | collective-permute-done | bytes 131104 | tf_op jit(solution)/shard_map/ppermute | solution.py:44
  59.2 1.5 %collective-permute-done.15.refs_6_ = bf16[128,512]{1,0:T(8,128)(2,1)S(1)} collective-permute-done((bf16[128,512]{1,0:T(8,128)(2,1)S(1)}, bf16[128,512]{1,0:T(8,128)(2,1)S(1)}, u32[]{:S(2)}, u32[]{:S(2)}) %collective-permute-start.15) | collective-permute-done | bytes 131104 | tf_op jit(solution)/shard_map/ppermute | solution.py:44
  60.7 1.4 %merge.1 = bf16[1024,512]{1,0:T(8,128)(2,1)} custom-call(s32[1]{0:T(128)} %bitcast.me_ref, bf16[128,512]{1,0:T(8,128)(2,1)S(1)} %collective-permute-done.9.refs_0_, bf16[128,512]{1,0:T(8,128)(2,1)S(1)} %collective-permute-done.10.refs_1_, bf16[128,512]{1,0:T(8,128)(2,1)S(1)} %collective-permute-done.11.refs_2_, ...), custom_call_target="tpu_custom_call" | custom-call | flops 268435456 | bytes 2097152 | tf_op jit(solution)/shard_map/merge/pallas_call | solution.py:279
  (21 shorter events, 4.2 us)
Async XLA Ops:
  0.0 21.6 %collective-permute-start.1 = (bf16[5,128,1024]{2,1,0:T(8,128)(2,1)}, bf16[5,128,1024]{2,1,0:T(8,128)(2,1)S(1)}, u32[]{:S(2)}, u32[]{:S(2)}) collective-permute-start(bf16[5,128,1024]{2,1,0:T(8,128)(2,1)} %bitcast.7), channel_id=1, source_target_pairs={{1,2},{2,1},{5,6},{6,5},{9,10},{10,9},{13,14},{14,13},{17,18},{18,... | collective-permute-start | bytes 3932168 | tf_op jit(solution)/shard_map/ppermute | solution.py:204
  0.7 22.5 %collective-permute-start = (bf16[5,128,1024]{2,1,0:T(8,128)(2,1)}, bf16[5,128,1024]{2,1,0:T(8,128)(2,1)S(1)}, u32[]{:S(2)}, u32[]{:S(2)}) collective-permute-start(bf16[5,128,1024]{2,1,0:T(8,128)(2,1)} %bitcast.8), channel_id=1, source_target_pairs={{0,1},{2,3},{1,0},{3,2},{4,5},{6,7},{5,4},{7,6},{8,9},{10,11},{9,8... | collective-permute-start | bytes 3932168 | tf_op jit(solution)/shard_map/ppermute | solution.py:204
  5.1 1.2 %copy-start.1 = (bf16[128,1,8,512]{3,2,1,0:T(8,128)(2,1)S(1)}, bf16[128,1,8,512]{3,2,1,0:T(8,128)(2,1)}, u32[]{:S(2)}) copy-start(bf16[128,1,8,512]{3,2,1,0:T(8,128)(2,1)} %param.5) | copy-start | bytes 3145732
  7.4 9.1 %collective-permute-start.2 = (bf16[128,512]{1,0:T(8,128)(2,1)S(1)}, bf16[128,512]{1,0:T(8,128)(2,1)S(1)}, u32[]{:S(2)}, u32[]{:S(2)}) collective-permute-start(bf16[128,512]{1,0:T(8,128)(2,1)S(1)} %get-tuple-element.24), channel_id=1, source_target_pairs={{0,28},{4,24},{8,20},{12,16},{16,12},{20,8},{24,4},{28,0},{1,29},{... | collective-permute-start | bytes 393224 | tf_op jit(solution)/shard_map/ppermute | solution.py:44
  11.9 9.5 %collective-permute-start.3 = (bf16[128,512]{1,0:T(8,128)(2,1)S(1)}, bf16[128,512]{1,0:T(8,128)(2,1)S(1)}, u32[]{:S(2)}, u32[]{:S(2)}) collective-permute-start(bf16[128,512]{1,0:T(8,128)(2,1)S(1)} %get-tuple-element.25), channel_id=1, source_target_pairs={{0,12},{4,8},{8,4},{12,0},{16,28},{20,24},{24,20},{28,16},{1,13},{... | collective-permute-start | bytes 393224 | tf_op jit(solution)/shard_map/ppermute | solution.py:44
  11.9 17.8 %collective-permute-start.4 = (bf16[128,512]{1,0:T(8,128)(2,1)}, bf16[128,512]{1,0:T(8,128)(2,1)S(1)}, u32[]{:S(2)}, u32[]{:S(2)}) collective-permute-start(bf16[128,512]{1,0:T(8,128)(2,1)} %get-tuple-element.26), channel_id=1, source_target_pairs={{0,24},{4,28},{8,16},{12,20},{16,8},{20,12},{24,0},{28,4},{1,25},{... | collective-permute-start | bytes 393224 | tf_op jit(solution)/shard_map/ppermute | solution.py:44
  16.5 16.1 %collective-permute-start.5 = (bf16[128,512]{1,0:T(8,128)(2,1)}, bf16[128,512]{1,0:T(8,128)(2,1)}, u32[]{:S(2)}, u32[]{:S(2)}) collective-permute-start(bf16[128,512]{1,0:T(8,128)(2,1)} %get-tuple-element.27), channel_id=1, source_target_pairs={{0,20},{4,16},{8,28},{12,24},{16,4},{20,0},{24,12},{28,8},{1,21},{... | collective-permute-start | bytes 393224 | tf_op jit(solution)/shard_map/ppermute | solution.py:44
  21.4 11.2 %collective-permute-start.6 = (bf16[128,512]{1,0:T(8,128)(2,1)S(1)}, bf16[128,512]{1,0:T(8,128)(2,1)}, u32[]{:S(2)}, u32[]{:S(2)}) collective-permute-start(bf16[128,512]{1,0:T(8,128)(2,1)S(1)} %get-tuple-element.28), channel_id=1, source_target_pairs={{0,8},{4,12},{8,0},{12,4},{16,24},{20,28},{24,16},{28,20},{1,9},{5... | collective-permute-start | bytes 393224 | tf_op jit(solution)/shard_map/ppermute | solution.py:44
  21.6 11.0 %collective-permute-start.7 = (bf16[128,512]{1,0:T(8,128)(2,1)S(1)}, bf16[128,512]{1,0:T(8,128)(2,1)}, u32[]{:S(2)}, u32[]{:S(2)}) collective-permute-start(bf16[128,512]{1,0:T(8,128)(2,1)S(1)} %get-tuple-element.29), channel_id=1, source_target_pairs={{0,4},{4,0},{8,12},{12,8},{16,20},{20,16},{24,28},{28,24},{1,5},{5... | collective-permute-start | bytes 393224 | tf_op jit(solution)/shard_map/ppermute | solution.py:44
  23.3 11.7 %collective-permute-start.8 = (bf16[128,512]{1,0:T(8,128)(2,1)S(1)}, bf16[128,512]{1,0:T(8,128)(2,1)S(1)}, u32[]{:S(2)}, u32[]{:S(2)}) collective-permute-start(bf16[128,512]{1,0:T(8,128)(2,1)S(1)} %get-tuple-element.32), channel_id=1, source_target_pairs={{0,16},{4,20},{8,24},{12,28},{16,0},{20,4},{24,8},{28,12},{1,17},{... | collective-permute-start | bytes 393224 | tf_op jit(solution)/shard_map/ppermute | solution.py:44
  25.1 1.3 %copy-start = (bf16[1,1,5,128,1024]{4,3,2,1,0:T(8,128)(2,1)S(1)}, bf16[1,1,5,128,1024]{4,3,2,1,0:T(8,128)(2,1)}, u32[]{:S(2)}) copy-start(bf16[1,1,5,128,1024]{4,3,2,1,0:T(8,128)(2,1)} %param.6) | copy-start | bytes 3932164
  26.4 0.7 %copy-start.2 = (s32[1,1,3]{2,1,0:T(1,128)S(1)}, s32[1,1,3]{2,1,0:T(1,128)}, u32[]{:S(2)}) copy-start(s32[1,1,3]{2,1,0:T(1,128)} %ids_hbm.1) | copy-start | bytes 40
  27.1 0.7 %copy-start.3 = (s32[1,1,3]{2,1,0:T(1,128)S(1)}, s32[1,1,3]{2,1,0:T(1,128)}, u32[]{:S(2)}) copy-start(s32[1,1,3]{2,1,0:T(1,128)} %src_hbm.1) | copy-start | bytes 40
  36.7 9.3 %collective-permute-start.9 = (bf16[128,512]{1,0:T(8,128)(2,1)S(1)}, bf16[128,512]{1,0:T(8,128)(2,1)S(1)}, u32[]{:S(2)}, u32[]{:S(2)}) collective-permute-start(bf16[128,512]{1,0:T(8,128)(2,1)S(1)} %get-tuple-element.33), channel_id=1, source_target_pairs={{0,28},{4,24},{8,20},{12,16},{16,12},{20,8},{24,4},{28,0},{1,29},{... | collective-permute-start | bytes 393224 | tf_op jit(solution)/shard_map/ppermute | solution.py:44
  40.0 11.2 %collective-permute-start.10 = (bf16[128,512]{1,0:T(8,128)(2,1)S(1)}, bf16[128,512]{1,0:T(8,128)(2,1)S(1)}, u32[]{:S(2)}, u32[]{:S(2)}) collective-permute-start(bf16[128,512]{1,0:T(8,128)(2,1)S(1)} %get-tuple-element.34), channel_id=1, source_target_pairs={{0,12},{4,8},{8,4},{12,0},{16,28},{20,24},{24,20},{28,16},{1,13},{... | collective-permute-start | bytes 393224 | tf_op jit(solution)/shard_map/ppermute | solution.py:44
  40.0 11.7 %collective-permute-start.11 = (bf16[128,512]{1,0:T(8,128)(2,1)S(1)}, bf16[128,512]{1,0:T(8,128)(2,1)S(1)}, u32[]{:S(2)}, u32[]{:S(2)}) collective-permute-start(bf16[128,512]{1,0:T(8,128)(2,1)S(1)} %get-tuple-element.35), channel_id=1, source_target_pairs={{0,24},{4,28},{8,16},{12,20},{16,8},{20,12},{24,0},{28,4},{1,25},{... | collective-permute-start | bytes 393224 | tf_op jit(solution)/shard_map/ppermute | solution.py:44
  41.5 11.1 %collective-permute-start.12 = (bf16[128,512]{1,0:T(8,128)(2,1)S(1)}, bf16[128,512]{1,0:T(8,128)(2,1)S(1)}, u32[]{:S(2)}, u32[]{:S(2)}) collective-permute-start(bf16[128,512]{1,0:T(8,128)(2,1)S(1)} %get-tuple-element.36), channel_id=1, source_target_pairs={{0,8},{4,12},{8,0},{12,4},{16,24},{20,28},{24,16},{28,20},{1,9},{5... | collective-permute-start | bytes 393224 | tf_op jit(solution)/shard_map/ppermute | solution.py:44
  42.7 16.6 %collective-permute-start.13 = (bf16[128,512]{1,0:T(8,128)(2,1)S(1)}, bf16[128,512]{1,0:T(8,128)(2,1)S(1)}, u32[]{:S(2)}, u32[]{:S(2)}) collective-permute-start(bf16[128,512]{1,0:T(8,128)(2,1)S(1)} %get-tuple-element.37), channel_id=1, source_target_pairs={{0,20},{4,16},{8,28},{12,24},{16,4},{20,0},{24,12},{28,8},{1,21},{... | collective-permute-start | bytes 393224 | tf_op jit(solution)/shard_map/ppermute | solution.py:44
  46.1 13.2 %collective-permute-start.14 = (bf16[128,512]{1,0:T(8,128)(2,1)S(1)}, bf16[128,512]{1,0:T(8,128)(2,1)S(1)}, u32[]{:S(2)}, u32[]{:S(2)}) collective-permute-start(bf16[128,512]{1,0:T(8,128)(2,1)S(1)} %get-tuple-element.38), channel_id=1, source_target_pairs={{0,4},{4,0},{8,12},{12,8},{16,20},{20,16},{24,28},{28,24},{1,5},{5... | collective-permute-start | bytes 393224 | tf_op jit(solution)/shard_map/ppermute | solution.py:44
  51.2 9.5 %collective-permute-start.15 = (bf16[128,512]{1,0:T(8,128)(2,1)S(1)}, bf16[128,512]{1,0:T(8,128)(2,1)S(1)}, u32[]{:S(2)}, u32[]{:S(2)}) collective-permute-start(bf16[128,512]{1,0:T(8,128)(2,1)S(1)} %get-tuple-element.39), channel_id=1, source_target_pairs={{0,16},{4,20},{8,24},{12,28},{16,0},{20,4},{24,8},{28,12},{1,17},{... | collective-permute-start | bytes 393224 | tf_op jit(solution)/shard_map/ppermute | solution.py:44

commit v8 on v7

--- a/solution.py
+++ b/solution.py
@@ -14,7 +14,7 @@
     return min(rows, max(16, 256 // patches))
 
 
-PARTS = 8
+PARTS = 4
 
 
 def is_late(k, count):
@@ -31,10 +31,8 @@
 
 
 def inward(count):
-    order = [k for k in partners(count) if not is_late(k, count)]
-    last_far = order.index(min(k for k in order if k >= count // 2))
-    order.insert(min(3, last_far), order.pop(last_far))
-    return order + [k for k in partners(count) if is_late(k, count)]
+    order = partners(count)
+    return [k for k in order if not is_late(k, count)] + [k for k in order if is_late(k, count)]
 
 
 def ppermute(value, axis, step):
@@ -63,7 +61,7 @@
 
 def merge_kernel(order, me_ref, *refs):
     patches = len(order)
-    piece_refs, out_ref = dict(zip(order, refs)), refs[-1]
+    piece_refs, (out_ref, whole, sem) = dict(zip(order, refs)), refs[patches:]
     rows = piece_refs[0].shape[0]
     group = rows_per_group(rows, patches)
     height = group * patches
@@ -71,11 +69,17 @@
     column = lax.broadcasted_iota(jnp.int32, (height, height), 1)
     source = (lax.rem(row, patches) ^ me_ref[0]) * group + lax.div(row, patches)
     shuffle = jnp.where(column == source, 1.0, 0.0).astype(jnp.bfloat16)
+    copies = []
     for step in range(rows // group):
         here = slice(step * group, (step + 1) * group)
         block = jnp.concatenate([piece_refs[k][here, :] for k in range(patches)], axis=0)
         moved = jnp.dot(shuffle, block, preferred_element_type=jnp.float32)
-        out_ref[step * height : (step + 1) * height, :] = moved.astype(jnp.bfloat16)
+        there = pl.ds(step * height, height)
+        whole[there, :] = moved.astype(jnp.bfloat16)
+        copies.append(pltpu.make_async_copy(whole.at[there, :], out_ref.at[there, :], sem.at[step]))
+        copies[-1].start()
+    for copy in copies:
+        copy.wait()
 
 
 def gram_kernel(
@@ -276,11 +280,16 @@
     order = back
     returned = [ppermute(piece, "member", k) for k, piece in zip(back, moved)]
 
+    steps = rows // rows_per_group(rows, patches)
     fresh = pl.pallas_call(
         functools.partial(merge_kernel, order),
         out_shape=jax.ShapeDtypeStruct((rows * patches, values), jnp.bfloat16),
         in_specs=[smem] + [vmem()] * patches,
-        out_specs=vmem(),
+        out_specs=pl.BlockSpec(memory_space=pl.ANY),
+        scratch_shapes=[
+            pltpu.VMEM((rows * patches, values), jnp.bfloat16),
+            pltpu.SemaphoreType.DMA((steps,)),
+        ],
         compiler_params=params(),
         cost_estimate=cost(2 * 256 * rows * patches * values, 4 * rows * patches * values),
         name="merge",

time: 62.4 us -> 65.2 us (1.045)
  waiting for transfers between devices: 22.1 us -> 25.5 us
    ppermute x14, waiting for transfers between devices: 22.1 us -> 25.5 us  [ppermute(): return lax.ppermute(value, axis, [(i, i ^ step) for i in range(count)])]
  transfers between devices with their start and end apart: 16 -> 16, of which waited for: 9 -> 9; matrix products, arithmetic and copies ran while one was open for 0% -> 0% of each run, Pallas kernels for 9% -> 8%
where the time goes in v8:
time: 65.2 us; the launch traced here: 65 us
  starting transfers between devices  26.3 us (40%)
  waiting for transfers between devices  25.5 us (39%)
  Pallas kernels  8.57 us (13%)
  local copies, waits for them, and re-layouts  3.85 us (6%)
  between operations  0.75 us (1%)
    ppermute x14, waiting for transfers between devices, ppermute(): return lax.ppermute(value, axis, [(i, i ^ step) for i in range(count)])  25.5 us
    ppermute x14, starting transfers between devices, ppermute(): return lax.ppermute(value, axis, [(i, i ^ step) for i in range(count)])  21.3 us
    ppermute x2, starting transfers between devices, swap(): return lax.ppermute(store, 'region', pairs + [(j, i) for i, j in pairs])  5.05 us
    unnamed x8, local copies, waits for them, and re-layouts  3.85 us
    pallas_call x1, Pallas kernels, shards(): pl.pallas_call(functools.partial(early_kernel, early), out_shape=[jax.Sha...  2.35 us
    pallas_call x1, Pallas kernels, shards(): pl.pallas_call(functools.partial(gram_kernel, 1.0 / (2.0 * size)), out_sh...  2.03 us
    pallas_call x1, Pallas kernels, shards(): pl.pallas_call(functools.partial(late_kernel, late, back), out_shape=[pie...  1.88 us
  transfers between devices with their start and end apart: 16, of which 9 were waited for; matrix products, arithmetic and copies ran while one was open for 0% of the time, Pallas kernels for 8%

profile of v8, /device:TPU:0, one launch (start us, length us, event | category | flops | bytes accessed | tf_op | source)
XLA Modules:
  0.0 65.0 jit_solution(16758089509806613864)
XLA Ops:
  0.7 4.3 %collective-permute-start = (bf16[5,128,1024]{2,1,0:T(8,128)(2,1)}, bf16[5,128,1024]{2,1,0:T(8,128)(2,1)S(1)}, u32[]{:S(2)}, u32[]{:S(2)}) collective-permute-start(bf16[5,128,1024]{2,1,0:T(8,128)(2,1)} %bitcast.8), channel_id=1, source_target_pairs={{0,1},{2,3},{1,0},{3,2},{4,5},{6,7},{5,4},{7,6},{8,9},{10,11},{9,8... | collective-permute-start | bytes 3932168 | tf_op jit(solution)/shard_map/ppermute | solution.py:208
  5.1 1.2 %copy-done.1 = bf16[128,1,8,512]{3,2,1,0:T(8,128)(2,1)S(1)} copy-done((bf16[128,1,8,512]{3,2,1,0:T(8,128)(2,1)S(1)}, bf16[128,1,8,512]{3,2,1,0:T(8,128)(2,1)}, u32[]{:S(2)}) %copy-start.1) | copy-done | bytes 1048600
  6.3 1.1 %split.1 = (bf16[128,512]{1,0:T(8,128)(2,1)S(1)}, bf16[128,512]{1,0:T(8,128)(2,1)S(1)}, bf16[128,512]{1,0:T(8,128)(2,1)S(1)}, bf16[128,512]{1,0:T(8,128)(2,1)}, ...) custom-call(s32[1]{0:T(128)} %bitcast.me_ref, ...), custom_call_target="tpu_custom_call" | custom-call | flops 268435456 | bytes 2097152 | tf_op jit(solution)/shard_map/split/pallas_call | solution.py:224
  7.4 4.5 %collective-permute-start.2 = (bf16[128,512]{1,0:T(8,128)(2,1)S(1)}, bf16[128,512]{1,0:T(8,128)(2,1)S(1)}, u32[]{:S(2)}, u32[]{:S(2)}) collective-permute-start(bf16[128,512]{1,0:T(8,128)(2,1)S(1)} %get-tuple-element.24), channel_id=1, source_target_pairs={{0,28},{4,24},{8,20},{12,16},{16,12},{20,8},{24,4},{28,0},{1,29},{... | collective-permute-start | bytes 393224 | tf_op jit(solution)/shard_map/ppermute | solution.py:42
  12.8 3.7 %collective-permute-done.2.refs_1_ = bf16[128,512]{1,0:T(8,128)(2,1)S(1)} collective-permute-done((bf16[128,512]{1,0:T(8,128)(2,1)S(1)}, bf16[128,512]{1,0:T(8,128)(2,1)S(1)}, u32[]{:S(2)}, u32[]{:S(2)}) %collective-permute-start.2) | collective-permute-done | bytes 131104 | tf_op jit(solution)/shard_map/ppermute | solution.py:42
  16.5 3.5 %collective-permute-start.5 = (bf16[128,512]{1,0:T(8,128)(2,1)S(1)}, bf16[128,512]{1,0:T(8,128)(2,1)}, u32[]{:S(2)}, u32[]{:S(2)}) collective-permute-start(bf16[128,512]{1,0:T(8,128)(2,1)S(1)} %get-tuple-element.27), channel_id=1, source_target_pairs={{0,8},{4,12},{8,0},{12,4},{16,24},{20,28},{24,16},{28,20},{1,9},{5... | collective-permute-start | bytes 393224 | tf_op jit(solution)/shard_map/ppermute | solution.py:42
  19.9 1.1 %collective-permute-done.3.refs_2_ = bf16[128,512]{1,0:T(8,128)(2,1)S(1)} collective-permute-done((bf16[128,512]{1,0:T(8,128)(2,1)S(1)}, bf16[128,512]{1,0:T(8,128)(2,1)S(1)}, u32[]{:S(2)}, u32[]{:S(2)}) %collective-permute-start.3) | collective-permute-done | bytes 131104 | tf_op jit(solution)/shard_map/ppermute | solution.py:42
  21.1 1.4 %collective-permute-start.6 = (bf16[128,512]{1,0:T(8,128)(2,1)S(1)}, bf16[128,512]{1,0:T(8,128)(2,1)}, u32[]{:S(2)}, u32[]{:S(2)}) collective-permute-start(bf16[128,512]{1,0:T(8,128)(2,1)S(1)} %get-tuple-element.28), channel_id=1, source_target_pairs={{0,4},{4,0},{8,12},{12,8},{16,20},{20,16},{24,28},{28,24},{1,5},{5... | collective-permute-start | bytes 393224 | tf_op jit(solution)/shard_map/ppermute | solution.py:42
  23.2 3.0 %collective-permute-start.8 = (bf16[128,512]{1,0:T(8,128)(2,1)S(1)}, bf16[128,512]{1,0:T(8,128)(2,1)S(1)}, u32[]{:S(2)}, u32[]{:S(2)}) collective-permute-start(bf16[128,512]{1,0:T(8,128)(2,1)S(1)} %get-tuple-element.32), channel_id=1, source_target_pairs={{0,16},{4,20},{8,24},{12,28},{16,0},{20,4},{24,8},{28,12},{1,17},{... | collective-permute-start | bytes 393224 | tf_op jit(solution)/shard_map/ppermute | solution.py:42
  26.2 1.3 %copy-done = bf16[1,1,5,128,1024]{4,3,2,1,0:T(8,128)(2,1)S(1)} copy-done((bf16[1,1,5,128,1024]{4,3,2,1,0:T(8,128)(2,1)S(1)}, bf16[1,1,5,128,1024]{4,3,2,1,0:T(8,128)(2,1)}, u32[]{:S(2)}) %copy-start) | copy-done | bytes 1310744
  28.8 2.0 %gram.1.gram_ref = bf16[1024,1024]{1,0:T(8,128)(2,1)S(1)} custom-call(s32[1]{0:T(128)} %bitcast.1.region_ref, s32[1,1,3]{2,1,0:T(1,128)S(1)} %copy-done.2, s32[1,1,3]{2,1,0:T(1,128)S(1)} %copy-done.3, s32[1,1]{1,0:T(1,128)S(6)} %copy.7.count_hbm, bf16[5,128,1024]{2,1,0:T(8,128)(2,1)S(1)} %bitcast.9, bf16[5,128,1024]{2,1,0:T(8,128)(2,1)S(1)} %collective-permute-done.even, ...), custom_call_target="tpu_custom_call" | custom-call | flops 805306368 | bytes 4194304 | tf_op jit(solution)/shard_map/gram/pallas_call | solution.py:235
  30.9 2.3 %early.1 = (f32[1024,512]{1,0:T(8,128)S(1)}, bf16[1024,512]{1,0:T(8,128)(2,1)S(1)}) custom-call(s32[1]{0:T(128)} %bitcast.me_ref, bf16[1024,1024]{1,0:T(8,128)(2,1)S(1)} %gram.1.gram_ref, bf16[128,512]{1,0:T(8,128)(2,1)S(1)} %get-tuple-element.23.refs_0_, bf16[128,512]{1,0:T(8,128)(2,1)S(1)} %collective-permute-done.2.refs_1_, ...), custom_call_target="tpu_custom_call" | custom-call | flops 1073741824 | bytes 6291456 | tf_op jit(solution)/shard_map/early/pallas_call | solution.py:256
  33.3 1.8 %collective-permute-done.7.refs_0_ = bf16[128,512]{1,0:T(8,128)(2,1)S(1)} collective-permute-done((bf16[128,512]{1,0:T(8,128)(2,1)S(1)}, bf16[128,512]{1,0:T(8,128)(2,1)S(1)}, u32[]{:S(2)}, u32[]{:S(2)}) %collective-permute-start.7) | collective-permute-done | bytes 131104 | tf_op jit(solution)/shard_map/ppermute | solution.py:42
  35.1 1.4 %collective-permute-done.8.refs_1_ = bf16[128,512]{1,0:T(8,128)(2,1)S(1)} collective-permute-done((bf16[128,512]{1,0:T(8,128)(2,1)S(1)}, bf16[128,512]{1,0:T(8,128)(2,1)S(1)}, u32[]{:S(2)}, u32[]{:S(2)}) %collective-permute-start.8) | collective-permute-done | bytes 131104 | tf_op jit(solution)/shard_map/ppermute | solution.py:42
  36.5 1.9 %late.1 = (bf16[128,512]{1,0:T(8,128)(2,1)S(1)}, bf16[128,512]{1,0:T(8,128)(2,1)S(1)}, bf16[128,512]{1,0:T(8,128)(2,1)S(1)}, bf16[128,512]{1,0:T(8,128)(2,1)S(1)...) custom-call(s32[1]{0:T(128)} %bitcast.me_ref, ...), custom_call_target="tpu_custom_call" | custom-call | flops 1610612736 | bytes 7340032 | tf_op jit(solution)/shard_map/late/pallas_call | solution.py:266
  38.4 3.5 %collective-permute-start.9 = (bf16[128,512]{1,0:T(8,128)(2,1)S(1)}, bf16[128,512]{1,0:T(8,128)(2,1)S(1)}, u32[]{:S(2)}, u32[]{:S(2)}) collective-permute-start(bf16[128,512]{1,0:T(8,128)(2,1)S(1)} %get-tuple-element.33), channel_id=1, source_target_pairs={{0,28},{4,24},{8,20},{12,16},{16,12},{20,8},{24,4},{28,0},{1,29},{... | collective-permute-start | bytes 393224 | tf_op jit(solution)/shard_map/ppermute | solution.py:42
  42.3 2.1 %collective-permute-start.12 = (bf16[128,512]{1,0:T(8,128)(2,1)S(1)}, bf16[128,512]{1,0:T(8,128)(2,1)S(1)}, u32[]{:S(2)}, u32[]{:S(2)}) collective-permute-start(bf16[128,512]{1,0:T(8,128)(2,1)S(1)} %get-tuple-element.36), channel_id=1, source_target_pairs={{0,8},{4,12},{8,0},{12,4},{16,24},{20,28},{24,16},{28,20},{1,9},{5... | collective-permute-start | bytes 393224 | tf_op jit(solution)/shard_map/ppermute | solution.py:42
  44.3 2.0 %collective-permute-start.13 = (bf16[128,512]{1,0:T(8,128)(2,1)S(1)}, bf16[128,512]{1,0:T(8,128)(2,1)S(1)}, u32[]{:S(2)}, u32[]{:S(2)}) collective-permute-start(bf16[128,512]{1,0:T(8,128)(2,1)S(1)} %get-tuple-element.37), channel_id=1, source_target_pairs={{0,20},{4,16},{8,28},{12,24},{16,4},{20,0},{24,12},{28,8},{1,21},{... | collective-permute-start | bytes 393224 | tf_op jit(solution)/shard_map/ppermute | solution.py:42
  46.3 1.4 %collective-permute-done.9.refs_0_ = bf16[128,512]{1,0:T(8,128)(2,1)S(1)} collective-permute-done((bf16[128,512]{1,0:T(8,128)(2,1)S(1)}, bf16[128,512]{1,0:T(8,128)(2,1)S(1)}, u32[]{:S(2)}, u32[]{:S(2)}) %collective-permute-start.9) | collective-permute-done | bytes 131104 | tf_op jit(solution)/shard_map/ppermute | solution.py:42
  47.8 4.6 %collective-permute-done.10.refs_1_ = bf16[128,512]{1,0:T(8,128)(2,1)S(1)} collective-permute-done((bf16[128,512]{1,0:T(8,128)(2,1)S(1)}, bf16[128,512]{1,0:T(8,128)(2,1)S(1)}, u32[]{:S(2)}, u32[]{:S(2)}) %collective-permute-start.10) | collective-permute-done | bytes 131104 | tf_op jit(solution)/shard_map/ppermute | solution.py:42
  52.4 2.1 %collective-permute-done.12.refs_3_ = bf16[128,512]{1,0:T(8,128)(2,1)S(1)} collective-permute-done((bf16[128,512]{1,0:T(8,128)(2,1)S(1)}, bf16[128,512]{1,0:T(8,128)(2,1)S(1)}, u32[]{:S(2)}, u32[]{:S(2)}) %collective-permute-start.12) | collective-permute-done | bytes 131104 | tf_op jit(solution)/shard_map/ppermute | solution.py:42
  54.4 6.9 %collective-permute-done.13.refs_4_ = bf16[128,512]{1,0:T(8,128)(2,1)S(1)} collective-permute-done((bf16[128,512]{1,0:T(8,128)(2,1)S(1)}, bf16[128,512]{1,0:T(8,128)(2,1)S(1)}, u32[]{:S(2)}, u32[]{:S(2)}) %collective-permute-start.13) | collective-permute-done | bytes 131104 | tf_op jit(solution)/shard_map/ppermute | solution.py:42
  61.3 2.4 %collective-permute-done.15.refs_6_ = bf16[128,512]{1,0:T(8,128)(2,1)S(1)} collective-permute-done((bf16[128,512]{1,0:T(8,128)(2,1)S(1)}, bf16[128,512]{1,0:T(8,128)(2,1)S(1)}, u32[]{:S(2)}, u32[]{:S(2)}) %collective-permute-start.15) | collective-permute-done | bytes 131104 | tf_op jit(solution)/shard_map/ppermute | solution.py:42
  63.7 1.2 %merge.1 = bf16[1024,512]{1,0:T(8,128)(2,1)} custom-call(s32[1]{0:T(128)} %bitcast.me_ref, bf16[128,512]{1,0:T(8,128)(2,1)S(1)} %collective-permute-done.9.refs_0_, bf16[128,512]{1,0:T(8,128)(2,1)S(1)} %collective-permute-done.10.refs_1_, bf16[128,512]{1,0:T(8,128)(2,1)S(1)} %collective-permute-done.11.refs_2_, ...), custom_call_target="tpu_custom_call" | custom-call | flops 268435456 | bytes 2097152 | tf_op jit(solution)/shard_map/merge/pallas_call | solution.py:284
  (21 shorter events, 3.4 us)
Async XLA Ops:
  0.0 23.1 %collective-permute-start.1 = (bf16[5,128,1024]{2,1,0:T(8,128)(2,1)}, bf16[5,128,1024]{2,1,0:T(8,128)(2,1)S(1)}, u32[]{:S(2)}, u32[]{:S(2)}) collective-permute-start(bf16[5,128,1024]{2,1,0:T(8,128)(2,1)} %bitcast.7), channel_id=1, source_target_pairs={{1,2},{2,1},{5,6},{6,5},{9,10},{10,9},{13,14},{14,13},{17,18},{18,... | collective-permute-start | bytes 3932168 | tf_op jit(solution)/shard_map/ppermute | solution.py:208
  0.7 22.5 %collective-permute-start = (bf16[5,128,1024]{2,1,0:T(8,128)(2,1)}, bf16[5,128,1024]{2,1,0:T(8,128)(2,1)S(1)}, u32[]{:S(2)}, u32[]{:S(2)}) collective-permute-start(bf16[5,128,1024]{2,1,0:T(8,128)(2,1)} %bitcast.8), channel_id=1, source_target_pairs={{0,1},{2,3},{1,0},{3,2},{4,5},{6,7},{5,4},{7,6},{8,9},{10,11},{9,8... | collective-permute-start | bytes 3932168 | tf_op jit(solution)/shard_map/ppermute | solution.py:208
  5.1 1.2 %copy-start.1 = (bf16[128,1,8,512]{3,2,1,0:T(8,128)(2,1)S(1)}, bf16[128,1,8,512]{3,2,1,0:T(8,128)(2,1)}, u32[]{:S(2)}) copy-start(bf16[128,1,8,512]{3,2,1,0:T(8,128)(2,1)} %param.5) | copy-start | bytes 3145732
  7.4 9.1 %collective-permute-start.2 = (bf16[128,512]{1,0:T(8,128)(2,1)S(1)}, bf16[128,512]{1,0:T(8,128)(2,1)S(1)}, u32[]{:S(2)}, u32[]{:S(2)}) collective-permute-start(bf16[128,512]{1,0:T(8,128)(2,1)S(1)} %get-tuple-element.24), channel_id=1, source_target_pairs={{0,28},{4,24},{8,20},{12,16},{16,12},{20,8},{24,4},{28,0},{1,29},{... | collective-permute-start | bytes 393224 | tf_op jit(solution)/shard_map/ppermute | solution.py:42
  11.9 9.2 %collective-permute-start.3 = (bf16[128,512]{1,0:T(8,128)(2,1)S(1)}, bf16[128,512]{1,0:T(8,128)(2,1)S(1)}, u32[]{:S(2)}, u32[]{:S(2)}) collective-permute-start(bf16[128,512]{1,0:T(8,128)(2,1)S(1)} %get-tuple-element.25), channel_id=1, source_target_pairs={{0,12},{4,8},{8,4},{12,0},{16,28},{20,24},{24,20},{28,16},{1,13},{... | collective-permute-start | bytes 393224 | tf_op jit(solution)/shard_map/ppermute | solution.py:42
  11.9 19.0 %collective-permute-start.4 = (bf16[128,512]{1,0:T(8,128)(2,1)}, bf16[128,512]{1,0:T(8,128)(2,1)}, u32[]{:S(2)}, u32[]{:S(2)}) collective-permute-start(bf16[128,512]{1,0:T(8,128)(2,1)} %get-tuple-element.26), channel_id=1, source_target_pairs={{0,24},{4,28},{8,16},{12,20},{16,8},{20,12},{24,0},{28,4},{1,25},{... | collective-permute-start | bytes 393224 | tf_op jit(solution)/shard_map/ppermute | solution.py:42
  16.5 14.4 %collective-permute-start.5 = (bf16[128,512]{1,0:T(8,128)(2,1)S(1)}, bf16[128,512]{1,0:T(8,128)(2,1)}, u32[]{:S(2)}, u32[]{:S(2)}) collective-permute-start(bf16[128,512]{1,0:T(8,128)(2,1)S(1)} %get-tuple-element.27), channel_id=1, source_target_pairs={{0,8},{4,12},{8,0},{12,4},{16,24},{20,28},{24,16},{28,20},{1,9},{5... | collective-permute-start | bytes 393224 | tf_op jit(solution)/shard_map/ppermute | solution.py:42
  21.1 9.8 %collective-permute-start.6 = (bf16[128,512]{1,0:T(8,128)(2,1)S(1)}, bf16[128,512]{1,0:T(8,128)(2,1)}, u32[]{:S(2)}, u32[]{:S(2)}) collective-permute-start(bf16[128,512]{1,0:T(8,128)(2,1)S(1)} %get-tuple-element.28), channel_id=1, source_target_pairs={{0,4},{4,0},{8,12},{12,8},{16,20},{20,16},{24,28},{28,24},{1,5},{5... | collective-permute-start | bytes 393224 | tf_op jit(solution)/shard_map/ppermute | solution.py:42
  23.1 12.0 %collective-permute-start.7 = (bf16[128,512]{1,0:T(8,128)(2,1)S(1)}, bf16[128,512]{1,0:T(8,128)(2,1)S(1)}, u32[]{:S(2)}, u32[]{:S(2)}) collective-permute-start(bf16[128,512]{1,0:T(8,128)(2,1)S(1)} %get-tuple-element.31), channel_id=1, source_target_pairs={{0,20},{4,16},{8,28},{12,24},{16,4},{20,0},{24,12},{28,8},{1,21},{... | collective-permute-start | bytes 393224 | tf_op jit(solution)/shard_map/ppermute | solution.py:42
  23.2 13.3 %collective-permute-start.8 = (bf16[128,512]{1,0:T(8,128)(2,1)S(1)}, bf16[128,512]{1,0:T(8,128)(2,1)S(1)}, u32[]{:S(2)}, u32[]{:S(2)}) collective-permute-start(bf16[128,512]{1,0:T(8,128)(2,1)S(1)} %get-tuple-element.32), channel_id=1, source_target_pairs={{0,16},{4,20},{8,24},{12,28},{16,0},{20,4},{24,8},{28,12},{1,17},{... | collective-permute-start | bytes 393224 | tf_op jit(solution)/shard_map/ppermute | solution.py:42
  26.2 1.3 %copy-start = (bf16[1,1,5,128,1024]{4,3,2,1,0:T(8,128)(2,1)S(1)}, bf16[1,1,5,128,1024]{4,3,2,1,0:T(8,128)(2,1)}, u32[]{:S(2)}) copy-start(bf16[1,1,5,128,1024]{4,3,2,1,0:T(8,128)(2,1)} %param.6) | copy-start | bytes 3932164
  27.5 0.7 %copy-start.2 = (s32[1,1,3]{2,1,0:T(1,128)S(1)}, s32[1,1,3]{2,1,0:T(1,128)}, u32[]{:S(2)}) copy-start(s32[1,1,3]{2,1,0:T(1,128)} %ids_hbm.1) | copy-start | bytes 40
  28.2 0.7 %copy-start.3 = (s32[1,1,3]{2,1,0:T(1,128)S(1)}, s32[1,1,3]{2,1,0:T(1,128)}, u32[]{:S(2)}) copy-start(s32[1,1,3]{2,1,0:T(1,128)} %src_hbm.1) | copy-start | bytes 40
  38.4 9.3 %collective-permute-start.9 = (bf16[128,512]{1,0:T(8,128)(2,1)S(1)}, bf16[128,512]{1,0:T(8,128)(2,1)S(1)}, u32[]{:S(2)}, u32[]{:S(2)}) collective-permute-start(bf16[128,512]{1,0:T(8,128)(2,1)S(1)} %get-tuple-element.33), channel_id=1, source_target_pairs={{0,28},{4,24},{8,20},{12,16},{16,12},{20,8},{24,4},{28,0},{1,29},{... | collective-permute-start | bytes 393224 | tf_op jit(solution)/shard_map/ppermute | solution.py:42
  41.9 10.4 %collective-permute-start.10 = (bf16[128,512]{1,0:T(8,128)(2,1)S(1)}, bf16[128,512]{1,0:T(8,128)(2,1)S(1)}, u32[]{:S(2)}, u32[]{:S(2)}) collective-permute-start(bf16[128,512]{1,0:T(8,128)(2,1)S(1)} %get-tuple-element.34), channel_id=1, source_target_pairs={{0,12},{4,8},{8,4},{12,0},{16,28},{20,24},{24,20},{28,16},{1,13},{... | collective-permute-start | bytes 393224 | tf_op jit(solution)/shard_map/ppermute | solution.py:42
  41.9 10.4 %collective-permute-start.11 = (bf16[128,512]{1,0:T(8,128)(2,1)S(1)}, bf16[128,512]{1,0:T(8,128)(2,1)S(1)}, u32[]{:S(2)}, u32[]{:S(2)}) collective-permute-start(bf16[128,512]{1,0:T(8,128)(2,1)S(1)} %get-tuple-element.35), channel_id=1, source_target_pairs={{0,24},{4,28},{8,16},{12,20},{16,8},{20,12},{24,0},{28,4},{1,25},{... | collective-permute-start | bytes 393224 | tf_op jit(solution)/shard_map/ppermute | solution.py:42
  42.3 12.2 %collective-permute-start.12 = (bf16[128,512]{1,0:T(8,128)(2,1)S(1)}, bf16[128,512]{1,0:T(8,128)(2,1)S(1)}, u32[]{:S(2)}, u32[]{:S(2)}) collective-permute-start(bf16[128,512]{1,0:T(8,128)(2,1)S(1)} %get-tuple-element.36), channel_id=1, source_target_pairs={{0,8},{4,12},{8,0},{12,4},{16,24},{20,28},{24,16},{28,20},{1,9},{5... | collective-permute-start | bytes 393224 | tf_op jit(solution)/shard_map/ppermute | solution.py:42
  44.3 17.0 %collective-permute-start.13 = (bf16[128,512]{1,0:T(8,128)(2,1)S(1)}, bf16[128,512]{1,0:T(8,128)(2,1)S(1)}, u32[]{:S(2)}, u32[]{:S(2)}) collective-permute-start(bf16[128,512]{1,0:T(8,128)(2,1)S(1)} %get-tuple-element.37), channel_id=1, source_target_pairs={{0,20},{4,16},{8,28},{12,24},{16,4},{20,0},{24,12},{28,8},{1,21},{... | collective-permute-start | bytes 393224 | tf_op jit(solution)/shard_map/ppermute | solution.py:42
  47.7 13.6 %collective-permute-start.14 = (bf16[128,512]{1,0:T(8,128)(2,1)S(1)}, bf16[128,512]{1,0:T(8,128)(2,1)S(1)}, u32[]{:S(2)}, u32[]{:S(2)}) collective-permute-start(bf16[128,512]{1,0:T(8,128)(2,1)S(1)} %get-tuple-element.38), channel_id=1, source_target_pairs={{0,4},{4,0},{8,12},{12,8},{16,20},{20,16},{24,28},{28,24},{1,5},{5... | collective-permute-start | bytes 393224 | tf_op jit(solution)/shard_map/ppermute | solution.py:42
  52.4 11.4 %collective-permute-start.15 = (bf16[128,512]{1,0:T(8,128)(2,1)S(1)}, bf16[128,512]{1,0:T(8,128)(2,1)S(1)}, u32[]{:S(2)}, u32[]{:S(2)}) collective-permute-start(bf16[128,512]{1,0:T(8,128)(2,1)S(1)} %get-tuple-element.39), channel_id=1, source_target_pairs={{0,16},{4,20},{8,24},{12,28},{16,0},{20,4},{24,8},{28,12},{1,17},{... | collective-permute-start | bytes 393224 | tf_op jit(solution)/shard_map/ppermute | solution.py:42

commit v9 on v8

--- a/solution.py
+++ b/solution.py
@@ -82,35 +82,25 @@
         copy.wait()
 
 
-def gram_kernel(
-    scale, region_ref, ids_hbm, src_hbm, count_hbm, own, even, odd, gram_ref,
-    ids_ref, src_ref, count_ref, stacked, table_sem, sem,
-):
-    tables = [
-        pltpu.make_async_copy(hbm, smem, table_sem.at[i])
-        for i, (hbm, smem) in enumerate(
-            ((ids_hbm, ids_ref), (src_hbm, src_ref), (count_hbm, count_ref))
-        )
-    ]
-    for copy in tables:
-        copy.start()
-    for copy in tables:
-        copy.wait()
-    slots = ids_ref.shape[2]
-    rows = own.shape[1]
+def gram_kernel(scale, region_ref, table_ref, both, odd, gram_ref, stacked, sem):
+    slots = (table_ref.shape[0] - 1) // 2
+    rows = odd.shape[1]
     parity = lax.rem(region_ref[0], 2)
-    count = count_ref[0, 0]
+    count = table_ref[2 * slots]
     for slot in range(slots):
         live = slot < count
         target = stacked.at[pl.ds(slot * rows, rows), :]
-        source = src_ref[0, 0, slot]
-        where = jnp.where(source == 1, 0, jnp.where((source == 2) == (parity == 0), 1, 2))
-        for code, store in enumerate((own, even, odd)):
-
-            @pl.when(live & (where == code))
-            def _():
-                block = store.at[ids_ref[0, 0, slot]]
-                pltpu.make_async_copy(block, target, sem.at[slot]).start()
+        index, source = table_ref[slot], table_ref[slots + slot]
+        swapped = (source != 1) & ((source == 2) != (parity == 0))
+        member = jnp.where(source == 1, parity, 1 - parity)
+
+        @pl.when(live & jnp.logical_not(swapped))
+        def _():
+            pltpu.make_async_copy(both.at[member, index], target, sem.at[slot]).start()
+
+        @pl.when(live & swapped)
+        def _():
+            pltpu.make_async_copy(odd.at[index], target, sem.at[slot]).start()
 
         @pl.when(jnp.logical_not(live))
         def _():
@@ -121,7 +111,7 @@
         @pl.when(slot < count)
         def _():
             target = stacked.at[pl.ds(slot * rows, rows), :]
-            pltpu.make_async_copy(own.at[0], target, sem.at[slot]).wait()
+            pltpu.make_async_copy(odd.at[0], target, sem.at[slot]).wait()
 
     size = gram_ref.shape[0]
     part = min(size, 256)
@@ -202,10 +192,12 @@
     return pl.CostEstimate(flops=flops, bytes_accessed=nbytes, transcendentals=0)
 
 
-def swap(store, first):
+def halo(store):
     count = lax.axis_size("region")
-    pairs = [(i, i + 1) for i in range(first, count - 1, 2)]
-    return lax.ppermute(store, "region", pairs + [(j, i) for i, j in pairs])
+    groups = [[i, i + 1] for i in range(0, count, 2)]
+    both = lax.all_gather(store, "region", axis_index_groups=groups)
+    pairs = [(i, i + 1) for i in range(1, count - 1, 2)]
+    return both, lax.ppermute(store, "region", pairs + [(j, i) for i, j in pairs])
 
 
 def shards(ensemble, obs_store, block_ids, block_src, block_count):
@@ -219,7 +211,7 @@
     hbm = pl.BlockSpec(memory_space=pltpu.HBM)
     piece_shape = jax.ShapeDtypeStruct((rows, values), jnp.bfloat16)
 
-    odd, even = swap(store, 1), swap(store, 0)
+    both, odd = halo(store)
     steps = [0] + inward(patches)
     pieces = pl.pallas_call(
         functools.partial(split_kernel, steps),
@@ -232,23 +224,20 @@
     )(me, ensemble.reshape(rows * patches, values))
     arrived = {k: ppermute(piece, "member", k) for k, piece in zip(steps, pieces)}
 
+    table = jnp.concatenate([block_ids.ravel(), block_src.ravel(), block_count.ravel()])
     gram = pl.pallas_call(
         functools.partial(gram_kernel, 1.0 / (2.0 * size)),
         out_shape=jax.ShapeDtypeStruct((size, size), jnp.bfloat16),
-        in_specs=[smem] + [hbm] * 6,
+        in_specs=[smem] * 2 + [hbm] * 2,
         out_specs=vmem(),
         scratch_shapes=[
-            pltpu.SMEM(block_ids.shape, jnp.int32),
-            pltpu.SMEM(block_src.shape, jnp.int32),
-            pltpu.SMEM(block_count.shape, jnp.int32),
             pltpu.VMEM((slots * store.shape[1], size), jnp.bfloat16),
-            pltpu.SemaphoreType.DMA((3,)),
             pltpu.SemaphoreType.DMA((slots,)),
         ],
         compiler_params=params(),
         cost_estimate=cost(2 * slots * store.shape[1] * size * size, 4 * size * size),
         name="gram",
-    )(region, block_ids, block_src, block_count, store, even, odd)
+    )(region, table, both, odd)
 
     early = [k for k in steps if not is_late(k, patches)]
     late = [k for k in steps if is_late(k, patches)]

time: 65.2 us -> 74.5 us (1.14)
  between operations: 0.75 us -> 14.2 us
  starting transfers between devices: 26.3 us -> 21.7 us
  waiting for transfers between devices: 25.5 us -> 28.6 us
  Pallas kernels: 8.57 us -> 6.82 us
  local copies, waits for them, and re-layouts: 3.85 us -> 2.97 us
    ppermute x2 -> x1, starting transfers between devices: 5.05 us -> 0.74 us  [halo(): lax.ppermute(store, 'region', pairs + [(j, i) for i, j in pairs])]
    ppermute x14, waiting for transfers between devices: 25.5 us -> 27.9 us  [ppermute(): return lax.ppermute(value, axis, [(i, i ^ step) for i in range(count)])]
    pallas_call x1, Pallas kernels: 2.35 us -> 1.32 us  [shards(): pl.pallas_call(functools.partial(early_kernel, early), out_shape=[jax.Sha...]
    unnamed x8, local copies, waits for them, and re-layouts: 3.85 us -> 2.97 us
  transfers between devices with their start and end apart: 16 -> 16, of which waited for: 9 -> 8; matrix products, arithmetic and copies ran while one was open for 0% -> 0% of each run, Pallas kernels for 8% -> 5%
where the time goes in v9:
time: 74.5 us; the launch traced here: 74.3 us
  waiting for transfers between devices  28.6 us (38%)
  starting transfers between devices  21.7 us (29%)
  between operations  14.2 us (19%)
  Pallas kernels  6.82 us (9%)
  local copies, waits for them, and re-layouts  2.97 us (4%)
    ppermute x14, waiting for transfers between devices, ppermute(): return lax.ppermute(value, axis, [(i, i ^ step) for i in range(count)])  27.9 us
    ppermute x14, starting transfers between devices, ppermute(): return lax.ppermute(value, axis, [(i, i ^ step) for i in range(count)])  20.9 us
    unnamed x8, local copies, waits for them, and re-layouts  2.97 us
    pallas_call x1, Pallas kernels, shards(): pl.pallas_call(functools.partial(gram_kernel, 1.0 / (2.0 * size)), out_sh...  1.97 us
    pallas_call x1, Pallas kernels, shards(): pl.pallas_call(functools.partial(late_kernel, late, back), out_shape=[pie...  1.87 us
  transfers between devices with their start and end apart: 16, of which 8 were waited for; matrix products, arithmetic and copies ran while one was open for 0% of the time, Pallas kernels for 5%

profile of v9, /device:TPU:0, one launch (start us, length us, event | category | flops | bytes accessed | tf_op | source)
XLA Modules:
  0.0 74.3 jit_solution(8378108187578529368)
XLA Ops:
  7.3 0.7 %collective-permute-start = (bf16[5,128,1024]{2,1,0:T(8,128)(2,1)}, bf16[5,128,1024]{2,1,0:T(8,128)(2,1)S(1)}, u32[]{:S(2)}, u32[]{:S(2)}) collective-permute-start(bf16[5,128,1024]{2,1,0:T(8,128)(2,1)} %bitcast.14), channel_id=1, source_target_pairs={{1,2},{2,1},{5,6},{6,5},{9,10},{10,9},{13,14},{14,13},{17,18},{18,... | collective-permute-start | bytes 3932168 | tf_op jit(solution)/shard_map/ppermute | solution.py:200
  8.0 1.2 %copy-done.1 = bf16[128,1,8,512]{3,2,1,0:T(8,128)(2,1)S(1)} copy-done((bf16[128,1,8,512]{3,2,1,0:T(8,128)(2,1)S(1)}, bf16[128,1,8,512]{3,2,1,0:T(8,128)(2,1)}, u32[]{:S(2)}) %copy-start.1) | copy-done | bytes 1048600
  9.7 6.0 %collective-permute-start.1 = (bf16[128,512]{1,0:T(8,128)(2,1)S(1)}, bf16[128,512]{1,0:T(8,128)(2,1)S(1)}, u32[]{:S(2)}, u32[]{:S(2)}) collective-permute-start(bf16[128,512]{1,0:T(8,128)(2,1)S(1)} %get-tuple-element.24), channel_id=1, source_target_pairs={{0,28},{4,24},{8,20},{12,16},{16,12},{20,8},{24,4},{28,0},{1,29},{... | collective-permute-start | bytes 393224 | tf_op jit(solution)/shard_map/ppermute | solution.py:42
  15.7 0.9 %collective-permute-start.3 = (bf16[128,512]{1,0:T(8,128)(2,1)S(1)}, bf16[128,512]{1,0:T(8,128)(2,1)S(1)}, u32[]{:S(2)}, u32[]{:S(2)}) collective-permute-start(bf16[128,512]{1,0:T(8,128)(2,1)S(1)} %get-tuple-element.26), channel_id=1, source_target_pairs={{0,24},{4,28},{8,16},{12,20},{16,8},{20,12},{24,0},{28,4},{1,25},{... | collective-permute-start | bytes 393224 | tf_op jit(solution)/shard_map/ppermute | solution.py:42
  16.6 1.1 %collective-permute-start.4 = (bf16[128,512]{1,0:T(8,128)(2,1)S(1)}, bf16[128,512]{1,0:T(8,128)(2,1)S(1)}, u32[]{:S(2)}, u32[]{:S(2)}) collective-permute-start(bf16[128,512]{1,0:T(8,128)(2,1)S(1)} %get-tuple-element.27), channel_id=1, source_target_pairs={{0,8},{4,12},{8,0},{12,4},{16,24},{20,28},{24,16},{28,20},{1,9},{5... | collective-permute-start | bytes 393224 | tf_op jit(solution)/shard_map/ppermute | solution.py:42
  18.8 1.7 %collective-permute-start.5 = (bf16[128,512]{1,0:T(8,128)(2,1)S(1)}, bf16[128,512]{1,0:T(8,128)(2,1)S(1)}, u32[]{:S(2)}, u32[]{:S(2)}) collective-permute-start(bf16[128,512]{1,0:T(8,128)(2,1)S(1)} %get-tuple-element.28), channel_id=1, source_target_pairs={{0,4},{4,0},{8,12},{12,8},{16,20},{20,16},{24,28},{28,24},{1,5},{5... | collective-permute-start | bytes 393224 | tf_op jit(solution)/shard_map/ppermute | solution.py:42
  20.5 4.1 %collective-permute-done.2.refs_2_ = bf16[128,512]{1,0:T(8,128)(2,1)S(1)} collective-permute-done((bf16[128,512]{1,0:T(8,128)(2,1)S(1)}, bf16[128,512]{1,0:T(8,128)(2,1)S(1)}, u32[]{:S(2)}, u32[]{:S(2)}) %collective-permute-start.2) | collective-permute-done | bytes 131104 | tf_op jit(solution)/shard_map/ppermute | solution.py:42
  24.7 3.0 %collective-permute-start.7 = (bf16[128,512]{1,0:T(8,128)(2,1)S(1)}, bf16[128,512]{1,0:T(8,128)(2,1)S(1)}, u32[]{:S(2)}, u32[]{:S(2)}) collective-permute-start(bf16[128,512]{1,0:T(8,128)(2,1)S(1)} %get-tuple-element.32), channel_id=1, source_target_pairs={{0,16},{4,20},{8,24},{12,28},{16,0},{20,4},{24,8},{28,12},{1,17},{... | collective-permute-start | bytes 393224 | tf_op jit(solution)/shard_map/ppermute | solution.py:42
  27.7 1.7 %copy-done = bf16[2,1,5,128,1024]{4,3,2,1,0:T(8,128)(2,1)S(1)} copy-done((bf16[2,1,5,128,1024]{4,3,2,1,0:T(8,128)(2,1)S(1)}, bf16[2,1,5,128,1024]{4,3,2,1,0:T(8,128)(2,1)}, u32[]{:S(2)}) %copy-start) | copy-done | bytes 2621464
  29.4 2.0 %gram.1.gram_ref = bf16[1024,1024]{1,0:T(8,128)(2,1)S(1)} custom-call(s32[1]{0:T(128)} %bitcast.1.region_ref, s32[7]{0:T(128)S(1)} %pad_add_fusion.table_ref, bf16[2,5,128,1024]{3,2,1,0:T(8,128)(2,1)S(1)} %bitcast.12, bf16[5,128,1024]{2,1,0:T(8,128)(2,1)S(1)} %collective-permute-done.odd), custom_call_target="tpu_custom_call" | custom-call | flops 805306368 | bytes 4194304 | tf_op jit(solution)/shard_map/gram/pallas_call | solution.py:228
  31.4 1.3 %early.1 = (f32[1024,512]{1,0:T(8,128)S(1)}, bf16[1024,512]{1,0:T(8,128)(2,1)S(1)}) custom-call(s32[1]{0:T(128)} %bitcast.me_ref, bf16[1024,1024]{1,0:T(8,128)(2,1)S(1)} %gram.1.gram_ref, bf16[128,512]{1,0:T(8,128)(2,1)S(1)} %get-tuple-element.23.refs_0_, bf16[128,512]{1,0:T(8,128)(2,1)S(1)} %collective-permute-done.1.refs_1_, ...), custom_call_target="tpu_custom_call" | custom-call | flops 1073741824 | bytes 6291456 | tf_op jit(solution)/shard_map/early/pallas_call | solution.py:245
  32.7 4.6 %collective-permute-done.6.refs_0_ = bf16[128,512]{1,0:T(8,128)(2,1)S(1)} collective-permute-done((bf16[128,512]{1,0:T(8,128)(2,1)S(1)}, bf16[128,512]{1,0:T(8,128)(2,1)S(1)}, u32[]{:S(2)}, u32[]{:S(2)}) %collective-permute-start.6) | collective-permute-done | bytes 131104 | tf_op jit(solution)/shard_map/ppermute | solution.py:42
  37.3 2.2 %collective-permute-done.7.refs_1_ = bf16[128,512]{1,0:T(8,128)(2,1)S(1)} collective-permute-done((bf16[128,512]{1,0:T(8,128)(2,1)S(1)}, bf16[128,512]{1,0:T(8,128)(2,1)S(1)}, u32[]{:S(2)}, u32[]{:S(2)}) %collective-permute-start.7) | collective-permute-done | bytes 131104 | tf_op jit(solution)/shard_map/ppermute | solution.py:42
  39.5 1.9 %late.1 = (bf16[128,512]{1,0:T(8,128)(2,1)S(1)}, bf16[128,512]{1,0:T(8,128)(2,1)S(1)}, bf16[128,512]{1,0:T(8,128)(2,1)S(1)}, bf16[128,512]{1,0:T(8,128)(2,1)S(1)...) custom-call(s32[1]{0:T(128)} %bitcast.me_ref, ...), custom_call_target="tpu_custom_call" | custom-call | flops 1610612736 | bytes 7340032 | tf_op jit(solution)/shard_map/late/pallas_call | solution.py:255
  41.4 1.8 %collective-permute-start.8 = (bf16[128,512]{1,0:T(8,128)(2,1)S(1)}, bf16[128,512]{1,0:T(8,128)(2,1)S(1)}, u32[]{:S(2)}, u32[]{:S(2)}) collective-permute-start(bf16[128,512]{1,0:T(8,128)(2,1)S(1)} %get-tuple-element.33), channel_id=1, source_target_pairs={{0,28},{4,24},{8,20},{12,16},{16,12},{20,8},{24,4},{28,0},{1,29},{... | collective-permute-start | bytes 393224 | tf_op jit(solution)/shard_map/ppermute | solution.py:42
  43.2 2.7 %collective-permute-start.10 = (bf16[128,512]{1,0:T(8,128)(2,1)S(1)}, bf16[128,512]{1,0:T(8,128)(2,1)S(1)}, u32[]{:S(2)}, u32[]{:S(2)}) collective-permute-start(bf16[128,512]{1,0:T(8,128)(2,1)S(1)} %get-tuple-element.35), channel_id=1, source_target_pairs={{0,24},{4,28},{8,16},{12,20},{16,8},{20,12},{24,0},{28,4},{1,25},{... | collective-permute-start | bytes 393224 | tf_op jit(solution)/shard_map/ppermute | solution.py:42
  45.9 1.4 %collective-permute-start.11 = (bf16[128,512]{1,0:T(8,128)(2,1)S(1)}, bf16[128,512]{1,0:T(8,128)(2,1)S(1)}, u32[]{:S(2)}, u32[]{:S(2)}) collective-permute-start(bf16[128,512]{1,0:T(8,128)(2,1)S(1)} %get-tuple-element.36), channel_id=1, source_target_pairs={{0,8},{4,12},{8,0},{12,4},{16,24},{20,28},{24,16},{28,20},{1,9},{5... | collective-permute-start | bytes 393224 | tf_op jit(solution)/shard_map/ppermute | solution.py:42
  47.3 1.2 %collective-permute-start.12 = (bf16[128,512]{1,0:T(8,128)(2,1)S(1)}, bf16[128,512]{1,0:T(8,128)(2,1)S(1)}, u32[]{:S(2)}, u32[]{:S(2)}) collective-permute-start(bf16[128,512]{1,0:T(8,128)(2,1)S(1)} %get-tuple-element.37), channel_id=1, source_target_pairs={{0,20},{4,16},{8,28},{12,24},{16,4},{20,0},{24,12},{28,8},{1,21},{... | collective-permute-start | bytes 393224 | tf_op jit(solution)/shard_map/ppermute | solution.py:42
  48.5 2.1 %collective-permute-done.8.refs_0_ = bf16[128,512]{1,0:T(8,128)(2,1)S(1)} collective-permute-done((bf16[128,512]{1,0:T(8,128)(2,1)S(1)}, bf16[128,512]{1,0:T(8,128)(2,1)S(1)}, u32[]{:S(2)}, u32[]{:S(2)}) %collective-permute-start.8) | collective-permute-done | bytes 131104 | tf_op jit(solution)/shard_map/ppermute | solution.py:42
  50.6 1.1 %collective-permute-start.13 = (bf16[128,512]{1,0:T(8,128)(2,1)S(1)}, bf16[128,512]{1,0:T(8,128)(2,1)S(1)}, u32[]{:S(2)}, u32[]{:S(2)}) collective-permute-start(bf16[128,512]{1,0:T(8,128)(2,1)S(1)} %get-tuple-element.38), channel_id=1, source_target_pairs={{0,4},{4,0},{8,12},{12,8},{16,20},{20,16},{24,28},{28,24},{1,5},{5... | collective-permute-start | bytes 393224 | tf_op jit(solution)/shard_map/ppermute | solution.py:42
  51.7 5.8 %collective-permute-done.9.refs_1_ = bf16[128,512]{1,0:T(8,128)(2,1)S(1)} collective-permute-done((bf16[128,512]{1,0:T(8,128)(2,1)S(1)}, bf16[128,512]{1,0:T(8,128)(2,1)S(1)}, u32[]{:S(2)}, u32[]{:S(2)}) %collective-permute-start.9) | collective-permute-done | bytes 131104 | tf_op jit(solution)/shard_map/ppermute | solution.py:42
  57.5 3.3 %collective-permute-done.11.refs_3_ = bf16[128,512]{1,0:T(8,128)(2,1)S(1)} collective-permute-done((bf16[128,512]{1,0:T(8,128)(2,1)S(1)}, bf16[128,512]{1,0:T(8,128)(2,1)S(1)}, u32[]{:S(2)}, u32[]{:S(2)}) %collective-permute-start.11) | collective-permute-done | bytes 131104 | tf_op jit(solution)/shard_map/ppermute | solution.py:42
  60.8 5.5 %collective-permute-done.14.refs_6_ = bf16[128,512]{1,0:T(8,128)(2,1)S(1)} collective-permute-done((bf16[128,512]{1,0:T(8,128)(2,1)S(1)}, bf16[128,512]{1,0:T(8,128)(2,1)S(1)}, u32[]{:S(2)}, u32[]{:S(2)}) %collective-permute-start.14) | collective-permute-done | bytes 131104 | tf_op jit(solution)/shard_map/ppermute | solution.py:42
  66.2 1.2 %merge.1 = bf16[1024,512]{1,0:T(8,128)(2,1)} custom-call(s32[1]{0:T(128)} %bitcast.me_ref, bf16[128,512]{1,0:T(8,128)(2,1)S(1)} %collective-permute-done.8.refs_0_, bf16[128,512]{1,0:T(8,128)(2,1)S(1)} %collective-permute-done.9.refs_1_, bf16[128,512]{1,0:T(8,128)(2,1)S(1)} %collective-permute-done.10.refs_2_, ...), custom_call_target="tpu_custom_call" | custom-call | flops 268435456 | bytes 2097152 | tf_op jit(solution)/shard_map/merge/pallas_call | solution.py:273
  (23 shorter events, 1.7 us)
Async XLA Ops:
  6.5 13.9 %copy-start.2 = (s32[1,1,3]{2,1,0:T(1,128)S(1)}, s32[1,1,3]{2,1,0:T(1,128)}, u32[]{:S(2)}) copy-start(s32[1,1,3]{2,1,0:T(1,128)} %param.8) | copy-start | bytes 40
  6.5 13.9 %copy-start.3 = (s32[1,1,3]{2,1,0:T(1,128)S(1)}, s32[1,1,3]{2,1,0:T(1,128)}, u32[]{:S(2)}) copy-start(s32[1,1,3]{2,1,0:T(1,128)} %param.7) | copy-start | bytes 40
  6.5 21.1 %all-gather.3.cloned.1.call-start = ((), (), s32[]{:S(2)}) async-start(), calls=%async_computation | async-start | bytes 3932160 | tf_op jit(solution)/shard_map/all_gather | solution.py:198
  7.3 17.4 %collective-permute-start = (bf16[5,128,1024]{2,1,0:T(8,128)(2,1)}, bf16[5,128,1024]{2,1,0:T(8,128)(2,1)S(1)}, u32[]{:S(2)}, u32[]{:S(2)}) collective-permute-start(bf16[5,128,1024]{2,1,0:T(8,128)(2,1)} %bitcast.14), channel_id=1, source_target_pairs={{1,2},{2,1},{5,6},{6,5},{9,10},{10,9},{13,14},{14,13},{17,18},{18,... | collective-permute-start | bytes 3932168 | tf_op jit(solution)/shard_map/ppermute | solution.py:200
  8.0 1.2 %copy-start.1 = (bf16[128,1,8,512]{3,2,1,0:T(8,128)(2,1)S(1)}, bf16[128,1,8,512]{3,2,1,0:T(8,128)(2,1)}, u32[]{:S(2)}) copy-start(bf16[128,1,8,512]{3,2,1,0:T(8,128)(2,1)} %param.5) | copy-start | bytes 3145732
  9.7 9.1 %collective-permute-start.1 = (bf16[128,512]{1,0:T(8,128)(2,1)S(1)}, bf16[128,512]{1,0:T(8,128)(2,1)S(1)}, u32[]{:S(2)}, u32[]{:S(2)}) collective-permute-start(bf16[128,512]{1,0:T(8,128)(2,1)S(1)} %get-tuple-element.24), channel_id=1, source_target_pairs={{0,28},{4,24},{8,20},{12,16},{16,12},{20,8},{24,4},{28,0},{1,29},{... | collective-permute-start | bytes 393224 | tf_op jit(solution)/shard_map/ppermute | solution.py:42
  15.7 8.9 %collective-permute-start.2 = (bf16[128,512]{1,0:T(8,128)(2,1)S(1)}, bf16[128,512]{1,0:T(8,128)(2,1)S(1)}, u32[]{:S(2)}, u32[]{:S(2)}) collective-permute-start(bf16[128,512]{1,0:T(8,128)(2,1)S(1)} %get-tuple-element.25), channel_id=1, source_target_pairs={{0,12},{4,8},{8,4},{12,0},{16,28},{20,24},{24,20},{28,16},{1,13},{... | collective-permute-start | bytes 393224 | tf_op jit(solution)/shard_map/ppermute | solution.py:42
  15.7 15.7 %collective-permute-start.3 = (bf16[128,512]{1,0:T(8,128)(2,1)S(1)}, bf16[128,512]{1,0:T(8,128)(2,1)S(1)}, u32[]{:S(2)}, u32[]{:S(2)}) collective-permute-start(bf16[128,512]{1,0:T(8,128)(2,1)S(1)} %get-tuple-element.26), channel_id=1, source_target_pairs={{0,24},{4,28},{8,16},{12,20},{16,8},{20,12},{24,0},{28,4},{1,25},{... | collective-permute-start | bytes 393224 | tf_op jit(solution)/shard_map/ppermute | solution.py:42
  16.6 14.8 %collective-permute-start.4 = (bf16[128,512]{1,0:T(8,128)(2,1)S(1)}, bf16[128,512]{1,0:T(8,128)(2,1)S(1)}, u32[]{:S(2)}, u32[]{:S(2)}) collective-permute-start(bf16[128,512]{1,0:T(8,128)(2,1)S(1)} %get-tuple-element.27), channel_id=1, source_target_pairs={{0,8},{4,12},{8,0},{12,4},{16,24},{20,28},{24,16},{28,20},{1,9},{5... | collective-permute-start | bytes 393224 | tf_op jit(solution)/shard_map/ppermute | solution.py:42
  18.8 12.6 %collective-permute-start.5 = (bf16[128,512]{1,0:T(8,128)(2,1)S(1)}, bf16[128,512]{1,0:T(8,128)(2,1)S(1)}, u32[]{:S(2)}, u32[]{:S(2)}) collective-permute-start(bf16[128,512]{1,0:T(8,128)(2,1)S(1)} %get-tuple-element.28), channel_id=1, source_target_pairs={{0,4},{4,0},{8,12},{12,8},{16,20},{20,16},{24,28},{28,24},{1,5},{5... | collective-permute-start | bytes 393224 | tf_op jit(solution)/shard_map/ppermute | solution.py:42
  24.7 12.7 %collective-permute-start.6 = (bf16[128,512]{1,0:T(8,128)(2,1)S(1)}, bf16[128,512]{1,0:T(8,128)(2,1)S(1)}, u32[]{:S(2)}, u32[]{:S(2)}) collective-permute-start(bf16[128,512]{1,0:T(8,128)(2,1)S(1)} %get-tuple-element.31), channel_id=1, source_target_pairs={{0,20},{4,16},{8,28},{12,24},{16,4},{20,0},{24,12},{28,8},{1,21},{... | collective-permute-start | bytes 393224 | tf_op jit(solution)/shard_map/ppermute | solution.py:42
  24.7 14.9 %collective-permute-start.7 = (bf16[128,512]{1,0:T(8,128)(2,1)S(1)}, bf16[128,512]{1,0:T(8,128)(2,1)S(1)}, u32[]{:S(2)}, u32[]{:S(2)}) collective-permute-start(bf16[128,512]{1,0:T(8,128)(2,1)S(1)} %get-tuple-element.32), channel_id=1, source_target_pairs={{0,16},{4,20},{8,24},{12,28},{16,0},{20,4},{24,8},{28,12},{1,17},{... | collective-permute-start | bytes 393224 | tf_op jit(solution)/shard_map/ppermute | solution.py:42
  27.7 1.7 %copy-start = (bf16[2,1,5,128,1024]{4,3,2,1,0:T(8,128)(2,1)S(1)}, bf16[2,1,5,128,1024]{4,3,2,1,0:T(8,128)(2,1)}, u32[]{:S(2)}) copy-start(bf16[2,1,5,128,1024]{4,3,2,1,0:T(8,128)(2,1)} %all-gather.3.cloned.1.call-done) | copy-start | bytes 7864324
  41.4 9.2 %collective-permute-start.8 = (bf16[128,512]{1,0:T(8,128)(2,1)S(1)}, bf16[128,512]{1,0:T(8,128)(2,1)S(1)}, u32[]{:S(2)}, u32[]{:S(2)}) collective-permute-start(bf16[128,512]{1,0:T(8,128)(2,1)S(1)} %get-tuple-element.33), channel_id=1, source_target_pairs={{0,28},{4,24},{8,20},{12,16},{16,12},{20,8},{24,4},{28,0},{1,29},{... | collective-permute-start | bytes 393224 | tf_op jit(solution)/shard_map/ppermute | solution.py:42
  43.2 14.2 %collective-permute-start.9 = (bf16[128,512]{1,0:T(8,128)(2,1)S(1)}, bf16[128,512]{1,0:T(8,128)(2,1)S(1)}, u32[]{:S(2)}, u32[]{:S(2)}) collective-permute-start(bf16[128,512]{1,0:T(8,128)(2,1)S(1)} %get-tuple-element.34), channel_id=1, source_target_pairs={{0,12},{4,8},{8,4},{12,0},{16,28},{20,24},{24,20},{28,16},{1,13},{... | collective-permute-start | bytes 393224 | tf_op jit(solution)/shard_map/ppermute | solution.py:42
  43.2 14.3 %collective-permute-start.10 = (bf16[128,512]{1,0:T(8,128)(2,1)S(1)}, bf16[128,512]{1,0:T(8,128)(2,1)S(1)}, u32[]{:S(2)}, u32[]{:S(2)}) collective-permute-start(bf16[128,512]{1,0:T(8,128)(2,1)S(1)} %get-tuple-element.35), channel_id=1, source_target_pairs={{0,24},{4,28},{8,16},{12,20},{16,8},{20,12},{24,0},{28,4},{1,25},{... | collective-permute-start | bytes 393224 | tf_op jit(solution)/shard_map/ppermute | solution.py:42
  45.9 14.9 %collective-permute-start.11 = (bf16[128,512]{1,0:T(8,128)(2,1)S(1)}, bf16[128,512]{1,0:T(8,128)(2,1)S(1)}, u32[]{:S(2)}, u32[]{:S(2)}) collective-permute-start(bf16[128,512]{1,0:T(8,128)(2,1)S(1)} %get-tuple-element.36), channel_id=1, source_target_pairs={{0,8},{4,12},{8,0},{12,4},{16,24},{20,28},{24,16},{28,20},{1,9},{5... | collective-permute-start | bytes 393224 | tf_op jit(solution)/shard_map/ppermute | solution.py:42
  47.3 13.4 %collective-permute-start.12 = (bf16[128,512]{1,0:T(8,128)(2,1)S(1)}, bf16[128,512]{1,0:T(8,128)(2,1)S(1)}, u32[]{:S(2)}, u32[]{:S(2)}) collective-permute-start(bf16[128,512]{1,0:T(8,128)(2,1)S(1)} %get-tuple-element.37), channel_id=1, source_target_pairs={{0,20},{4,16},{8,28},{12,24},{16,4},{20,0},{24,12},{28,8},{1,21},{... | collective-permute-start | bytes 393224 | tf_op jit(solution)/shard_map/ppermute | solution.py:42
  50.6 10.2 %collective-permute-start.13 = (bf16[128,512]{1,0:T(8,128)(2,1)S(1)}, bf16[128,512]{1,0:T(8,128)(2,1)S(1)}, u32[]{:S(2)}, u32[]{:S(2)}) collective-permute-start(bf16[128,512]{1,0:T(8,128)(2,1)S(1)} %get-tuple-element.38), channel_id=1, source_target_pairs={{0,4},{4,0},{8,12},{12,8},{16,20},{20,16},{24,28},{28,24},{1,5},{5... | collective-permute-start | bytes 393224 | tf_op jit(solution)/shard_map/ppermute | solution.py:42
  57.5 8.8 %collective-permute-start.14 = (bf16[128,512]{1,0:T(8,128)(2,1)S(1)}, bf16[128,512]{1,0:T(8,128)(2,1)S(1)}, u32[]{:S(2)}, u32[]{:S(2)}) collective-permute-start(bf16[128,512]{1,0:T(8,128)(2,1)S(1)} %get-tuple-element.39), channel_id=1, source_target_pairs={{0,16},{4,20},{8,24},{12,28},{16,0},{20,4},{24,8},{28,12},{1,17},{... | collective-permute-start | bytes 393224 | tf_op jit(solution)/shard_map/ppermute | solution.py:42
Sparse Core Ops, SparseCore 0:
  8.9 14.0 all-gather.2

commit v10 on v9

--- a/solution.py
+++ b/solution.py
@@ -14,7 +14,7 @@
     return min(rows, max(16, 256 // patches))
 
 
-PARTS = 4
+PARTS = 8
 
 
 def is_late(k, count):
@@ -31,8 +31,10 @@
 
 
 def inward(count):
-    order = partners(count)
-    return [k for k in order if not is_late(k, count)] + [k for k in order if is_late(k, count)]
+    order = [k for k in partners(count) if not is_late(k, count)]
+    last_far = order.index(min(k for k in order if k >= count // 2))
+    order.insert(min(3, last_far), order.pop(last_far))
+    return order + [k for k in partners(count) if is_late(k, count)]
 
 
 def ppermute(value, axis, step):
@@ -82,25 +84,21 @@
         copy.wait()
 
 
-def gram_kernel(scale, region_ref, table_ref, both, odd, gram_ref, stacked, sem):
+def gram_kernel(scale, region_ref, table_ref, own, even, odd, gram_ref, stacked, sem):
     slots = (table_ref.shape[0] - 1) // 2
-    rows = odd.shape[1]
+    rows = own.shape[1]
     parity = lax.rem(region_ref[0], 2)
     count = table_ref[2 * slots]
     for slot in range(slots):
         live = slot < count
         target = stacked.at[pl.ds(slot * rows, rows), :]
         index, source = table_ref[slot], table_ref[slots + slot]
-        swapped = (source != 1) & ((source == 2) != (parity == 0))
-        member = jnp.where(source == 1, parity, 1 - parity)
-
-        @pl.when(live & jnp.logical_not(swapped))
-        def _():
-            pltpu.make_async_copy(both.at[member, index], target, sem.at[slot]).start()
-
-        @pl.when(live & swapped)
-        def _():
-            pltpu.make_async_copy(odd.at[index], target, sem.at[slot]).start()
+        where = jnp.where(source == 1, 0, jnp.where((source == 2) == (parity == 0), 1, 2))
+        for code, store in enumerate((own, even, odd)):
+
+            @pl.when(live & (where == code))
+            def _():
+                pltpu.make_async_copy(store.at[index], target, sem.at[slot]).start()
 
         @pl.when(jnp.logical_not(live))
         def _():
@@ -192,12 +190,10 @@
     return pl.CostEstimate(flops=flops, bytes_accessed=nbytes, transcendentals=0)
 
 
-def halo(store):
+def swap(store, first):
     count = lax.axis_size("region")
-    groups = [[i, i + 1] for i in range(0, count, 2)]
-    both = lax.all_gather(store, "region", axis_index_groups=groups)
-    pairs = [(i, i + 1) for i in range(1, count - 1, 2)]
-    return both, lax.ppermute(store, "region", pairs + [(j, i) for i, j in pairs])
+    pairs = [(i, i + 1) for i in range(first, count - 1, 2)]
+    return lax.ppermute(store, "region", pairs + [(j, i) for i, j in pairs])
 
 
 def shards(ensemble, obs_store, block_ids, block_src, block_count):
@@ -211,7 +207,7 @@
     hbm = pl.BlockSpec(memory_space=pltpu.HBM)
     piece_shape = jax.ShapeDtypeStruct((rows, values), jnp.bfloat16)
 
-    both, odd = halo(store)
+    odd, even = swap(store, 1), swap(store, 0)
     steps = [0] + inward(patches)
     pieces = pl.pallas_call(
         functools.partial(split_kernel, steps),
@@ -228,7 +224,7 @@
     gram = pl.pallas_call(
         functools.partial(gram_kernel, 1.0 / (2.0 * size)),
         out_shape=jax.ShapeDtypeStruct((size, size), jnp.bfloat16),
-        in_specs=[smem] * 2 + [hbm] * 2,
+        in_specs=[smem] * 2 + [hbm] * 3,
         out_specs=vmem(),
         scratch_shapes=[
             pltpu.VMEM((slots * store.shape[1], size), jnp.bfloat16),
@@ -237,7 +233,7 @@
         compiler_params=params(),
         cost_estimate=cost(2 * slots * store.shape[1] * size * size, 4 * size * size),
         name="gram",
-    )(region, table, both, odd)
+    )(region, table, store, even, odd)
 
     early = [k for k in steps if not is_late(k, patches)]
     late = [k for k in steps if is_late(k, patches)]

time: 74.5 us -> 62.2 us (0.83)
  between operations: 14.2 us -> 0.72 us
  waiting for transfers between devices: 28.6 us -> 22.8 us
  starting transfers between devices: 21.7 us -> 26.7 us
  Pallas kernels: 6.82 us -> 8.42 us
    ppermute x14, waiting for transfers between devices: 27.9 us -> 22.8 us  [ppermute(): return lax.ppermute(value, axis, [(i, i ^ step) for i in range(count)])]
    ppermute x1 -> x2, starting transfers between devices: 0.74 us -> 5.05 us  [swap(): return lax.ppermute(store, 'region', pairs + [(j, i) for i, j in pairs])]
    pallas_call x1, Pallas kernels: 1.32 us -> 2.34 us  [shards(): pl.pallas_call(functools.partial(early_kernel, early), out_shape=[jax.Sha...]
    ppermute x14, starting transfers between devices: 20.9 us -> 21.7 us  [ppermute(): return lax.ppermute(value, axis, [(i, i ^ step) for i in range(count)])]
    unnamed x8 -> x4, local copies, waits for them, and re-layouts: 2.97 us -> 2.54 us
  transfers between devices with their start and end apart: 16 -> 16, of which waited for: 8 -> 9; matrix products, arithmetic and copies ran while one was open for 0% -> 1% of each run, Pallas kernels for 5% -> 9%
where the time goes in v10:
time: 62.2 us; the launch traced here: 62 us
  starting transfers between devices  26.7 us (43%)
  waiting for transfers between devices  22.8 us (37%)
  Pallas kernels  8.42 us (14%)
  local copies, waits for them, and re-layouts  2.54 us (4%)
  other arithmetic  0.75 us (1%)
  between operations  0.72 us (1%)
    ppermute x14, waiting for transfers between devices, ppermute(): return lax.ppermute(value, axis, [(i, i ^ step) for i in range(count)])  22.8 us
    ppermute x14, starting transfers between devices, ppermute(): return lax.ppermute(value, axis, [(i, i ^ step) for i in range(count)])  21.7 us
    ppermute x2, starting transfers between devices, swap(): return lax.ppermute(store, 'region', pairs + [(j, i) for i, j in pairs])  5.05 us
    unnamed x4, local copies, waits for them, and re-layouts  2.54 us
    pallas_call x1, Pallas kernels, shards(): pl.pallas_call(functools.partial(early_kernel, early), out_shape=[jax.Sha...  2.34 us
    pallas_call x1, Pallas kernels, shards(): pl.pallas_call(functools.partial(gram_kernel, 1.0 / (2.0 * size)), out_sh...  1.98 us
    pallas_call x1, Pallas kernels, shards(): pl.pallas_call(functools.partial(late_kernel, late, back), out_shape=[pie...  1.75 us
  transfers between devices with their start and end apart: 16, of which 9 were waited for; matrix products, arithmetic and copies ran while one was open for 1% of the time, Pallas kernels for 9%

profile of v10, /device:TPU:0, one launch (start us, length us, event | category | flops | bytes accessed | tf_op | source)
XLA Modules:
  0.0 62.0 jit_solution(8165972002999319828)
XLA Ops:
  0.7 4.3 %collective-permute-start = (bf16[5,128,1024]{2,1,0:T(8,128)(2,1)}, bf16[5,128,1024]{2,1,0:T(8,128)(2,1)S(1)}, u32[]{:S(2)}, u32[]{:S(2)}) collective-permute-start(bf16[5,128,1024]{2,1,0:T(8,128)(2,1)} %bitcast.12), channel_id=1, source_target_pairs={{0,1},{2,3},{1,0},{3,2},{4,5},{6,7},{5,4},{7,6},{8,9},{10,11},{9,8... | collective-permute-start | bytes 3932168 | tf_op jit(solution)/shard_map/ppermute | solution.py:196
  5.1 1.2 %copy-done.1 = bf16[128,1,8,512]{3,2,1,0:T(8,128)(2,1)S(1)} copy-done((bf16[128,1,8,512]{3,2,1,0:T(8,128)(2,1)S(1)}, bf16[128,1,8,512]{3,2,1,0:T(8,128)(2,1)}, u32[]{:S(2)}) %copy-start.1) | copy-done | bytes 1048600
  6.3 1.1 %split.1 = (bf16[128,512]{1,0:T(8,128)(2,1)S(1)}, bf16[128,512]{1,0:T(8,128)(2,1)S(1)}, bf16[128,512]{1,0:T(8,128)(2,1)S(1)}, bf16[128,512]{1,0:T(8,128)(2,1)}, ...) custom-call(s32[1]{0:T(128)} %bitcast.me_ref, ...), custom_call_target="tpu_custom_call" | custom-call | flops 268435456 | bytes 2097152 | tf_op jit(solution)/shard_map/split/pallas_call | solution.py:212
  7.4 4.5 %collective-permute-start.2 = (bf16[128,512]{1,0:T(8,128)(2,1)S(1)}, bf16[128,512]{1,0:T(8,128)(2,1)S(1)}, u32[]{:S(2)}, u32[]{:S(2)}) collective-permute-start(bf16[128,512]{1,0:T(8,128)(2,1)S(1)} %get-tuple-element.24), channel_id=1, source_target_pairs={{0,28},{4,24},{8,20},{12,16},{16,12},{20,8},{24,4},{28,0},{1,29},{... | collective-permute-start | bytes 393224 | tf_op jit(solution)/shard_map/ppermute | solution.py:44
  13.5 3.0 %collective-permute-done.2.refs_1_ = bf16[128,512]{1,0:T(8,128)(2,1)S(1)} collective-permute-done((bf16[128,512]{1,0:T(8,128)(2,1)S(1)}, bf16[128,512]{1,0:T(8,128)(2,1)S(1)}, u32[]{:S(2)}, u32[]{:S(2)}) %collective-permute-start.2) | collective-permute-done | bytes 131104 | tf_op jit(solution)/shard_map/ppermute | solution.py:44
  16.5 4.3 %collective-permute-start.5 = (bf16[128,512]{1,0:T(8,128)(2,1)}, bf16[128,512]{1,0:T(8,128)(2,1)}, u32[]{:S(2)}, u32[]{:S(2)}) collective-permute-start(bf16[128,512]{1,0:T(8,128)(2,1)} %get-tuple-element.27), channel_id=1, source_target_pairs={{0,20},{4,16},{8,28},{12,24},{16,4},{20,0},{24,12},{28,8},{1,21},{... | collective-permute-start | bytes 393224 | tf_op jit(solution)/shard_map/ppermute | solution.py:44
  21.6 1.0 %collective-permute-start.7 = (bf16[128,512]{1,0:T(8,128)(2,1)S(1)}, bf16[128,512]{1,0:T(8,128)(2,1)}, u32[]{:S(2)}, u32[]{:S(2)}) collective-permute-start(bf16[128,512]{1,0:T(8,128)(2,1)S(1)} %get-tuple-element.29), channel_id=1, source_target_pairs={{0,4},{4,0},{8,12},{12,8},{16,20},{20,16},{24,28},{28,24},{1,5},{5... | collective-permute-start | bytes 393224 | tf_op jit(solution)/shard_map/ppermute | solution.py:44
  23.4 1.8 %collective-permute-start.8 = (bf16[128,512]{1,0:T(8,128)(2,1)S(1)}, bf16[128,512]{1,0:T(8,128)(2,1)S(1)}, u32[]{:S(2)}, u32[]{:S(2)}) collective-permute-start(bf16[128,512]{1,0:T(8,128)(2,1)S(1)} %get-tuple-element.32), channel_id=1, source_target_pairs={{0,16},{4,20},{8,24},{12,28},{16,0},{20,4},{24,8},{28,12},{1,17},{... | collective-permute-start | bytes 393224 | tf_op jit(solution)/shard_map/ppermute | solution.py:44
  25.1 1.3 %copy-done = bf16[1,1,5,128,1024]{4,3,2,1,0:T(8,128)(2,1)S(1)} copy-done((bf16[1,1,5,128,1024]{4,3,2,1,0:T(8,128)(2,1)S(1)}, bf16[1,1,5,128,1024]{4,3,2,1,0:T(8,128)(2,1)}, u32[]{:S(2)}) %copy-start) | copy-done | bytes 1310744
  26.5 2.0 %gram.1.gram_ref = bf16[1024,1024]{1,0:T(8,128)(2,1)S(1)} custom-call(s32[1]{0:T(128)} %bitcast.1.region_ref, s32[7]{0:T(128)S(1)} %pad_add_fusion.table_ref, bf16[5,128,1024]{2,1,0:T(8,128)(2,1)S(1)} %bitcast.13, bf16[5,128,1024]{2,1,0:T(8,128)(2,1)S(1)} %collective-permute-done.even, bf16[5,128,1024]{2,1,0:T(8,128)(2,1)S(1)} %collective-permute-done.1.odd), custom_call_target="tpu_custom_call" | custom-call | flops 805306368 | bytes 4194304 | tf_op jit(solution)/shard_map/gram/pallas_call | solution.py:224
  28.5 4.2 %collective-permute-done.5.refs_4_ = bf16[128,512]{1,0:T(8,128)(2,1)} collective-permute-done((bf16[128,512]{1,0:T(8,128)(2,1)}, bf16[128,512]{1,0:T(8,128)(2,1)}, u32[]{:S(2)}, u32[]{:S(2)}) %collective-permute-start.5) | collective-permute-done | bytes 131104 | tf_op jit(solution)/shard_map/ppermute | solution.py:44
  32.6 2.3 %early.1 = (f32[1024,512]{1,0:T(8,128)S(1)}, bf16[1024,512]{1,0:T(8,128)(2,1)S(1)}) custom-call(s32[1]{0:T(128)} %bitcast.me_ref, bf16[1024,1024]{1,0:T(8,128)(2,1)S(1)} %gram.1.gram_ref, bf16[128,512]{1,0:T(8,128)(2,1)S(1)} %get-tuple-element.23.refs_0_, bf16[128,512]{1,0:T(8,128)(2,1)S(1)} %collective-permute-done.2.refs_1_, ...), custom_call_target="tpu_custom_call" | custom-call | flops 1073741824 | bytes 6291456 | tf_op jit(solution)/shard_map/early/pallas_call | solution.py:241
  35.0 1.7 %late.1 = (bf16[128,512]{1,0:T(8,128)(2,1)S(1)}, bf16[128,512]{1,0:T(8,128)(2,1)S(1)}, bf16[128,512]{1,0:T(8,128)(2,1)S(1)}, bf16[128,512]{1,0:T(8,128)(2,1)S(1)...) custom-call(s32[1]{0:T(128)} %bitcast.me_ref, ...), custom_call_target="tpu_custom_call" | custom-call | flops 1610612736 | bytes 7340032 | tf_op jit(solution)/shard_map/late/pallas_call | solution.py:251
  36.7 3.3 %collective-permute-start.9 = (bf16[128,512]{1,0:T(8,128)(2,1)S(1)}, bf16[128,512]{1,0:T(8,128)(2,1)S(1)}, u32[]{:S(2)}, u32[]{:S(2)}) collective-permute-start(bf16[128,512]{1,0:T(8,128)(2,1)S(1)} %get-tuple-element.33), channel_id=1, source_target_pairs={{0,28},{4,24},{8,20},{12,16},{16,12},{20,8},{24,4},{28,0},{1,29},{... | collective-permute-start | bytes 393224 | tf_op jit(solution)/shard_map/ppermute | solution.py:44
  40.0 1.5 %collective-permute-start.11 = (bf16[128,512]{1,0:T(8,128)(2,1)S(1)}, bf16[128,512]{1,0:T(8,128)(2,1)S(1)}, u32[]{:S(2)}, u32[]{:S(2)}) collective-permute-start(bf16[128,512]{1,0:T(8,128)(2,1)S(1)} %get-tuple-element.35), channel_id=1, source_target_pairs={{0,24},{4,28},{8,16},{12,20},{16,8},{20,12},{24,0},{28,4},{1,25},{... | collective-permute-start | bytes 393224 | tf_op jit(solution)/shard_map/ppermute | solution.py:44
  41.5 1.1 %collective-permute-start.12 = (bf16[128,512]{1,0:T(8,128)(2,1)S(1)}, bf16[128,512]{1,0:T(8,128)(2,1)S(1)}, u32[]{:S(2)}, u32[]{:S(2)}) collective-permute-start(bf16[128,512]{1,0:T(8,128)(2,1)S(1)} %get-tuple-element.36), channel_id=1, source_target_pairs={{0,8},{4,12},{8,0},{12,4},{16,24},{20,28},{24,16},{28,20},{1,9},{5... | collective-permute-start | bytes 393224 | tf_op jit(solution)/shard_map/ppermute | solution.py:44
  42.7 1.8 %collective-permute-start.13 = (bf16[128,512]{1,0:T(8,128)(2,1)S(1)}, bf16[128,512]{1,0:T(8,128)(2,1)S(1)}, u32[]{:S(2)}, u32[]{:S(2)}) collective-permute-start(bf16[128,512]{1,0:T(8,128)(2,1)S(1)} %get-tuple-element.37), channel_id=1, source_target_pairs={{0,20},{4,16},{8,28},{12,24},{16,4},{20,0},{24,12},{28,8},{1,21},{... | collective-permute-start | bytes 393224 | tf_op jit(solution)/shard_map/ppermute | solution.py:44
  44.4 1.6 %collective-permute-done.9.refs_0_ = bf16[128,512]{1,0:T(8,128)(2,1)S(1)} collective-permute-done((bf16[128,512]{1,0:T(8,128)(2,1)S(1)}, bf16[128,512]{1,0:T(8,128)(2,1)S(1)}, u32[]{:S(2)}, u32[]{:S(2)}) %collective-permute-start.9) | collective-permute-done | bytes 131104 | tf_op jit(solution)/shard_map/ppermute | solution.py:44
  46.1 1.4 %collective-permute-start.14 = (bf16[128,512]{1,0:T(8,128)(2,1)S(1)}, bf16[128,512]{1,0:T(8,128)(2,1)S(1)}, u32[]{:S(2)}, u32[]{:S(2)}) collective-permute-start(bf16[128,512]{1,0:T(8,128)(2,1)S(1)} %get-tuple-element.38), channel_id=1, source_target_pairs={{0,4},{4,0},{8,12},{12,8},{16,20},{20,16},{24,28},{28,24},{1,5},{5... | collective-permute-start | bytes 393224 | tf_op jit(solution)/shard_map/ppermute | solution.py:44
  47.4 3.8 %collective-permute-done.10.refs_1_ = bf16[128,512]{1,0:T(8,128)(2,1)S(1)} collective-permute-done((bf16[128,512]{1,0:T(8,128)(2,1)S(1)}, bf16[128,512]{1,0:T(8,128)(2,1)S(1)}, u32[]{:S(2)}, u32[]{:S(2)}) %collective-permute-start.10) | collective-permute-done | bytes 131104 | tf_op jit(solution)/shard_map/ppermute | solution.py:44
  51.7 0.9 %collective-permute-done.12.refs_3_ = bf16[128,512]{1,0:T(8,128)(2,1)S(1)} collective-permute-done((bf16[128,512]{1,0:T(8,128)(2,1)S(1)}, bf16[128,512]{1,0:T(8,128)(2,1)S(1)}, u32[]{:S(2)}, u32[]{:S(2)}) %collective-permute-start.12) | collective-permute-done | bytes 131104 | tf_op jit(solution)/shard_map/ppermute | solution.py:44
  52.6 6.7 %collective-permute-done.13.refs_4_ = bf16[128,512]{1,0:T(8,128)(2,1)S(1)} collective-permute-done((bf16[128,512]{1,0:T(8,128)(2,1)S(1)}, bf16[128,512]{1,0:T(8,128)(2,1)S(1)}, u32[]{:S(2)}, u32[]{:S(2)}) %collective-permute-start.13) | collective-permute-done | bytes 131104 | tf_op jit(solution)/shard_map/ppermute | solution.py:44
  59.2 1.5 %collective-permute-done.15.refs_6_ = bf16[128,512]{1,0:T(8,128)(2,1)S(1)} collective-permute-done((bf16[128,512]{1,0:T(8,128)(2,1)S(1)}, bf16[128,512]{1,0:T(8,128)(2,1)S(1)}, u32[]{:S(2)}, u32[]{:S(2)}) %collective-permute-start.15) | collective-permute-done | bytes 131104 | tf_op jit(solution)/shard_map/ppermute | solution.py:44
  60.7 1.2 %merge.1 = bf16[1024,512]{1,0:T(8,128)(2,1)} custom-call(s32[1]{0:T(128)} %bitcast.me_ref, bf16[128,512]{1,0:T(8,128)(2,1)S(1)} %collective-permute-done.9.refs_0_, bf16[128,512]{1,0:T(8,128)(2,1)S(1)} %collective-permute-done.10.refs_1_, bf16[128,512]{1,0:T(8,128)(2,1)S(1)} %collective-permute-done.11.refs_2_, ...), custom_call_target="tpu_custom_call" | custom-call | flops 268435456 | bytes 2097152 | tf_op jit(solution)/shard_map/merge/pallas_call | solution.py:269
  (18 shorter events, 3.6 us)
Async XLA Ops:
  0.0 21.6 %collective-permute-start.1 = (bf16[5,128,1024]{2,1,0:T(8,128)(2,1)}, bf16[5,128,1024]{2,1,0:T(8,128)(2,1)S(1)}, u32[]{:S(2)}, u32[]{:S(2)}) collective-permute-start(bf16[5,128,1024]{2,1,0:T(8,128)(2,1)} %bitcast.11), channel_id=1, source_target_pairs={{1,2},{2,1},{5,6},{6,5},{9,10},{10,9},{13,14},{14,13},{17,18},{18,... | collective-permute-start | bytes 3932168 | tf_op jit(solution)/shard_map/ppermute | solution.py:196
  0.7 22.6 %collective-permute-start = (bf16[5,128,1024]{2,1,0:T(8,128)(2,1)}, bf16[5,128,1024]{2,1,0:T(8,128)(2,1)S(1)}, u32[]{:S(2)}, u32[]{:S(2)}) collective-permute-start(bf16[5,128,1024]{2,1,0:T(8,128)(2,1)} %bitcast.12), channel_id=1, source_target_pairs={{0,1},{2,3},{1,0},{3,2},{4,5},{6,7},{5,4},{7,6},{8,9},{10,11},{9,8... | collective-permute-start | bytes 3932168 | tf_op jit(solution)/shard_map/ppermute | solution.py:196
  5.1 1.2 %copy-start.1 = (bf16[128,1,8,512]{3,2,1,0:T(8,128)(2,1)S(1)}, bf16[128,1,8,512]{3,2,1,0:T(8,128)(2,1)}, u32[]{:S(2)}) copy-start(bf16[128,1,8,512]{3,2,1,0:T(8,128)(2,1)} %param.5) | copy-start | bytes 3145732
  7.4 9.1 %collective-permute-start.2 = (bf16[128,512]{1,0:T(8,128)(2,1)S(1)}, bf16[128,512]{1,0:T(8,128)(2,1)S(1)}, u32[]{:S(2)}, u32[]{:S(2)}) collective-permute-start(bf16[128,512]{1,0:T(8,128)(2,1)S(1)} %get-tuple-element.24), channel_id=1, source_target_pairs={{0,28},{4,24},{8,20},{12,16},{16,12},{20,8},{24,4},{28,0},{1,29},{... | collective-permute-start | bytes 393224 | tf_op jit(solution)/shard_map/ppermute | solution.py:44
  11.9 9.5 %collective-permute-start.3 = (bf16[128,512]{1,0:T(8,128)(2,1)S(1)}, bf16[128,512]{1,0:T(8,128)(2,1)S(1)}, u32[]{:S(2)}, u32[]{:S(2)}) collective-permute-start(bf16[128,512]{1,0:T(8,128)(2,1)S(1)} %get-tuple-element.25), channel_id=1, source_target_pairs={{0,12},{4,8},{8,4},{12,0},{16,28},{20,24},{24,20},{28,16},{1,13},{... | collective-permute-start | bytes 393224 | tf_op jit(solution)/shard_map/ppermute | solution.py:44
  11.9 16.5 %collective-permute-start.4 = (bf16[128,512]{1,0:T(8,128)(2,1)}, bf16[128,512]{1,0:T(8,128)(2,1)S(1)}, u32[]{:S(2)}, u32[]{:S(2)}) collective-permute-start(bf16[128,512]{1,0:T(8,128)(2,1)} %get-tuple-element.26), channel_id=1, source_target_pairs={{0,24},{4,28},{8,16},{12,20},{16,8},{20,12},{24,0},{28,4},{1,25},{... | collective-permute-start | bytes 393224 | tf_op jit(solution)/shard_map/ppermute | solution.py:44
  16.5 16.1 %collective-permute-start.5 = (bf16[128,512]{1,0:T(8,128)(2,1)}, bf16[128,512]{1,0:T(8,128)(2,1)}, u32[]{:S(2)}, u32[]{:S(2)}) collective-permute-start(bf16[128,512]{1,0:T(8,128)(2,1)} %get-tuple-element.27), channel_id=1, source_target_pairs={{0,20},{4,16},{8,28},{12,24},{16,4},{20,0},{24,12},{28,8},{1,21},{... | collective-permute-start | bytes 393224 | tf_op jit(solution)/shard_map/ppermute | solution.py:44
  21.4 11.2 %collective-permute-start.6 = (bf16[128,512]{1,0:T(8,128)(2,1)S(1)}, bf16[128,512]{1,0:T(8,128)(2,1)}, u32[]{:S(2)}, u32[]{:S(2)}) collective-permute-start(bf16[128,512]{1,0:T(8,128)(2,1)S(1)} %get-tuple-element.28), channel_id=1, source_target_pairs={{0,8},{4,12},{8,0},{12,4},{16,24},{20,28},{24,16},{28,20},{1,9},{5... | collective-permute-start | bytes 393224 | tf_op jit(solution)/shard_map/ppermute | solution.py:44
  21.6 11.0 %collective-permute-start.7 = (bf16[128,512]{1,0:T(8,128)(2,1)S(1)}, bf16[128,512]{1,0:T(8,128)(2,1)}, u32[]{:S(2)}, u32[]{:S(2)}) collective-permute-start(bf16[128,512]{1,0:T(8,128)(2,1)S(1)} %get-tuple-element.29), channel_id=1, source_target_pairs={{0,4},{4,0},{8,12},{12,8},{16,20},{20,16},{24,28},{28,24},{1,5},{5... | collective-permute-start | bytes 393224 | tf_op jit(solution)/shard_map/ppermute | solution.py:44
  23.4 11.6 %collective-permute-start.8 = (bf16[128,512]{1,0:T(8,128)(2,1)S(1)}, bf16[128,512]{1,0:T(8,128)(2,1)S(1)}, u32[]{:S(2)}, u32[]{:S(2)}) collective-permute-start(bf16[128,512]{1,0:T(8,128)(2,1)S(1)} %get-tuple-element.32), channel_id=1, source_target_pairs={{0,16},{4,20},{8,24},{12,28},{16,0},{20,4},{24,8},{28,12},{1,17},{... | collective-permute-start | bytes 393224 | tf_op jit(solution)/shard_map/ppermute | solution.py:44
  25.1 1.3 %copy-start = (bf16[1,1,5,128,1024]{4,3,2,1,0:T(8,128)(2,1)S(1)}, bf16[1,1,5,128,1024]{4,3,2,1,0:T(8,128)(2,1)}, u32[]{:S(2)}) copy-start(bf16[1,1,5,128,1024]{4,3,2,1,0:T(8,128)(2,1)} %param.6) | copy-start | bytes 3932164
  36.7 9.3 %collective-permute-start.9 = (bf16[128,512]{1,0:T(8,128)(2,1)S(1)}, bf16[128,512]{1,0:T(8,128)(2,1)S(1)}, u32[]{:S(2)}, u32[]{:S(2)}) collective-permute-start(bf16[128,512]{1,0:T(8,128)(2,1)S(1)} %get-tuple-element.33), channel_id=1, source_target_pairs={{0,28},{4,24},{8,20},{12,16},{16,12},{20,8},{24,4},{28,0},{1,29},{... | collective-permute-start | bytes 393224 | tf_op jit(solution)/shard_map/ppermute | solution.py:44
  40.0 11.2 %collective-permute-start.10 = (bf16[128,512]{1,0:T(8,128)(2,1)S(1)}, bf16[128,512]{1,0:T(8,128)(2,1)S(1)}, u32[]{:S(2)}, u32[]{:S(2)}) collective-permute-start(bf16[128,512]{1,0:T(8,128)(2,1)S(1)} %get-tuple-element.34), channel_id=1, source_target_pairs={{0,12},{4,8},{8,4},{12,0},{16,28},{20,24},{24,20},{28,16},{1,13},{... | collective-permute-start | bytes 393224 | tf_op jit(solution)/shard_map/ppermute | solution.py:44
  40.0 11.7 %collective-permute-start.11 = (bf16[128,512]{1,0:T(8,128)(2,1)S(1)}, bf16[128,512]{1,0:T(8,128)(2,1)S(1)}, u32[]{:S(2)}, u32[]{:S(2)}) collective-permute-start(bf16[128,512]{1,0:T(8,128)(2,1)S(1)} %get-tuple-element.35), channel_id=1, source_target_pairs={{0,24},{4,28},{8,16},{12,20},{16,8},{20,12},{24,0},{28,4},{1,25},{... | collective-permute-start | bytes 393224 | tf_op jit(solution)/shard_map/ppermute | solution.py:44
  41.5 11.1 %collective-permute-start.12 = (bf16[128,512]{1,0:T(8,128)(2,1)S(1)}, bf16[128,512]{1,0:T(8,128)(2,1)S(1)}, u32[]{:S(2)}, u32[]{:S(2)}) collective-permute-start(bf16[128,512]{1,0:T(8,128)(2,1)S(1)} %get-tuple-element.36), channel_id=1, source_target_pairs={{0,8},{4,12},{8,0},{12,4},{16,24},{20,28},{24,16},{28,20},{1,9},{5... | collective-permute-start | bytes 393224 | tf_op jit(solution)/shard_map/ppermute | solution.py:44
  42.7 16.6 %collective-permute-start.13 = (bf16[128,512]{1,0:T(8,128)(2,1)S(1)}, bf16[128,512]{1,0:T(8,128)(2,1)S(1)}, u32[]{:S(2)}, u32[]{:S(2)}) collective-permute-start(bf16[128,512]{1,0:T(8,128)(2,1)S(1)} %get-tuple-element.37), channel_id=1, source_target_pairs={{0,20},{4,16},{8,28},{12,24},{16,4},{20,0},{24,12},{28,8},{1,21},{... | collective-permute-start | bytes 393224 | tf_op jit(solution)/shard_map/ppermute | solution.py:44
  46.1 13.2 %collective-permute-start.14 = (bf16[128,512]{1,0:T(8,128)(2,1)S(1)}, bf16[128,512]{1,0:T(8,128)(2,1)S(1)}, u32[]{:S(2)}, u32[]{:S(2)}) collective-permute-start(bf16[128,512]{1,0:T(8,128)(2,1)S(1)} %get-tuple-element.38), channel_id=1, source_target_pairs={{0,4},{4,0},{8,12},{12,8},{16,20},{20,16},{24,28},{28,24},{1,5},{5... | collective-permute-start | bytes 393224 | tf_op jit(solution)/shard_map/ppermute | solution.py:44
  51.2 9.5 %collective-permute-start.15 = (bf16[128,512]{1,0:T(8,128)(2,1)S(1)}, bf16[128,512]{1,0:T(8,128)(2,1)S(1)}, u32[]{:S(2)}, u32[]{:S(2)}) collective-permute-start(bf16[128,512]{1,0:T(8,128)(2,1)S(1)} %get-tuple-element.39), channel_id=1, source_target_pairs={{0,16},{4,20},{8,24},{12,28},{16,0},{20,4},{24,8},{28,12},{1,17},{... | collective-permute-start | bytes 393224 | tf_op jit(solution)/shard_map/ppermute | solution.py:44

commit v11 on v10

--- a/solution.py
+++ b/solution.py
@@ -14,7 +14,8 @@
     return min(rows, max(16, 256 // patches))
 
 
-PARTS = 8
+PARTS = 4
+WEIGHT = 40
 
 
 def is_late(k, count):
@@ -31,10 +32,12 @@
 
 
 def inward(count):
-    order = [k for k in partners(count) if not is_late(k, count)]
-    last_far = order.index(min(k for k in order if k >= count // 2))
-    order.insert(min(3, last_far), order.pop(last_far))
-    return order + [k for k in partners(count) if is_late(k, count)]
+    quarter = count // PARTS
+    return (
+        list(range(count - 1, 3 * quarter - 1, -1))
+        + list(range(2 * quarter - 1, 0, -1))
+        + list(range(3 * quarter - 1, 2 * quarter - 1, -1))
+    )
 
 
 def ppermute(value, axis, step):
@@ -131,9 +134,16 @@
     return pl.ds(pl.multiple_of(lax.rem(me_ref[0] ^ k, quarter) * rows, rows), rows)
 
 
-def early_kernel(steps, me_ref, gram_ref, *refs):
+def ahead_kernel(*refs):
+    out_ref = refs[-1]
+    for i, piece in enumerate(refs[:-1]):
+        out_ref[i] = piece[...]
+
+
+def early_kernel(steps, me_ref, gram_ref, ahead_ref, *refs):
     piece_refs, (acc_ref, members_ref) = refs[:-2], refs[-2:]
     rows = piece_refs[0].shape[0]
+    piece_refs = [ahead_ref.at[i] for i in range(ahead_ref.shape[0])] + list(piece_refs)
     size = gram_ref.shape[0]
     there = block(me_ref, PARTS // 2, size // rows // PARTS, size // PARTS)
     members_ref[there, :] = jnp.zeros((size // PARTS, members_ref.shape[1]), members_ref.dtype)
@@ -147,9 +157,10 @@
         )
 
 
-def late_kernel(late_steps, out_steps, me_ref, gram_ref, acc_ref, members_ref, *refs):
+def late_kernel(late_steps, out_steps, me_ref, *refs):
     count = len(late_steps)
-    late_refs, outs = refs[:count], dict(zip(out_steps, refs[count:-3]))
+    late_refs, outs = refs[:count], dict(zip(out_steps, refs[count + 3 : -3]))
+    gram_ref, acc_ref, members_ref = refs[count : count + 3]
     first, late, fresh = refs[-3:]
     rows = late_refs[0].shape[0]
     size = gram_ref.shape[0]
@@ -207,7 +218,6 @@
     hbm = pl.BlockSpec(memory_space=pltpu.HBM)
     piece_shape = jax.ShapeDtypeStruct((rows, values), jnp.bfloat16)
 
-    odd, even = swap(store, 1), swap(store, 0)
     steps = [0] + inward(patches)
     pieces = pl.pallas_call(
         functools.partial(split_kernel, steps),
@@ -219,6 +229,8 @@
         name="split",
     )(me, ensemble.reshape(rows * patches, values))
     arrived = {k: ppermute(piece, "member", k) for k, piece in zip(steps, pieces)}
+    store, _ = lax.optimization_barrier((store, pieces[0]))
+    odd, even = swap(store, 1), swap(store, 0)
 
     table = jnp.concatenate([block_ids.ravel(), block_src.ravel(), block_count.ravel()])
     gram = pl.pallas_call(
@@ -235,18 +247,29 @@
         name="gram",
     )(region, table, store, even, odd)
 
-    early = [k for k in steps if not is_late(k, patches)]
+    early = [k for k in steps if k and not is_late(k, patches)]
     late = [k for k in steps if is_late(k, patches)]
     matrix = jax.ShapeDtypeStruct((size, values), jnp.bfloat16)
+    count = patches // PARTS + 1
+    first_steps, early = early[:count], early[count:] + [0]
+    ahead = pl.pallas_call(
+        ahead_kernel,
+        out_shape=jax.ShapeDtypeStruct((count, rows, values), jnp.bfloat16),
+        in_specs=[vmem()] * count,
+        out_specs=vmem(),
+        compiler_params=params(),
+        cost_estimate=cost(WEIGHT * size * size * values, 4 * count * rows * values),
+        name="ahead",
+    )(*[arrived[k] for k in first_steps])
     acc, members = pl.pallas_call(
-        functools.partial(early_kernel, early),
+        functools.partial(early_kernel, first_steps + early),
         out_shape=[jax.ShapeDtypeStruct((size, values), jnp.float32), matrix],
-        in_specs=[smem] + [vmem()] * (1 + len(early)),
+        in_specs=[smem] + [vmem()] * (2 + len(early)),
         out_specs=[vmem()] * 2,
         compiler_params=params(),
-        cost_estimate=cost(2 * size * size * values, 2 * size * size + 8 * size * values),
+        cost_estimate=cost(1, 1),
         name="early",
-    )(me, gram, *[arrived[k] for k in early])
+    )(me, gram, ahead, *[arrived[k] for k in early])
     back = partners(patches) + [0]
     moved = pl.pallas_call(
         functools.partial(late_kernel, late, back),
@@ -261,7 +284,7 @@
         compiler_params=params(),
         cost_estimate=cost(3 * size * size * values, 2 * size * size + 10 * size * values),
         name="late",
-    )(me, gram, acc, members, *[arrived[k] for k in late])
+    )(me, *[arrived[k] for k in late], gram, acc, members)
     order = back
     returned = [ppermute(piece, "member", k) for k, piece in zip(back, moved)]
 

time: 62.2 us -> 60.2 us (0.968)
  the two profiles are of different devices: /device:TPU:0 before, /device:TPU:1 now
where the time goes in v11:
time: 60.2 us; the launch traced here: 60 us
  starting transfers between devices  29.3 us (49%)
  waiting for transfers between devices  19.4 us (32%)
  Pallas kernels  8.57 us (14%)
  local copies, waits for them, and re-layouts  1.23 us (2%)
  other arithmetic  0.75 us (1%)
  between operations  0.75 us (1%)
    ppermute x14, starting transfers between devices, ppermute(): return lax.ppermute(value, axis, [(i, i ^ step) for i in range(count)])  24.8 us
    ppermute x14, waiting for transfers between devices, ppermute(): return lax.ppermute(value, axis, [(i, i ^ step) for i in range(count)])  19.4 us
    ppermute x2, starting transfers between devices, swap(): return lax.ppermute(store, 'region', pairs + [(j, i) for i, j in pairs])  4.53 us
    pallas_call x1, Pallas kernels, shards(): pl.pallas_call(functools.partial(gram_kernel, 1.0 / (2.0 * size)), out_sh...  1.99 us
    pallas_call x1, Pallas kernels, shards(): pl.pallas_call(functools.partial(late_kernel, late, back), out_shape=[pie...  1.81 us
    pallas_call x1, Pallas kernels, shards(): pl.pallas_call(functools.partial(early_kernel, first_steps + early), out_...  1.35 us
    unnamed x4, local copies, waits for them, and re-layouts  1.23 us
    pallas_call x1, Pallas kernels, shards(): pl.pallas_call(functools.partial(merge_kernel, order), out_shape=jax.Shap...  1.23 us
  transfers between devices with their start and end apart: 16, of which 7 were waited for; matrix products, arithmetic and copies ran while one was open for 1% of the time, Pallas kernels for 7%

profile of v11, /device:TPU:1, one launch (start us, length us, event | category | flops | bytes accessed | tf_op | source)
XLA Modules:
  0.0 60.0 jit_solution(12312124883536539893)
XLA Ops:
  0.0 1.2 %copy-done.1 = bf16[128,1,8,512]{3,2,1,0:T(8,128)(2,1)S(1)} copy-done((bf16[128,1,8,512]{3,2,1,0:T(8,128)(2,1)S(1)}, bf16[128,1,8,512]{3,2,1,0:T(8,128)(2,1)}, u32[]{:S(2)}) %copy-start.1) | copy-done | bytes 1048600
  1.2 1.1 %split.1 = (bf16[128,512]{1,0:T(8,128)(2,1)S(1)}, bf16[128,512]{1,0:T(8,128)(2,1)}, bf16[128,512]{1,0:T(8,128)(2,1)}, bf16[128,512]{1,0:T(8,128)(2,1)S(1)}, bf16...) custom-call(s32[1]{0:T(128)} %bitcast.me_ref, ...), custom_call_target="tpu_custom_call" | custom-call | flops 268435456 | bytes 2097152 | tf_op jit(solution)/shard_map/split/pallas_call | solution.py:222
  2.4 4.5 %collective-permute-start.3 = (bf16[5,128,1024]{2,1,0:T(8,128)(2,1)}, bf16[5,128,1024]{2,1,0:T(8,128)(2,1)S(1)}, u32[]{:S(2)}, u32[]{:S(2)}) collective-permute-start(bf16[5,128,1024]{2,1,0:T(8,128)(2,1)} %bitcast.11), channel_id=1, source_target_pairs={{1,2},{2,1},{5,6},{6,5},{9,10},{10,9},{13,14},{14,13},{17,18},{18,... | collective-permute-start | bytes 3932168 | tf_op jit(solution)/shard_map/ppermute | solution.py:207
  6.9 4.3 %collective-permute-start.4 = (bf16[128,512]{1,0:T(8,128)(2,1)}, bf16[128,512]{1,0:T(8,128)(2,1)S(1)}, u32[]{:S(2)}, u32[]{:S(2)}) collective-permute-start(bf16[128,512]{1,0:T(8,128)(2,1)} %get-tuple-element.28), channel_id=1, source_target_pairs={{0,28},{4,24},{8,20},{12,16},{16,12},{20,8},{24,4},{28,0},{1,29},{... | collective-permute-start | bytes 393224 | tf_op jit(solution)/shard_map/ppermute | solution.py:47
  11.9 0.7 %pad_add_fusion.table_ref = s32[7]{0:T(128)S(1)} fusion(s32[1]{0:T(128)} %bitcast.10, s32[3]{0:T(128)} %bitcast.15, s32[3]{0:T(128)} %bitcast.16), kind=kLoop, calls=%fused_computation | loop fusion | flops 14 | bytes 56 | tf_op jit(solution)/shard_map/concatenate | solution.py:235
  12.6 2.3 %collective-permute-done.4.refs_0_ = bf16[128,512]{1,0:T(8,128)(2,1)S(1)} collective-permute-done((bf16[128,512]{1,0:T(8,128)(2,1)}, bf16[128,512]{1,0:T(8,128)(2,1)S(1)}, u32[]{:S(2)}, u32[]{:S(2)}) %collective-permute-start.4) | collective-permute-done | bytes 131104 | tf_op jit(solution)/shard_map/ppermute | solution.py:47
  14.9 7.3 %collective-permute-start = (bf16[128,512]{1,0:T(8,128)(2,1)S(1)}, bf16[128,512]{1,0:T(8,128)(2,1)S(1)}, u32[]{:S(2)}, u32[]{:S(2)}) collective-permute-start(bf16[128,512]{1,0:T(8,128)(2,1)S(1)} %get-tuple-element.24), channel_id=1, source_target_pairs={{0,20},{4,16},{8,28},{12,24},{16,4},{20,0},{24,12},{28,8},{1,21},{... | collective-permute-start | bytes 393224 | tf_op jit(solution)/shard_map/ppermute | solution.py:47
  22.2 6.4 %collective-permute-start.1 = (bf16[128,512]{1,0:T(8,128)(2,1)S(1)}, bf16[128,512]{1,0:T(8,128)(2,1)S(1)}, u32[]{:S(2)}, u32[]{:S(2)}) collective-permute-start(bf16[128,512]{1,0:T(8,128)(2,1)S(1)} %get-tuple-element.25), channel_id=1, source_target_pairs={{0,16},{4,20},{8,24},{12,28},{16,0},{20,4},{24,8},{28,12},{1,17},{... | collective-permute-start | bytes 393224 | tf_op jit(solution)/shard_map/ppermute | solution.py:47
  29.0 1.1 %ahead.1.ahead_ref = bf16[3,128,512]{2,1,0:T(8,128)(2,1)S(1)} custom-call(bf16[128,512]{1,0:T(8,128)(2,1)S(1)} %collective-permute-done.4.refs_0_, bf16[128,512]{1,0:T(8,128)(2,1)} %collective-permute-done.5.refs_1_, bf16[128,512]{1,0:T(8,128)(2,1)} %collective-permute-done.6.refs_2_), custom_call_target="tpu_custom_call" | custom-call | flops 21474836480 | bytes 786432 | tf_op jit(solution)/shard_map/ahead/pallas_call | solution.py:255
  30.1 2.0 %gram.1.gram_ref.refs_2_ = bf16[1024,1024]{1,0:T(8,128)(2,1)S(1)} custom-call(s32[1]{0:T(128)} %bitcast.2.region_ref, s32[7]{0:T(128)S(1)} %pad_add_fusion.table_ref, bf16[5,128,1024]{2,1,0:T(8,128)(2,1)S(1)} %bitcast.13, bf16[5,128,1024]{2,1,0:T(8,128)(2,1)S(1)} %collective-permute-done.2.even, bf16[5,128,1024]{2,1,0:T(8,128)(2,1)S(1)} %collective-permute-done.3.odd), custom_call_target="tpu_custom_call" | custom-call | flops 805306368 | bytes 4194304 | tf_op jit(solution)/shard_map/gram/pallas_call | solution.py:236
  32.0 1.5 %collective-permute-done.7.refs_0_ = bf16[128,512]{1,0:T(8,128)(2,1)S(1)} collective-permute-done((bf16[128,512]{1,0:T(8,128)(2,1)S(1)}, bf16[128,512]{1,0:T(8,128)(2,1)S(1)}, u32[]{:S(2)}, u32[]{:S(2)}) %collective-permute-start.7) | collective-permute-done | bytes 131104 | tf_op jit(solution)/shard_map/ppermute | solution.py:47
  33.6 1.4 %early.1 = (f32[1024,512]{1,0:T(8,128)S(1)}, bf16[1024,512]{1,0:T(8,128)(2,1)S(1)}) custom-call(s32[1]{0:T(128)} %bitcast.me_ref, bf16[1024,1024]{1,0:T(8,128)(2,1)S(1)} %gram.1.gram_ref.refs_2_, bf16[3,128,512]{2,1,0:T(8,128)(2,1)S(1)} %ahead.1.ahead_ref, bf16[128,512]{1,0:T(8,128)(2,1)S(1)} %collective-permute-done.7.refs_0_, ...), custom_call_target="tpu_custom_call" | custom-call | flops 1 | bytes 1 | tf_op jit(solution)/shard_map/early/pallas_call | solution.py:264
  35.0 1.8 %late.1 = (bf16[128,512]{1,0:T(8,128)(2,1)S(1)}, bf16[128,512]{1,0:T(8,128)(2,1)S(1)}, bf16[128,512]{1,0:T(8,128)(2,1)S(1)}, bf16[128,512]{1,0:T(8,128)(2,1)S(1)...) custom-call(s32[1]{0:T(128)} %bitcast.me_ref, ...), custom_call_target="tpu_custom_call" | custom-call | flops 1610612736 | bytes 7340032 | tf_op jit(solution)/shard_map/late/pallas_call | solution.py:274
  36.8 0.8 %collective-permute-start.9 = (bf16[128,512]{1,0:T(8,128)(2,1)S(1)}, bf16[128,512]{1,0:T(8,128)(2,1)S(1)}, u32[]{:S(2)}, u32[]{:S(2)}) collective-permute-start(bf16[128,512]{1,0:T(8,128)(2,1)S(1)} %get-tuple-element.35), channel_id=1, source_target_pairs={{0,28},{4,24},{8,20},{12,16},{16,12},{20,8},{24,4},{28,0},{1,29},{... | collective-permute-start | bytes 393224 | tf_op jit(solution)/shard_map/ppermute | solution.py:47
  37.6 2.8 %collective-permute-start.11 = (bf16[128,512]{1,0:T(8,128)(2,1)S(1)}, bf16[128,512]{1,0:T(8,128)(2,1)S(1)}, u32[]{:S(2)}, u32[]{:S(2)}) collective-permute-start(bf16[128,512]{1,0:T(8,128)(2,1)S(1)} %get-tuple-element.37), channel_id=1, source_target_pairs={{0,24},{4,28},{8,16},{12,20},{16,8},{20,12},{24,0},{28,4},{1,25},{... | collective-permute-start | bytes 393224 | tf_op jit(solution)/shard_map/ppermute | solution.py:47
  40.4 1.1 %collective-permute-start.12 = (bf16[128,512]{1,0:T(8,128)(2,1)S(1)}, bf16[128,512]{1,0:T(8,128)(2,1)S(1)}, u32[]{:S(2)}, u32[]{:S(2)}) collective-permute-start(bf16[128,512]{1,0:T(8,128)(2,1)S(1)} %get-tuple-element.38), channel_id=1, source_target_pairs={{0,8},{4,12},{8,0},{12,4},{16,24},{20,28},{24,16},{28,20},{1,9},{5... | collective-permute-start | bytes 393224 | tf_op jit(solution)/shard_map/ppermute | solution.py:47
  41.6 0.4 collective-permute-start.13
  42.0 2.8 %collective-permute-done.9.refs_0_ = bf16[128,512]{1,0:T(8,128)(2,1)S(1)} collective-permute-done((bf16[128,512]{1,0:T(8,128)(2,1)S(1)}, bf16[128,512]{1,0:T(8,128)(2,1)S(1)}, u32[]{:S(2)}, u32[]{:S(2)}) %collective-permute-start.9) | collective-permute-done | bytes 131104 | tf_op jit(solution)/shard_map/ppermute | solution.py:47
  45.1 2.2 %collective-permute-done.10.refs_1_ = bf16[128,512]{1,0:T(8,128)(2,1)S(1)} collective-permute-done((bf16[128,512]{1,0:T(8,128)(2,1)S(1)}, bf16[128,512]{1,0:T(8,128)(2,1)S(1)}, u32[]{:S(2)}, u32[]{:S(2)}) %collective-permute-start.10) | collective-permute-done | bytes 131104 | tf_op jit(solution)/shard_map/ppermute | solution.py:47
  47.2 1.0 %collective-permute-start.15 = (bf16[128,512]{1,0:T(8,128)(2,1)S(1)}, bf16[128,512]{1,0:T(8,128)(2,1)S(1)}, u32[]{:S(2)}, u32[]{:S(2)}) collective-permute-start(bf16[128,512]{1,0:T(8,128)(2,1)S(1)} %get-tuple-element.41), channel_id=1, source_target_pairs={{0,16},{4,20},{8,24},{12,28},{16,0},{20,4},{24,8},{28,12},{1,17},{... | collective-permute-start | bytes 393224 | tf_op jit(solution)/shard_map/ppermute | solution.py:47
  48.2 1.4 %collective-permute-done.11.refs_2_ = bf16[128,512]{1,0:T(8,128)(2,1)S(1)} collective-permute-done((bf16[128,512]{1,0:T(8,128)(2,1)S(1)}, bf16[128,512]{1,0:T(8,128)(2,1)S(1)}, u32[]{:S(2)}, u32[]{:S(2)}) %collective-permute-start.11) | collective-permute-done | bytes 131104 | tf_op jit(solution)/shard_map/ppermute | solution.py:47
  49.6 7.8 %collective-permute-done.13.refs_4_ = bf16[128,512]{1,0:T(8,128)(2,1)S(1)} collective-permute-done((bf16[128,512]{1,0:T(8,128)(2,1)S(1)}, bf16[128,512]{1,0:T(8,128)(2,1)S(1)}, u32[]{:S(2)}, u32[]{:S(2)}) %collective-permute-start.13) | collective-permute-done | bytes 131104 | tf_op jit(solution)/shard_map/ppermute | solution.py:47
  57.4 1.4 %collective-permute-done.15.refs_6_ = bf16[128,512]{1,0:T(8,128)(2,1)S(1)} collective-permute-done((bf16[128,512]{1,0:T(8,128)(2,1)S(1)}, bf16[128,512]{1,0:T(8,128)(2,1)S(1)}, u32[]{:S(2)}, u32[]{:S(2)}) %collective-permute-start.15) | collective-permute-done | bytes 131104 | tf_op jit(solution)/shard_map/ppermute | solution.py:47
  58.8 1.2 %merge.1 = bf16[1024,512]{1,0:T(8,128)(2,1)} custom-call(s32[1]{0:T(128)} %bitcast.me_ref, bf16[128,512]{1,0:T(8,128)(2,1)S(1)} %collective-permute-done.9.refs_0_, bf16[128,512]{1,0:T(8,128)(2,1)S(1)} %collective-permute-done.10.refs_1_, bf16[128,512]{1,0:T(8,128)(2,1)S(1)} %collective-permute-done.11.refs_2_, ...), custom_call_target="tpu_custom_call" | custom-call | flops 268435456 | bytes 2097152 | tf_op jit(solution)/shard_map/merge/pallas_call | solution.py:292
  (19 shorter events, 0.7 us)
Async XLA Ops:
  0.0 1.2 %copy-start.1 = (bf16[128,1,8,512]{3,2,1,0:T(8,128)(2,1)S(1)}, bf16[128,1,8,512]{3,2,1,0:T(8,128)(2,1)}, u32[]{:S(2)}) copy-start(bf16[128,1,8,512]{3,2,1,0:T(8,128)(2,1)} %param.5) | copy-start | bytes 3145732
  2.4 26.3 %collective-permute-start.3 = (bf16[5,128,1024]{2,1,0:T(8,128)(2,1)}, bf16[5,128,1024]{2,1,0:T(8,128)(2,1)S(1)}, u32[]{:S(2)}, u32[]{:S(2)}) collective-permute-start(bf16[5,128,1024]{2,1,0:T(8,128)(2,1)} %bitcast.11), channel_id=1, source_target_pairs={{1,2},{2,1},{5,6},{6,5},{9,10},{10,9},{13,14},{14,13},{17,18},{18,... | collective-permute-start | bytes 3932168 | tf_op jit(solution)/shard_map/ppermute | solution.py:207
  6.9 8.0 %collective-permute-start.4 = (bf16[128,512]{1,0:T(8,128)(2,1)}, bf16[128,512]{1,0:T(8,128)(2,1)S(1)}, u32[]{:S(2)}, u32[]{:S(2)}) collective-permute-start(bf16[128,512]{1,0:T(8,128)(2,1)} %get-tuple-element.28), channel_id=1, source_target_pairs={{0,28},{4,24},{8,20},{12,16},{16,12},{20,8},{24,4},{28,0},{1,29},{... | collective-permute-start | bytes 393224 | tf_op jit(solution)/shard_map/ppermute | solution.py:47
  11.2 11.0 %collective-permute-start.5 = (bf16[128,512]{1,0:T(8,128)(2,1)}, bf16[128,512]{1,0:T(8,128)(2,1)}, u32[]{:S(2)}, u32[]{:S(2)}) collective-permute-start(bf16[128,512]{1,0:T(8,128)(2,1)} %get-tuple-element.29), channel_id=1, source_target_pairs={{0,24},{4,28},{8,16},{12,20},{16,8},{20,12},{24,0},{28,4},{1,25},{... | collective-permute-start | bytes 393224 | tf_op jit(solution)/shard_map/ppermute | solution.py:47
  11.2 17.4 %collective-permute-start.6 = (bf16[128,512]{1,0:T(8,128)(2,1)S(1)}, bf16[128,512]{1,0:T(8,128)(2,1)}, u32[]{:S(2)}, u32[]{:S(2)}) collective-permute-start(bf16[128,512]{1,0:T(8,128)(2,1)S(1)} %get-tuple-element.30), channel_id=1, source_target_pairs={{0,12},{4,8},{8,4},{12,0},{16,28},{20,24},{24,20},{28,16},{1,13},{... | collective-permute-start | bytes 393224 | tf_op jit(solution)/shard_map/ppermute | solution.py:47
  11.2 18.8 %collective-permute-start.2 = (bf16[5,128,1024]{2,1,0:T(8,128)(2,1)}, bf16[5,128,1024]{2,1,0:T(8,128)(2,1)S(1)}, u32[]{:S(2)}, u32[]{:S(2)}) collective-permute-start(bf16[5,128,1024]{2,1,0:T(8,128)(2,1)} %bitcast.12), channel_id=1, source_target_pairs={{0,1},{2,3},{1,0},{3,2},{4,5},{6,7},{5,4},{7,6},{8,9},{10,11},{9,8... | collective-permute-start | bytes 3932168 | tf_op jit(solution)/shard_map/ppermute | solution.py:207
  14.9 20.0 %collective-permute-start = (bf16[128,512]{1,0:T(8,128)(2,1)S(1)}, bf16[128,512]{1,0:T(8,128)(2,1)S(1)}, u32[]{:S(2)}, u32[]{:S(2)}) collective-permute-start(bf16[128,512]{1,0:T(8,128)(2,1)S(1)} %get-tuple-element.24), channel_id=1, source_target_pairs={{0,20},{4,16},{8,28},{12,24},{16,4},{20,0},{24,12},{28,8},{1,21},{... | collective-permute-start | bytes 393224 | tf_op jit(solution)/shard_map/ppermute | solution.py:47
  22.2 12.7 %collective-permute-start.1 = (bf16[128,512]{1,0:T(8,128)(2,1)S(1)}, bf16[128,512]{1,0:T(8,128)(2,1)S(1)}, u32[]{:S(2)}, u32[]{:S(2)}) collective-permute-start(bf16[128,512]{1,0:T(8,128)(2,1)S(1)} %get-tuple-element.25), channel_id=1, source_target_pairs={{0,16},{4,20},{8,24},{12,28},{16,0},{20,4},{24,8},{28,12},{1,17},{... | collective-permute-start | bytes 393224 | tf_op jit(solution)/shard_map/ppermute | solution.py:47
  28.6 4.9 %collective-permute-start.7 = (bf16[128,512]{1,0:T(8,128)(2,1)S(1)}, bf16[128,512]{1,0:T(8,128)(2,1)S(1)}, u32[]{:S(2)}, u32[]{:S(2)}) collective-permute-start(bf16[128,512]{1,0:T(8,128)(2,1)S(1)} %get-tuple-element.31), channel_id=1, source_target_pairs={{0,8},{4,12},{8,0},{12,4},{16,24},{20,28},{24,16},{28,20},{1,9},{5... | collective-permute-start | bytes 393224 | tf_op jit(solution)/shard_map/ppermute | solution.py:47
  28.6 1.4 %copy-start = (bf16[1,1,5,128,1024]{4,3,2,1,0:T(8,128)(2,1)S(1)}, bf16[1,1,5,128,1024]{4,3,2,1,0:T(8,128)(2,1)}, u32[]{:S(2)}) copy-start(bf16[1,1,5,128,1024]{4,3,2,1,0:T(8,128)(2,1)} %param.6) | copy-start | bytes 3932164
  28.6 4.9 %collective-permute-start.8 = (bf16[128,512]{1,0:T(8,128)(2,1)S(1)}, bf16[128,512]{1,0:T(8,128)(2,1)S(1)}, u32[]{:S(2)}, u32[]{:S(2)}) collective-permute-start(bf16[128,512]{1,0:T(8,128)(2,1)S(1)} %get-tuple-element.32), channel_id=1, source_target_pairs={{0,4},{4,0},{8,12},{12,8},{16,20},{20,16},{24,28},{28,24},{1,5},{5... | collective-permute-start | bytes 393224 | tf_op jit(solution)/shard_map/ppermute | solution.py:47
  36.8 8.0 %collective-permute-start.9 = (bf16[128,512]{1,0:T(8,128)(2,1)S(1)}, bf16[128,512]{1,0:T(8,128)(2,1)S(1)}, u32[]{:S(2)}, u32[]{:S(2)}) collective-permute-start(bf16[128,512]{1,0:T(8,128)(2,1)S(1)} %get-tuple-element.35), channel_id=1, source_target_pairs={{0,28},{4,24},{8,20},{12,16},{16,12},{20,8},{24,4},{28,0},{1,29},{... | collective-permute-start | bytes 393224 | tf_op jit(solution)/shard_map/ppermute | solution.py:47
  37.5 9.7 %collective-permute-start.10 = (bf16[128,512]{1,0:T(8,128)(2,1)S(1)}, bf16[128,512]{1,0:T(8,128)(2,1)S(1)}, u32[]{:S(2)}, u32[]{:S(2)}) collective-permute-start(bf16[128,512]{1,0:T(8,128)(2,1)S(1)} %get-tuple-element.36), channel_id=1, source_target_pairs={{0,12},{4,8},{8,4},{12,0},{16,28},{20,24},{24,20},{28,16},{1,13},{... | collective-permute-start | bytes 393224 | tf_op jit(solution)/shard_map/ppermute | solution.py:47
  37.6 12.0 %collective-permute-start.11 = (bf16[128,512]{1,0:T(8,128)(2,1)S(1)}, bf16[128,512]{1,0:T(8,128)(2,1)S(1)}, u32[]{:S(2)}, u32[]{:S(2)}) collective-permute-start(bf16[128,512]{1,0:T(8,128)(2,1)S(1)} %get-tuple-element.37), channel_id=1, source_target_pairs={{0,24},{4,28},{8,16},{12,20},{16,8},{20,12},{24,0},{28,4},{1,25},{... | collective-permute-start | bytes 393224 | tf_op jit(solution)/shard_map/ppermute | solution.py:47
  40.4 9.2 %collective-permute-start.12 = (bf16[128,512]{1,0:T(8,128)(2,1)S(1)}, bf16[128,512]{1,0:T(8,128)(2,1)S(1)}, u32[]{:S(2)}, u32[]{:S(2)}) collective-permute-start(bf16[128,512]{1,0:T(8,128)(2,1)S(1)} %get-tuple-element.38), channel_id=1, source_target_pairs={{0,8},{4,12},{8,0},{12,4},{16,24},{20,28},{24,16},{28,20},{1,9},{5... | collective-permute-start | bytes 393224 | tf_op jit(solution)/shard_map/ppermute | solution.py:47
  41.6 15.8 %collective-permute-start.13 = (bf16[128,512]{1,0:T(8,128)(2,1)S(1)}, bf16[128,512]{1,0:T(8,128)(2,1)S(1)}, u32[]{:S(2)}, u32[]{:S(2)}) collective-permute-start(bf16[128,512]{1,0:T(8,128)(2,1)S(1)} %get-tuple-element.39), channel_id=1, source_target_pairs={{0,20},{4,16},{8,28},{12,24},{16,4},{20,0},{24,12},{28,8},{1,21},{... | collective-permute-start | bytes 393224 | tf_op jit(solution)/shard_map/ppermute | solution.py:47
  44.8 12.6 %collective-permute-start.14 = (bf16[128,512]{1,0:T(8,128)(2,1)S(1)}, bf16[128,512]{1,0:T(8,128)(2,1)S(1)}, u32[]{:S(2)}, u32[]{:S(2)}) collective-permute-start(bf16[128,512]{1,0:T(8,128)(2,1)S(1)} %get-tuple-element.40), channel_id=1, source_target_pairs={{0,4},{4,0},{8,12},{12,8},{16,20},{20,16},{24,28},{28,24},{1,5},{5... | collective-permute-start | bytes 393224 | tf_op jit(solution)/shard_map/ppermute | solution.py:47
  47.2 11.6 %collective-permute-start.15 = (bf16[128,512]{1,0:T(8,128)(2,1)S(1)}, bf16[128,512]{1,0:T(8,128)(2,1)S(1)}, u32[]{:S(2)}, u32[]{:S(2)}) collective-permute-start(bf16[128,512]{1,0:T(8,128)(2,1)S(1)} %get-tuple-element.41), channel_id=1, source_target_pairs={{0,16},{4,20},{8,24},{12,28},{16,0},{20,4},{24,8},{28,12},{1,17},{... | collective-permute-start | bytes 393224 | tf_op jit(solution)/shard_map/ppermute | solution.py:47

commit v12 on v11

--- a/solution.py
+++ b/solution.py
@@ -33,11 +33,9 @@
 
 def inward(count):
     quarter = count // PARTS
-    return (
-        list(range(count - 1, 3 * quarter - 1, -1))
-        + list(range(2 * quarter - 1, 0, -1))
-        + list(range(3 * quarter - 1, 2 * quarter - 1, -1))
-    )
+    near = list(range(2 * quarter - 1, 0, -1))
+    far = list(range(count - 1, 3 * quarter - 1, -1))
+    return near[:1] + far + near[1:] + list(range(3 * quarter - 1, 2 * quarter - 1, -1))
 
 
 def ppermute(value, axis, step):
@@ -215,7 +213,7 @@
     me = lax.axis_index("member").astype(jnp.int32).reshape(1)
     region = lax.axis_index("region").astype(jnp.int32).reshape(1)
     smem = pl.BlockSpec(memory_space=pltpu.SMEM)
-    hbm = pl.BlockSpec(memory_space=pltpu.HBM)
+    anywhere = pl.BlockSpec(memory_space=pl.ANY)
     piece_shape = jax.ShapeDtypeStruct((rows, values), jnp.bfloat16)
 
     steps = [0] + inward(patches)
@@ -236,7 +234,7 @@
     gram = pl.pallas_call(
         functools.partial(gram_kernel, 1.0 / (2.0 * size)),
         out_shape=jax.ShapeDtypeStruct((size, size), jnp.bfloat16),
-        in_specs=[smem] * 2 + [hbm] * 3,
+        in_specs=[smem] * 2 + [anywhere] * 3,
         out_specs=vmem(),
         scratch_shapes=[
             pltpu.VMEM((slots * store.shape[1], size), jnp.bfloat16),

time: 60.2 us -> 64.5 us (1.071)
  the two profiles are of different devices: /device:TPU:1 before, /device:TPU:0 now
where the time goes in v12:
time: 64.5 us; the launch traced here: 64.3 us
  starting transfers between devices  32.2 us (50%)
  waiting for transfers between devices  20.7 us (32%)
  Pallas kernels  8.58 us (13%)
  local copies, waits for them, and re-layouts  1.3 us (2%)
  other arithmetic  0.75 us (1%)
  between operations  0.72 us (1%)
    ppermute x14, starting transfers between devices, ppermute(): return lax.ppermute(value, axis, [(i, i ^ step) for i in range(count)])  29.5 us
    ppermute x14, waiting for transfers between devices, ppermute(): return lax.ppermute(value, axis, [(i, i ^ step) for i in range(count)])  20.7 us
    ppermute x2, starting transfers between devices, swap(): return lax.ppermute(store, 'region', pairs + [(j, i) for i, j in pairs])  2.69 us
    pallas_call x1, Pallas kernels, shards(): pl.pallas_call(functools.partial(gram_kernel, 1.0 / (2.0 * size)), out_sh...  1.98 us
    pallas_call x1, Pallas kernels, shards(): pl.pallas_call(functools.partial(late_kernel, late, back), out_shape=[pie...  1.81 us
    pallas_call x1, Pallas kernels, shards(): pl.pallas_call(functools.partial(early_kernel, first_steps + early), out_...  1.35 us
    unnamed x4, local copies, waits for them, and re-layouts  1.3 us
  transfers between devices with their start and end apart: 16, of which 6 were waited for; matrix products, arithmetic and copies ran while one was open for 1% of the time, Pallas kernels for 7%

profile of v12, /device:TPU:0, one launch (start us, length us, event | category | flops | bytes accessed | tf_op | source)
XLA Modules:
  0.0 64.3 jit_solution(16363968721964930962)
XLA Ops:
  0.0 1.2 %copy-done.1 = bf16[128,1,8,512]{3,2,1,0:T(8,128)(2,1)S(1)} copy-done((bf16[128,1,8,512]{3,2,1,0:T(8,128)(2,1)S(1)}, bf16[128,1,8,512]{3,2,1,0:T(8,128)(2,1)}, u32[]{:S(2)}) %copy-start.1) | copy-done | bytes 1048600
  1.2 1.1 %split.1 = (bf16[128,512]{1,0:T(8,128)(2,1)S(1)}, bf16[128,512]{1,0:T(8,128)(2,1)}, bf16[128,512]{1,0:T(8,128)(2,1)}, bf16[128,512]{1,0:T(8,128)(2,1)S(1)}, bf16...) custom-call(s32[1]{0:T(128)} %bitcast.me_ref, ...), custom_call_target="tpu_custom_call" | custom-call | flops 268435456 | bytes 2097152 | tf_op jit(solution)/shard_map/split/pallas_call | solution.py:220
  3.1 4.0 %collective-permute-start.4 = (bf16[128,512]{1,0:T(8,128)(2,1)}, bf16[128,512]{1,0:T(8,128)(2,1)S(1)}, u32[]{:S(2)}, u32[]{:S(2)}) collective-permute-start(bf16[128,512]{1,0:T(8,128)(2,1)} %get-tuple-element.28), channel_id=1, source_target_pairs={{0,12},{4,8},{8,4},{12,0},{16,28},{20,24},{24,20},{28,16},{1,13},{... | collective-permute-start | bytes 393224 | tf_op jit(solution)/shard_map/ppermute | solution.py:45
  7.1 2.4 %collective-permute-start.5 = (bf16[128,512]{1,0:T(8,128)(2,1)}, bf16[128,512]{1,0:T(8,128)(2,1)}, u32[]{:S(2)}, u32[]{:S(2)}) collective-permute-start(bf16[128,512]{1,0:T(8,128)(2,1)} %get-tuple-element.29), channel_id=1, source_target_pairs={{0,28},{4,24},{8,20},{12,16},{16,12},{20,8},{24,4},{28,0},{1,29},{... | collective-permute-start | bytes 393224 | tf_op jit(solution)/shard_map/ppermute | solution.py:45
  9.5 1.3 %collective-permute-start.6 = (bf16[128,512]{1,0:T(8,128)(2,1)S(1)}, bf16[128,512]{1,0:T(8,128)(2,1)}, u32[]{:S(2)}, u32[]{:S(2)}) collective-permute-start(bf16[128,512]{1,0:T(8,128)(2,1)S(1)} %get-tuple-element.30), channel_id=1, source_target_pairs={{0,24},{4,28},{8,16},{12,20},{16,8},{20,12},{24,0},{28,4},{1,25},{... | collective-permute-start | bytes 393224 | tf_op jit(solution)/shard_map/ppermute | solution.py:45
  10.9 2.0 %collective-permute-start.2 = (bf16[5,128,1024]{2,1,0:T(8,128)(2,1)}, bf16[5,128,1024]{2,1,0:T(8,128)(2,1)S(1)}, u32[]{:S(2)}, u32[]{:S(2)}) collective-permute-start(bf16[5,128,1024]{2,1,0:T(8,128)(2,1)} %bitcast.12), channel_id=1, source_target_pairs={{0,1},{2,3},{1,0},{3,2},{4,5},{6,7},{5,4},{7,6},{8,9},{10,11},{9,8... | collective-permute-start | bytes 3932168 | tf_op jit(solution)/shard_map/ppermute | solution.py:205
  14.2 1.7 %collective-permute-start = (bf16[128,512]{1,0:T(8,128)(2,1)S(1)}, bf16[128,512]{1,0:T(8,128)(2,1)S(1)}, u32[]{:S(2)}, u32[]{:S(2)}) collective-permute-start(bf16[128,512]{1,0:T(8,128)(2,1)S(1)} %get-tuple-element.24), channel_id=1, source_target_pairs={{0,20},{4,16},{8,28},{12,24},{16,4},{20,0},{24,12},{28,8},{1,21},{... | collective-permute-start | bytes 393224 | tf_op jit(solution)/shard_map/ppermute | solution.py:45
  16.4 6.8 %collective-permute-start.1 = (bf16[128,512]{1,0:T(8,128)(2,1)S(1)}, bf16[128,512]{1,0:T(8,128)(2,1)S(1)}, u32[]{:S(2)}, u32[]{:S(2)}) collective-permute-start(bf16[128,512]{1,0:T(8,128)(2,1)S(1)} %get-tuple-element.25), channel_id=1, source_target_pairs={{0,16},{4,20},{8,24},{12,28},{16,0},{20,4},{24,8},{28,12},{1,17},{... | collective-permute-start | bytes 393224 | tf_op jit(solution)/shard_map/ppermute | solution.py:45
  23.1 3.2 %collective-permute-start.7 = (bf16[128,512]{1,0:T(8,128)(2,1)S(1)}, bf16[128,512]{1,0:T(8,128)(2,1)S(1)}, u32[]{:S(2)}, u32[]{:S(2)}) collective-permute-start(bf16[128,512]{1,0:T(8,128)(2,1)S(1)} %get-tuple-element.31), channel_id=1, source_target_pairs={{0,8},{4,12},{8,0},{12,4},{16,24},{20,28},{24,16},{28,20},{1,9},{5... | collective-permute-start | bytes 393224 | tf_op jit(solution)/shard_map/ppermute | solution.py:45
  26.6 1.1 %ahead.1.ahead_ref = bf16[3,128,512]{2,1,0:T(8,128)(2,1)S(1)} custom-call(bf16[128,512]{1,0:T(8,128)(2,1)S(1)} %collective-permute-done.4.refs_0_, bf16[128,512]{1,0:T(8,128)(2,1)} %collective-permute-done.5.refs_1_, bf16[128,512]{1,0:T(8,128)(2,1)} %collective-permute-done.6.refs_2_), custom_call_target="tpu_custom_call" | custom-call | flops 21474836480 | bytes 786432 | tf_op jit(solution)/shard_map/ahead/pallas_call | solution.py:253
  27.8 2.0 %gram.1.gram_ref.refs_2_ = bf16[1024,1024]{1,0:T(8,128)(2,1)S(1)} custom-call(s32[1]{0:T(128)} %bitcast.2.region_ref, s32[7]{0:T(128)S(1)} %pad_add_fusion.table_ref, bf16[5,128,1024]{2,1,0:T(8,128)(2,1)S(1)} %bitcast.13, bf16[5,128,1024]{2,1,0:T(8,128)(2,1)S(1)} %collective-permute-done.2.even, bf16[5,128,1024]{2,1,0:T(8,128)(2,1)S(1)} %collective-permute-done.3.odd), custom_call_target="tpu_custom_call" | custom-call | flops 805306368 | bytes 4194304 | tf_op jit(solution)/shard_map/gram/pallas_call | solution.py:234
  29.8 4.4 %collective-permute-done.7.refs_0_ = bf16[128,512]{1,0:T(8,128)(2,1)S(1)} collective-permute-done((bf16[128,512]{1,0:T(8,128)(2,1)S(1)}, bf16[128,512]{1,0:T(8,128)(2,1)S(1)}, u32[]{:S(2)}, u32[]{:S(2)}) %collective-permute-start.7) | collective-permute-done | bytes 131104 | tf_op jit(solution)/shard_map/ppermute | solution.py:45
  34.2 1.4 %early.1 = (f32[1024,512]{1,0:T(8,128)S(1)}, bf16[1024,512]{1,0:T(8,128)(2,1)S(1)}) custom-call(s32[1]{0:T(128)} %bitcast.me_ref, bf16[1024,1024]{1,0:T(8,128)(2,1)S(1)} %gram.1.gram_ref.refs_2_, bf16[3,128,512]{2,1,0:T(8,128)(2,1)S(1)} %ahead.1.ahead_ref, bf16[128,512]{1,0:T(8,128)(2,1)S(1)} %collective-permute-done.7.refs_0_, ...), custom_call_target="tpu_custom_call" | custom-call | flops 1 | bytes 1 | tf_op jit(solution)/shard_map/early/pallas_call | solution.py:262
  35.6 1.8 %late.1 = (bf16[128,512]{1,0:T(8,128)(2,1)S(1)}, bf16[128,512]{1,0:T(8,128)(2,1)S(1)}, bf16[128,512]{1,0:T(8,128)(2,1)S(1)}, bf16[128,512]{1,0:T(8,128)(2,1)S(1)...) custom-call(s32[1]{0:T(128)} %bitcast.me_ref, ...), custom_call_target="tpu_custom_call" | custom-call | flops 1610612736 | bytes 7340032 | tf_op jit(solution)/shard_map/late/pallas_call | solution.py:272
  37.4 1.2 %collective-permute-start.9 = (bf16[128,512]{1,0:T(8,128)(2,1)S(1)}, bf16[128,512]{1,0:T(8,128)(2,1)S(1)}, u32[]{:S(2)}, u32[]{:S(2)}) collective-permute-start(bf16[128,512]{1,0:T(8,128)(2,1)S(1)} %get-tuple-element.35), channel_id=1, source_target_pairs={{0,28},{4,24},{8,20},{12,16},{16,12},{20,8},{24,4},{28,0},{1,29},{... | collective-permute-start | bytes 393224 | tf_op jit(solution)/shard_map/ppermute | solution.py:45
  38.5 3.9 %collective-permute-start.11 = (bf16[128,512]{1,0:T(8,128)(2,1)S(1)}, bf16[128,512]{1,0:T(8,128)(2,1)S(1)}, u32[]{:S(2)}, u32[]{:S(2)}) collective-permute-start(bf16[128,512]{1,0:T(8,128)(2,1)S(1)} %get-tuple-element.37), channel_id=1, source_target_pairs={{0,24},{4,28},{8,16},{12,20},{16,8},{20,12},{24,0},{28,4},{1,25},{... | collective-permute-start | bytes 393224 | tf_op jit(solution)/shard_map/ppermute | solution.py:45
  42.5 0.8 %collective-permute-start.12 = (bf16[128,512]{1,0:T(8,128)(2,1)S(1)}, bf16[128,512]{1,0:T(8,128)(2,1)S(1)}, u32[]{:S(2)}, u32[]{:S(2)}) collective-permute-start(bf16[128,512]{1,0:T(8,128)(2,1)S(1)} %get-tuple-element.38), channel_id=1, source_target_pairs={{0,8},{4,12},{8,0},{12,4},{16,24},{20,28},{24,16},{28,20},{1,9},{5... | collective-permute-start | bytes 393224 | tf_op jit(solution)/shard_map/ppermute | solution.py:45
  43.9 2.4 %collective-permute-done.9.refs_0_ = bf16[128,512]{1,0:T(8,128)(2,1)S(1)} collective-permute-done((bf16[128,512]{1,0:T(8,128)(2,1)S(1)}, bf16[128,512]{1,0:T(8,128)(2,1)S(1)}, u32[]{:S(2)}, u32[]{:S(2)}) %collective-permute-start.9) | collective-permute-done | bytes 131104 | tf_op jit(solution)/shard_map/ppermute | solution.py:45
  46.4 1.9 %collective-permute-start.14 = (bf16[128,512]{1,0:T(8,128)(2,1)S(1)}, bf16[128,512]{1,0:T(8,128)(2,1)S(1)}, u32[]{:S(2)}, u32[]{:S(2)}) collective-permute-start(bf16[128,512]{1,0:T(8,128)(2,1)S(1)} %get-tuple-element.40), channel_id=1, source_target_pairs={{0,4},{4,0},{8,12},{12,8},{16,20},{20,16},{24,28},{28,24},{1,5},{5... | collective-permute-start | bytes 393224 | tf_op jit(solution)/shard_map/ppermute | solution.py:45
  48.3 1.3 %collective-permute-start.15 = (bf16[128,512]{1,0:T(8,128)(2,1)S(1)}, bf16[128,512]{1,0:T(8,128)(2,1)S(1)}, u32[]{:S(2)}, u32[]{:S(2)}) collective-permute-start(bf16[128,512]{1,0:T(8,128)(2,1)S(1)} %get-tuple-element.41), channel_id=1, source_target_pairs={{0,16},{4,20},{8,24},{12,28},{16,0},{20,4},{24,8},{28,12},{1,17},{... | collective-permute-start | bytes 393224 | tf_op jit(solution)/shard_map/ppermute | solution.py:45
  49.6 2.9 %collective-permute-done.11.refs_2_ = bf16[128,512]{1,0:T(8,128)(2,1)S(1)} collective-permute-done((bf16[128,512]{1,0:T(8,128)(2,1)S(1)}, bf16[128,512]{1,0:T(8,128)(2,1)S(1)}, u32[]{:S(2)}, u32[]{:S(2)}) %collective-permute-start.11) | collective-permute-done | bytes 131104 | tf_op jit(solution)/shard_map/ppermute | solution.py:45
  52.6 2.4 %collective-permute-done.12.refs_3_ = bf16[128,512]{1,0:T(8,128)(2,1)S(1)} collective-permute-done((bf16[128,512]{1,0:T(8,128)(2,1)S(1)}, bf16[128,512]{1,0:T(8,128)(2,1)S(1)}, u32[]{:S(2)}, u32[]{:S(2)}) %collective-permute-start.12) | collective-permute-done | bytes 131104 | tf_op jit(solution)/shard_map/ppermute | solution.py:45
  55.0 8.0 %collective-permute-done.15.refs_6_ = bf16[128,512]{1,0:T(8,128)(2,1)S(1)} collective-permute-done((bf16[128,512]{1,0:T(8,128)(2,1)S(1)}, bf16[128,512]{1,0:T(8,128)(2,1)S(1)}, u32[]{:S(2)}, u32[]{:S(2)}) %collective-permute-start.15) | collective-permute-done | bytes 131104 | tf_op jit(solution)/shard_map/ppermute | solution.py:45
  63.1 1.2 %merge.1 = bf16[1024,512]{1,0:T(8,128)(2,1)} custom-call(s32[1]{0:T(128)} %bitcast.me_ref, bf16[128,512]{1,0:T(8,128)(2,1)S(1)} %collective-permute-done.9.refs_0_, bf16[128,512]{1,0:T(8,128)(2,1)S(1)} %collective-permute-done.10.refs_1_, bf16[128,512]{1,0:T(8,128)(2,1)S(1)} %collective-permute-done.11.refs_2_, ...), custom_call_target="tpu_custom_call" | custom-call | flops 268435456 | bytes 2097152 | tf_op jit(solution)/shard_map/merge/pallas_call | solution.py:290
  (19 shorter events, 2.9 us)
Async XLA Ops:
  0.0 1.2 %copy-start.1 = (bf16[128,1,8,512]{3,2,1,0:T(8,128)(2,1)S(1)}, bf16[128,1,8,512]{3,2,1,0:T(8,128)(2,1)}, u32[]{:S(2)}) copy-start(bf16[128,1,8,512]{3,2,1,0:T(8,128)(2,1)} %param.5) | copy-start | bytes 3145732
  2.3 24.0 %collective-permute-start.3 = (bf16[5,128,1024]{2,1,0:T(8,128)(2,1)}, bf16[5,128,1024]{2,1,0:T(8,128)(2,1)S(1)}, u32[]{:S(2)}, u32[]{:S(2)}) collective-permute-start(bf16[5,128,1024]{2,1,0:T(8,128)(2,1)} %bitcast.11), channel_id=1, source_target_pairs={{1,2},{2,1},{5,6},{6,5},{9,10},{10,9},{13,14},{14,13},{17,18},{18,... | collective-permute-start | bytes 3932168 | tf_op jit(solution)/shard_map/ppermute | solution.py:205
  3.1 11.2 %collective-permute-start.4 = (bf16[128,512]{1,0:T(8,128)(2,1)}, bf16[128,512]{1,0:T(8,128)(2,1)S(1)}, u32[]{:S(2)}, u32[]{:S(2)}) collective-permute-start(bf16[128,512]{1,0:T(8,128)(2,1)} %get-tuple-element.28), channel_id=1, source_target_pairs={{0,12},{4,8},{8,4},{12,0},{16,28},{20,24},{24,20},{28,16},{1,13},{... | collective-permute-start | bytes 393224 | tf_op jit(solution)/shard_map/ppermute | solution.py:45
  7.1 9.3 %collective-permute-start.5 = (bf16[128,512]{1,0:T(8,128)(2,1)}, bf16[128,512]{1,0:T(8,128)(2,1)}, u32[]{:S(2)}, u32[]{:S(2)}) collective-permute-start(bf16[128,512]{1,0:T(8,128)(2,1)} %get-tuple-element.29), channel_id=1, source_target_pairs={{0,28},{4,24},{8,20},{12,16},{16,12},{20,8},{24,4},{28,0},{1,29},{... | collective-permute-start | bytes 393224 | tf_op jit(solution)/shard_map/ppermute | solution.py:45
  9.5 13.6 %collective-permute-start.6 = (bf16[128,512]{1,0:T(8,128)(2,1)S(1)}, bf16[128,512]{1,0:T(8,128)(2,1)}, u32[]{:S(2)}, u32[]{:S(2)}) collective-permute-start(bf16[128,512]{1,0:T(8,128)(2,1)S(1)} %get-tuple-element.30), channel_id=1, source_target_pairs={{0,24},{4,28},{8,16},{12,20},{16,8},{20,12},{24,0},{28,4},{1,25},{... | collective-permute-start | bytes 393224 | tf_op jit(solution)/shard_map/ppermute | solution.py:45
  10.9 16.8 %collective-permute-start.2 = (bf16[5,128,1024]{2,1,0:T(8,128)(2,1)}, bf16[5,128,1024]{2,1,0:T(8,128)(2,1)S(1)}, u32[]{:S(2)}, u32[]{:S(2)}) collective-permute-start(bf16[5,128,1024]{2,1,0:T(8,128)(2,1)} %bitcast.12), channel_id=1, source_target_pairs={{0,1},{2,3},{1,0},{3,2},{4,5},{6,7},{5,4},{7,6},{8,9},{10,11},{9,8... | collective-permute-start | bytes 3932168 | tf_op jit(solution)/shard_map/ppermute | solution.py:205
  14.2 21.3 %collective-permute-start = (bf16[128,512]{1,0:T(8,128)(2,1)S(1)}, bf16[128,512]{1,0:T(8,128)(2,1)S(1)}, u32[]{:S(2)}, u32[]{:S(2)}) collective-permute-start(bf16[128,512]{1,0:T(8,128)(2,1)S(1)} %get-tuple-element.24), channel_id=1, source_target_pairs={{0,20},{4,16},{8,28},{12,24},{16,4},{20,0},{24,12},{28,8},{1,21},{... | collective-permute-start | bytes 393224 | tf_op jit(solution)/shard_map/ppermute | solution.py:45
  16.4 19.2 %collective-permute-start.1 = (bf16[128,512]{1,0:T(8,128)(2,1)S(1)}, bf16[128,512]{1,0:T(8,128)(2,1)S(1)}, u32[]{:S(2)}, u32[]{:S(2)}) collective-permute-start(bf16[128,512]{1,0:T(8,128)(2,1)S(1)} %get-tuple-element.25), channel_id=1, source_target_pairs={{0,16},{4,20},{8,24},{12,28},{16,0},{20,4},{24,8},{28,12},{1,17},{... | collective-permute-start | bytes 393224 | tf_op jit(solution)/shard_map/ppermute | solution.py:45
  23.1 11.0 %collective-permute-start.7 = (bf16[128,512]{1,0:T(8,128)(2,1)S(1)}, bf16[128,512]{1,0:T(8,128)(2,1)S(1)}, u32[]{:S(2)}, u32[]{:S(2)}) collective-permute-start(bf16[128,512]{1,0:T(8,128)(2,1)S(1)} %get-tuple-element.31), channel_id=1, source_target_pairs={{0,8},{4,12},{8,0},{12,4},{16,24},{20,28},{24,16},{28,20},{1,9},{5... | collective-permute-start | bytes 393224 | tf_op jit(solution)/shard_map/ppermute | solution.py:45
  26.4 1.4 %copy-start = (bf16[1,1,5,128,1024]{4,3,2,1,0:T(8,128)(2,1)S(1)}, bf16[1,1,5,128,1024]{4,3,2,1,0:T(8,128)(2,1)}, u32[]{:S(2)}) copy-start(bf16[1,1,5,128,1024]{4,3,2,1,0:T(8,128)(2,1)} %param.6) | copy-start | bytes 3932164
  26.4 7.8 %collective-permute-start.8 = (bf16[128,512]{1,0:T(8,128)(2,1)S(1)}, bf16[128,512]{1,0:T(8,128)(2,1)S(1)}, u32[]{:S(2)}, u32[]{:S(2)}) collective-permute-start(bf16[128,512]{1,0:T(8,128)(2,1)S(1)} %get-tuple-element.32), channel_id=1, source_target_pairs={{0,4},{4,0},{8,12},{12,8},{16,20},{20,16},{24,28},{28,24},{1,5},{5... | collective-permute-start | bytes 393224 | tf_op jit(solution)/shard_map/ppermute | solution.py:45
  37.4 9.0 %collective-permute-start.9 = (bf16[128,512]{1,0:T(8,128)(2,1)S(1)}, bf16[128,512]{1,0:T(8,128)(2,1)S(1)}, u32[]{:S(2)}, u32[]{:S(2)}) collective-permute-start(bf16[128,512]{1,0:T(8,128)(2,1)S(1)} %get-tuple-element.35), channel_id=1, source_target_pairs={{0,28},{4,24},{8,20},{12,16},{16,12},{20,8},{24,4},{28,0},{1,29},{... | collective-permute-start | bytes 393224 | tf_op jit(solution)/shard_map/ppermute | solution.py:45
  38.5 9.8 %collective-permute-start.10 = (bf16[128,512]{1,0:T(8,128)(2,1)S(1)}, bf16[128,512]{1,0:T(8,128)(2,1)S(1)}, u32[]{:S(2)}, u32[]{:S(2)}) collective-permute-start(bf16[128,512]{1,0:T(8,128)(2,1)S(1)} %get-tuple-element.36), channel_id=1, source_target_pairs={{0,12},{4,8},{8,4},{12,0},{16,28},{20,24},{24,20},{28,16},{1,13},{... | collective-permute-start | bytes 393224 | tf_op jit(solution)/shard_map/ppermute | solution.py:45
  38.5 14.0 %collective-permute-start.11 = (bf16[128,512]{1,0:T(8,128)(2,1)S(1)}, bf16[128,512]{1,0:T(8,128)(2,1)S(1)}, u32[]{:S(2)}, u32[]{:S(2)}) collective-permute-start(bf16[128,512]{1,0:T(8,128)(2,1)S(1)} %get-tuple-element.37), channel_id=1, source_target_pairs={{0,24},{4,28},{8,16},{12,20},{16,8},{20,12},{24,0},{28,4},{1,25},{... | collective-permute-start | bytes 393224 | tf_op jit(solution)/shard_map/ppermute | solution.py:45
  42.5 12.5 %collective-permute-start.12 = (bf16[128,512]{1,0:T(8,128)(2,1)S(1)}, bf16[128,512]{1,0:T(8,128)(2,1)S(1)}, u32[]{:S(2)}, u32[]{:S(2)}) collective-permute-start(bf16[128,512]{1,0:T(8,128)(2,1)S(1)} %get-tuple-element.38), channel_id=1, source_target_pairs={{0,8},{4,12},{8,0},{12,4},{16,24},{20,28},{24,16},{28,20},{1,9},{5... | collective-permute-start | bytes 393224 | tf_op jit(solution)/shard_map/ppermute | solution.py:45
  43.3 11.7 %collective-permute-start.13 = (bf16[128,512]{1,0:T(8,128)(2,1)S(1)}, bf16[128,512]{1,0:T(8,128)(2,1)S(1)}, u32[]{:S(2)}, u32[]{:S(2)}) collective-permute-start(bf16[128,512]{1,0:T(8,128)(2,1)S(1)} %get-tuple-element.39), channel_id=1, source_target_pairs={{0,20},{4,16},{8,28},{12,24},{16,4},{20,0},{24,12},{28,8},{1,21},{... | collective-permute-start | bytes 393224 | tf_op jit(solution)/shard_map/ppermute | solution.py:45
  46.4 8.6 %collective-permute-start.14 = (bf16[128,512]{1,0:T(8,128)(2,1)S(1)}, bf16[128,512]{1,0:T(8,128)(2,1)S(1)}, u32[]{:S(2)}, u32[]{:S(2)}) collective-permute-start(bf16[128,512]{1,0:T(8,128)(2,1)S(1)} %get-tuple-element.40), channel_id=1, source_target_pairs={{0,4},{4,0},{8,12},{12,8},{16,20},{20,16},{24,28},{28,24},{1,5},{5... | collective-permute-start | bytes 393224 | tf_op jit(solution)/shard_map/ppermute | solution.py:45
  48.3 14.7 %collective-permute-start.15 = (bf16[128,512]{1,0:T(8,128)(2,1)S(1)}, bf16[128,512]{1,0:T(8,128)(2,1)S(1)}, u32[]{:S(2)}, u32[]{:S(2)}) collective-permute-start(bf16[128,512]{1,0:T(8,128)(2,1)S(1)} %get-tuple-element.41), channel_id=1, source_target_pairs={{0,16},{4,20},{8,24},{12,28},{16,0},{20,4},{24,8},{28,12},{1,17},{... | collective-permute-start | bytes 393224 | tf_op jit(solution)/shard_map/ppermute | solution.py:45

commit v13 on v11

--- a/solution.py
+++ b/solution.py
@@ -87,7 +87,7 @@
         copy.wait()
 
 
-def gram_kernel(scale, region_ref, table_ref, own, even, odd, gram_ref, stacked, sem):
+def gram_kernel(scale, region_ref, table_ref, own, odd, even, gram_ref, stacked, sem):
     slots = (table_ref.shape[0] - 1) // 2
     rows = own.shape[1]
     parity = lax.rem(region_ref[0], 2)
@@ -126,67 +126,37 @@
         gram_ref[step * part : (step + 1) * part, :] = (block * scale).astype(jnp.bfloat16)
 
 
-def block(me_ref, j, width, rows):
-    return pl.ds(pl.multiple_of((lax.div(me_ref[0], width) ^ j) * rows, rows), rows)
-
-
-def within(me_ref, k, quarter, rows):
-    return pl.ds(pl.multiple_of(lax.rem(me_ref[0] ^ k, quarter) * rows, rows), rows)
-
-
 def ahead_kernel(*refs):
-    out_ref = refs[-1]
-    for i, piece in enumerate(refs[:-1]):
-        out_ref[i] = piece[...]
-
-
-def early_kernel(steps, me_ref, gram_ref, ahead_ref, *refs):
-    piece_refs, (acc_ref, members_ref) = refs[:-2], refs[-2:]
-    rows = piece_refs[0].shape[0]
-    piece_refs = [ahead_ref.at[i] for i in range(ahead_ref.shape[0])] + list(piece_refs)
+    token = refs[-1]
+    token[...] = jnp.zeros(token.shape, token.dtype)
+
+
+def transform_kernel(steps, out_steps, me_ref, *refs):
+    count = len(steps)
+    pieces, outs = dict(zip(steps, refs)), dict(zip(out_steps, refs[count + 2 : -3]))
+    gram_ref = refs[count]
+    members, first, fresh = refs[-3:]
+    rows = pieces[0].shape[0]
+
+    def place(k):
+        return pl.ds(pl.multiple_of((me_ref[0] ^ k) * rows, rows), rows)
+
+    for k, piece in pieces.items():
+        members[place(k), :] = piece[...]
     size = gram_ref.shape[0]
-    there = block(me_ref, PARTS // 2, size // rows // PARTS, size // PARTS)
-    members_ref[there, :] = jnp.zeros((size // PARTS, members_ref.shape[1]), members_ref.dtype)
-    for k, piece in zip(steps, piece_refs):
-        members_ref[pl.ds(pl.multiple_of((me_ref[0] ^ k) * rows, rows), rows), :] = piece[...]
-    tall = size // 4
-    for step in range(4):
-        here = slice(step * tall, (step + 1) * tall)
-        acc_ref[here, :] = jnp.dot(
-            gram_ref[here, :], members_ref[...], preferred_element_type=jnp.float32
-        )
-
-
-def late_kernel(late_steps, out_steps, me_ref, *refs):
-    count = len(late_steps)
-    late_refs, outs = refs[:count], dict(zip(out_steps, refs[count + 3 : -3]))
-    gram_ref, acc_ref, members_ref = refs[count : count + 3]
-    first, late, fresh = refs[-3:]
-    rows = late_refs[0].shape[0]
-    size = gram_ref.shape[0]
-    width = late.shape[0] // rows
-    for k, piece in zip(late_steps, late_refs):
-        late[within(me_ref, k, width, rows), :] = piece[...]
-    there = block(me_ref, PARTS // 2, width, late.shape[0])
-    tall = size // 4
-    for step in range(4):
-        here = slice(step * tall, (step + 1) * tall)
-        part = jnp.dot(gram_ref[here, there], late[...], preferred_element_type=jnp.float32)
-        first[here, :] = (acc_ref[here, :] + part).astype(jnp.bfloat16)
-    quarter = tall // rows
-    for j in (3, 2, 1, 0):
-        there = block(me_ref, j, quarter, tall)
-        second = jnp.dot(gram_ref[there, :], first[...], preferred_element_type=jnp.float32)
-        rest = members_ref[there, :].astype(jnp.float32) - first[there, :].astype(jnp.float32)
-        fresh[...] = rest + second
-        for k in late_steps:
-            if k // quarter == j:
-                here = within(me_ref, k, quarter, rows)
-                fresh[here, :] += late[within(me_ref, k, width, rows), :].astype(jnp.float32)
-        for k, out_ref in outs.items():
-            if k // quarter == j:
-                here = within(me_ref, k, quarter, rows)
-                out_ref[...] = fresh[here, :].astype(jnp.bfloat16)
+    part = min(size, 256)
+    for step in range(size // part):
+        here = slice(step * part, (step + 1) * part)
+        first[here, :] = jnp.dot(
+            gram_ref[here, :], members[...], preferred_element_type=jnp.float32
+        ).astype(jnp.bfloat16)
+    for step in range(size // part):
+        here = slice(step * part, (step + 1) * part)
+        second = jnp.dot(gram_ref[here, :], first[...], preferred_element_type=jnp.float32)
+        rest = members[here, :].astype(jnp.float32) - first[here, :].astype(jnp.float32)
+        fresh[here, :] = (rest + second).astype(jnp.bfloat16)
+    for k, out_ref in outs.items():
+        out_ref[...] = fresh[place(k), :]
 
 
 def vmem():
@@ -215,7 +185,7 @@
     me = lax.axis_index("member").astype(jnp.int32).reshape(1)
     region = lax.axis_index("region").astype(jnp.int32).reshape(1)
     smem = pl.BlockSpec(memory_space=pltpu.SMEM)
-    hbm = pl.BlockSpec(memory_space=pltpu.HBM)
+    anywhere = pl.BlockSpec(memory_space=pl.ANY)
     piece_shape = jax.ShapeDtypeStruct((rows, values), jnp.bfloat16)
 
     steps = [0] + inward(patches)
@@ -236,7 +206,7 @@
     gram = pl.pallas_call(
         functools.partial(gram_kernel, 1.0 / (2.0 * size)),
         out_shape=jax.ShapeDtypeStruct((size, size), jnp.bfloat16),
-        in_specs=[smem] * 2 + [hbm] * 3,
+        in_specs=[smem] * 2 + [anywhere] * 3,
         out_specs=vmem(),
         scratch_shapes=[
             pltpu.VMEM((slots * store.shape[1], size), jnp.bfloat16),
@@ -245,46 +215,33 @@
         compiler_params=params(),
         cost_estimate=cost(2 * slots * store.shape[1] * size * size, 4 * size * size),
         name="gram",
-    )(region, table, store, even, odd)
-
-    early = [k for k in steps if k and not is_late(k, patches)]
-    late = [k for k in steps if is_late(k, patches)]
-    matrix = jax.ShapeDtypeStruct((size, values), jnp.bfloat16)
+    )(region, table, store, odd, even)
+
     count = patches // PARTS + 1
-    first_steps, early = early[:count], early[count:] + [0]
-    ahead = pl.pallas_call(
+    first_steps = steps[1 : count + 1]
+    token = pl.pallas_call(
         ahead_kernel,
-        out_shape=jax.ShapeDtypeStruct((count, rows, values), jnp.bfloat16),
-        in_specs=[vmem()] * count,
+        out_shape=jax.ShapeDtypeStruct((8, 128), jnp.float32),
+        in_specs=[anywhere] * count,
         out_specs=vmem(),
         compiler_params=params(),
         cost_estimate=cost(WEIGHT * size * size * values, 4 * count * rows * values),
         name="ahead",
     )(*[arrived[k] for k in first_steps])
-    acc, members = pl.pallas_call(
-        functools.partial(early_kernel, first_steps + early),
-        out_shape=[jax.ShapeDtypeStruct((size, values), jnp.float32), matrix],
-        in_specs=[smem] + [vmem()] * (2 + len(early)),
-        out_specs=[vmem()] * 2,
-        compiler_params=params(),
-        cost_estimate=cost(1, 1),
-        name="early",
-    )(me, gram, ahead, *[arrived[k] for k in early])
+    late = [k for k in steps if is_late(k, patches)]
+    middle = [k for k in steps[count + 1 :] if k not in late]
+    steps = late + middle + first_steps + [0]
     back = partners(patches) + [0]
     moved = pl.pallas_call(
-        functools.partial(late_kernel, late, back),
+        functools.partial(transform_kernel, steps, back),
         out_shape=[piece_shape] * patches,
-        in_specs=[smem] + [vmem()] * (3 + len(late)),
+        in_specs=[smem] + [vmem()] * (patches + 1) + [anywhere],
         out_specs=[vmem()] * patches,
-        scratch_shapes=[
-            pltpu.VMEM((size, values), jnp.bfloat16),
-            pltpu.VMEM((size // PARTS, values), jnp.bfloat16),
-            pltpu.VMEM((size // 4, values), jnp.float32),
-        ],
-        compiler_params=params(),
-        cost_estimate=cost(3 * size * size * values, 2 * size * size + 10 * size * values),
-        name="late",
-    )(me, *[arrived[k] for k in late], gram, acc, members)
+        scratch_shapes=[pltpu.VMEM((size, values), jnp.bfloat16)] * 3,
+        compiler_params=params(),
+        cost_estimate=cost(4 * size * size * values, 2 * size * size + 4 * size * values),
+        name="transform",
+    )(me, *[arrived[k] for k in steps], gram, token)
     order = back
     returned = [ppermute(piece, "member", k) for k, piece in zip(back, moved)]
 

time: 60.2 us -> 61.5 us (1.022)
  the two profiles are of different devices: /device:TPU:1 before, /device:TPU:0 now
where the time goes in v13:
time: 61.5 us; the launch traced here: 61.3 us
  starting transfers between devices  27.3 us (44%)
  waiting for transfers between devices  23.1 us (38%)
  Pallas kernels  6.92 us (11%)
  local copies, waits for them, and re-layouts  2.53 us (4%)
  other arithmetic  0.75 us (1%)
  between operations  0.71 us (1%)
    ppermute x14, starting transfers between devices, ppermute(): return lax.ppermute(value, axis, [(i, i ^ step) for i in range(count)])  24.3 us
    ppermute x14, waiting for transfers between devices, ppermute(): return lax.ppermute(value, axis, [(i, i ^ step) for i in range(count)])  23.1 us
    ppermute x2, starting transfers between devices, swap(): return lax.ppermute(store, 'region', pairs + [(j, i) for i, j in pairs])  3.03 us
    pallas_call x1, Pallas kernels, shards(): pl.pallas_call(functools.partial(transform_kernel, steps, back), out_shap...  2.53 us
    unnamed x6, local copies, waits for them, and re-layouts  2.53 us
    pallas_call x1, Pallas kernels, shards(): pl.pallas_call(functools.partial(gram_kernel, 1.0 / (2.0 * size)), out_sh...  1.99 us
    pallas_call x1, Pallas kernels, shards(): pl.pallas_call(functools.partial(merge_kernel, order), out_shape=jax.Shap...  1.23 us
  transfers between devices with their start and end apart: 16, of which 7 were waited for; matrix products, arithmetic and copies ran while one was open for 1% of the time, Pallas kernels for 3%

profile of v13, /device:TPU:0, one launch (start us, length us, event | category | flops | bytes accessed | tf_op | source)
XLA Modules:
  0.0 61.3 jit_solution(8689021299729517972)
XLA Ops:
  0.0 1.2 %copy-done.1 = bf16[128,1,8,512]{3,2,1,0:T(8,128)(2,1)S(1)} copy-done((bf16[128,1,8,512]{3,2,1,0:T(8,128)(2,1)S(1)}, bf16[128,1,8,512]{3,2,1,0:T(8,128)(2,1)}, u32[]{:S(2)}) %copy-start.1) | copy-done | bytes 1048600
  1.2 1.2 %split.1 = (bf16[128,512]{1,0:T(8,128)(2,1)S(1)}, bf16[128,512]{1,0:T(8,128)(2,1)}, bf16[128,512]{1,0:T(8,128)(2,1)}, bf16[128,512]{1,0:T(8,128)(2,1)}, bf16[128...) custom-call(s32[1]{0:T(128)} %bitcast.me_ref, ...), custom_call_target="tpu_custom_call" | custom-call | flops 268435456 | bytes 2097152 | tf_op jit(solution)/shard_map/split/pallas_call | solution.py:192
  3.0 0.7 %collective-permute-start.7 = (bf16[5,128,1024]{2,1,0:T(8,128)(2,1)}, bf16[5,128,1024]{2,1,0:T(8,128)(2,1)S(1)}, u32[]{:S(2)}, u32[]{:S(2)}) collective-permute-start(bf16[5,128,1024]{2,1,0:T(8,128)(2,1)} %bitcast.11), channel_id=1, source_target_pairs={{1,2},{2,1},{5,6},{6,5},{9,10},{10,9},{13,14},{14,13},{17,18},{18,... | collective-permute-start | bytes 3932168 | tf_op jit(solution)/shard_map/ppermute | solution.py:177
  3.8 6.0 %collective-permute-start.4 = (bf16[128,512]{1,0:T(8,128)(2,1)}, bf16[128,512]{1,0:T(8,128)(2,1)S(1)}, u32[]{:S(2)}, u32[]{:S(2)}) collective-permute-start(bf16[128,512]{1,0:T(8,128)(2,1)} %get-tuple-element.26), channel_id=1, source_target_pairs={{0,28},{4,24},{8,20},{12,16},{16,12},{20,8},{24,4},{28,0},{1,29},{... | collective-permute-start | bytes 393224 | tf_op jit(solution)/shard_map/ppermute | solution.py:47
  10.1 2.3 %collective-permute-start.8 = (bf16[5,128,1024]{2,1,0:T(8,128)(2,1)}, bf16[5,128,1024]{2,1,0:T(8,128)(2,1)S(1)}, u32[]{:S(2)}, u32[]{:S(2)}) collective-permute-start(bf16[5,128,1024]{2,1,0:T(8,128)(2,1)} %bitcast.12), channel_id=1, source_target_pairs={{0,1},{2,3},{1,0},{3,2},{4,5},{6,7},{5,4},{7,6},{8,9},{10,11},{9,8... | collective-permute-start | bytes 3932168 | tf_op jit(solution)/shard_map/ppermute | solution.py:177
  13.0 0.7 %pad_add_fusion.table_ref = s32[7]{0:T(128)S(1)} fusion(s32[1]{0:T(128)} %bitcast.10, s32[3]{0:T(128)} %bitcast.15, s32[3]{0:T(128)} %bitcast.16), kind=kLoop, calls=%fused_computation | loop fusion | flops 14 | bytes 56 | tf_op jit(solution)/shard_map/concatenate | solution.py:205
  13.8 4.7 %collective-permute-start = (bf16[128,512]{1,0:T(8,128)(2,1)}, bf16[128,512]{1,0:T(8,128)(2,1)S(1)}, u32[]{:S(2)}, u32[]{:S(2)}) collective-permute-start(bf16[128,512]{1,0:T(8,128)(2,1)} %copy-done.2), channel_id=1, source_target_pairs={{0,20},{4,16},{8,28},{12,24},{16,4},{20,0},{24,12},{28,8},{1,21},{... | collective-permute-start | bytes 393224 | tf_op jit(solution)/shard_map/ppermute | solution.py:47
  18.5 3.4 %collective-permute-start.1 = (bf16[128,512]{1,0:T(8,128)(2,1)S(1)}, bf16[128,512]{1,0:T(8,128)(2,1)S(1)}, u32[]{:S(2)}, u32[]{:S(2)}) collective-permute-start(bf16[128,512]{1,0:T(8,128)(2,1)S(1)} %get-tuple-element.23), channel_id=1, source_target_pairs={{0,16},{4,20},{8,24},{12,28},{16,0},{20,4},{24,8},{28,12},{1,17},{... | collective-permute-start | bytes 393224 | tf_op jit(solution)/shard_map/ppermute | solution.py:47
  22.0 0.6 %collective-permute-start.3 = (bf16[128,512]{1,0:T(8,128)(2,1)S(1)}, bf16[128,512]{1,0:T(8,128)(2,1)S(1)}, u32[]{:S(2)}, u32[]{:S(2)}) collective-permute-start(bf16[128,512]{1,0:T(8,128)(2,1)S(1)} %get-tuple-element.25), channel_id=1, source_target_pairs={{0,4},{4,0},{8,12},{12,8},{16,20},{20,16},{24,28},{28,24},{1,5},{5... | collective-permute-start | bytes 393224 | tf_op jit(solution)/shard_map/ppermute | solution.py:47
  22.6 0.7 %copy-done = bf16[1,1,5,128,1024]{4,3,2,1,0:T(8,128)(2,1)S(1)} copy-done((bf16[1,1,5,128,1024]{4,3,2,1,0:T(8,128)(2,1)S(1)}, bf16[1,1,5,128,1024]{4,3,2,1,0:T(8,128)(2,1)}, u32[]{:S(2)}) %copy-start) | copy-done | bytes 1310744
  23.3 2.0 %gram.1.refs_8_ = bf16[1024,1024]{1,0:T(8,128)(2,1)S(1)} custom-call(s32[1]{0:T(128)} %bitcast.2.region_ref, s32[7]{0:T(128)S(1)} %pad_add_fusion.table_ref, bf16[5,128,1024]{2,1,0:T(8,128)(2,1)S(1)} %bitcast.13, bf16[5,128,1024]{2,1,0:T(8,128)(2,1)S(1)} %collective-permute-done.7.odd, bf16[5,128,1024]{2,1,0:T(8,128)(2,1)S(1)} %collective-permute-done.8.even), custom_call_target="tpu_custom_call" | custom-call | flops 805306368 | bytes 4194304 | tf_op jit(solution)/shard_map/gram/pallas_call | solution.py:206
  25.3 6.9 %collective-permute-done.1.refs_1_ = bf16[128,512]{1,0:T(8,128)(2,1)S(1)} collective-permute-done((bf16[128,512]{1,0:T(8,128)(2,1)S(1)}, bf16[128,512]{1,0:T(8,128)(2,1)S(1)}, u32[]{:S(2)}, u32[]{:S(2)}) %collective-permute-start.1) | collective-permute-done | bytes 131104 | tf_op jit(solution)/shard_map/ppermute | solution.py:47
  32.2 2.5 %transform.1 = (bf16[128,512]{1,0:T(8,128)(2,1)S(1)}, bf16[128,512]{1,0:T(8,128)(2,1)S(1)}, bf16[128,512]{1,0:T(8,128)(2,1)S(1)}, bf16[128,512]{1,0:T(8,128)(2,1...) custom-call(s32[1]{0:T(128)} %bitcast.me_ref, ...), custom_call_target="tpu_custom_call" | custom-call | flops 2147483648 | bytes 4194304 | tf_op jit(solution)/shard_map/transform/pallas_call | solution.py:235
  34.7 0.8 %collective-permute-start.9 = (bf16[128,512]{1,0:T(8,128)(2,1)S(1)}, bf16[128,512]{1,0:T(8,128)(2,1)S(1)}, u32[]{:S(2)}, u32[]{:S(2)}) collective-permute-start(bf16[128,512]{1,0:T(8,128)(2,1)S(1)} %get-tuple-element.31), channel_id=1, source_target_pairs={{0,28},{4,24},{8,20},{12,16},{16,12},{20,8},{24,4},{28,0},{1,29},{... | collective-permute-start | bytes 393224 | tf_op jit(solution)/shard_map/ppermute | solution.py:47
  35.5 3.3 %collective-permute-start.11 = (bf16[128,512]{1,0:T(8,128)(2,1)S(1)}, bf16[128,512]{1,0:T(8,128)(2,1)S(1)}, u32[]{:S(2)}, u32[]{:S(2)}) collective-permute-start(bf16[128,512]{1,0:T(8,128)(2,1)S(1)} %get-tuple-element.33), channel_id=1, source_target_pairs={{0,24},{4,28},{8,16},{12,20},{16,8},{20,12},{24,0},{28,4},{1,25},{... | collective-permute-start | bytes 393224 | tf_op jit(solution)/shard_map/ppermute | solution.py:47
  38.7 1.9 %collective-permute-start.12 = (bf16[128,512]{1,0:T(8,128)(2,1)S(1)}, bf16[128,512]{1,0:T(8,128)(2,1)S(1)}, u32[]{:S(2)}, u32[]{:S(2)}) collective-permute-start(bf16[128,512]{1,0:T(8,128)(2,1)S(1)} %get-tuple-element.34), channel_id=1, source_target_pairs={{0,8},{4,12},{8,0},{12,4},{16,24},{20,28},{24,16},{28,20},{1,9},{5... | collective-permute-start | bytes 393224 | tf_op jit(solution)/shard_map/ppermute | solution.py:47
  40.6 1.9 %collective-permute-done.9.refs_0_ = bf16[128,512]{1,0:T(8,128)(2,1)S(1)} collective-permute-done((bf16[128,512]{1,0:T(8,128)(2,1)S(1)}, bf16[128,512]{1,0:T(8,128)(2,1)S(1)}, u32[]{:S(2)}, u32[]{:S(2)}) %collective-permute-start.9) | collective-permute-done | bytes 131104 | tf_op jit(solution)/shard_map/ppermute | solution.py:47
  42.5 0.7 %collective-permute-start.14 = (bf16[128,512]{1,0:T(8,128)(2,1)S(1)}, bf16[128,512]{1,0:T(8,128)(2,1)S(1)}, u32[]{:S(2)}, u32[]{:S(2)}) collective-permute-start(bf16[128,512]{1,0:T(8,128)(2,1)S(1)} %get-tuple-element.36), channel_id=1, source_target_pairs={{0,4},{4,0},{8,12},{12,8},{16,20},{20,16},{24,28},{28,24},{1,5},{5... | collective-permute-start | bytes 393224 | tf_op jit(solution)/shard_map/ppermute | solution.py:47
  43.2 2.6 %collective-permute-start.15 = (bf16[128,512]{1,0:T(8,128)(2,1)S(1)}, bf16[128,512]{1,0:T(8,128)(2,1)S(1)}, u32[]{:S(2)}, u32[]{:S(2)}) collective-permute-start(bf16[128,512]{1,0:T(8,128)(2,1)S(1)} %get-tuple-element.37), channel_id=1, source_target_pairs={{0,16},{4,20},{8,24},{12,28},{16,0},{20,4},{24,8},{28,12},{1,17},{... | collective-permute-start | bytes 393224 | tf_op jit(solution)/shard_map/ppermute | solution.py:47
  45.8 1.5 %collective-permute-done.11.refs_2_ = bf16[128,512]{1,0:T(8,128)(2,1)S(1)} collective-permute-done((bf16[128,512]{1,0:T(8,128)(2,1)S(1)}, bf16[128,512]{1,0:T(8,128)(2,1)S(1)}, u32[]{:S(2)}, u32[]{:S(2)}) %collective-permute-start.11) | collective-permute-done | bytes 131104 | tf_op jit(solution)/shard_map/ppermute | solution.py:47
  47.3 4.7 %collective-permute-done.12.refs_3_ = bf16[128,512]{1,0:T(8,128)(2,1)S(1)} collective-permute-done((bf16[128,512]{1,0:T(8,128)(2,1)S(1)}, bf16[128,512]{1,0:T(8,128)(2,1)S(1)}, u32[]{:S(2)}, u32[]{:S(2)}) %collective-permute-start.12) | collective-permute-done | bytes 131104 | tf_op jit(solution)/shard_map/ppermute | solution.py:47
  52.0 6.0 %collective-permute-done.13.refs_4_ = bf16[128,512]{1,0:T(8,128)(2,1)S(1)} collective-permute-done((bf16[128,512]{1,0:T(8,128)(2,1)S(1)}, bf16[128,512]{1,0:T(8,128)(2,1)S(1)}, u32[]{:S(2)}, u32[]{:S(2)}) %collective-permute-start.13) | collective-permute-done | bytes 131104 | tf_op jit(solution)/shard_map/ppermute | solution.py:47
  58.0 2.1 %collective-permute-done.15.refs_6_ = bf16[128,512]{1,0:T(8,128)(2,1)S(1)} collective-permute-done((bf16[128,512]{1,0:T(8,128)(2,1)S(1)}, bf16[128,512]{1,0:T(8,128)(2,1)S(1)}, u32[]{:S(2)}, u32[]{:S(2)}) %collective-permute-start.15) | collective-permute-done | bytes 131104 | tf_op jit(solution)/shard_map/ppermute | solution.py:47
  60.1 1.2 %merge.1 = bf16[1024,512]{1,0:T(8,128)(2,1)} custom-call(s32[1]{0:T(128)} %bitcast.me_ref, bf16[128,512]{1,0:T(8,128)(2,1)S(1)} %collective-permute-done.9.refs_0_, bf16[128,512]{1,0:T(8,128)(2,1)S(1)} %collective-permute-done.10.refs_1_, bf16[128,512]{1,0:T(8,128)(2,1)S(1)} %collective-permute-done.11.refs_2_, ...), custom_call_target="tpu_custom_call" | custom-call | flops 268435456 | bytes 2097152 | tf_op jit(solution)/shard_map/merge/pallas_call | solution.py:249
  (20 shorter events, 1.0 us)
Async XLA Ops:
  0.0 1.2 %copy-start.1 = (bf16[128,1,8,512]{3,2,1,0:T(8,128)(2,1)S(1)}, bf16[128,1,8,512]{3,2,1,0:T(8,128)(2,1)}, u32[]{:S(2)}) copy-start(bf16[128,1,8,512]{3,2,1,0:T(8,128)(2,1)} %param.5) | copy-start | bytes 3145732
  2.4 0.6 %copy-start.2 = (bf16[128,512]{1,0:T(8,128)(2,1)}, bf16[128,512]{1,0:T(8,128)(2,1)S(1)}, u32[]{:S(2)}) copy-start(bf16[128,512]{1,0:T(8,128)(2,1)S(1)} %get-tuple-element.22) | copy-start | bytes 393220
  3.0 18.9 %collective-permute-start.7 = (bf16[5,128,1024]{2,1,0:T(8,128)(2,1)}, bf16[5,128,1024]{2,1,0:T(8,128)(2,1)S(1)}, u32[]{:S(2)}, u32[]{:S(2)}) collective-permute-start(bf16[5,128,1024]{2,1,0:T(8,128)(2,1)} %bitcast.11), channel_id=1, source_target_pairs={{1,2},{2,1},{5,6},{6,5},{9,10},{10,9},{13,14},{14,13},{17,18},{18,... | collective-permute-start | bytes 3932168 | tf_op jit(solution)/shard_map/ppermute | solution.py:177
  3.8 10.0 %collective-permute-start.4 = (bf16[128,512]{1,0:T(8,128)(2,1)}, bf16[128,512]{1,0:T(8,128)(2,1)S(1)}, u32[]{:S(2)}, u32[]{:S(2)}) collective-permute-start(bf16[128,512]{1,0:T(8,128)(2,1)} %get-tuple-element.26), channel_id=1, source_target_pairs={{0,28},{4,24},{8,20},{12,16},{16,12},{20,8},{24,4},{28,0},{1,29},{... | collective-permute-start | bytes 393224 | tf_op jit(solution)/shard_map/ppermute | solution.py:47
  9.8 8.7 %collective-permute-start.5 = (bf16[128,512]{1,0:T(8,128)(2,1)}, bf16[128,512]{1,0:T(8,128)(2,1)S(1)}, u32[]{:S(2)}, u32[]{:S(2)}) collective-permute-start(bf16[128,512]{1,0:T(8,128)(2,1)} %get-tuple-element.27), channel_id=1, source_target_pairs={{0,24},{4,28},{8,16},{12,20},{16,8},{20,12},{24,0},{28,4},{1,25},{... | collective-permute-start | bytes 393224 | tf_op jit(solution)/shard_map/ppermute | solution.py:47
  10.1 11.9 %collective-permute-start.6 = (bf16[128,512]{1,0:T(8,128)(2,1)}, bf16[128,512]{1,0:T(8,128)(2,1)S(1)}, u32[]{:S(2)}, u32[]{:S(2)}) collective-permute-start(bf16[128,512]{1,0:T(8,128)(2,1)} %get-tuple-element.28), channel_id=1, source_target_pairs={{0,12},{4,8},{8,4},{12,0},{16,28},{20,24},{24,20},{28,16},{1,13},{... | collective-permute-start | bytes 393224 | tf_op jit(solution)/shard_map/ppermute | solution.py:47
  10.1 12.6 %collective-permute-start.8 = (bf16[5,128,1024]{2,1,0:T(8,128)(2,1)}, bf16[5,128,1024]{2,1,0:T(8,128)(2,1)S(1)}, u32[]{:S(2)}, u32[]{:S(2)}) collective-permute-start(bf16[5,128,1024]{2,1,0:T(8,128)(2,1)} %bitcast.12), channel_id=1, source_target_pairs={{0,1},{2,3},{1,0},{3,2},{4,5},{6,7},{5,4},{7,6},{8,9},{10,11},{9,8... | collective-permute-start | bytes 3932168 | tf_op jit(solution)/shard_map/ppermute | solution.py:177
  13.8 11.5 %collective-permute-start = (bf16[128,512]{1,0:T(8,128)(2,1)}, bf16[128,512]{1,0:T(8,128)(2,1)S(1)}, u32[]{:S(2)}, u32[]{:S(2)}) collective-permute-start(bf16[128,512]{1,0:T(8,128)(2,1)} %copy-done.2), channel_id=1, source_target_pairs={{0,20},{4,16},{8,28},{12,24},{16,4},{20,0},{24,12},{28,8},{1,21},{... | collective-permute-start | bytes 393224 | tf_op jit(solution)/shard_map/ppermute | solution.py:47
  18.5 13.7 %collective-permute-start.1 = (bf16[128,512]{1,0:T(8,128)(2,1)S(1)}, bf16[128,512]{1,0:T(8,128)(2,1)S(1)}, u32[]{:S(2)}, u32[]{:S(2)}) collective-permute-start(bf16[128,512]{1,0:T(8,128)(2,1)S(1)} %get-tuple-element.23), channel_id=1, source_target_pairs={{0,16},{4,20},{8,24},{12,28},{16,0},{20,4},{24,8},{28,12},{1,17},{... | collective-permute-start | bytes 393224 | tf_op jit(solution)/shard_map/ppermute | solution.py:47
  21.9 10.2 %collective-permute-start.2 = (bf16[128,512]{1,0:T(8,128)(2,1)S(1)}, bf16[128,512]{1,0:T(8,128)(2,1)S(1)}, u32[]{:S(2)}, u32[]{:S(2)}) collective-permute-start(bf16[128,512]{1,0:T(8,128)(2,1)S(1)} %get-tuple-element.24), channel_id=1, source_target_pairs={{0,8},{4,12},{8,0},{12,4},{16,24},{20,28},{24,16},{28,20},{1,9},{5... | collective-permute-start | bytes 393224 | tf_op jit(solution)/shard_map/ppermute | solution.py:47
  21.9 1.3 %copy-start = (bf16[1,1,5,128,1024]{4,3,2,1,0:T(8,128)(2,1)S(1)}, bf16[1,1,5,128,1024]{4,3,2,1,0:T(8,128)(2,1)}, u32[]{:S(2)}) copy-start(bf16[1,1,5,128,1024]{4,3,2,1,0:T(8,128)(2,1)} %param.6) | copy-start | bytes 3932164
  22.0 10.2 %collective-permute-start.3 = (bf16[128,512]{1,0:T(8,128)(2,1)S(1)}, bf16[128,512]{1,0:T(8,128)(2,1)S(1)}, u32[]{:S(2)}, u32[]{:S(2)}) collective-permute-start(bf16[128,512]{1,0:T(8,128)(2,1)S(1)} %get-tuple-element.25), channel_id=1, source_target_pairs={{0,4},{4,0},{8,12},{12,8},{16,20},{20,16},{24,28},{28,24},{1,5},{5... | collective-permute-start | bytes 393224 | tf_op jit(solution)/shard_map/ppermute | solution.py:47
  34.7 7.8 %collective-permute-start.9 = (bf16[128,512]{1,0:T(8,128)(2,1)S(1)}, bf16[128,512]{1,0:T(8,128)(2,1)S(1)}, u32[]{:S(2)}, u32[]{:S(2)}) collective-permute-start(bf16[128,512]{1,0:T(8,128)(2,1)S(1)} %get-tuple-element.31), channel_id=1, source_target_pairs={{0,28},{4,24},{8,20},{12,16},{16,12},{20,8},{24,4},{28,0},{1,29},{... | collective-permute-start | bytes 393224 | tf_op jit(solution)/shard_map/ppermute | solution.py:47
  35.5 7.8 %collective-permute-start.10 = (bf16[128,512]{1,0:T(8,128)(2,1)S(1)}, bf16[128,512]{1,0:T(8,128)(2,1)S(1)}, u32[]{:S(2)}, u32[]{:S(2)}) collective-permute-start(bf16[128,512]{1,0:T(8,128)(2,1)S(1)} %get-tuple-element.32), channel_id=1, source_target_pairs={{0,12},{4,8},{8,4},{12,0},{16,28},{20,24},{24,20},{28,16},{1,13},{... | collective-permute-start | bytes 393224 | tf_op jit(solution)/shard_map/ppermute | solution.py:47
  35.5 11.8 %collective-permute-start.11 = (bf16[128,512]{1,0:T(8,128)(2,1)S(1)}, bf16[128,512]{1,0:T(8,128)(2,1)S(1)}, u32[]{:S(2)}, u32[]{:S(2)}) collective-permute-start(bf16[128,512]{1,0:T(8,128)(2,1)S(1)} %get-tuple-element.33), channel_id=1, source_target_pairs={{0,24},{4,28},{8,16},{12,20},{16,8},{20,12},{24,0},{28,4},{1,25},{... | collective-permute-start | bytes 393224 | tf_op jit(solution)/shard_map/ppermute | solution.py:47
  38.7 13.3 %collective-permute-start.12 = (bf16[128,512]{1,0:T(8,128)(2,1)S(1)}, bf16[128,512]{1,0:T(8,128)(2,1)S(1)}, u32[]{:S(2)}, u32[]{:S(2)}) collective-permute-start(bf16[128,512]{1,0:T(8,128)(2,1)S(1)} %get-tuple-element.34), channel_id=1, source_target_pairs={{0,8},{4,12},{8,0},{12,4},{16,24},{20,28},{24,16},{28,20},{1,9},{5... | collective-permute-start | bytes 393224 | tf_op jit(solution)/shard_map/ppermute | solution.py:47
  40.6 17.4 %collective-permute-start.13 = (bf16[128,512]{1,0:T(8,128)(2,1)S(1)}, bf16[128,512]{1,0:T(8,128)(2,1)S(1)}, u32[]{:S(2)}, u32[]{:S(2)}) collective-permute-start(bf16[128,512]{1,0:T(8,128)(2,1)S(1)} %get-tuple-element.35), channel_id=1, source_target_pairs={{0,20},{4,16},{8,28},{12,24},{16,4},{20,0},{24,12},{28,8},{1,21},{... | collective-permute-start | bytes 393224 | tf_op jit(solution)/shard_map/ppermute | solution.py:47
  42.5 15.5 %collective-permute-start.14 = (bf16[128,512]{1,0:T(8,128)(2,1)S(1)}, bf16[128,512]{1,0:T(8,128)(2,1)S(1)}, u32[]{:S(2)}, u32[]{:S(2)}) collective-permute-start(bf16[128,512]{1,0:T(8,128)(2,1)S(1)} %get-tuple-element.36), channel_id=1, source_target_pairs={{0,4},{4,0},{8,12},{12,8},{16,20},{20,16},{24,28},{28,24},{1,5},{5... | collective-permute-start | bytes 393224 | tf_op jit(solution)/shard_map/ppermute | solution.py:47
  43.2 16.9 %collective-permute-start.15 = (bf16[128,512]{1,0:T(8,128)(2,1)S(1)}, bf16[128,512]{1,0:T(8,128)(2,1)S(1)}, u32[]{:S(2)}, u32[]{:S(2)}) collective-permute-start(bf16[128,512]{1,0:T(8,128)(2,1)S(1)} %get-tuple-element.37), channel_id=1, source_target_pairs={{0,16},{4,20},{8,24},{12,28},{16,0},{20,4},{24,8},{28,12},{1,17},{... | collective-permute-start | bytes 393224 | tf_op jit(solution)/shard_map/ppermute | solution.py:47

commit v14 on v11

--- a/solution.py
+++ b/solution.py
@@ -47,7 +47,9 @@
     return lax.ppermute(value, axis, [(i, i ^ step) for i in range(count)])
 
 
-def split_kernel(steps, me_ref, members_ref, *out_refs):
+def split_kernel(steps, me_ref, members_ref, *refs):
+    out_refs, token = refs[:-1], refs[-1]
+    token[...] = jnp.zeros(token.shape, token.dtype)
     patches = len(steps)
     rows = out_refs[0].shape[0]
     group = rows_per_group(rows, patches)
@@ -135,15 +137,12 @@
 
 
 def ahead_kernel(*refs):
-    out_ref = refs[-1]
-    for i, piece in enumerate(refs[:-1]):
-        out_ref[i] = piece[...]
-
-
-def early_kernel(steps, me_ref, gram_ref, ahead_ref, *refs):
+    refs[-1][...] = refs[0][...]
+
+
+def early_kernel(steps, me_ref, gram_ref, token, *refs):
     piece_refs, (acc_ref, members_ref) = refs[:-2], refs[-2:]
     rows = piece_refs[0].shape[0]
-    piece_refs = [ahead_ref.at[i] for i in range(ahead_ref.shape[0])] + list(piece_refs)
     size = gram_ref.shape[0]
     there = block(me_ref, PARTS // 2, size // rows // PARTS, size // PARTS)
     members_ref[there, :] = jnp.zeros((size // PARTS, members_ref.shape[1]), members_ref.dtype)
@@ -215,28 +214,29 @@
     me = lax.axis_index("member").astype(jnp.int32).reshape(1)
     region = lax.axis_index("region").astype(jnp.int32).reshape(1)
     smem = pl.BlockSpec(memory_space=pltpu.SMEM)
-    hbm = pl.BlockSpec(memory_space=pltpu.HBM)
+    anywhere = pl.BlockSpec(memory_space=pl.ANY)
     piece_shape = jax.ShapeDtypeStruct((rows, values), jnp.bfloat16)
 
     steps = [0] + inward(patches)
-    pieces = pl.pallas_call(
+    mark = jax.ShapeDtypeStruct((8, 128), jnp.float32)
+    *pieces, token = pl.pallas_call(
         functools.partial(split_kernel, steps),
-        out_shape=[piece_shape] * patches,
+        out_shape=[piece_shape] * patches + [mark],
         in_specs=[smem, vmem()],
-        out_specs=[vmem()] * patches,
+        out_specs=[vmem()] * (patches + 1),
         compiler_params=params(),
         cost_estimate=cost(2 * 256 * rows * patches * values, 4 * rows * patches * values),
         name="split",
     )(me, ensemble.reshape(rows * patches, values))
     arrived = {k: ppermute(piece, "member", k) for k, piece in zip(steps, pieces)}
-    store, _ = lax.optimization_barrier((store, pieces[0]))
+    store, token = lax.optimization_barrier((store, token))
     odd, even = swap(store, 1), swap(store, 0)
 
     table = jnp.concatenate([block_ids.ravel(), block_src.ravel(), block_count.ravel()])
     gram = pl.pallas_call(
         functools.partial(gram_kernel, 1.0 / (2.0 * size)),
         out_shape=jax.ShapeDtypeStruct((size, size), jnp.bfloat16),
-        in_specs=[smem] * 2 + [hbm] * 3,
+        in_specs=[smem] * 2 + [anywhere] * 3,
         out_specs=vmem(),
         scratch_shapes=[
             pltpu.VMEM((slots * store.shape[1], size), jnp.bfloat16),
@@ -251,25 +251,25 @@
     late = [k for k in steps if is_late(k, patches)]
     matrix = jax.ShapeDtypeStruct((size, values), jnp.bfloat16)
     count = patches // PARTS + 1
-    first_steps, early = early[:count], early[count:] + [0]
-    ahead = pl.pallas_call(
+    first_steps, early = early[:count], early + [0]
+    token = pl.pallas_call(
         ahead_kernel,
-        out_shape=jax.ShapeDtypeStruct((count, rows, values), jnp.bfloat16),
-        in_specs=[vmem()] * count,
+        out_shape=mark,
+        in_specs=[vmem()] + [anywhere] * count,
         out_specs=vmem(),
         compiler_params=params(),
         cost_estimate=cost(WEIGHT * size * size * values, 4 * count * rows * values),
         name="ahead",
-    )(*[arrived[k] for k in first_steps])
+    )(token, *[arrived[k] for k in first_steps])
     acc, members = pl.pallas_call(
-        functools.partial(early_kernel, first_steps + early),
+        functools.partial(early_kernel, early),
         out_shape=[jax.ShapeDtypeStruct((size, values), jnp.float32), matrix],
-        in_specs=[smem] + [vmem()] * (2 + len(early)),
+        in_specs=[smem, vmem(), anywhere] + [vmem()] * len(early),
         out_specs=[vmem()] * 2,
         compiler_params=params(),
         cost_estimate=cost(1, 1),
         name="early",
-    )(me, gram, ahead, *[arrived[k] for k in early])
+    )(me, gram, token, *[arrived[k] for k in early])
     back = partners(patches) + [0]
     moved = pl.pallas_call(
         functools.partial(late_kernel, late, back),

time: 60.2 us -> 60.9 us (1.012)
  the two profiles are of different devices: /device:TPU:1 before, /device:TPU:0 now
where the time goes in v14:
time: 60.9 us; the launch traced here: 59.8 us
  starting transfers between devices  28.9 us (47%)
  waiting for transfers between devices  19.3 us (32%)
  Pallas kernels  7.55 us (12%)
  local copies, waits for them, and re-layouts  2.52 us (4%)
  other arithmetic  0.75 us (1%)
  between operations  0.72 us (1%)
    ppermute x14, starting transfers between devices, ppermute(): return lax.ppermute(value, axis, [(i, i ^ step) for i in range(count)])  25.9 us
    ppermute x14, waiting for transfers between devices, ppermute(): return lax.ppermute(value, axis, [(i, i ^ step) for i in range(count)])  19.3 us
    ppermute x2, starting transfers between devices, swap(): return lax.ppermute(store, 'region', pairs + [(j, i) for i, j in pairs])  3.03 us
    unnamed x6, local copies, waits for them, and re-layouts  2.52 us
    pallas_call x1, Pallas kernels, shards(): pl.pallas_call(functools.partial(gram_kernel, 1.0 / (2.0 * size)), out_sh...  1.99 us
    pallas_call x1, Pallas kernels, shards(): pl.pallas_call(functools.partial(late_kernel, late, back), out_shape=[pie...  1.81 us
    pallas_call x1, Pallas kernels, shards(): pl.pallas_call(functools.partial(early_kernel, early), out_shape=[jax.Sha...  1.35 us
    pallas_call x1, Pallas kernels, shards(): pl.pallas_call(functools.partial(merge_kernel, order), out_shape=jax.Shap...  1.23 us
  transfers between devices with their start and end apart: 16, of which 6 were waited for; matrix products, arithmetic and copies ran while one was open for 1% of the time, Pallas kernels for 6%

profile of v14, /device:TPU:0, one launch (start us, length us, event | category | flops | bytes accessed | tf_op | source)
XLA Modules:
  0.0 59.8 jit_solution(17336995440001598659)
XLA Ops:
  0.0 1.2 %copy-done.1 = bf16[128,1,8,512]{3,2,1,0:T(8,128)(2,1)S(1)} copy-done((bf16[128,1,8,512]{3,2,1,0:T(8,128)(2,1)S(1)}, bf16[128,1,8,512]{3,2,1,0:T(8,128)(2,1)}, u32[]{:S(2)}) %copy-start.1) | copy-done | bytes 1048600
  1.2 1.2 %split.1 = (bf16[128,512]{1,0:T(8,128)(2,1)S(1)}, bf16[128,512]{1,0:T(8,128)(2,1)}, bf16[128,512]{1,0:T(8,128)(2,1)}, bf16[128,512]{1,0:T(8,128)(2,1)}, bf16[128...) custom-call(s32[1]{0:T(128)} %bitcast.me_ref, ...), custom_call_target="tpu_custom_call" | custom-call | flops 268435456 | bytes 2097152 | tf_op jit(solution)/shard_map/split/pallas_call | solution.py:222
  3.0 0.7 %collective-permute-start.3 = (bf16[5,128,1024]{2,1,0:T(8,128)(2,1)}, bf16[5,128,1024]{2,1,0:T(8,128)(2,1)S(1)}, u32[]{:S(2)}, u32[]{:S(2)}) collective-permute-start(bf16[5,128,1024]{2,1,0:T(8,128)(2,1)} %bitcast.11), channel_id=1, source_target_pairs={{1,2},{2,1},{5,6},{6,5},{9,10},{10,9},{13,14},{14,13},{17,18},{18,... | collective-permute-start | bytes 3932168 | tf_op jit(solution)/shard_map/ppermute | solution.py:206
  3.8 6.0 %collective-permute-start.4 = (bf16[128,512]{1,0:T(8,128)(2,1)}, bf16[128,512]{1,0:T(8,128)(2,1)S(1)}, u32[]{:S(2)}, u32[]{:S(2)}) collective-permute-start(bf16[128,512]{1,0:T(8,128)(2,1)} %get-tuple-element.31), channel_id=1, source_target_pairs={{0,28},{4,24},{8,20},{12,16},{16,12},{20,8},{24,4},{28,0},{1,29},{... | collective-permute-start | bytes 393224 | tf_op jit(solution)/shard_map/ppermute | solution.py:47
  10.1 2.3 %collective-permute-start.2 = (bf16[5,128,1024]{2,1,0:T(8,128)(2,1)}, bf16[5,128,1024]{2,1,0:T(8,128)(2,1)S(1)}, u32[]{:S(2)}, u32[]{:S(2)}) collective-permute-start(bf16[5,128,1024]{2,1,0:T(8,128)(2,1)} %bitcast.12), channel_id=1, source_target_pairs={{0,1},{2,3},{1,0},{3,2},{4,5},{6,7},{5,4},{7,6},{8,9},{10,11},{9,8... | collective-permute-start | bytes 3932168 | tf_op jit(solution)/shard_map/ppermute | solution.py:206
  13.0 0.7 %pad_add_fusion.table_ref = s32[7]{0:T(128)S(1)} fusion(s32[1]{0:T(128)} %bitcast.10, s32[3]{0:T(128)} %bitcast.15, s32[3]{0:T(128)} %bitcast.16), kind=kLoop, calls=%fused_computation | loop fusion | flops 14 | bytes 56 | tf_op jit(solution)/shard_map/concatenate | solution.py:235
  13.8 4.7 %collective-permute-start = (bf16[128,512]{1,0:T(8,128)(2,1)S(1)}, bf16[128,512]{1,0:T(8,128)(2,1)S(1)}, u32[]{:S(2)}, u32[]{:S(2)}) collective-permute-start(bf16[128,512]{1,0:T(8,128)(2,1)S(1)} %get-tuple-element.26), channel_id=1, source_target_pairs={{0,20},{4,16},{8,28},{12,24},{16,4},{20,0},{24,12},{28,8},{1,21},{... | collective-permute-start | bytes 393224 | tf_op jit(solution)/shard_map/ppermute | solution.py:47
  18.5 3.4 %collective-permute-start.1 = (bf16[128,512]{1,0:T(8,128)(2,1)S(1)}, bf16[128,512]{1,0:T(8,128)(2,1)S(1)}, u32[]{:S(2)}, u32[]{:S(2)}) collective-permute-start(bf16[128,512]{1,0:T(8,128)(2,1)S(1)} %get-tuple-element.27), channel_id=1, source_target_pairs={{0,16},{4,20},{8,24},{12,28},{16,0},{20,4},{24,8},{28,12},{1,17},{... | collective-permute-start | bytes 393224 | tf_op jit(solution)/shard_map/ppermute | solution.py:47
  22.6 0.7 %copy-done = bf16[1,1,5,128,1024]{4,3,2,1,0:T(8,128)(2,1)S(1)} copy-done((bf16[1,1,5,128,1024]{4,3,2,1,0:T(8,128)(2,1)S(1)}, bf16[1,1,5,128,1024]{4,3,2,1,0:T(8,128)(2,1)}, u32[]{:S(2)}) %copy-start) | copy-done | bytes 1310744
  23.3 2.0 %gram.1.gram_ref.refs_2_ = bf16[1024,1024]{1,0:T(8,128)(2,1)S(1)} custom-call(s32[1]{0:T(128)} %bitcast.2.region_ref, s32[7]{0:T(128)S(1)} %pad_add_fusion.table_ref, bf16[5,128,1024]{2,1,0:T(8,128)(2,1)S(1)} %bitcast.13, bf16[5,128,1024]{2,1,0:T(8,128)(2,1)S(1)} %collective-permute-done.2.even, bf16[5,128,1024]{2,1,0:T(8,128)(2,1)S(1)} %collective-permute-done.3.odd), custom_call_target="tpu_custom_call" | custom-call | flops 805306368 | bytes 4194304 | tf_op jit(solution)/shard_map/gram/pallas_call | solution.py:236
  25.3 2.1 %collective-permute-done.7.refs_3_ = bf16[128,512]{1,0:T(8,128)(2,1)S(1)} collective-permute-done((bf16[128,512]{1,0:T(8,128)(2,1)}, bf16[128,512]{1,0:T(8,128)(2,1)S(1)}, u32[]{:S(2)}, u32[]{:S(2)}) %collective-permute-start.7) | collective-permute-done | bytes 131104 | tf_op jit(solution)/shard_map/ppermute | solution.py:47
  27.4 1.4 %early.1 = (f32[1024,512]{1,0:T(8,128)S(1)}, bf16[1024,512]{1,0:T(8,128)(2,1)S(1)}) custom-call(s32[1]{0:T(128)} %bitcast.me_ref, bf16[1024,1024]{1,0:T(8,128)(2,1)S(1)} %gram.1.gram_ref.refs_2_, f32[8,128]{1,0:T(8,128)S(1)} %ahead.1.token, bf16[128,512]{1,0:T(8,128)(2,1)S(1)} %collective-permute-done.4.refs_1_.refs_0_, ...), custom_call_target="tpu_custom_call" | custom-call | flops 1 | bytes 1 | tf_op jit(solution)/shard_map/early/pallas_call | solution.py:264
  28.7 1.9 %collective-permute-done.1.refs_1_ = bf16[128,512]{1,0:T(8,128)(2,1)S(1)} collective-permute-done((bf16[128,512]{1,0:T(8,128)(2,1)S(1)}, bf16[128,512]{1,0:T(8,128)(2,1)S(1)}, u32[]{:S(2)}, u32[]{:S(2)}) %collective-permute-start.1) | collective-permute-done | bytes 131104 | tf_op jit(solution)/shard_map/ppermute | solution.py:47
  30.7 1.8 %late.1 = (bf16[128,512]{1,0:T(8,128)(2,1)S(1)}, bf16[128,512]{1,0:T(8,128)(2,1)S(1)}, bf16[128,512]{1,0:T(8,128)(2,1)S(1)}, bf16[128,512]{1,0:T(8,128)(2,1)S(1)...) custom-call(s32[1]{0:T(128)} %bitcast.me_ref, ...), custom_call_target="tpu_custom_call" | custom-call | flops 1610612736 | bytes 7340032 | tf_op jit(solution)/shard_map/late/pallas_call | solution.py:274
  32.5 2.0 %collective-permute-start.9 = (bf16[128,512]{1,0:T(8,128)(2,1)S(1)}, bf16[128,512]{1,0:T(8,128)(2,1)S(1)}, u32[]{:S(2)}, u32[]{:S(2)}) collective-permute-start(bf16[128,512]{1,0:T(8,128)(2,1)S(1)} %get-tuple-element.39), channel_id=1, source_target_pairs={{0,28},{4,24},{8,20},{12,16},{16,12},{20,8},{24,4},{28,0},{1,29},{... | collective-permute-start | bytes 393224 | tf_op jit(solution)/shard_map/ppermute | solution.py:47
  34.5 0.8 %collective-permute-start.10 = (bf16[128,512]{1,0:T(8,128)(2,1)S(1)}, bf16[128,512]{1,0:T(8,128)(2,1)S(1)}, u32[]{:S(2)}, u32[]{:S(2)}) collective-permute-start(bf16[128,512]{1,0:T(8,128)(2,1)S(1)} %get-tuple-element.40), channel_id=1, source_target_pairs={{0,12},{4,8},{8,4},{12,0},{16,28},{20,24},{24,20},{28,16},{1,13},{... | collective-permute-start | bytes 393224 | tf_op jit(solution)/shard_map/ppermute | solution.py:47
  35.3 1.5 %collective-permute-start.11 = (bf16[128,512]{1,0:T(8,128)(2,1)S(1)}, bf16[128,512]{1,0:T(8,128)(2,1)S(1)}, u32[]{:S(2)}, u32[]{:S(2)}) collective-permute-start(bf16[128,512]{1,0:T(8,128)(2,1)S(1)} %get-tuple-element.41), channel_id=1, source_target_pairs={{0,24},{4,28},{8,16},{12,20},{16,8},{20,12},{24,0},{28,4},{1,25},{... | collective-permute-start | bytes 393224 | tf_op jit(solution)/shard_map/ppermute | solution.py:47
  36.8 1.6 %collective-permute-start.12 = (bf16[128,512]{1,0:T(8,128)(2,1)S(1)}, bf16[128,512]{1,0:T(8,128)(2,1)S(1)}, u32[]{:S(2)}, u32[]{:S(2)}) collective-permute-start(bf16[128,512]{1,0:T(8,128)(2,1)S(1)} %get-tuple-element.42), channel_id=1, source_target_pairs={{0,8},{4,12},{8,0},{12,4},{16,24},{20,28},{24,16},{28,20},{1,9},{5... | collective-permute-start | bytes 393224 | tf_op jit(solution)/shard_map/ppermute | solution.py:47
  38.4 2.3 %collective-permute-start.13 = (bf16[128,512]{1,0:T(8,128)(2,1)S(1)}, bf16[128,512]{1,0:T(8,128)(2,1)S(1)}, u32[]{:S(2)}, u32[]{:S(2)}) collective-permute-start(bf16[128,512]{1,0:T(8,128)(2,1)S(1)} %get-tuple-element.43), channel_id=1, source_target_pairs={{0,20},{4,16},{8,28},{12,24},{16,4},{20,0},{24,12},{28,8},{1,21},{... | collective-permute-start | bytes 393224 | tf_op jit(solution)/shard_map/ppermute | solution.py:47
  41.6 2.1 %collective-permute-start.15 = (bf16[128,512]{1,0:T(8,128)(2,1)S(1)}, bf16[128,512]{1,0:T(8,128)(2,1)S(1)}, u32[]{:S(2)}, u32[]{:S(2)}) collective-permute-start(bf16[128,512]{1,0:T(8,128)(2,1)S(1)} %get-tuple-element.45), channel_id=1, source_target_pairs={{0,16},{4,20},{8,24},{12,28},{16,0},{20,4},{24,8},{28,12},{1,17},{... | collective-permute-start | bytes 393224 | tf_op jit(solution)/shard_map/ppermute | solution.py:47
  43.7 2.4 %collective-permute-done.12.refs_3_ = bf16[128,512]{1,0:T(8,128)(2,1)S(1)} collective-permute-done((bf16[128,512]{1,0:T(8,128)(2,1)S(1)}, bf16[128,512]{1,0:T(8,128)(2,1)S(1)}, u32[]{:S(2)}, u32[]{:S(2)}) %collective-permute-start.12) | collective-permute-done | bytes 131104 | tf_op jit(solution)/shard_map/ppermute | solution.py:47
  46.1 5.9 %collective-permute-done.13.refs_4_ = bf16[128,512]{1,0:T(8,128)(2,1)S(1)} collective-permute-done((bf16[128,512]{1,0:T(8,128)(2,1)S(1)}, bf16[128,512]{1,0:T(8,128)(2,1)S(1)}, u32[]{:S(2)}, u32[]{:S(2)}) %collective-permute-start.13) | collective-permute-done | bytes 131104 | tf_op jit(solution)/shard_map/ppermute | solution.py:47
  52.0 6.5 %collective-permute-done.15.refs_6_ = bf16[128,512]{1,0:T(8,128)(2,1)S(1)} collective-permute-done((bf16[128,512]{1,0:T(8,128)(2,1)S(1)}, bf16[128,512]{1,0:T(8,128)(2,1)S(1)}, u32[]{:S(2)}, u32[]{:S(2)}) %collective-permute-start.15) | collective-permute-done | bytes 131104 | tf_op jit(solution)/shard_map/ppermute | solution.py:47
  58.5 1.2 %merge.1 = bf16[1024,512]{1,0:T(8,128)(2,1)} custom-call(s32[1]{0:T(128)} %bitcast.me_ref, bf16[128,512]{1,0:T(8,128)(2,1)S(1)} %collective-permute-done.9.refs_0_, bf16[128,512]{1,0:T(8,128)(2,1)S(1)} %collective-permute-done.10.refs_1_, bf16[128,512]{1,0:T(8,128)(2,1)S(1)} %collective-permute-done.11.refs_2_, ...), custom_call_target="tpu_custom_call" | custom-call | flops 268435456 | bytes 2097152 | tf_op jit(solution)/shard_map/merge/pallas_call | solution.py:292
  (21 shorter events, 2.5 us)
Async XLA Ops:
  0.0 1.2 %copy-start.1 = (bf16[128,1,8,512]{3,2,1,0:T(8,128)(2,1)S(1)}, bf16[128,1,8,512]{3,2,1,0:T(8,128)(2,1)}, u32[]{:S(2)}) copy-start(bf16[128,1,8,512]{3,2,1,0:T(8,128)(2,1)} %param.5) | copy-start | bytes 3145732
  2.4 0.6 %copy-start.2 = (bf16[128,512]{1,0:T(8,128)(2,1)}, bf16[128,512]{1,0:T(8,128)(2,1)S(1)}, u32[]{:S(2)}) copy-start(bf16[128,512]{1,0:T(8,128)(2,1)S(1)} %get-tuple-element.34) | copy-start | bytes 393220
  3.0 18.9 %collective-permute-start.3 = (bf16[5,128,1024]{2,1,0:T(8,128)(2,1)}, bf16[5,128,1024]{2,1,0:T(8,128)(2,1)S(1)}, u32[]{:S(2)}, u32[]{:S(2)}) collective-permute-start(bf16[5,128,1024]{2,1,0:T(8,128)(2,1)} %bitcast.11), channel_id=1, source_target_pairs={{1,2},{2,1},{5,6},{6,5},{9,10},{10,9},{13,14},{14,13},{17,18},{18,... | collective-permute-start | bytes 3932168 | tf_op jit(solution)/shard_map/ppermute | solution.py:206
  3.8 10.0 %collective-permute-start.4 = (bf16[128,512]{1,0:T(8,128)(2,1)}, bf16[128,512]{1,0:T(8,128)(2,1)S(1)}, u32[]{:S(2)}, u32[]{:S(2)}) collective-permute-start(bf16[128,512]{1,0:T(8,128)(2,1)} %get-tuple-element.31), channel_id=1, source_target_pairs={{0,28},{4,24},{8,20},{12,16},{16,12},{20,8},{24,4},{28,0},{1,29},{... | collective-permute-start | bytes 393224 | tf_op jit(solution)/shard_map/ppermute | solution.py:47
  9.8 8.7 %collective-permute-start.5 = (bf16[128,512]{1,0:T(8,128)(2,1)}, bf16[128,512]{1,0:T(8,128)(2,1)S(1)}, u32[]{:S(2)}, u32[]{:S(2)}) collective-permute-start(bf16[128,512]{1,0:T(8,128)(2,1)} %get-tuple-element.32), channel_id=1, source_target_pairs={{0,24},{4,28},{8,16},{12,20},{16,8},{20,12},{24,0},{28,4},{1,25},{... | collective-permute-start | bytes 393224 | tf_op jit(solution)/shard_map/ppermute | solution.py:47
  10.0 11.9 %collective-permute-start.6 = (bf16[128,512]{1,0:T(8,128)(2,1)}, bf16[128,512]{1,0:T(8,128)(2,1)S(1)}, u32[]{:S(2)}, u32[]{:S(2)}) collective-permute-start(bf16[128,512]{1,0:T(8,128)(2,1)} %get-tuple-element.33), channel_id=1, source_target_pairs={{0,12},{4,8},{8,4},{12,0},{16,28},{20,24},{24,20},{28,16},{1,13},{... | collective-permute-start | bytes 393224 | tf_op jit(solution)/shard_map/ppermute | solution.py:47
  10.1 12.6 %collective-permute-start.2 = (bf16[5,128,1024]{2,1,0:T(8,128)(2,1)}, bf16[5,128,1024]{2,1,0:T(8,128)(2,1)S(1)}, u32[]{:S(2)}, u32[]{:S(2)}) collective-permute-start(bf16[5,128,1024]{2,1,0:T(8,128)(2,1)} %bitcast.12), channel_id=1, source_target_pairs={{0,1},{2,3},{1,0},{3,2},{4,5},{6,7},{5,4},{7,6},{8,9},{10,11},{9,8... | collective-permute-start | bytes 3932168 | tf_op jit(solution)/shard_map/ppermute | solution.py:206
  13.8 15.0 %collective-permute-start = (bf16[128,512]{1,0:T(8,128)(2,1)S(1)}, bf16[128,512]{1,0:T(8,128)(2,1)S(1)}, u32[]{:S(2)}, u32[]{:S(2)}) collective-permute-start(bf16[128,512]{1,0:T(8,128)(2,1)S(1)} %get-tuple-element.26), channel_id=1, source_target_pairs={{0,20},{4,16},{8,28},{12,24},{16,4},{20,0},{24,12},{28,8},{1,21},{... | collective-permute-start | bytes 393224 | tf_op jit(solution)/shard_map/ppermute | solution.py:47
  18.5 12.2 %collective-permute-start.1 = (bf16[128,512]{1,0:T(8,128)(2,1)S(1)}, bf16[128,512]{1,0:T(8,128)(2,1)S(1)}, u32[]{:S(2)}, u32[]{:S(2)}) collective-permute-start(bf16[128,512]{1,0:T(8,128)(2,1)S(1)} %get-tuple-element.27), channel_id=1, source_target_pairs={{0,16},{4,20},{8,24},{12,28},{16,0},{20,4},{24,8},{28,12},{1,17},{... | collective-permute-start | bytes 393224 | tf_op jit(solution)/shard_map/ppermute | solution.py:47
  21.9 5.4 %collective-permute-start.7 = (bf16[128,512]{1,0:T(8,128)(2,1)}, bf16[128,512]{1,0:T(8,128)(2,1)S(1)}, u32[]{:S(2)}, u32[]{:S(2)}) collective-permute-start(bf16[128,512]{1,0:T(8,128)(2,1)} %copy-done.2), channel_id=1, source_target_pairs={{0,8},{4,12},{8,0},{12,4},{16,24},{20,28},{24,16},{28,20},{1,9},{5... | collective-permute-start | bytes 393224 | tf_op jit(solution)/shard_map/ppermute | solution.py:47
  21.9 1.3 %copy-start = (bf16[1,1,5,128,1024]{4,3,2,1,0:T(8,128)(2,1)S(1)}, bf16[1,1,5,128,1024]{4,3,2,1,0:T(8,128)(2,1)}, u32[]{:S(2)}) copy-start(bf16[1,1,5,128,1024]{4,3,2,1,0:T(8,128)(2,1)} %param.6) | copy-start | bytes 3932164
  21.9 5.4 %collective-permute-start.8 = (bf16[128,512]{1,0:T(8,128)(2,1)S(1)}, bf16[128,512]{1,0:T(8,128)(2,1)S(1)}, u32[]{:S(2)}, u32[]{:S(2)}) collective-permute-start(bf16[128,512]{1,0:T(8,128)(2,1)S(1)} %get-tuple-element.35), channel_id=1, source_target_pairs={{0,4},{4,0},{8,12},{12,8},{16,20},{20,16},{24,28},{28,24},{1,5},{5... | collective-permute-start | bytes 393224 | tf_op jit(solution)/shard_map/ppermute | solution.py:47
  32.5 8.2 %collective-permute-start.9 = (bf16[128,512]{1,0:T(8,128)(2,1)S(1)}, bf16[128,512]{1,0:T(8,128)(2,1)S(1)}, u32[]{:S(2)}, u32[]{:S(2)}) collective-permute-start(bf16[128,512]{1,0:T(8,128)(2,1)S(1)} %get-tuple-element.39), channel_id=1, source_target_pairs={{0,28},{4,24},{8,20},{12,16},{16,12},{20,8},{24,4},{28,0},{1,29},{... | collective-permute-start | bytes 393224 | tf_op jit(solution)/shard_map/ppermute | solution.py:47
  34.5 7.1 %collective-permute-start.10 = (bf16[128,512]{1,0:T(8,128)(2,1)S(1)}, bf16[128,512]{1,0:T(8,128)(2,1)S(1)}, u32[]{:S(2)}, u32[]{:S(2)}) collective-permute-start(bf16[128,512]{1,0:T(8,128)(2,1)S(1)} %get-tuple-element.40), channel_id=1, source_target_pairs={{0,12},{4,8},{8,4},{12,0},{16,28},{20,24},{24,20},{28,16},{1,13},{... | collective-permute-start | bytes 393224 | tf_op jit(solution)/shard_map/ppermute | solution.py:47
  35.3 8.4 %collective-permute-start.11 = (bf16[128,512]{1,0:T(8,128)(2,1)S(1)}, bf16[128,512]{1,0:T(8,128)(2,1)S(1)}, u32[]{:S(2)}, u32[]{:S(2)}) collective-permute-start(bf16[128,512]{1,0:T(8,128)(2,1)S(1)} %get-tuple-element.41), channel_id=1, source_target_pairs={{0,24},{4,28},{8,16},{12,20},{16,8},{20,12},{24,0},{28,4},{1,25},{... | collective-permute-start | bytes 393224 | tf_op jit(solution)/shard_map/ppermute | solution.py:47
  36.8 9.3 %collective-permute-start.12 = (bf16[128,512]{1,0:T(8,128)(2,1)S(1)}, bf16[128,512]{1,0:T(8,128)(2,1)S(1)}, u32[]{:S(2)}, u32[]{:S(2)}) collective-permute-start(bf16[128,512]{1,0:T(8,128)(2,1)S(1)} %get-tuple-element.42), channel_id=1, source_target_pairs={{0,8},{4,12},{8,0},{12,4},{16,24},{20,28},{24,16},{28,20},{1,9},{5... | collective-permute-start | bytes 393224 | tf_op jit(solution)/shard_map/ppermute | solution.py:47
  38.4 13.6 %collective-permute-start.13 = (bf16[128,512]{1,0:T(8,128)(2,1)S(1)}, bf16[128,512]{1,0:T(8,128)(2,1)S(1)}, u32[]{:S(2)}, u32[]{:S(2)}) collective-permute-start(bf16[128,512]{1,0:T(8,128)(2,1)S(1)} %get-tuple-element.43), channel_id=1, source_target_pairs={{0,20},{4,16},{8,28},{12,24},{16,4},{20,0},{24,12},{28,8},{1,21},{... | collective-permute-start | bytes 393224 | tf_op jit(solution)/shard_map/ppermute | solution.py:47
  40.7 11.3 %collective-permute-start.14 = (bf16[128,512]{1,0:T(8,128)(2,1)S(1)}, bf16[128,512]{1,0:T(8,128)(2,1)S(1)}, u32[]{:S(2)}, u32[]{:S(2)}) collective-permute-start(bf16[128,512]{1,0:T(8,128)(2,1)S(1)} %get-tuple-element.44), channel_id=1, source_target_pairs={{0,4},{4,0},{8,12},{12,8},{16,20},{20,16},{24,28},{28,24},{1,5},{5... | collective-permute-start | bytes 393224 | tf_op jit(solution)/shard_map/ppermute | solution.py:47
  41.6 16.9 %collective-permute-start.15 = (bf16[128,512]{1,0:T(8,128)(2,1)S(1)}, bf16[128,512]{1,0:T(8,128)(2,1)S(1)}, u32[]{:S(2)}, u32[]{:S(2)}) collective-permute-start(bf16[128,512]{1,0:T(8,128)(2,1)S(1)} %get-tuple-element.45), channel_id=1, source_target_pairs={{0,16},{4,20},{8,24},{12,28},{16,0},{20,4},{24,8},{28,12},{1,17},{... | collective-permute-start | bytes 393224 | tf_op jit(solution)/shard_map/ppermute | solution.py:47

commit v15 on v11

--- a/solution.py
+++ b/solution.py
@@ -22,13 +22,10 @@
     return k // (count // PARTS) == PARTS // 2
 
 
-def partners(count):
+def outward(count):
     far = list(range(count - 1, count // 2 - 1, -1))
     near = list(range(count // 2 - 1, 0, -1))
-    order = []
-    for i in range(len(far)):
-        order += far[i : i + 1] + near[i : i + 1]
-    return order
+    return far[:1] + near[:1] + far[1:] + near[1:]
 
 
 def inward(count):
@@ -270,7 +267,7 @@
         cost_estimate=cost(1, 1),
         name="early",
     )(me, gram, ahead, *[arrived[k] for k in early])
-    back = partners(patches) + [0]
+    back = outward(patches) + [0]
     moved = pl.pallas_call(
         functools.partial(late_kernel, late, back),
         out_shape=[piece_shape] * patches,

time: 60.2 us -> 60.2 us (level)
  waiting for transfers between devices: 19.4 us -> 13.4 us
  starting transfers between devices: 29.3 us -> 35.3 us
    ppermute x14, starting transfers between devices: 24.8 us -> 30.8 us  [ppermute(): return lax.ppermute(value, axis, [(i, i ^ step) for i in range(count)])]
    ppermute x14, waiting for transfers between devices: 19.4 us -> 13.4 us  [ppermute(): return lax.ppermute(value, axis, [(i, i ^ step) for i in range(count)])]
  transfers between devices with their start and end apart: 16 -> 16, of which waited for: 7 -> 5; matrix products, arithmetic and copies ran while one was open for 1% -> 1% of each run, Pallas kernels for 7% -> 7%
where the time goes in v15:
time: 60.2 us; the launch traced here: 60 us
  starting transfers between devices  35.3 us (59%)
  waiting for transfers between devices  13.4 us (22%)
  Pallas kernels  8.57 us (14%)
  local copies, waits for them, and re-layouts  1.23 us (2%)
  other arithmetic  0.75 us (1%)
  between operations  0.75 us (1%)
    ppermute x14, starting transfers between devices, ppermute(): return lax.ppermute(value, axis, [(i, i ^ step) for i in range(count)])  30.8 us
    ppermute x14, waiting for transfers between devices, ppermute(): return lax.ppermute(value, axis, [(i, i ^ step) for i in range(count)])  13.4 us
    ppermute x2, starting transfers between devices, swap(): return lax.ppermute(store, 'region', pairs + [(j, i) for i, j in pairs])  4.53 us
    pallas_call x1, Pallas kernels, shards(): pl.pallas_call(functools.partial(gram_kernel, 1.0 / (2.0 * size)), out_sh...  1.98 us
    pallas_call x1, Pallas kernels, shards(): pl.pallas_call(functools.partial(late_kernel, late, back), out_shape=[pie...  1.81 us
    pallas_call x1, Pallas kernels, shards(): pl.pallas_call(functools.partial(early_kernel, first_steps + early), out_...  1.35 us
    pallas_call x1, Pallas kernels, shards(): pl.pallas_call(functools.partial(merge_kernel, order), out_shape=jax.Shap...  1.23 us
    unnamed x4, local copies, waits for them, and re-layouts  1.23 us
  transfers between devices with their start and end apart: 16, of which 5 were waited for; matrix products, arithmetic and copies ran while one was open for 1% of the time, Pallas kernels for 7%

profile of v15, /device:TPU:1, one launch (start us, length us, event | category | flops | bytes accessed | tf_op | source)
XLA Modules:
  0.0 60.0 jit_solution(428315520504979788)
XLA Ops:
  0.0 1.2 %copy-done.1 = bf16[128,1,8,512]{3,2,1,0:T(8,128)(2,1)S(1)} copy-done((bf16[128,1,8,512]{3,2,1,0:T(8,128)(2,1)S(1)}, bf16[128,1,8,512]{3,2,1,0:T(8,128)(2,1)}, u32[]{:S(2)}) %copy-start.1) | copy-done | bytes 1048600
  1.2 1.1 %split.1 = (bf16[128,512]{1,0:T(8,128)(2,1)S(1)}, bf16[128,512]{1,0:T(8,128)(2,1)}, bf16[128,512]{1,0:T(8,128)(2,1)}, bf16[128,512]{1,0:T(8,128)(2,1)S(1)}, bf16...) custom-call(s32[1]{0:T(128)} %bitcast.me_ref, ...), custom_call_target="tpu_custom_call" | custom-call | flops 268435456 | bytes 2097152 | tf_op jit(solution)/shard_map/split/pallas_call | solution.py:219
  2.4 4.5 %collective-permute-start.3 = (bf16[5,128,1024]{2,1,0:T(8,128)(2,1)}, bf16[5,128,1024]{2,1,0:T(8,128)(2,1)S(1)}, u32[]{:S(2)}, u32[]{:S(2)}) collective-permute-start(bf16[5,128,1024]{2,1,0:T(8,128)(2,1)} %bitcast.11), channel_id=1, source_target_pairs={{1,2},{2,1},{5,6},{6,5},{9,10},{10,9},{13,14},{14,13},{17,18},{18,... | collective-permute-start | bytes 3932168 | tf_op jit(solution)/shard_map/ppermute | solution.py:204
  6.9 4.3 %collective-permute-start.4 = (bf16[128,512]{1,0:T(8,128)(2,1)}, bf16[128,512]{1,0:T(8,128)(2,1)S(1)}, u32[]{:S(2)}, u32[]{:S(2)}) collective-permute-start(bf16[128,512]{1,0:T(8,128)(2,1)} %get-tuple-element.28), channel_id=1, source_target_pairs={{0,28},{4,24},{8,20},{12,16},{16,12},{20,8},{24,4},{28,0},{1,29},{... | collective-permute-start | bytes 393224 | tf_op jit(solution)/shard_map/ppermute | solution.py:44
  11.9 0.7 %pad_add_fusion.table_ref = s32[7]{0:T(128)S(1)} fusion(s32[1]{0:T(128)} %bitcast.10, s32[3]{0:T(128)} %bitcast.15, s32[3]{0:T(128)} %bitcast.16), kind=kLoop, calls=%fused_computation | loop fusion | flops 14 | bytes 56 | tf_op jit(solution)/shard_map/concatenate | solution.py:232
  12.6 2.3 %collective-permute-done.4.refs_0_ = bf16[128,512]{1,0:T(8,128)(2,1)S(1)} collective-permute-done((bf16[128,512]{1,0:T(8,128)(2,1)}, bf16[128,512]{1,0:T(8,128)(2,1)S(1)}, u32[]{:S(2)}, u32[]{:S(2)}) %collective-permute-start.4) | collective-permute-done | bytes 131104 | tf_op jit(solution)/shard_map/ppermute | solution.py:44
  14.9 7.3 %collective-permute-start = (bf16[128,512]{1,0:T(8,128)(2,1)S(1)}, bf16[128,512]{1,0:T(8,128)(2,1)S(1)}, u32[]{:S(2)}, u32[]{:S(2)}) collective-permute-start(bf16[128,512]{1,0:T(8,128)(2,1)S(1)} %get-tuple-element.24), channel_id=1, source_target_pairs={{0,20},{4,16},{8,28},{12,24},{16,4},{20,0},{24,12},{28,8},{1,21},{... | collective-permute-start | bytes 393224 | tf_op jit(solution)/shard_map/ppermute | solution.py:44
  22.2 6.4 %collective-permute-start.1 = (bf16[128,512]{1,0:T(8,128)(2,1)S(1)}, bf16[128,512]{1,0:T(8,128)(2,1)S(1)}, u32[]{:S(2)}, u32[]{:S(2)}) collective-permute-start(bf16[128,512]{1,0:T(8,128)(2,1)S(1)} %get-tuple-element.25), channel_id=1, source_target_pairs={{0,16},{4,20},{8,24},{12,28},{16,0},{20,4},{24,8},{28,12},{1,17},{... | collective-permute-start | bytes 393224 | tf_op jit(solution)/shard_map/ppermute | solution.py:44
  28.6 0.3 collective-permute-start.8
  29.0 1.1 %ahead.1.ahead_ref = bf16[3,128,512]{2,1,0:T(8,128)(2,1)S(1)} custom-call(bf16[128,512]{1,0:T(8,128)(2,1)S(1)} %collective-permute-done.4.refs_0_, bf16[128,512]{1,0:T(8,128)(2,1)} %collective-permute-done.5.refs_1_, bf16[128,512]{1,0:T(8,128)(2,1)} %collective-permute-done.6.refs_2_), custom_call_target="tpu_custom_call" | custom-call | flops 21474836480 | bytes 786432 | tf_op jit(solution)/shard_map/ahead/pallas_call | solution.py:252
  30.1 2.0 %gram.1.gram_ref.refs_2_ = bf16[1024,1024]{1,0:T(8,128)(2,1)S(1)} custom-call(s32[1]{0:T(128)} %bitcast.2.region_ref, s32[7]{0:T(128)S(1)} %pad_add_fusion.table_ref, bf16[5,128,1024]{2,1,0:T(8,128)(2,1)S(1)} %bitcast.13, bf16[5,128,1024]{2,1,0:T(8,128)(2,1)S(1)} %collective-permute-done.2.even, bf16[5,128,1024]{2,1,0:T(8,128)(2,1)S(1)} %collective-permute-done.3.odd), custom_call_target="tpu_custom_call" | custom-call | flops 805306368 | bytes 4194304 | tf_op jit(solution)/shard_map/gram/pallas_call | solution.py:233
  32.0 1.5 %collective-permute-done.7.refs_0_ = bf16[128,512]{1,0:T(8,128)(2,1)S(1)} collective-permute-done((bf16[128,512]{1,0:T(8,128)(2,1)S(1)}, bf16[128,512]{1,0:T(8,128)(2,1)S(1)}, u32[]{:S(2)}, u32[]{:S(2)}) %collective-permute-start.7) | collective-permute-done | bytes 131104 | tf_op jit(solution)/shard_map/ppermute | solution.py:44
  33.6 1.4 %early.1 = (f32[1024,512]{1,0:T(8,128)S(1)}, bf16[1024,512]{1,0:T(8,128)(2,1)S(1)}) custom-call(s32[1]{0:T(128)} %bitcast.me_ref, bf16[1024,1024]{1,0:T(8,128)(2,1)S(1)} %gram.1.gram_ref.refs_2_, bf16[3,128,512]{2,1,0:T(8,128)(2,1)S(1)} %ahead.1.ahead_ref, bf16[128,512]{1,0:T(8,128)(2,1)S(1)} %collective-permute-done.7.refs_0_, ...), custom_call_target="tpu_custom_call" | custom-call | flops 1 | bytes 1 | tf_op jit(solution)/shard_map/early/pallas_call | solution.py:261
  35.0 1.8 %late.1 = (bf16[128,512]{1,0:T(8,128)(2,1)S(1)}, bf16[128,512]{1,0:T(8,128)(2,1)S(1)}, bf16[128,512]{1,0:T(8,128)(2,1)S(1)}, bf16[128,512]{1,0:T(8,128)(2,1)S(1)...) custom-call(s32[1]{0:T(128)} %bitcast.me_ref, ...), custom_call_target="tpu_custom_call" | custom-call | flops 1610612736 | bytes 7340032 | tf_op jit(solution)/shard_map/late/pallas_call | solution.py:271
  36.8 0.8 %collective-permute-start.9 = (bf16[128,512]{1,0:T(8,128)(2,1)S(1)}, bf16[128,512]{1,0:T(8,128)(2,1)S(1)}, u32[]{:S(2)}, u32[]{:S(2)}) collective-permute-start(bf16[128,512]{1,0:T(8,128)(2,1)S(1)} %get-tuple-element.35), channel_id=1, source_target_pairs={{0,28},{4,24},{8,20},{12,16},{16,12},{20,8},{24,4},{28,0},{1,29},{... | collective-permute-start | bytes 393224 | tf_op jit(solution)/shard_map/ppermute | solution.py:44
  37.6 2.8 %collective-permute-start.11 = (bf16[128,512]{1,0:T(8,128)(2,1)S(1)}, bf16[128,512]{1,0:T(8,128)(2,1)S(1)}, u32[]{:S(2)}, u32[]{:S(2)}) collective-permute-start(bf16[128,512]{1,0:T(8,128)(2,1)S(1)} %get-tuple-element.37), channel_id=1, source_target_pairs={{0,24},{4,28},{8,16},{12,20},{16,8},{20,12},{24,0},{28,4},{1,25},{... | collective-permute-start | bytes 393224 | tf_op jit(solution)/shard_map/ppermute | solution.py:44
  40.4 0.8 %collective-permute-start.12 = (bf16[128,512]{1,0:T(8,128)(2,1)S(1)}, bf16[128,512]{1,0:T(8,128)(2,1)S(1)}, u32[]{:S(2)}, u32[]{:S(2)}) collective-permute-start(bf16[128,512]{1,0:T(8,128)(2,1)S(1)} %get-tuple-element.38), channel_id=1, source_target_pairs={{0,20},{4,16},{8,28},{12,24},{16,4},{20,0},{24,12},{28,8},{1,21},{... | collective-permute-start | bytes 393224 | tf_op jit(solution)/shard_map/ppermute | solution.py:44
  41.3 2.1 %collective-permute-start.13 = (bf16[128,512]{1,0:T(8,128)(2,1)S(1)}, bf16[128,512]{1,0:T(8,128)(2,1)S(1)}, u32[]{:S(2)}, u32[]{:S(2)}) collective-permute-start(bf16[128,512]{1,0:T(8,128)(2,1)S(1)} %get-tuple-element.39), channel_id=1, source_target_pairs={{0,16},{4,20},{8,24},{12,28},{16,0},{20,4},{24,8},{28,12},{1,17},{... | collective-permute-start | bytes 393224 | tf_op jit(solution)/shard_map/ppermute | solution.py:44
  43.4 1.4 %collective-permute-done.9.refs_0_ = bf16[128,512]{1,0:T(8,128)(2,1)S(1)} collective-permute-done((bf16[128,512]{1,0:T(8,128)(2,1)S(1)}, bf16[128,512]{1,0:T(8,128)(2,1)S(1)}, u32[]{:S(2)}, u32[]{:S(2)}) %collective-permute-start.9) | collective-permute-done | bytes 131104 | tf_op jit(solution)/shard_map/ppermute | solution.py:44
  44.8 5.2 %collective-permute-start.14 = (bf16[128,512]{1,0:T(8,128)(2,1)S(1)}, bf16[128,512]{1,0:T(8,128)(2,1)S(1)}, u32[]{:S(2)}, u32[]{:S(2)}) collective-permute-start(bf16[128,512]{1,0:T(8,128)(2,1)S(1)} %get-tuple-element.40), channel_id=1, source_target_pairs={{0,8},{4,12},{8,0},{12,4},{16,24},{20,28},{24,16},{28,20},{1,9},{5... | collective-permute-start | bytes 393224 | tf_op jit(solution)/shard_map/ppermute | solution.py:44
  50.0 0.7 %collective-permute-start.15 = (bf16[128,512]{1,0:T(8,128)(2,1)S(1)}, bf16[128,512]{1,0:T(8,128)(2,1)S(1)}, u32[]{:S(2)}, u32[]{:S(2)}) collective-permute-start(bf16[128,512]{1,0:T(8,128)(2,1)S(1)} %get-tuple-element.41), channel_id=1, source_target_pairs={{0,4},{4,0},{8,12},{12,8},{16,20},{20,16},{24,28},{28,24},{1,5},{5... | collective-permute-start | bytes 393224 | tf_op jit(solution)/shard_map/ppermute | solution.py:44
  50.6 6.7 %collective-permute-done.12.refs_3_ = bf16[128,512]{1,0:T(8,128)(2,1)S(1)} collective-permute-done((bf16[128,512]{1,0:T(8,128)(2,1)S(1)}, bf16[128,512]{1,0:T(8,128)(2,1)S(1)}, u32[]{:S(2)}, u32[]{:S(2)}) %collective-permute-start.12) | collective-permute-done | bytes 131104 | tf_op jit(solution)/shard_map/ppermute | solution.py:44
  57.4 1.4 %collective-permute-done.13.refs_4_ = bf16[128,512]{1,0:T(8,128)(2,1)S(1)} collective-permute-done((bf16[128,512]{1,0:T(8,128)(2,1)S(1)}, bf16[128,512]{1,0:T(8,128)(2,1)S(1)}, u32[]{:S(2)}, u32[]{:S(2)}) %collective-permute-start.13) | collective-permute-done | bytes 131104 | tf_op jit(solution)/shard_map/ppermute | solution.py:44
  58.8 1.2 %merge.1 = bf16[1024,512]{1,0:T(8,128)(2,1)} custom-call(s32[1]{0:T(128)} %bitcast.me_ref, bf16[128,512]{1,0:T(8,128)(2,1)S(1)} %collective-permute-done.9.refs_0_, bf16[128,512]{1,0:T(8,128)(2,1)S(1)} %collective-permute-done.10.refs_1_, bf16[128,512]{1,0:T(8,128)(2,1)S(1)} %collective-permute-done.11.refs_2_, ...), custom_call_target="tpu_custom_call" | custom-call | flops 268435456 | bytes 2097152 | tf_op jit(solution)/shard_map/merge/pallas_call | solution.py:289
  (19 shorter events, 0.2 us)
Async XLA Ops:
  0.0 1.2 %copy-start.1 = (bf16[128,1,8,512]{3,2,1,0:T(8,128)(2,1)S(1)}, bf16[128,1,8,512]{3,2,1,0:T(8,128)(2,1)}, u32[]{:S(2)}) copy-start(bf16[128,1,8,512]{3,2,1,0:T(8,128)(2,1)} %param.5) | copy-start | bytes 3145732
  2.4 26.3 %collective-permute-start.3 = (bf16[5,128,1024]{2,1,0:T(8,128)(2,1)}, bf16[5,128,1024]{2,1,0:T(8,128)(2,1)S(1)}, u32[]{:S(2)}, u32[]{:S(2)}) collective-permute-start(bf16[5,128,1024]{2,1,0:T(8,128)(2,1)} %bitcast.11), channel_id=1, source_target_pairs={{1,2},{2,1},{5,6},{6,5},{9,10},{10,9},{13,14},{14,13},{17,18},{18,... | collective-permute-start | bytes 3932168 | tf_op jit(solution)/shard_map/ppermute | solution.py:204
  6.9 8.0 %collective-permute-start.4 = (bf16[128,512]{1,0:T(8,128)(2,1)}, bf16[128,512]{1,0:T(8,128)(2,1)S(1)}, u32[]{:S(2)}, u32[]{:S(2)}) collective-permute-start(bf16[128,512]{1,0:T(8,128)(2,1)} %get-tuple-element.28), channel_id=1, source_target_pairs={{0,28},{4,24},{8,20},{12,16},{16,12},{20,8},{24,4},{28,0},{1,29},{... | collective-permute-start | bytes 393224 | tf_op jit(solution)/shard_map/ppermute | solution.py:44
  11.2 11.0 %collective-permute-start.5 = (bf16[128,512]{1,0:T(8,128)(2,1)}, bf16[128,512]{1,0:T(8,128)(2,1)}, u32[]{:S(2)}, u32[]{:S(2)}) collective-permute-start(bf16[128,512]{1,0:T(8,128)(2,1)} %get-tuple-element.29), channel_id=1, source_target_pairs={{0,24},{4,28},{8,16},{12,20},{16,8},{20,12},{24,0},{28,4},{1,25},{... | collective-permute-start | bytes 393224 | tf_op jit(solution)/shard_map/ppermute | solution.py:44
  11.2 17.4 %collective-permute-start.6 = (bf16[128,512]{1,0:T(8,128)(2,1)S(1)}, bf16[128,512]{1,0:T(8,128)(2,1)}, u32[]{:S(2)}, u32[]{:S(2)}) collective-permute-start(bf16[128,512]{1,0:T(8,128)(2,1)S(1)} %get-tuple-element.30), channel_id=1, source_target_pairs={{0,12},{4,8},{8,4},{12,0},{16,28},{20,24},{24,20},{28,16},{1,13},{... | collective-permute-start | bytes 393224 | tf_op jit(solution)/shard_map/ppermute | solution.py:44
  11.2 18.8 %collective-permute-start.2 = (bf16[5,128,1024]{2,1,0:T(8,128)(2,1)}, bf16[5,128,1024]{2,1,0:T(8,128)(2,1)S(1)}, u32[]{:S(2)}, u32[]{:S(2)}) collective-permute-start(bf16[5,128,1024]{2,1,0:T(8,128)(2,1)} %bitcast.12), channel_id=1, source_target_pairs={{0,1},{2,3},{1,0},{3,2},{4,5},{6,7},{5,4},{7,6},{8,9},{10,11},{9,8... | collective-permute-start | bytes 3932168 | tf_op jit(solution)/shard_map/ppermute | solution.py:204
  14.9 20.0 %collective-permute-start = (bf16[128,512]{1,0:T(8,128)(2,1)S(1)}, bf16[128,512]{1,0:T(8,128)(2,1)S(1)}, u32[]{:S(2)}, u32[]{:S(2)}) collective-permute-start(bf16[128,512]{1,0:T(8,128)(2,1)S(1)} %get-tuple-element.24), channel_id=1, source_target_pairs={{0,20},{4,16},{8,28},{12,24},{16,4},{20,0},{24,12},{28,8},{1,21},{... | collective-permute-start | bytes 393224 | tf_op jit(solution)/shard_map/ppermute | solution.py:44
  22.2 12.7 %collective-permute-start.1 = (bf16[128,512]{1,0:T(8,128)(2,1)S(1)}, bf16[128,512]{1,0:T(8,128)(2,1)S(1)}, u32[]{:S(2)}, u32[]{:S(2)}) collective-permute-start(bf16[128,512]{1,0:T(8,128)(2,1)S(1)} %get-tuple-element.25), channel_id=1, source_target_pairs={{0,16},{4,20},{8,24},{12,28},{16,0},{20,4},{24,8},{28,12},{1,17},{... | collective-permute-start | bytes 393224 | tf_op jit(solution)/shard_map/ppermute | solution.py:44
  28.6 4.9 %collective-permute-start.7 = (bf16[128,512]{1,0:T(8,128)(2,1)S(1)}, bf16[128,512]{1,0:T(8,128)(2,1)S(1)}, u32[]{:S(2)}, u32[]{:S(2)}) collective-permute-start(bf16[128,512]{1,0:T(8,128)(2,1)S(1)} %get-tuple-element.31), channel_id=1, source_target_pairs={{0,8},{4,12},{8,0},{12,4},{16,24},{20,28},{24,16},{28,20},{1,9},{5... | collective-permute-start | bytes 393224 | tf_op jit(solution)/shard_map/ppermute | solution.py:44
  28.6 1.4 %copy-start = (bf16[1,1,5,128,1024]{4,3,2,1,0:T(8,128)(2,1)S(1)}, bf16[1,1,5,128,1024]{4,3,2,1,0:T(8,128)(2,1)}, u32[]{:S(2)}) copy-start(bf16[1,1,5,128,1024]{4,3,2,1,0:T(8,128)(2,1)} %param.6) | copy-start | bytes 3932164
  28.6 4.9 %collective-permute-start.8 = (bf16[128,512]{1,0:T(8,128)(2,1)S(1)}, bf16[128,512]{1,0:T(8,128)(2,1)S(1)}, u32[]{:S(2)}, u32[]{:S(2)}) collective-permute-start(bf16[128,512]{1,0:T(8,128)(2,1)S(1)} %get-tuple-element.32), channel_id=1, source_target_pairs={{0,4},{4,0},{8,12},{12,8},{16,20},{20,16},{24,28},{28,24},{1,5},{5... | collective-permute-start | bytes 393224 | tf_op jit(solution)/shard_map/ppermute | solution.py:44
  36.8 8.0 %collective-permute-start.9 = (bf16[128,512]{1,0:T(8,128)(2,1)S(1)}, bf16[128,512]{1,0:T(8,128)(2,1)S(1)}, u32[]{:S(2)}, u32[]{:S(2)}) collective-permute-start(bf16[128,512]{1,0:T(8,128)(2,1)S(1)} %get-tuple-element.35), channel_id=1, source_target_pairs={{0,28},{4,24},{8,20},{12,16},{16,12},{20,8},{24,4},{28,0},{1,29},{... | collective-permute-start | bytes 393224 | tf_op jit(solution)/shard_map/ppermute | solution.py:44
  37.5 12.4 %collective-permute-start.10 = (bf16[128,512]{1,0:T(8,128)(2,1)S(1)}, bf16[128,512]{1,0:T(8,128)(2,1)S(1)}, u32[]{:S(2)}, u32[]{:S(2)}) collective-permute-start(bf16[128,512]{1,0:T(8,128)(2,1)S(1)} %get-tuple-element.36), channel_id=1, source_target_pairs={{0,12},{4,8},{8,4},{12,0},{16,28},{20,24},{24,20},{28,16},{1,13},{... | collective-permute-start | bytes 393224 | tf_op jit(solution)/shard_map/ppermute | solution.py:44
  37.6 13.0 %collective-permute-start.11 = (bf16[128,512]{1,0:T(8,128)(2,1)S(1)}, bf16[128,512]{1,0:T(8,128)(2,1)S(1)}, u32[]{:S(2)}, u32[]{:S(2)}) collective-permute-start(bf16[128,512]{1,0:T(8,128)(2,1)S(1)} %get-tuple-element.37), channel_id=1, source_target_pairs={{0,24},{4,28},{8,16},{12,20},{16,8},{20,12},{24,0},{28,4},{1,25},{... | collective-permute-start | bytes 393224 | tf_op jit(solution)/shard_map/ppermute | solution.py:44
  40.4 17.0 %collective-permute-start.12 = (bf16[128,512]{1,0:T(8,128)(2,1)S(1)}, bf16[128,512]{1,0:T(8,128)(2,1)S(1)}, u32[]{:S(2)}, u32[]{:S(2)}) collective-permute-start(bf16[128,512]{1,0:T(8,128)(2,1)S(1)} %get-tuple-element.38), channel_id=1, source_target_pairs={{0,20},{4,16},{8,28},{12,24},{16,4},{20,0},{24,12},{28,8},{1,21},{... | collective-permute-start | bytes 393224 | tf_op jit(solution)/shard_map/ppermute | solution.py:44
  41.3 17.6 %collective-permute-start.13 = (bf16[128,512]{1,0:T(8,128)(2,1)S(1)}, bf16[128,512]{1,0:T(8,128)(2,1)S(1)}, u32[]{:S(2)}, u32[]{:S(2)}) collective-permute-start(bf16[128,512]{1,0:T(8,128)(2,1)S(1)} %get-tuple-element.39), channel_id=1, source_target_pairs={{0,16},{4,20},{8,24},{12,28},{16,0},{20,4},{24,8},{28,12},{1,17},{... | collective-permute-start | bytes 393224 | tf_op jit(solution)/shard_map/ppermute | solution.py:44
  44.8 14.0 %collective-permute-start.14 = (bf16[128,512]{1,0:T(8,128)(2,1)S(1)}, bf16[128,512]{1,0:T(8,128)(2,1)S(1)}, u32[]{:S(2)}, u32[]{:S(2)}) collective-permute-start(bf16[128,512]{1,0:T(8,128)(2,1)S(1)} %get-tuple-element.40), channel_id=1, source_target_pairs={{0,8},{4,12},{8,0},{12,4},{16,24},{20,28},{24,16},{28,20},{1,9},{5... | collective-permute-start | bytes 393224 | tf_op jit(solution)/shard_map/ppermute | solution.py:44
  50.0 8.8 %collective-permute-start.15 = (bf16[128,512]{1,0:T(8,128)(2,1)S(1)}, bf16[128,512]{1,0:T(8,128)(2,1)S(1)}, u32[]{:S(2)}, u32[]{:S(2)}) collective-permute-start(bf16[128,512]{1,0:T(8,128)(2,1)S(1)} %get-tuple-element.41), channel_id=1, source_target_pairs={{0,4},{4,0},{8,12},{12,8},{16,20},{20,16},{24,28},{28,24},{1,5},{5... | collective-permute-start | bytes 393224 | tf_op jit(solution)/shard_map/ppermute | solution.py:44
